TPU v7x, 32 devices: a whole 2x2x4 slice. The times are simulated.
32 devices in a mesh: dp: 8 (over z, x), fsdp: 4 (over y, core).
Axes of the slice: x: 2, y: 2, z: 4, core: 2. Of those that a mesh axis runs over, the one named last changes fastest.
Arguments:
- counts: bfloat16 [8192, 13500], P(('dp', 'fsdp')), may hold values from 0 to 8
- library: float32 [8192], P(('dp', 'fsdp')), may hold values from 1000 to 100000
- coords: int32 [2, 8192], P(None, ('dp', 'fsdp')), may hold values from 0 to 2047
- lengths: int32 [8, 1], P('dp'), may hold values from 768 to 1024, as said below
- cotangent: bfloat16 [8192, 13500], P(('dp', 'fsdp')), may hold values from -6 to 6
- w_enc: bfloat16 [13500, 1024], P(None, ('dp', 'fsdp')), may hold values from -0.0546875 to 0.0546875
- w_qkv: bfloat16 [1024, 3072], P(('dp', 'fsdp')), may hold values from -0.25 to 0.25
- w_out: bfloat16 [1024, 1024], P(('dp', 'fsdp')), may hold values from -1 to 1
- gain_one: bfloat16 [1024], P(('dp', 'fsdp')), may hold values from 0.5 to 1.5
- shift_one: bfloat16 [1024], P(('dp', 'fsdp')), may hold values from -3 to 3
- w_up: bfloat16 [1024, 4096], P(('dp', 'fsdp')), may hold values from -0.1875 to 0.1875
- w_down: bfloat16 [4096, 1024], P(('dp', 'fsdp')), may hold values from -0.09375 to 0.09375
- gain_two: bfloat16 [1024], P(('dp', 'fsdp')), may hold values from 0.5 to 1.5
- shift_two: bfloat16 [1024], P(('dp', 'fsdp')), may hold values from -3 to 3
- w_dec: bfloat16 [13500, 1024], P(None, ('dp', 'fsdp')), may hold values from -0.1875 to 0.1875
Outputs:
- logits: bfloat16 [8192, 13500], P(('dp', 'fsdp'))
- counts_grad: float32 [8192, 13500], P(('dp', 'fsdp'))
- grad_enc: float32 [13500, 1024], P(None, ('dp', 'fsdp'))
- grad_qkv: float32 [1024, 3072], P(('dp', 'fsdp'))
- grad_out: float32 [1024, 1024], P(('dp', 'fsdp'))
- grad_gain_one: float32 [1024], P(('dp', 'fsdp'))
- grad_shift_one: float32 [1024], P(('dp', 'fsdp'))
- grad_up: float32 [1024, 4096], P(('dp', 'fsdp'))
- grad_down: float32 [4096, 1024], P(('dp', 'fsdp'))
- grad_gain_two: float32 [1024], P(('dp', 'fsdp'))
- grad_shift_two: float32 [1024], P(('dp', 'fsdp'))
- grad_dec: float32 [13500, 1024], P(None, ('dp', 'fsdp'))
Inputs may be any that keep to these rules, and one draw needn't show every extreme that they name: `lengths`: each group holds 1 slide starting at its first slot; the slots after it are padding. In every draw some group has no padding.
All inputs are finite; a program needn't handle non-finite values.
Results may differ from a plain program's by a relative error of at most 0.012.
Values may be sent and summed in bfloat16 or wider, within the bound.
A program may use at most 576 MiB of HBM per device.

v0:
```python
import math

import jax
import jax.numpy as jnp
from jax import lax
from jax.sharding import PartitionSpec as P

HEADS = 16


eps = 1e-05


def layer_norm(value, gain, shift):
    mean = jnp.mean(value, axis=1, keepdims=True)
    centred = value - mean
    variance = jnp.mean(centred * centred, axis=1, keepdims=True)
    return centred * lax.rsqrt(variance + eps) * gain + shift


def positions(coords, width):
    quarter = width // 4
    freqs = 0.05 * jnp.exp(-jnp.arange(quarter, dtype=jnp.float32) * (math.log(10000.0) / quarter))
    along_x = coords[0].astype(jnp.float32)[:, None] * freqs[None, :]
    along_y = coords[1].astype(jnp.float32)[:, None] * freqs[None, :]
    return jnp.concatenate(
        [jnp.sin(along_x), jnp.cos(along_x), jnp.sin(along_y), jnp.cos(along_y)], axis=1
    )


def contract_rows(left, right):
    return lax.dot_general(
        left, right, (((0,), (0,)), ((), ())), preferred_element_type=jnp.float32
    )


def contract_cols(left, right):
    return lax.dot_general(
        left, right, (((1,), (1,)), ((), ())), preferred_element_type=jnp.float32
    )


def matmul(left, right):
    return jnp.dot(left, right, preferred_element_type=jnp.float32)


def reduce_columns(term, owned):
    return lax.psum_scatter(
        term(jnp.int32(0), lax.axis_size(("dp", "fsdp")) * owned),
        ("dp", "fsdp"),
        scatter_dimension=0,
        tiled=True,
    )


def on_device(
    counts,
    library,
    coords,
    lengths,
    cotangent,
    w_enc,
    w_qkv,
    w_out,
    gain_one,
    shift_one,
    w_up,
    w_down,
    gain_two,
    shift_two,
    w_dec,
):
    rows = counts.shape[0]
    width = w_qkv.shape[1] // 3
    heads = HEADS
    head_width = width // heads
    att_scale = head_width ** (-0.5)
    group_size = lax.axis_size("fsdp")
    slots = rows * group_size
    owned = w_dec.shape[1]
    scale = 10000.0 / library
    counts_f = counts.astype(jnp.float32)
    xb = jnp.log1p(counts_f * scale[:, None]).astype(jnp.bfloat16)
    pe = positions(coords, width)
    ends = jnp.cumsum(lengths[0])
    place = jnp.arange(slots, dtype=jnp.int32)
    seg_all = jnp.sum((place[:, None] >= ends[None, :]).astype(jnp.int32), axis=1)
    seg_mine = lax.dynamic_slice_in_dim(seg_all, lax.axis_index("fsdp") * rows, rows)
    same = (seg_mine[:, None] == seg_all[None, :])[None]
    h0 = matmul(xb, lax.all_gather(w_enc, ("dp", "fsdp"), axis=1, tiled=True)) + pe
    qkv_all, out_all, g1_all, b1_all = (
        lax.all_gather(w_qkv, ("dp", "fsdp"), axis=0, tiled=True),
        lax.all_gather(w_out, ("dp", "fsdp"), axis=0, tiled=True),
        lax.all_gather(gain_one, ("dp", "fsdp"), axis=0, tiled=True),
        lax.all_gather(shift_one, ("dp", "fsdp"), axis=0, tiled=True),
    )
    a1 = layer_norm(h0, g1_all.astype(jnp.float32), b1_all.astype(jnp.float32)).astype(jnp.bfloat16)
    qkv = matmul(a1, qkv_all).astype(jnp.bfloat16)
    query = qkv[:, :width].reshape(rows, heads, head_width)
    kv_all = lax.all_gather(qkv[:, width:], "fsdp", axis=0, tiled=True)
    keys = kv_all[:, :width].reshape(slots, heads, head_width)
    values = kv_all[:, width:].reshape(slots, heads, head_width)

    def scores_of():
        raw = (
            jnp.einsum("qhd,khd->hqk", query, keys, preferred_element_type=jnp.float32) * att_scale
        )
        return jnp.where(same, raw, -1000000000.0)

    scores = scores_of()
    top = jnp.max(scores, axis=-1, keepdims=True)
    expo = jnp.exp(scores - top)
    total = jnp.sum(expo, axis=-1, keepdims=True)
    log_total = top + jnp.log(total)
    probs_b = (expo / total).astype(jnp.bfloat16)
    attended = jnp.einsum("hqk,khd->qhd", probs_b, values, preferred_element_type=jnp.float32)
    attended_b = attended.reshape(rows, width).astype(jnp.bfloat16)
    h1 = h0 + matmul(attended_b, out_all)
    up_all, down_all, g2_all, b2_all = (
        lax.all_gather(w_up, ("dp", "fsdp"), axis=0, tiled=True),
        lax.all_gather(w_down, ("dp", "fsdp"), axis=0, tiled=True),
        lax.all_gather(gain_two, ("dp", "fsdp"), axis=0, tiled=True),
        lax.all_gather(shift_two, ("dp", "fsdp"), axis=0, tiled=True),
    )
    a2 = layer_norm(h1, g2_all.astype(jnp.float32), b2_all.astype(jnp.float32)).astype(jnp.bfloat16)
    hidden = matmul(a2, up_all)
    act = jax.nn.gelu(hidden, approximate=False).astype(jnp.bfloat16)
    h2 = h1 + matmul(act, down_all)
    hb = h2.astype(jnp.bfloat16)
    columns = hb
    logits = contract_cols(columns, lax.all_gather(w_dec, ("dp", "fsdp"), axis=1, tiled=True))
    logits = logits.astype(jnp.bfloat16)

    def dec_term(start, count):
        return contract_rows(hb, cotangent)

    grad_dec = reduce_columns(dec_term, owned).T
    dh2 = matmul(cotangent, lax.all_gather(w_dec, ("dp", "fsdp"), axis=1, tiled=True))
    qkv_back, out_back, g1_all, b1_all, up_back, down_back, g2_all, b2_all = (
        lax.all_gather(w_qkv, ("dp", "fsdp"), axis=0, tiled=True),
        lax.all_gather(w_out, ("dp", "fsdp"), axis=0, tiled=True),
        lax.all_gather(gain_one, ("dp", "fsdp"), axis=0, tiled=True),
        lax.all_gather(shift_one, ("dp", "fsdp"), axis=0, tiled=True),
        lax.all_gather(w_up, ("dp", "fsdp"), axis=0, tiled=True),
        lax.all_gather(w_down, ("dp", "fsdp"), axis=0, tiled=True),
        lax.all_gather(gain_two, ("dp", "fsdp"), axis=0, tiled=True),
        lax.all_gather(shift_two, ("dp", "fsdp"), axis=0, tiled=True),
    )
    g1f = g1_all.astype(jnp.float32)
    b1f = b1_all.astype(jnp.float32)
    g2f = g2_all.astype(jnp.float32)
    b2f = b2_all.astype(jnp.float32)
    dfb = dh2.astype(jnp.bfloat16)
    grad_down = contract_rows(act, dfb)
    d_act = contract_cols(dfb, down_back)
    slope = jax.vjp(lambda v: jax.nn.gelu(v, approximate=False), hidden)[1](d_act)[0]
    d_hidden = slope.astype(jnp.bfloat16)
    grad_up = contract_rows(a2, d_hidden)
    da2 = contract_cols(d_hidden, up_back)
    norm_pull = jax.vjp(layer_norm, h1, g2f, b2f)[1]
    dh1_norm, grad_gain_two, grad_shift_two = norm_pull(da2)
    dh1 = dh2 + dh1_norm
    grad_up, grad_down, grad_gain_two, grad_shift_two = (
        lax.psum_scatter(grad_up, ("dp", "fsdp"), scatter_dimension=0, tiled=True),
        lax.psum_scatter(grad_down, ("dp", "fsdp"), scatter_dimension=0, tiled=True),
        lax.psum_scatter(grad_gain_two, ("dp", "fsdp"), scatter_dimension=0, tiled=True),
        lax.psum_scatter(grad_shift_two, ("dp", "fsdp"), scatter_dimension=0, tiled=True),
    )
    dab = dh1.astype(jnp.bfloat16)
    grad_out = contract_rows(attended_b, dab)
    d_attended = contract_cols(dab, out_back).astype(jnp.bfloat16).reshape(rows, heads, head_width)
    probs = jnp.exp(scores_of() - log_total)
    probs_b = probs.astype(jnp.bfloat16)
    d_probs = jnp.einsum("qhd,khd->hqk", d_attended, values, preferred_element_type=jnp.float32)
    inner = jnp.sum(probs * d_probs, axis=-1, keepdims=True)
    d_scores = (probs * (d_probs - inner)).astype(jnp.bfloat16)
    d_query = (
        jnp.einsum("hqk,khd->qhd", d_scores, keys, preferred_element_type=jnp.float32) * att_scale
    )
    d_keys = (
        jnp.einsum("hqk,qhd->khd", d_scores, query, preferred_element_type=jnp.float32) * att_scale
    )
    d_values = jnp.einsum("hqk,qhd->khd", probs_b, d_attended, preferred_element_type=jnp.float32)
    d_kv = jnp.concatenate([d_keys.reshape(slots, width), d_values.reshape(slots, width)], axis=1)
    d_kv = lax.psum_scatter(
        d_kv.astype(jnp.bfloat16), "fsdp", scatter_dimension=0, tiled=True
    ).astype(jnp.float32)
    d_qkv = jnp.concatenate([d_query.reshape(rows, width), d_kv], axis=1).astype(jnp.bfloat16)
    grad_qkv = contract_rows(a1, d_qkv)
    da1 = contract_cols(d_qkv, qkv_back)
    first_pull = jax.vjp(layer_norm, h0, g1f, b1f)[1]
    dh0_norm, grad_gain_one, grad_shift_one = first_pull(da1)
    grad_qkv, grad_out, grad_gain_one, grad_shift_one = (
        lax.psum_scatter(grad_qkv, ("dp", "fsdp"), scatter_dimension=0, tiled=True),
        lax.psum_scatter(grad_out, ("dp", "fsdp"), scatter_dimension=0, tiled=True),
        lax.psum_scatter(grad_gain_one, ("dp", "fsdp"), scatter_dimension=0, tiled=True),
        lax.psum_scatter(grad_shift_one, ("dp", "fsdp"), scatter_dimension=0, tiled=True),
    )
    dh0b = (dh1 + dh0_norm).astype(jnp.bfloat16)

    def enc_term(start, count):
        return contract_rows(dh0b, xb)

    grad_enc = reduce_columns(enc_term, owned).T
    columns = dh0b
    d_xb = contract_cols(columns, lax.all_gather(w_enc, ("dp", "fsdp"), axis=1, tiled=True))
    counts_grad = d_xb * scale[:, None] / (1.0 + counts_f * scale[:, None])
    return (
        logits,
        counts_grad,
        grad_enc,
        grad_qkv,
        grad_out,
        grad_gain_one,
        grad_shift_one,
        grad_up,
        grad_down,
        grad_gain_two,
        grad_shift_two,
        grad_dec,
    )


def solution(mesh):
    placed = (
        P(("dp", "fsdp"), None),
        P(("dp", "fsdp")),
        P(None, ("dp", "fsdp")),
        P("dp", None),
        P(("dp", "fsdp"), None),
        P(None, ("dp", "fsdp")),
        P(("dp", "fsdp"), None),
        P(("dp", "fsdp"), None),
        P(("dp", "fsdp")),
        P(("dp", "fsdp")),
        P(("dp", "fsdp"), None),
        P(("dp", "fsdp"), None),
        P(("dp", "fsdp")),
        P(("dp", "fsdp")),
        P(None, ("dp", "fsdp")),
    )
    return jax.shard_map(
        on_device,
        mesh=mesh,
        in_specs=placed,
        out_specs=(
            P(("dp", "fsdp"), None),
            P(("dp", "fsdp"), None),
            P(None, ("dp", "fsdp")),
            P(("dp", "fsdp"), None),
            P(("dp", "fsdp"), None),
            P(("dp", "fsdp")),
            P(("dp", "fsdp")),
            P(("dp", "fsdp"), None),
            P(("dp", "fsdp"), None),
            P(("dp", "fsdp")),
            P(("dp", "fsdp")),
            P(None, ("dp", "fsdp")),
        ),
        check_vma=False,
    )
```

profile of v0, /device:TPU:0, one launch (start us, length us, event | category | flops | bytes accessed | tf_op | source)
XLA Modules:
  0.0 2631.8 jit_solution(768806898839338673)
XLA Ops:
  8.0 0.7 all-gather.10.cloned.1.call-update
  9.5 0.8 dynamic-update-slice.3
  10.3 0.8 dynamic-update-slice
  11.1 0.8 dynamic-update-slice.1
  12.0 0.8 dynamic-update-slice.2
  12.8 43.5 %all-reduce.9 = (bf16[1024]{0:T(1024)(128)(2,1)S(1)}, bf16[1024]{0:T(1024)(128)(2,1)S(1)}, bf16[1024]{0:T(1024)(128)(2,1)S(1)}, bf16[1024]{0:T(1024)(128)(2,1)S(1)}) all-reduce(bf16[1024]{0:T(1024)(128)(2,1)S(1)} %dynamic-update-slice.1, bf16[1024]{0:T(1024)(128)(2,1)S(1)} %dynamic-update-slice, ...), channel_id=1, replica_groups=mesh['dp'=8,'fsdp'=4] {'dp','fsdp'}, use_global_device_ids=true, to_apply=%add.1 | all-reduce | flops 4096 | bytes 16384
  56.4 0.7 broadcast_divide_fusion
  57.0 0.8 slice_convert_fusion.1
  57.8 1.9 multiply_sine_fusion.1
  59.7 122.7 %all-gather.8.cloned.1.call-done = bf16[13500,1024]{0,1:T(8,128)(2,1)} async-done(((bf16[13500,32]{0,1:T(8,128)(2,1)}), bf16[13500,1024]{0,1:T(8,128)(2,1)}) %all-gather.8.cloned.1.call-update) | async-done | bytes 27648016 | tf_op jit(solution)/shard_map/all_gather | solution.py:90
  182.4 28.6 %fusion.44 = (f32[256]{0:T(256)S(1)}, f32[256,1024]{1,0:T(8,128)S(1)}) fusion(f32[256,256]{1,0:T(8,128)S(1)} %get-tuple-element.40, f32[256,256]{1,0:T(8,128)S(1)} %get-tuple-element.41, f32[256,256]{1,0:T(8,128)S(1)} %get-tuple-element.35, f32[256,256]{1,0:T(8,128)S(1)} %get-tuple-element.34, bf16[13500,1024]{0,1:T(8,128)(2,1)} %all-gather.8.cloned.1.call-done, ...), kind=kOutput, calls=%fused_computation.99 | convolution fusion | flops 7089566720 | bytes 36659200 | tf_op jit(solution)/shard_map/dot_general | solution.py:44
  211.3 41.8 %all-gather.10.cloned.1.call-done = bf16[1024,3072]{1,0:T(8,128)(2,1)} async-done(((bf16[32,3072]{1,0:T(8,128)(2,1)}), bf16[1024,3072]{1,0:T(8,128)(2,1)}) %all-gather.10.cloned.1.call-update) | async-done | bytes 6291472 | tf_op jit(solution)/shard_map/all_gather | solution.py:92
  253.1 4.7 convolution_convert_fusion.1
  257.8 1.1 slice.24
  260.1 0.7 all-gather.18.cloned.1.call-update
  262.2 159.5 %all-gather.20.cloned.1.call-done = bf16[13500,1024]{0,1:T(8,128)(2,1)} async-done(((bf16[13500,32]{0,1:T(8,128)(2,1)}), bf16[13500,1024]{0,1:T(8,128)(2,1)}) %all-gather.20.cloned.1.call-update) | async-done | bytes 27648016 | tf_op jit(solution)/shard_map/all_gather | solution.py:131
  421.7 16.2 fusion.47
  437.9 18.5 all-gather.12.cloned.1.call-done
  456.4 4.7 fusion.43
  461.0 2.9 copy.41
  463.9 4.6 copy.39
  468.5 3.0 fusion.45
  471.6 3.8 fusion.1
  475.4 2.4 copy-done
  477.9 4.3 fusion.21
  482.2 33.4 %all-gather.14.cloned.1.call-done = bf16[1024,1024]{1,0:T(8,128)(2,1)} async-done(((bf16[32,1024]{1,0:T(8,128)(2,1)}), bf16[1024,1024]{1,0:T(8,128)(2,1)}) %all-gather.14.cloned.1.call-update) | async-done | bytes 2097168 | tf_op jit(solution)/shard_map/all_gather | solution.py:93
  515.5 2.4 fusion.46
  518.3 76.4 %all-gather.16.cloned.1.call-done = bf16[1024,4096]{1,0:T(8,128)(2,1)} async-done(((bf16[32,4096]{1,0:T(8,128)(2,1)}), bf16[1024,4096]{1,0:T(8,128)(2,1)}) %all-gather.16.cloned.1.call-update) | async-done | bytes 8388624 | tf_op jit(solution)/shard_map/all_gather | solution.py:120
  594.7 16.0 multiply_convert_fusion.2
  610.8 63.0 %all-gather.18.cloned.1.call-done = bf16[4096,1024]{1,0:T(8,128)(2,1)} async-done(((bf16[128,1024]{1,0:T(8,128)(2,1)}), bf16[4096,1024]{1,0:T(8,128)(2,1)}) %all-gather.18.cloned.1.call-update) | async-done | bytes 8388624 | tf_op jit(solution)/shard_map/all_gather | solution.py:121
  673.8 11.3 add_convert_fusion
  685.0 7.4 multiply_reduce_fusion.1
  693.1 1.0 copy-done.7
  694.0 0.7 convolution_convert_fusion.2
  695.0 0.8 copy-done.13
  695.8 9.6 fusion.15
  705.4 14.2 multiply_reduce_fusion
  719.7 7.7 multiply_convert_fusion
  727.4 3.1 multiply_convert_fusion.1
  731.1 2.5 pad_maximum_fusion
  733.7 4.3 fusion.24
  738.1 8.0 fusion.20
  746.0 30.8 %reduce-scatter.8.cloned.1.call-done = bf16[256,2048]{0,1:T(8,128)(2,1)} async-done(((bf16[1024,2048]{0,1:T(8,128)(2,1)}), bf16[256,2048]{0,1:T(8,128)(2,1)}) %reduce-scatter.8.cloned.1.call-update) | async-done | bytes 1048592 | tf_op jit(solution)/shard_map/reduce_scatter | solution.py:185
  776.9 8.2 fusion.22
  785.4 1.4 copy-done.19
  786.7 8.3 fusion.38
  795.1 1.2 copy-done.15
  796.2 9.7 fusion.27
  806.0 1.5 copy-done.16
  807.5 5.7 fusion.19
  813.3 0.8 copy-done.21
  814.1 22.4 fusion.48
  836.6 1.1 copy-done.6
  837.9 5.2 multiply_reduce_fusion.2
  843.8 31.5 %fusion.7 = f32[1024,13500]{1,0:T(8,128)} fusion(bf16[256,1024]{1,0:T(8,128)(2,1)S(1)} %add_convert_fusion.1, bf16[256,13500]{0,1:T(8,128)(2,1)} %param.15, f32[256]{0:T(256)S(1)} %copy-done.37), kind=kOutput, calls=%fused_computation.17 | convolution fusion | flops 7088256000 | bytes 62733312 | tf_op jit(solution)/shard_map/dot_general | solution.py:32
  875.3 1.0 copy-done.22
  876.3 17.4 convolution_convert_fusion
  893.7 40.1 %all-reduce.8 = (f32[1024]{0:T(1024)S(1)}, f32[1024]{0:T(1024)S(1)}, f32[1024]{0:T(1024)S(1)}, f32[1024]{0:T(1024)S(1)}) all-reduce(f32[1024]{0:T(1024)S(1)} %get-tuple-element.14, f32[1024]{0:T(1024)S(1)} %get-tuple-element.17, f32[1024]{0:T(1024)S(1)} %copy-done.38, ...), channel_id=6, replica_groups=mesh['dp'=8,'fsdp'=4] {'dp','fsdp'}, use_global_device_ids=true, to_apply=%region_16.17.clone | all-reduce | flops 4096 | bytes 32768
  936.1 23.3 fusion
  959.3 121.2 %reduce-scatter.12.cloned.1.call-done = f32[32,3072]{1,0:T(8,128)} async-done(((f32[1024,3072]{1,0:T(8,128)}), f32[32,3072]{1,0:T(8,128)}) %reduce-scatter.12.cloned.1.call-update) | async-done | bytes 393232 | tf_op jit(solution)/shard_map/reduce_scatter | solution.py:194
  1080.6 185.0 %reduce-scatter.16.cloned.1.call-done = f32[32,4096]{1,0:T(8,128)} async-done(((f32[1024,4096]{1,0:T(8,128)}), f32[32,4096]{1,0:T(8,128)}) %reduce-scatter.16.cloned.1.call-update) | async-done | bytes 524304 | tf_op jit(solution)/shard_map/reduce_scatter | solution.py:164
  1265.6 187.3 %reduce-scatter.18.cloned.1.call-done = f32[128,1024]{1,0:T(8,128)} async-done(((f32[4096,1024]{1,0:T(8,128)}), f32[128,1024]{1,0:T(8,128)}) %reduce-scatter.18.cloned.1.call-update) | async-done | bytes 524304 | tf_op jit(solution)/shard_map/reduce_scatter | solution.py:165
  1452.9 582.6 %reduce-scatter.20.cloned.1.call-done = f32[32,13500]{1,0:T(8,128)} async-done(((f32[1024,13500]{1,0:T(8,128)}), f32[32,13500]{1,0:T(8,128)}) %reduce-scatter.20.cloned.1.call-update) | async-done | bytes 1728016 | tf_op jit(solution)/shard_map/reduce_scatter | solution.py:48
  2035.5 589.3 %reduce-scatter.10.cloned.1.call-done = f32[32,13500]{1,0:T(8,128)} async-done(((f32[1024,13500]{1,0:T(8,128)}), f32[32,13500]{1,0:T(8,128)}) %reduce-scatter.10.cloned.1.call-update) | async-done | bytes 1728016 | tf_op jit(solution)/shard_map/reduce_scatter | solution.py:48
  (141 shorter events, 9.1 us)
Async XLA Ops:
  7.2 175.2 %all-gather.8.cloned.1.call-start = ((), (), s32[]{:S(2)}) async-start(), calls=%async_computation.7 | async-start | bytes 28655616 | tf_op jit(solution)/shard_map/all_gather | solution.py:90
  7.9 245.2 %all-gather.10.cloned.1.call-start = ((), (), s32[]{:S(2)}) async-start(), calls=%async_computation.8 | async-start | bytes 6488064 | tf_op jit(solution)/shard_map/all_gather | solution.py:92
  8.7 413.0 %all-gather.20.cloned.1.call-start = ((), (), s32[]{:S(2)}) async-start(), calls=%async_computation.13 | async-start | bytes 28655616 | tf_op jit(solution)/shard_map/all_gather | solution.py:131
  9.4 447.0 %all-gather.12.cloned.1.call-start = ((), (), s32[]{:S(2)}) async-start(), calls=%async_computation.9 | async-start | bytes 5242880 | tf_op jit(solution)/shard_map/all_gather | solution.py:100
  56.3 196.7 %copy-start.24 = (f32[1024]{0:T(1024)}, f32[1024]{0:T(1024)S(1)}, u32[]{:S(2)}) copy-start(f32[1024]{0:T(1024)S(1)} %convert_element_type.118) | copy-start | bytes 12292
  57.0 153.9 %copy-start.36 = (f32[256]{0:T(256)}, f32[256]{0:T(256)S(1)}, u32[]{:S(2)}) copy-start(f32[256]{0:T(256)S(1)} %broadcast_divide_fusion) | copy-start | bytes 3076
  210.9 46.8 %copy-start.4 = (f32[256,1024]{1,0:T(8,128)}, f32[256,1024]{1,0:T(8,128)S(1)}, u32[]{:S(2)}) copy-start(f32[256,1024]{1,0:T(8,128)S(1)} %get-tuple-element.43) | copy-start | bytes 3145732
  211.0 46.8 %copy-start.28 = (f32[256]{0:T(256)}, f32[256]{0:T(256)S(1)}, u32[]{:S(2)}) copy-start(f32[256]{0:T(256)S(1)} %broadcast_multiply_fusion.1) | copy-start | bytes 3076
  211.2 46.5 %copy-start.34 = (f32[256]{0:T(256)}, f32[256]{0:T(256)S(1)}, u32[]{:S(2)}) copy-start(f32[256]{0:T(256)S(1)} %multiply_reduce_fusion.6) | copy-start | bytes 3076
  211.3 46.5 %copy-start.32 = (f32[256]{0:T(256)}, f32[256]{0:T(256)S(1)}, u32[]{:S(2)}) copy-start(f32[256]{0:T(256)S(1)} %fusion.34) | copy-start | bytes 3076
  258.9 256.7 %all-gather.14.cloned.1.call-start = ((), (), s32[]{:S(2)}) async-start(), calls=%async_computation.10 | async-start | bytes 2162688 | tf_op jit(solution)/shard_map/all_gather | solution.py:93
  259.5 335.3 %all-gather.16.cloned.1.call-start = ((), (), s32[]{:S(2)}) async-start(), calls=%async_computation.11 | async-start | bytes 8650752 | tf_op jit(solution)/shard_map/all_gather | solution.py:120
  260.0 413.7 %all-gather.18.cloned.1.call-start = ((), (), s32[]{:S(2)}) async-start(), calls=%async_computation.12 | async-start | bytes 8650752 | tf_op jit(solution)/shard_map/all_gather | solution.py:121
  260.8 516.1 %reduce-scatter.8.cloned.1.call-start = ((), (), s32[]{:S(2)}) async-start(), calls=%async_computation.14 | async-start | bytes 5242880 | tf_op jit(solution)/shard_map/reduce_scatter | solution.py:185
  262.2 206.3 %copy-start.12 = (bf16[256,1024]{0,1:T(8,128)(2,1)}, bf16[256,1024]{0,1:T(8,128)(2,1)S(1)}, u32[]{:S(2)}) copy-start(bf16[256,1024]{0,1:T(8,128)(2,1)S(1)} %copy.40) | copy-start | bytes 1572868
  463.9 7.6 copy-start.2
  471.5 6.3 copy-start
  471.5 6.3 copy-start.10
  477.9 37.7 %copy-start.5 = (f32[256,1024]{1,0:T(8,128)S(1)}, f32[256,1024]{1,0:T(8,128)}, u32[]{:S(2)}) copy-start(f32[256,1024]{1,0:T(8,128)} %copy-done.4) | copy-start | bytes 3145732
  482.2 128.6 %copy-start.17 = (bf16[16,64,256]{2,1,0:T(8,128)(2,1)}, bf16[16,64,256]{2,1,0:T(8,128)(2,1)S(1)}, u32[]{:S(2)}) copy-start(bf16[16,64,256]{2,1,0:T(8,128)(2,1)S(1)} %fusion.21) | copy-start | bytes 1572868
  518.0 174.4 %copy-start.26 = (f32[256]{0:T(256)}, f32[256]{0:T(256)S(1)}, u32[]{:S(2)}) copy-start(f32[256]{0:T(256)S(1)} %broadcast_multiply_fusion) | copy-start | bytes 3076
  518.2 174.2 %copy-start.30 = (f32[256]{0:T(256)}, f32[256]{0:T(256)S(1)}, u32[]{:S(2)}) copy-start(f32[256]{0:T(256)S(1)} %fusion.35) | copy-start | bytes 3076
  518.3 176.7 %copy-start.23 = (f32[16,256]{1,0:T(8,128)}, f32[16,256]{1,0:T(8,128)S(1)}, u32[]{:S(2)}) copy-start(f32[16,256]{1,0:T(8,128)S(1)} %log_add_fusion) | copy-start | bytes 49156
  518.3 155.5 %copy-start.14 = (f32[256,1024]{1,0:T(8,128)S(1)}, f32[256,1024]{1,0:T(8,128)}, u32[]{:S(2)}) copy-start(f32[256,1024]{1,0:T(8,128)} %fusion.47) | copy-start | bytes 3145732
  685.0 7.4 copy-start.18
  692.4 1.6 copy-start.9
  693.0 1.0 copy-start.7
  695.0 0.8 copy-start.13
  695.8 23.9 slice-start
  695.8 23.9 slice-start.1
  705.4 14.3 slice-start.2
  705.4 14.3 slice-start.3
  727.4 3.7 copy-start.1
  727.4 3.7 copy-start.11
  733.6 4.4 copy-start.3
  733.6 225.7 %reduce-scatter.14.cloned.1.call-start = ((), (), s32[]{:S(2)}) async-start(), calls=%async_computation.17 | async-start | bytes 4325376 | tf_op jit(solution)/shard_map/reduce_scatter | solution.py:195
  738.0 38.9 %copy-start.25 = (f32[1024]{0:T(1024)S(1)}, f32[1024]{0:T(1024)}, u32[]{:S(2)}) copy-start(f32[1024]{0:T(1024)} %copy-done.24) | copy-start | bytes 12292
  738.0 38.9 %copy-start.29 = (f32[256]{0:T(256)S(1)}, f32[256]{0:T(256)}, u32[]{:S(2)}) copy-start(f32[256]{0:T(256)} %copy-done.28) | copy-start | bytes 3076
  738.0 38.9 %copy-start.33 = (f32[256]{0:T(256)S(1)}, f32[256]{0:T(256)}, u32[]{:S(2)}) copy-start(f32[256]{0:T(256)} %copy-done.32) | copy-start | bytes 3076
  738.0 342.6 %reduce-scatter.12.cloned.1.call-start = ((), (), s32[]{:S(2)}) async-start(), calls=%async_computation.16 | async-start | bytes 12976128 | tf_op jit(solution)/shard_map/reduce_scatter | solution.py:194
  785.1 1.6 copy-start.19
  785.1 1.6 copy-start.27
  785.1 1.6 copy-start.31
  785.1 480.4 %reduce-scatter.16.cloned.1.call-start = ((), (), s32[]{:S(2)}) async-start(), calls=%async_computation.18 | async-start | bytes 17301504 | tf_op jit(solution)/shard_map/reduce_scatter | solution.py:164
  795.0 1.2 copy-start.15
  795.0 657.9 %reduce-scatter.18.cloned.1.call-start = ((), (), s32[]{:S(2)}) async-start(), calls=%async_computation.19 | async-start | bytes 17301504 | tf_op jit(solution)/shard_map/reduce_scatter | solution.py:165
  805.9 1.6 copy-start.16
  806.0 1229.5 %reduce-scatter.20.cloned.1.call-start = ((), (), s32[]{:S(2)}) async-start(), calls=%async_computation.20 | async-start | bytes 57311232 | tf_op jit(solution)/shard_map/reduce_scatter | solution.py:48
  813.3 0.8 copy-start.21
  836.5 1.2 copy-start.6
  836.5 1.4 copy-start.20
  836.5 6.6 copy-start.35
  836.5 7.0 copy-start.8
  836.5 1788.3 %reduce-scatter.10.cloned.1.call-start = ((), (), s32[]{:S(2)}) async-start(), calls=%async_computation.15 | async-start | bytes 57311232 | tf_op jit(solution)/shard_map/reduce_scatter | solution.py:48
  843.1 0.7 copy-start.37
  875.3 1.0 copy-start.22
  876.3 17.4 copy-start.38
  876.3 17.4 copy-start.39
Sparse Core Ops, SparseCore 0:
  10.9 171.4 all-gather.7
  185.3 67.7 all-gather.9
  256.0 165.6 all-gather.19
  423.7 32.6 all-gather.11
  459.1 56.4 all-gather.13
  518.3 76.4 all-gather.15
  597.6 76.1 all-gather.17
  733.7 43.0 reduce-scatter.7
  779.8 141.9 reduce-scatter.13
  929.3 151.2 reduce-scatter.11
  1083.5 182.0 reduce-scatter.15
  1268.3 184.5 reduce-scatter.17
  1455.8 579.6 reduce-scatter.19
  2038.2 586.5 reduce-scatter.9
where the time goes:
time: 2650 us; the launch traced here: 2630 us
  waiting for transfers between devices  2220 us (84%)
  matrix products  265 us (10%)
  blocking collectives  83.6 us (3%)
  local copies, waits for them, and re-layouts  31.3 us (1%)
    reduce_scatter x2, waiting for transfers between devices, reduce_columns(): lax.psum_scatter(term(jnp.int32(0), lax.axis_size(('dp', 'fsdp')) * owned...  1170 us
    reduce_scatter x1, waiting for transfers between devices, on_device(): lax.psum_scatter(grad_down, ('dp', 'fsdp'), scatter_dimension=0, tiled=True)  187 us
    reduce_scatter x1, waiting for transfers between devices, on_device(): lax.psum_scatter(grad_up, ('dp', 'fsdp'), scatter_dimension=0, tiled=True)  185 us
    all_gather x1, waiting for transfers between devices, on_device(): lax.all_gather(w_dec, ('dp', 'fsdp'), axis=1, tiled=True)  159 us
    all_gather x1, waiting for transfers between devices, on_device(): lax.all_gather(w_enc, ('dp', 'fsdp'), axis=1, tiled=True)  123 us
    reduce_scatter x1, waiting for transfers between devices, on_device(): lax.psum_scatter(grad_qkv, ('dp', 'fsdp'), scatter_dimension=0, tiled=True)  121 us
    dot_general x6, matrix products, contract_rows(): lax.dot_general(left, right, (((0,), (0,)), ((), ())), preferred_element_...  84.4 us
    unnamed x2, blocking collectives  83.6 us
  transfers between devices with their start and end apart: 14, of which 13 were waited for; matrix products, arithmetic and copies ran while one was open for 9% of the time, Pallas kernels for 0%

commit v1 on v0

v1 whole, which is shorter than its diff:
```python
import math

import jax
import jax.numpy as jnp
from jax import lax
from jax.sharding import Mesh
from jax.sharding import PartitionSpec as P

HEADS = 16


eps = 1e-05


def layer_norm(value, gain, shift):
    mean = jnp.mean(value, axis=1, keepdims=True)
    centred = value - mean
    variance = jnp.mean(centred * centred, axis=1, keepdims=True)
    return centred * lax.rsqrt(variance + eps) * gain + shift


def positions(coords, width):
    quarter = width // 4
    freqs = 0.05 * jnp.exp(-jnp.arange(quarter, dtype=jnp.float32) * (math.log(10000.0) / quarter))
    along_x = coords[0].astype(jnp.float32)[:, None] * freqs[None, :]
    along_y = coords[1].astype(jnp.float32)[:, None] * freqs[None, :]
    return jnp.concatenate(
        [jnp.sin(along_x), jnp.cos(along_x), jnp.sin(along_y), jnp.cos(along_y)], axis=1
    )


def contract_rows(left, right):
    return lax.dot_general(
        left, right, (((0,), (0,)), ((), ())), preferred_element_type=jnp.float32
    )


def contract_cols(left, right):
    return lax.dot_general(
        left, right, (((1,), (1,)), ((), ())), preferred_element_type=jnp.float32
    )


def matmul(left, right):
    return jnp.dot(left, right, preferred_element_type=jnp.float32)


def swap(value, axis):
    return lax.ppermute(value, axis, [(0, 1), (1, 0)])


def by_owner(value, axis):
    n_h = lax.axis_size("h")
    at = value.shape
    block = at[axis] // (8 * n_h)
    split = value.reshape(at[:axis] + (n_h, 2, 2, 2, block) + at[axis + 1 :])
    order = list(range(axis)) + [axis + 3, axis + 1, axis + 2, axis, axis + 4]
    order += list(range(axis + 5, split.ndim))
    return split.transpose(order).reshape(at)


def from_owner(value, axis):
    n_h = lax.axis_size("h")
    at = value.shape
    block = at[axis] // (8 * n_h)
    split = value.reshape(at[:axis] + (2, 2, 2, n_h, block) + at[axis + 1 :])
    order = list(range(axis)) + [axis + 3, axis + 1, axis + 2, axis, axis + 4]
    order += list(range(axis + 5, split.ndim))
    return split.transpose(order).reshape(at)


def relative(value, axis):
    eighth = value.shape[axis] // 8
    mine = lax.axis_index("c") * 4 + lax.axis_index("x") * 2 + lax.axis_index("y")
    parts = [
        lax.dynamic_slice_in_dim(value, (mine ^ part) * eighth, eighth, axis) for part in range(8)
    ]
    return jnp.concatenate(parts, axis=axis)


def gather_parts(shard, first, second):
    own = lax.all_gather(shard, "h", axis=0, tiled=True)
    one = swap(own, first)
    two = swap(own, second)
    both = swap(one, second)
    four = [own, two, one, both] if first == "x" else [own, one, two, both]
    return four + [swap(part, "c") for part in four]


def gather_rows(shard, first, second):
    return jnp.concatenate(gather_parts(shard, first, second), axis=0)


def gather_columns(shard):
    cut = -(-shard.shape[1] // 256) * 128
    left = gather_parts(shard[:, :cut], "x", "y")
    right = gather_parts(shard[:, cut:], "y", "x")
    return jnp.concatenate(
        [jnp.concatenate([a, b], axis=1) for a, b in zip(left, right)], axis=0
    )


def scatter_rows(part, first, second):
    half = part.shape[0] // 2
    other = swap(part[half:], "c")
    part = part[:half].astype(jnp.float32) + other.astype(jnp.float32)
    part = part.astype(jnp.bfloat16).reshape((2, 2, half // 4, -1))
    if first == "x":
        part = part[0].astype(jnp.float32) + swap(part[1], "x").astype(jnp.float32)
    else:
        part = part[:, 0].astype(jnp.float32) + swap(part[:, 1], "y").astype(jnp.float32)
    part = part.astype(jnp.bfloat16)
    part = part[0].astype(jnp.float32) + swap(part[1], second).astype(jnp.float32)
    part = part.astype(jnp.bfloat16)
    return lax.psum_scatter(part, "h", scatter_dimension=0, tiled=True).astype(jnp.float32)


def scatter_columns(left, right):
    cut = -(-right.shape[1] // 256) * 128
    left = relative(left, 1)
    one = contract_rows(left, right[:, :cut]).astype(jnp.bfloat16)
    two = contract_rows(left, right[:, cut:]).astype(jnp.bfloat16)
    return jnp.concatenate(
        [scatter_rows(one, "x", "y"), scatter_rows(two, "y", "x")], axis=1
    ).T


def gather_group(mine):
    at_y, at_c = lax.axis_index("y"), lax.axis_index("c")
    pair = jnp.stack([mine, swap(mine, "y")])
    both = jnp.stack([pair, swap(pair, "c")])
    order = [
        lax.dynamic_index_in_dim(
            lax.dynamic_index_in_dim(both, at_c ^ c, 0, False), at_y ^ y, 0, False
        )
        for y in range(2)
        for c in range(2)
    ]
    return jnp.concatenate(order, axis=0)


def scatter_group(rows_all):
    at_y, at_c = lax.axis_index("y"), lax.axis_index("c")
    part = rows_all.astype(jnp.bfloat16).reshape((2, 2, rows_all.shape[0] // 4, -1))
    keep = lax.dynamic_index_in_dim(part, at_c, 1, False).astype(jnp.float32)
    send = lax.dynamic_index_in_dim(part, 1 - at_c, 1, False)
    part = (keep + swap(send, "c").astype(jnp.float32)).astype(jnp.bfloat16)
    keep = lax.dynamic_index_in_dim(part, at_y, 0, False).astype(jnp.float32)
    send = lax.dynamic_index_in_dim(part, 1 - at_y, 0, False)
    return keep + swap(send, "y").astype(jnp.float32)


def on_device(
    counts,
    library,
    coords,
    lengths,
    cotangent,
    w_enc,
    w_qkv,
    w_out,
    gain_one,
    shift_one,
    w_up,
    w_down,
    gain_two,
    shift_two,
    w_dec,
):
    rows = counts.shape[0]
    width = w_qkv.shape[1] // 3
    heads = HEADS
    head_width = width // heads
    att_scale = head_width ** (-0.5)
    group_size = 4
    slots = rows * group_size
    scale = 10000.0 / library
    counts_f = counts.astype(jnp.float32)
    xb = jnp.log1p(counts_f * scale[:, None]).astype(jnp.bfloat16)
    pe = by_owner(positions(coords, width), 1)
    ends = jnp.cumsum(lengths[0])
    place = jnp.arange(slots, dtype=jnp.int32)
    seg_all = jnp.sum((place[:, None] >= ends[None, :]).astype(jnp.int32), axis=1)
    seg_mine = lax.dynamic_slice_in_dim(seg_all, (lax.axis_index("y") * 2 + lax.axis_index("c")) * rows, rows)
    same = (seg_mine[:, None] == seg_all[None, :])[None]
    enc_all = gather_columns(w_enc.T)
    vectors = jnp.stack([gain_one, shift_one, gain_two, shift_two], axis=1)
    vectors = jnp.pad(vectors, ((0, 0), (0, 124)))
    qkv_all = gather_rows(jnp.concatenate([w_qkv, vectors], axis=1), "x", "y")
    out_all = gather_rows(by_owner(w_out, 1), "y", "x")
    up_all = gather_rows(by_owner(w_up, 1), "y", "x")
    down_all = gather_rows(by_owner(w_down, 1), "x", "y")
    dec_all = gather_columns(w_dec.T)
    vectors = relative(qkv_all[:, 3 * width :].astype(jnp.float32), 0).T
    qkv_all = qkv_all[:, : 3 * width]
    g1f, b1f, g2f, b2f = vectors[0], vectors[1], vectors[2], vectors[3]
    h0 = relative(contract_cols(xb, enc_all), 1) + pe
    a1 = layer_norm(h0, g1f, b1f).astype(jnp.bfloat16)
    a1_rel = relative(a1, 1)
    qkv = matmul(a1_rel, qkv_all).astype(jnp.bfloat16)
    query = qkv[:, :width].reshape(rows, heads, head_width)
    kv_all = gather_group(qkv[:, width:])
    keys = kv_all[:, :width].reshape(slots, heads, head_width)
    values = kv_all[:, width:].reshape(slots, heads, head_width)

    def scores_of():
        raw = (
            jnp.einsum("qhd,khd->hqk", query, keys, preferred_element_type=jnp.float32) * att_scale
        )
        return jnp.where(same, raw, -1000000000.0)

    scores = scores_of()
    top = jnp.max(scores, axis=-1, keepdims=True)
    expo = jnp.exp(scores - top)
    total = jnp.sum(expo, axis=-1, keepdims=True)
    log_total = top + jnp.log(total)
    probs_b = (expo / total).astype(jnp.bfloat16)
    attended = jnp.einsum("hqk,khd->qhd", probs_b, values, preferred_element_type=jnp.float32)
    attended_b = attended.reshape(rows, width).astype(jnp.bfloat16)
    attended_rel = relative(by_owner(attended_b, 1), 1)
    h1 = h0 + matmul(attended_rel, out_all)
    a2 = layer_norm(h1, g2f, b2f).astype(jnp.bfloat16)
    a2_rel = relative(a2, 1)
    hidden = matmul(a2_rel, up_all)
    act = jax.nn.gelu(hidden, approximate=False).astype(jnp.bfloat16)
    act_rel = relative(act, 1)
    h2 = h1 + matmul(act_rel, down_all)
    hb = h2.astype(jnp.bfloat16)
    logits = matmul(relative(hb, 1), dec_all).astype(jnp.bfloat16)
    grad_dec = scatter_columns(hb, cotangent)
    dh2 = relative(contract_cols(cotangent, dec_all), 1)
    dfb = dh2.astype(jnp.bfloat16)
    grad_down = contract_rows(act_rel, dfb)
    d_act = relative(contract_cols(dfb, down_all), 1)
    slope = jax.vjp(lambda v: jax.nn.gelu(v, approximate=False), hidden)[1](d_act)[0]
    d_hidden = slope.astype(jnp.bfloat16)
    grad_up = contract_rows(a2_rel, d_hidden)
    da2 = relative(contract_cols(d_hidden, up_all), 1)
    norm_pull = jax.vjp(layer_norm, h1, g2f, b2f)[1]
    dh1_norm, grad_gain_two, grad_shift_two = norm_pull(da2)
    dh1 = dh2 + dh1_norm
    grad_down = from_owner(scatter_rows(grad_down.astype(jnp.bfloat16), "x", "y"), 1)
    grad_up = from_owner(scatter_rows(grad_up.astype(jnp.bfloat16), "y", "x"), 1)
    dab = dh1.astype(jnp.bfloat16)
    grad_out = contract_rows(attended_rel, dab)
    d_attended = relative(contract_cols(dab, out_all).astype(jnp.bfloat16), 1)
    d_attended = from_owner(d_attended, 1).reshape(rows, heads, head_width)
    probs = jnp.exp(scores_of() - log_total)
    probs_b = probs.astype(jnp.bfloat16)
    d_probs = jnp.einsum("qhd,khd->hqk", d_attended, values, preferred_element_type=jnp.float32)
    inner = jnp.sum(probs * d_probs, axis=-1, keepdims=True)
    d_scores = (probs * (d_probs - inner)).astype(jnp.bfloat16)
    d_query = (
        jnp.einsum("hqk,khd->qhd", d_scores, keys, preferred_element_type=jnp.float32) * att_scale
    )
    d_keys = (
        jnp.einsum("hqk,qhd->khd", d_scores, query, preferred_element_type=jnp.float32) * att_scale
    )
    d_values = jnp.einsum("hqk,qhd->khd", probs_b, d_attended, preferred_element_type=jnp.float32)
    d_kv = jnp.concatenate([d_keys.reshape(slots, width), d_values.reshape(slots, width)], axis=1)
    d_kv = scatter_group(d_kv)
    d_qkv = jnp.concatenate([d_query.reshape(rows, width), d_kv], axis=1).astype(jnp.bfloat16)
    grad_qkv = contract_rows(a1_rel, d_qkv)
    da1 = relative(contract_cols(d_qkv, qkv_all), 1)
    first_pull = jax.vjp(layer_norm, h0, g1f, b1f)[1]
    dh0_norm, grad_gain_one, grad_shift_one = first_pull(da1)
    grad_vectors = jnp.stack([grad_gain_one, grad_shift_one, grad_gain_two, grad_shift_two], axis=1)
    grad_vectors = jnp.pad(relative(grad_vectors, 0), ((0, 0), (0, 124)))
    grad_qkv = jnp.concatenate([grad_qkv, grad_vectors], axis=1).astype(jnp.bfloat16)
    grad_out = from_owner(scatter_rows(grad_out.astype(jnp.bfloat16), "y", "x"), 1)
    grad_qkv = scatter_rows(grad_qkv, "x", "y")
    grad_gain_one, grad_shift_one, grad_gain_two, grad_shift_two = (
        grad_qkv[:, 3 * width + k] for k in range(4)
    )
    grad_qkv = grad_qkv[:, : 3 * width]
    dh0b = (dh1 + dh0_norm).astype(jnp.bfloat16)

    grad_enc = scatter_columns(dh0b, xb)
    d_xb = matmul(relative(dh0b, 1), enc_all)
    counts_grad = d_xb * scale[:, None] / (1.0 + counts_f * scale[:, None])
    return (
        logits,
        counts_grad,
        grad_enc,
        grad_qkv,
        grad_out,
        grad_gain_one,
        grad_shift_one,
        grad_up,
        grad_down,
        grad_gain_two,
        grad_shift_two,
        grad_dec,
    )


ALL = ("h", "x", "y", "c")


def solution(mesh):
    n_dp, n_fsdp = mesh.shape["dp"], mesh.shape["fsdp"]
    mesh = Mesh(mesh.devices.reshape((n_dp // 2, 2, 2, n_fsdp // 2)), ALL)
    placed = (
        P(ALL, None),
        P(ALL),
        P(None, ALL),
        P(("h", "x"), None),
        P(ALL, None),
        P(None, ALL),
        P(ALL, None),
        P(ALL, None),
        P(ALL),
        P(ALL),
        P(ALL, None),
        P(ALL, None),
        P(ALL),
        P(ALL),
        P(None, ALL),
    )
    return jax.shard_map(
        on_device,
        mesh=mesh,
        in_specs=placed,
        out_specs=(
            P(ALL, None),
            P(ALL, None),
            P(None, ALL),
            P(ALL, None),
            P(ALL, None),
            P(ALL),
            P(ALL),
            P(ALL, None),
            P(ALL, None),
            P(ALL),
            P(ALL),
            P(None, ALL),
        ),
        check_vma=False,
    )
```

time: 2650 us -> 1440 us (0.54)
  waiting for transfers between devices: 2220 us -> 535 us
  local copies, waits for them, and re-layouts: 31.3 us -> 375 us
  other arithmetic: 19.4 us -> 194 us
  matrix products: 265 us -> 209 us
  starting transfers between devices: 0.9 us -> 53.6 us
  blocking collectives: 83.6 us -> 47.6 us
    reduce_scatter x7, waiting for transfers between devices: 1700 us -> 14.6 us  [scatter_rows(): lax.psum_scatter(part, 'h', scatter_dimension=0, tiled=True)]
    ppermute x0 -> x84, waiting for transfers between devices: none -> 422 us  [swap(): return lax.ppermute(value, axis, [(0, 1), (1, 0)])]
    all_gather x7 -> x6, waiting for transfers between devices: 515 us -> 98.5 us  [gather_parts(): own = lax.all_gather(shard, 'h', axis=0, tiled=True)]
    unnamed x100 -> x358, local copies, waits for them, and re-layouts: 17.7 us -> 126 us
    convert_element_type x5 -> x31, other arithmetic: 0.23 us -> 108 us  [the longest x8 54 us: scatter_rows(): part = part.astype(jnp.bfloat16).reshape((2, 2, half // 4, -1))]
    slice x1 -> x21, local copies, waits for them, and re-layouts: 1.06 us -> 88.8 us  [the longest x8 34.4 us: scatter_rows(): other = swap(part[half:], 'c')]
    unnamed x2 -> x0, blocking collectives: 83.6 us -> none
    ppermute x0 -> x84, starting transfers between devices: none -> 52.7 us  [swap(): return lax.ppermute(value, axis, [(0, 1), (1, 0)])]
  transfers between devices with their start and end apart: 14 -> 98, of which waited for: 13 -> 25; matrix products, arithmetic and copies ran while one was open for 9% -> 43% of each run, Pallas kernels for 0% -> 0%
where the time goes in v1:
time: 1440 us; the launch traced here: 1430 us
  waiting for transfers between devices  535 us (37%)
  local copies, waits for them, and re-layouts  375 us (26%)
  matrix products  209 us (15%)
  other arithmetic  194 us (13%)
  starting transfers between devices  53.6 us (4%)
  blocking collectives  47.6 us (3%)
  between operations  17.3 us (1%)
    ppermute x84, waiting for transfers between devices, swap(): return lax.ppermute(value, axis, [(0, 1), (1, 0)])  422 us
    unnamed x358, local copies, waits for them, and re-layouts  126 us
    all_gather x6, waiting for transfers between devices, gather_parts(): own = lax.all_gather(shard, 'h', axis=0, tiled=True)  98.5 us
    dot_general x6, matrix products, matmul(): return jnp.dot(left, right, preferred_element_type=jnp.float32)  63.8 us
    dot_general x8, matrix products, contract_rows(): lax.dot_general(left, right, (((0,), (0,)), ((), ())), preferred_element_...  57.7 us
    convert_element_type x8, other arithmetic, scatter_rows(): part = part.astype(jnp.bfloat16).reshape((2, 2, half // 4, -1))  54 us
    ppermute x84, starting transfers between devices, swap(): return lax.ppermute(value, axis, [(0, 1), (1, 0)])  52.7 us
    all_gather x2, blocking collectives, gather_parts(): own = lax.all_gather(shard, 'h', axis=0, tiled=True)  47.6 us
  transfers between devices with their start and end apart: 98, of which 25 were waited for; matrix products, arithmetic and copies ran while one was open for 43% of the time, Pallas kernels for 0%

profile of v1, /device:TPU:0, one launch (start us, length us, event | category | flops | bytes accessed | tf_op | source)
XLA Modules:
  0.0 1431.7 jit_solution(1935410407927432884)
XLA Ops:
  15.4 32.3 %all_gather.26 = bf16[128,3200]{1,0:T(8,128)(2,1)} all-gather(bf16[32,3200]{1,0:T(8,128)(2,1)S(1)} %fusion.71), channel_id=1, replica_groups=mesh['h'=4,'x'=2,'y'=2,'c'=2] {'h'}, dimensions={0}, use_global_device_ids=true | all-gather | bytes 1024000 | tf_op jit(solution)/shard_map/all_gather | solution.py:82
  51.2 15.3 %all_gather.27 = bf16[128,1024]{1,0:T(8,128)(2,1)S(1)} all-gather(bf16[32,1024]{1,0:T(8,128)(2,1)S(1)} %reshape.469), channel_id=1, replica_groups=mesh['h'=4,'x'=2,'y'=2,'c'=2] {'h'}, dimensions={0}, use_global_device_ids=true | all-gather | bytes 327680 | tf_op jit(solution)/shard_map/all_gather | solution.py:82
  70.9 9.4 log-plus-one_convert_fusion
  107.0 10.0 collective-permute-done.16
  136.4 28.6 %all-gather.17.cloned.1.call-done = bf16[128,6716]{1,0:T(8,128)(2,1)} async-done(((bf16[32,6716]{1,0:T(8,128)(2,1)}), bf16[128,6716]{1,0:T(8,128)(2,1)}) %all-gather.17.cloned.1.call-update) | async-done | bytes 1719312 | tf_op jit(solution)/shard_map/all_gather | solution.py:82
  168.8 36.9 %all-gather.7.cloned.1.call-done = bf16[128,6784]{1,0:T(8,128)(2,1)} async-done(((bf16[32,6784]{1,0:T(8,128)(2,1)}), bf16[128,6784]{1,0:T(8,128)(2,1)}) %all-gather.7.cloned.1.call-update) | async-done | bytes 1736720 | tf_op jit(solution)/shard_map/all_gather | solution.py:82
  212.8 33.0 %all-gather.15.cloned.1.call-done = bf16[128,6784]{1,0:T(8,128)(2,1)} async-done(((bf16[32,6784]{1,0:T(8,128)(2,1)}), bf16[128,6784]{1,0:T(8,128)(2,1)}) %all-gather.15.cloned.1.call-update) | async-done | bytes 1736720 | tf_op jit(solution)/shard_map/all_gather | solution.py:82
  255.3 16.7 %collective-permute-done.39 = bf16[512,1024]{0,1:T(8,128)(2,1)} collective-permute-done((bf16[512,1024]{0,1:T(8,128)(2,1)}, bf16[512,1024]{0,1:T(8,128)(2,1)}, u32[]{:S(2)}, u32[]{:S(2)}) %collective-permute-start.39) | collective-permute-done | bytes 1048608 | tf_op jit(solution)/shard_map/ppermute | solution.py:49
  303.9 15.9 %collective-permute-done.45 = bf16[128,6716]{0,1:T(8,128)(2,1)} collective-permute-done((bf16[128,6716]{0,1:T(8,128)(2,1)S(1)}, bf16[128,6716]{0,1:T(8,128)(2,1)}, u32[]{:S(2)}, u32[]{:S(2)}) %collective-permute-start.45) | collective-permute-done | bytes 1719328 | tf_op jit(solution)/shard_map/ppermute | solution.py:49
  333.9 23.1 %collective-permute-done = bf16[128,6784]{1,0:T(8,128)(2,1)} collective-permute-done((bf16[128,6784]{1,0:T(8,128)(2,1)}, bf16[128,6784]{1,0:T(8,128)(2,1)}, u32[]{:S(2)}, u32[]{:S(2)}) %collective-permute-start) | collective-permute-done | bytes 1736736 | tf_op jit(solution)/shard_map/ppermute | solution.py:49
  365.2 28.7 %collective-permute-done.44 = bf16[128,6784]{1,0:T(8,128)(2,1)} collective-permute-done((bf16[128,6784]{1,0:T(8,128)(2,1)}, bf16[128,6784]{1,0:T(8,128)(2,1)}, u32[]{:S(2)}, u32[]{:S(2)}) %collective-permute-start.44) | collective-permute-done | bytes 1736736 | tf_op jit(solution)/shard_map/ppermute | solution.py:49
  395.8 36.9 %collective-permute-done.5 = bf16[128,6716]{0,1:T(8,128)(2,1)} collective-permute-done((bf16[128,6716]{0,1:T(8,128)(2,1)}, bf16[128,6716]{0,1:T(8,128)(2,1)}, u32[]{:S(2)}, u32[]{:S(2)}) %collective-permute-start.5) | collective-permute-done | bytes 1719328 | tf_op jit(solution)/shard_map/ppermute | solution.py:49
  452.8 15.9 %collective-permute-done.49 = bf16[128,6716]{0,1:T(8,128)(2,1)} collective-permute-done((bf16[128,6716]{0,1:T(8,128)(2,1)}, bf16[128,6716]{0,1:T(8,128)(2,1)}, u32[]{:S(2)}, u32[]{:S(2)}) %collective-permute-start.49) | collective-permute-done | bytes 1719328 | tf_op jit(solution)/shard_map/ppermute | solution.py:49
  495.2 30.0 %collective-permute-done.48 = bf16[128,6784]{1,0:T(8,128)(2,1)S(1)} collective-permute-done((bf16[128,6784]{1,0:T(8,128)(2,1)}, bf16[128,6784]{1,0:T(8,128)(2,1)S(1)}, u32[]{:S(2)}, u32[]{:S(2)}) %collective-permute-start.48) | collective-permute-done | bytes 1736736 | tf_op jit(solution)/shard_map/ppermute | solution.py:49
  544.6 14.8 %fusion.99 = f32[256,1024]{1,0:T(8,128)S(1)} fusion(bf16[256,13500]{0,1:T(8,128)(2,1)} %log-plus-one_convert_fusion, bf16[1024,13500]{1,0:T(8,128)(2,1)} %maximum_dynamic-update-slice_fusion), kind=kOutput, calls=%fused_computation.417 | convolution fusion | flops 7077888000 | bytes 35608576 | tf_op jit(solution)/shard_map/dot_general | solution.py:39
  562.8 16.5 %fusion.100 = f32[1024,256]{0,1:T(8,128)S(1)} fusion(bf16[1024,13500]{1,0:T(8,128)(2,1)} %maximum_dynamic-update-slice_fusion.8, bf16[256,13500]{0,1:T(8,128)(2,1)} %param.19), kind=kOutput, calls=%fused_computation.418 | convolution fusion | flops 7077888000 | bytes 35608576 | tf_op jit(solution)/shard_map/dot_general | solution.py:39
  599.6 17.7 %collective-permute-done.21 = bf16[256,2048]{1,0:T(8,128)(2,1)S(1)} collective-permute-done((bf16[256,2048]{1,0:T(8,128)(2,1)S(1)}, bf16[256,2048]{1,0:T(8,128)(2,1)S(1)}, u32[]{:S(2)}, u32[]{:S(2)}) %collective-permute-start.21) | collective-permute-done | bytes 1048608 | tf_op jit(solution)/shard_map/ppermute | solution.py:49
  624.5 6.1 fusion.69
  653.1 5.2 fusion.50
  660.9 16.3 %add_convert_fusion.8 = (bf16[256,4096]{1,0:T(8,128)(2,1)S(1)}, f32[256,4096]{1,0:T(8,128)}, f32[256,4096]{1,0:T(8,128)}) fusion(f32[256,4096]{1,0:T(8,128)S(1)} %copy-done.79, bf16[256,1024]{1,0:T(8,128)(2,1)S(1)} %constant_dynamic-update-slice_fusion.48, bf16[1024,4096]{1,0:T(8,128)(2,1)} %constant_dynamic-update-slice_fusion.56), kind=kOutput, calls=%fused_computation.66 | convolution fusion | flops 2222981120 | bytes 23592960 | tf_op jit(solution)/shard_map/dot_general | solution.py:45
  691.1 14.5 %multiply_reduce_fusion = (f32[16,256]{1,0:T(8,128)S(1)}, f32[16,256,1024]{2,1,0:T(8,128)}) fusion(f32[16,256,1024]{2,1,0:T(8,128)} %copy-done, f32[16,256]{1,0:T(8,128)S(1)} %log_add_fusion, bf16[256,16,64]{0,2,1:T(8,128)(2,1)S(1)} %bitcast.291, bf16[1024,16,64]{0,2,1:T(8,128)(2,1)} %bitcast.285), kind=kOutput, calls=%fused_computation.3 | convolution fusion | flops 549449728 | bytes 36208640 | tf_op jit(solution)/shard_map/qhd,khd->hqk/dot_general | solution.py:250
  705.6 9.3 convert_bitcast_fusion
  715.0 8.0 multiply_convert_fusion
  729.3 7.0 fusion.49
  738.3 5.7 convolution_convert_fusion.6
  756.5 4.7 copy.216
  765.7 6.6 copy.217
  779.0 4.7 slice.344
  784.2 11.0 convolution_convert_fusion.2
  795.2 10.7 convolution_convert_fusion.1
  813.4 9.2 collective-permute-done.70
  825.0 4.9 convolution_convert_fusion.5
  838.8 6.4 slice.358
  847.7 5.0 fusion.13
  863.0 9.3 convolution_convert_fusion.3
  872.4 6.4 slice.323
  883.8 5.6 add_convert_fusion.4
  896.3 5.2 add_convert_fusion.5
  909.7 9.4 convolution_convert_fusion.4
  919.2 6.4 slice.316
  928.5 15.7 %collective-permute-done.76 = bf16[2,512,1024]{1,2,0:T(8,128)(2,1)} collective-permute-done((bf16[2,512,1024]{1,2,0:T(8,128)(2,1)}, bf16[2,512,1024]{1,2,0:T(8,128)(2,1)}, u32[]{:S(2)}, u32[]{:S(2)}) %collective-permute-start.76) | collective-permute-done | bytes 2097184 | tf_op jit(solution)/shard_map/ppermute | solution.py:49
  962.2 9.8 add_convert_fusion.2
  972.0 14.7 %reshape.488 = bf16[2,2,128,6716]{2,1,0,3:T(2,128)(2,1)} reshape(bf16[512,6716]{0,1:T(8,128)(2,1)} %add_convert_fusion.2) | data formatting | bytes 13754368 | tf_op jit(solution)/shard_map/reshape | solution.py:107
  986.7 14.7 %fusion.91 = (bf16[2,1,128,6716]{2,1,0,3:T(2,128)(2,1)S(1)}, bf16[2,1,128,6716]{2,1,0,3:T(2,128)(2,1)}) fusion(bf16[2,2,128,6716]{2,1,0,3:T(2,128)(2,1)} %reshape.488), kind=kLoop, calls=%fused_computation.409 | loop fusion | bytes 13754368 | tf_op jit(solution)/shard_map/slice | solution.py:111
  1001.3 13.3 copy.265
  1018.2 9.7 add_convert_fusion
  1030.9 21.8 %collective-permute-done.67 = bf16[2,128,3200]{2,1,0:T(8,128)(2,1)} collective-permute-done((bf16[2,128,3200]{2,1,0:T(8,128)(2,1)}, bf16[2,128,3200]{2,1,0:T(8,128)(2,1)}, u32[]{:S(2)}, u32[]{:S(2)}) %collective-permute-start.67) | collective-permute-done | bytes 1638432 | tf_op jit(solution)/shard_map/ppermute | solution.py:49
  1056.1 6.6 fusion.89
  1063.3 47.0 %collective-permute-done.68 = bf16[128,3200]{1,0:T(8,128)(2,1)S(1)} collective-permute-done((bf16[128,3200]{1,0:T(8,128)(2,1)S(1)}, bf16[128,3200]{1,0:T(8,128)(2,1)S(1)}, u32[]{:S(2)}, u32[]{:S(2)}) %collective-permute-start.68) | collective-permute-done | bytes 819232 | tf_op jit(solution)/shard_map/ppermute | solution.py:49
  1111.7 9.8 add_convert_fusion.3
  1121.5 14.7 %reshape.476 = bf16[2,2,128,6716]{2,1,0,3:T(2,128)(2,1)} reshape(bf16[512,6716]{0,1:T(8,128)(2,1)} %add_convert_fusion.3) | data formatting | bytes 13754368 | tf_op jit(solution)/shard_map/reshape | solution.py:107
  1136.2 14.7 %fusion.92 = (bf16[2,1,128,6716]{2,1,0,3:T(2,128)(2,1)S(1)}, bf16[2,1,128,6716]{2,1,0,3:T(2,128)(2,1)}) fusion(bf16[2,2,128,6716]{2,1,0,3:T(2,128)(2,1)} %reshape.476), kind=kLoop, calls=%fused_computation.410 | loop fusion | bytes 13754368 | tf_op jit(solution)/shard_map/slice | solution.py:111
  1150.9 13.3 copy.266
  1165.8 9.5 add_convert_fusion.1
  1175.3 4.7 fusion.10
  1188.3 29.9 %collective-permute-done.83 = bf16[128,6716]{0,1:T(8,128)(2,1)S(1)} collective-permute-done((bf16[128,6716]{0,1:T(8,128)(2,1)S(1)}, bf16[128,6716]{0,1:T(8,128)(2,1)S(1)}, u32[]{:S(2)}, u32[]{:S(2)}) %collective-permute-start.83) | collective-permute-done | bytes 1719328 | tf_op jit(solution)/shard_map/ppermute | solution.py:49
  1223.8 6.5 fusion.90
  1231.7 45.1 %collective-permute-done.80 = bf16[128,6784]{1,0:T(8,128)(2,1)} collective-permute-done((bf16[128,6784]{1,0:T(8,128)(2,1)}, bf16[128,6784]{1,0:T(8,128)(2,1)}, u32[]{:S(2)}, u32[]{:S(2)}) %collective-permute-start.80) | collective-permute-done | bytes 1736736 | tf_op jit(solution)/shard_map/ppermute | solution.py:49
  1279.9 4.7 fusion.11
  1286.4 22.3 %collective-permute-done.61 = bf16[2,128,6784]{2,1,0:T(8,128)(2,1)} collective-permute-done((bf16[2,128,6784]{2,1,0:T(8,128)(2,1)}, bf16[2,128,6784]{2,1,0:T(8,128)(2,1)}, u32[]{:S(2)}, u32[]{:S(2)}) %collective-permute-start.61) | collective-permute-done | bytes 3473440 | tf_op jit(solution)/shard_map/ppermute | solution.py:49
  1313.3 28.7 %collective-permute-done.65 = bf16[128,6716]{0,1:T(8,128)(2,1)S(1)} collective-permute-done((bf16[128,6716]{0,1:T(8,128)(2,1)S(1)}, bf16[128,6716]{0,1:T(8,128)(2,1)S(1)}, u32[]{:S(2)}, u32[]{:S(2)}) %collective-permute-start.65) | collective-permute-done | bytes 1719328 | tf_op jit(solution)/shard_map/ppermute | solution.py:49
  1347.7 17.5 %convolution_convert_fusion = bf16[256,13500]{0,1:T(8,128)(2,1)} fusion(bf16[256,1024]{1,0:T(8,128)(2,1)} %constant_dynamic-update-slice_fusion.80, bf16[1024,13500]{1,0:T(8,128)(2,1)} %maximum_dynamic-update-slice_fusion.8), kind=kOutput, calls=%fused_computation.1 | convolution fusion | flops 7081344000 | bytes 35084288 | tf_op jit(solution)/shard_map/dot_general | solution.py:45
  1374.7 22.2 %fusion = f32[256,13500]{0,1:T(8,128)} fusion(bf16[256,1024]{1,0:T(8,128)(2,1)} %copy-done.47, bf16[1024,13500]{1,0:T(8,128)(2,1)} %maximum_dynamic-update-slice_fusion, bf16[256,13500]{0,1:T(8,128)(2,1)} %param.15, f32[256]{0:T(256)S(1)} %copy-done.89), kind=kOutput, calls=%fused_computation.8 | convolution fusion | flops 7095168000 | bytes 48909312 | tf_op jit(solution)/shard_map/dot_general | solution.py:45
  1407.9 14.6 %reduce-scatter.15.cloned.1.call-done = bf16[32,6784]{1,0:T(8,128)(2,1)} async-done(((bf16[128,6784]{1,0:T(8,128)(2,1)}), bf16[32,6784]{1,0:T(8,128)(2,1)}) %reduce-scatter.15.cloned.1.call-update) | async-done | bytes 434192 | tf_op jit(solution)/shard_map/reduce_scatter | solution.py:115
  (729 shorter events, 443.7 us)
Async XLA Ops:
  7.3 94.8 %all-gather.13.cloned.1.call-start = ((), (), s32[]{:S(2)}) async-start(), calls=%async_computation.11 | async-start | bytes 1310720 | tf_op jit(solution)/shard_map/all_gather | solution.py:82
  9.3 95.4 %all-gather.11.cloned.1.call-start = ((), (), s32[]{:S(2)}) async-start(), calls=%async_computation.10 | async-start | bytes 1310720 | tf_op jit(solution)/shard_map/all_gather | solution.py:82
  11.5 120.9 %all-gather.9.cloned.1.call-start = ((), (), s32[]{:S(2)}) async-start(), calls=%async_computation.9 | async-start | bytes 2170880 | tf_op jit(solution)/shard_map/all_gather | solution.py:82
  13.4 151.6 %all-gather.17.cloned.1.call-start = ((), (), s32[]{:S(2)}) async-start(), calls=%async_computation.13 | async-start | bytes 2170880 | tf_op jit(solution)/shard_map/all_gather | solution.py:82
  14.3 191.4 %all-gather.7.cloned.1.call-start = ((), (), s32[]{:S(2)}) async-start(), calls=%async_computation.8 | async-start | bytes 2170880 | tf_op jit(solution)/shard_map/all_gather | solution.py:82
  15.2 230.6 %all-gather.15.cloned.1.call-start = ((), (), s32[]{:S(2)}) async-start(), calls=%async_computation.12 | async-start | bytes 2170880 | tf_op jit(solution)/shard_map/all_gather | solution.py:82
  47.7 49.7 %collective-permute-start.14 = (bf16[128,3200]{1,0:T(8,128)(2,1)}, bf16[128,3200]{1,0:T(8,128)(2,1)}, u32[]{:S(2)}, u32[]{:S(2)}) collective-permute-start(bf16[128,3200]{1,0:T(8,128)(2,1)} %all_gather.26), channel_id=1, source_target_pairs={{0,2},{2,0},{1,3},{3,1},{4,6},{6,4},{5,7},{7,5},{8,10},{10,8},{9,1... | collective-permute-start | bytes 2457608 | tf_op jit(solution)/shard_map/ppermute | solution.py:49
  49.1 46.4 %collective-permute-start.15 = (bf16[128,3200]{1,0:T(8,128)(2,1)}, bf16[128,3200]{1,0:T(8,128)(2,1)}, u32[]{:S(2)}, u32[]{:S(2)}) collective-permute-start(bf16[128,3200]{1,0:T(8,128)(2,1)} %all_gather.26), channel_id=1, source_target_pairs={{0,4},{4,0},{1,5},{5,1},{2,6},{6,2},{3,7},{7,3},{8,12},{12,8},{9,1... | collective-permute-start | bytes 2457608 | tf_op jit(solution)/shard_map/ppermute | solution.py:49
  68.0 1297.2 %reduce-scatter.19.cloned.1.call-start = ((), (), s32[]{:S(2)}) async-start(), calls=%async_computation.16 | async-start | bytes 327680 | tf_op jit(solution)/shard_map/reduce_scatter | solution.py:115
  102.1 107.1 %collective-permute-start.37 = (bf16[512,1024]{0,1:T(8,128)(2,1)}, bf16[512,1024]{0,1:T(8,128)(2,1)}, u32[]{:S(2)}, u32[]{:S(2)}) collective-permute-start(bf16[512,1024]{0,1:T(8,128)(2,1)} %all-gather.13.cloned.1.call-done), channel_id=1, source_target_pairs={{0,2},{2,0},{1,3},{3,1},{4,6},{6,4},{5,7},{7,5},{8,10},{10,8},{9,1... | collective-permute-start | bytes 3145736 | tf_op jit(solution)/shard_map/ppermute | solution.py:49
  117.0 92.2 %collective-permute-start.38 = (bf16[512,1024]{0,1:T(8,128)(2,1)}, bf16[512,1024]{0,1:T(8,128)(2,1)}, u32[]{:S(2)}, u32[]{:S(2)}) collective-permute-start(bf16[512,1024]{0,1:T(8,128)(2,1)} %all-gather.13.cloned.1.call-done), channel_id=1, source_target_pairs={{0,4},{4,0},{1,5},{5,1},{2,6},{6,2},{3,7},{7,3},{8,12},{12,8},{9,1... | collective-permute-start | bytes 3145736 | tf_op jit(solution)/shard_map/ppermute | solution.py:49
  120.8 89.9 %collective-permute-start.40 = (bf16[512,1024]{0,1:T(8,128)(2,1)}, bf16[512,1024]{0,1:T(8,128)(2,1)}, u32[]{:S(2)}, u32[]{:S(2)}) collective-permute-start(bf16[512,1024]{0,1:T(8,128)(2,1)} %all-gather.13.cloned.1.call-done), channel_id=1, source_target_pairs={{0,1},{1,0},{2,3},{3,2},{4,5},{5,4},{6,7},{7,6},{8,9},{9,8},{10,11... | collective-permute-start | bytes 3145736 | tf_op jit(solution)/shard_map/ppermute | solution.py:49
  124.4 87.8 %collective-permute-start.30 = (bf16[128,4096]{1,0:T(8,128)(2,1)}, bf16[128,4096]{1,0:T(8,128)(2,1)}, u32[]{:S(2)}, u32[]{:S(2)}) collective-permute-start(bf16[128,4096]{1,0:T(8,128)(2,1)} %all-gather.11.cloned.1.call-done), channel_id=1, source_target_pairs={{0,2},{2,0},{1,3},{3,1},{4,6},{6,4},{5,7},{7,5},{8,10},{10,8},{9,1... | collective-permute-start | bytes 3145736 | tf_op jit(solution)/shard_map/ppermute | solution.py:49
  128.2 84.5 %collective-permute-start.31 = (bf16[128,4096]{1,0:T(8,128)(2,1)}, bf16[128,4096]{1,0:T(8,128)(2,1)}, u32[]{:S(2)}, u32[]{:S(2)}) collective-permute-start(bf16[128,4096]{1,0:T(8,128)(2,1)} %all-gather.11.cloned.1.call-done), channel_id=1, source_target_pairs={{0,4},{4,0},{1,5},{5,1},{2,6},{6,2},{3,7},{7,3},{8,12},{12,8},{9,1... | collective-permute-start | bytes 3145736 | tf_op jit(solution)/shard_map/ppermute | solution.py:49
  209.2 42.3 %collective-permute-start.33 = (bf16[128,4096]{1,0:T(8,128)(2,1)}, bf16[128,4096]{1,0:T(8,128)(2,1)}, u32[]{:S(2)}, u32[]{:S(2)}) collective-permute-start(bf16[128,4096]{1,0:T(8,128)(2,1)} %all-gather.11.cloned.1.call-done), channel_id=1, source_target_pairs={{0,1},{1,0},{2,3},{3,2},{4,5},{5,4},{6,7},{7,6},{8,9},{9,8},{10,11... | collective-permute-start | bytes 3145736 | tf_op jit(solution)/shard_map/ppermute | solution.py:49
  209.2 73.1 %collective-permute-start.1 = (bf16[128,6716]{0,1:T(8,128)(2,1)}, bf16[128,6716]{0,1:T(8,128)(2,1)}, u32[]{:S(2)}, u32[]{:S(2)}) collective-permute-start(bf16[128,6716]{0,1:T(8,128)(2,1)} %copy.175), channel_id=1, source_target_pairs={{0,2},{2,0},{1,3},{3,1},{4,6},{6,4},{5,7},{7,5},{8,10},{10,8},{9,1... | collective-permute-start | bytes 5157896 | tf_op jit(solution)/shard_map/ppermute | solution.py:49
  210.8 71.5 %collective-permute-start.3 = (bf16[128,6716]{0,1:T(8,128)(2,1)}, bf16[128,6716]{0,1:T(8,128)(2,1)S(1)}, u32[]{:S(2)}, u32[]{:S(2)}) collective-permute-start(bf16[128,6716]{0,1:T(8,128)(2,1)} %copy.175), channel_id=1, source_target_pairs={{0,4},{4,0},{1,5},{5,1},{2,6},{6,2},{3,7},{7,3},{8,12},{12,8},{9,1... | collective-permute-start | bytes 5157896 | tf_op jit(solution)/shard_map/ppermute | solution.py:49
  212.2 59.7 %collective-permute-start.39 = (bf16[512,1024]{0,1:T(8,128)(2,1)}, bf16[512,1024]{0,1:T(8,128)(2,1)}, u32[]{:S(2)}, u32[]{:S(2)}) collective-permute-start(bf16[512,1024]{0,1:T(8,128)(2,1)} %collective-permute-done.38), channel_id=1, source_target_pairs={{0,2},{2,0},{1,3},{3,1},{4,6},{6,4},{5,7},{7,5},{8,10},{10,8},{9,1... | collective-permute-start | bytes 3145736 | tf_op jit(solution)/shard_map/ppermute | solution.py:49
  212.8 59.2 %collective-permute-start.41 = (bf16[512,1024]{0,1:T(8,128)(2,1)}, bf16[512,1024]{0,1:T(8,128)(2,1)}, u32[]{:S(2)}, u32[]{:S(2)}) collective-permute-start(bf16[512,1024]{0,1:T(8,128)(2,1)} %collective-permute-done.37), channel_id=1, source_target_pairs={{0,1},{1,0},{2,3},{3,2},{4,5},{5,4},{6,7},{7,6},{8,9},{9,8},{10,11... | collective-permute-start | bytes 3145736 | tf_op jit(solution)/shard_map/ppermute | solution.py:49
  280.8 44.3 %collective-permute-start.47 = (bf16[128,6716]{0,1:T(8,128)(2,1)S(1)}, bf16[128,6716]{0,1:T(8,128)(2,1)}, u32[]{:S(2)}, u32[]{:S(2)}) collective-permute-start(bf16[128,6716]{0,1:T(8,128)(2,1)S(1)} %copy-done.63), channel_id=1, source_target_pairs={{0,4},{4,0},{1,5},{5,1},{2,6},{6,2},{3,7},{7,3},{8,12},{12,8},{9,1... | collective-permute-start | bytes 5157896 | tf_op jit(solution)/shard_map/ppermute | solution.py:49
  282.3 48.3 %collective-permute-start.51 = (bf16[128,6716]{0,1:T(8,128)(2,1)S(1)}, bf16[128,6716]{0,1:T(8,128)(2,1)}, u32[]{:S(2)}, u32[]{:S(2)}) collective-permute-start(bf16[128,6716]{0,1:T(8,128)(2,1)S(1)} %copy-done.63), channel_id=1, source_target_pairs={{0,1},{1,0},{2,3},{3,2},{4,5},{5,4},{6,7},{7,6},{8,9},{9,8},{10,11... | collective-permute-start | bytes 5157896 | tf_op jit(solution)/shard_map/ppermute | solution.py:49
  282.3 74.7 %collective-permute-start = (bf16[128,6784]{1,0:T(8,128)(2,1)}, bf16[128,6784]{1,0:T(8,128)(2,1)}, u32[]{:S(2)}, u32[]{:S(2)}) collective-permute-start(bf16[128,6784]{1,0:T(8,128)(2,1)} %all-gather.7.cloned.1.call-done), channel_id=1, source_target_pairs={{0,2},{2,0},{1,3},{3,1},{4,6},{6,4},{5,7},{7,5},{8,10},{10,8},{9,1... | collective-permute-start | bytes 5210120 | tf_op jit(solution)/shard_map/ppermute | solution.py:49
  291.9 69.2 %collective-permute-start.2 = (bf16[128,6784]{1,0:T(8,128)(2,1)}, bf16[128,6784]{1,0:T(8,128)(2,1)}, u32[]{:S(2)}, u32[]{:S(2)}) collective-permute-start(bf16[128,6784]{1,0:T(8,128)(2,1)} %all-gather.7.cloned.1.call-done), channel_id=1, source_target_pairs={{0,4},{4,0},{1,5},{5,1},{2,6},{6,2},{3,7},{7,3},{8,12},{12,8},{9,1... | collective-permute-start | bytes 5210120 | tf_op jit(solution)/shard_map/ppermute | solution.py:49
  319.8 74.0 %collective-permute-start.44 = (bf16[128,6784]{1,0:T(8,128)(2,1)}, bf16[128,6784]{1,0:T(8,128)(2,1)}, u32[]{:S(2)}, u32[]{:S(2)}) collective-permute-start(bf16[128,6784]{1,0:T(8,128)(2,1)} %all-gather.15.cloned.1.call-done), channel_id=1, source_target_pairs={{0,2},{2,0},{1,3},{3,1},{4,6},{6,4},{5,7},{7,5},{8,10},{10,8},{9,1... | collective-permute-start | bytes 5210120 | tf_op jit(solution)/shard_map/ppermute | solution.py:49
  325.1 70.6 %collective-permute-start.46 = (bf16[128,6784]{1,0:T(8,128)(2,1)}, bf16[128,6784]{1,0:T(8,128)(2,1)}, u32[]{:S(2)}, u32[]{:S(2)}) collective-permute-start(bf16[128,6784]{1,0:T(8,128)(2,1)} %all-gather.15.cloned.1.call-done), channel_id=1, source_target_pairs={{0,4},{4,0},{1,5},{5,1},{2,6},{6,2},{3,7},{7,3},{8,12},{12,8},{9,1... | collective-permute-start | bytes 5210120 | tf_op jit(solution)/shard_map/ppermute | solution.py:49
  330.6 102.1 %collective-permute-start.5 = (bf16[128,6716]{0,1:T(8,128)(2,1)}, bf16[128,6716]{0,1:T(8,128)(2,1)}, u32[]{:S(2)}, u32[]{:S(2)}) collective-permute-start(bf16[128,6716]{0,1:T(8,128)(2,1)} %collective-permute-done.1), channel_id=1, source_target_pairs={{0,4},{4,0},{1,5},{5,1},{2,6},{6,2},{3,7},{7,3},{8,12},{12,8},{9,1... | collective-permute-start | bytes 5157896 | tf_op jit(solution)/shard_map/ppermute | solution.py:49
  357.0 75.6 %collective-permute-start.9 = (bf16[128,6716]{0,1:T(8,128)(2,1)}, bf16[128,6716]{0,1:T(8,128)(2,1)S(1)}, u32[]{:S(2)}, u32[]{:S(2)}) collective-permute-start(bf16[128,6716]{0,1:T(8,128)(2,1)} %collective-permute-done.1), channel_id=1, source_target_pairs={{0,1},{1,0},{2,3},{3,2},{4,5},{5,4},{6,7},{7,6},{8,9},{9,8},{10,11... | collective-permute-start | bytes 5157896 | tf_op jit(solution)/shard_map/ppermute | solution.py:49
  361.1 75.7 %collective-permute-start.11 = (bf16[128,6716]{0,1:T(8,128)(2,1)S(1)}, bf16[128,6716]{0,1:T(8,128)(2,1)S(1)}, u32[]{:S(2)}, u32[]{:S(2)}) collective-permute-start(bf16[128,6716]{0,1:T(8,128)(2,1)S(1)} %copy-done.62), channel_id=1, source_target_pairs={{0,1},{1,0},{2,3},{3,2},{4,5},{5,4},{6,7},{7,6},{8,9},{9,8},{10,11... | collective-permute-start | bytes 5157896 | tf_op jit(solution)/shard_map/ppermute | solution.py:49
  393.9 74.9 %collective-permute-start.49 = (bf16[128,6716]{0,1:T(8,128)(2,1)}, bf16[128,6716]{0,1:T(8,128)(2,1)}, u32[]{:S(2)}, u32[]{:S(2)}) collective-permute-start(bf16[128,6716]{0,1:T(8,128)(2,1)} %collective-permute-done.45), channel_id=1, source_target_pairs={{0,4},{4,0},{1,5},{5,1},{2,6},{6,2},{3,7},{7,3},{8,12},{12,8},{9,1... | collective-permute-start | bytes 5157896 | tf_op jit(solution)/shard_map/ppermute | solution.py:49
  395.8 76.8 %collective-permute-start.53 = (bf16[128,6716]{0,1:T(8,128)(2,1)}, bf16[128,6716]{0,1:T(8,128)(2,1)}, u32[]{:S(2)}, u32[]{:S(2)}) collective-permute-start(bf16[128,6716]{0,1:T(8,128)(2,1)} %collective-permute-done.45), channel_id=1, source_target_pairs={{0,1},{1,0},{2,3},{3,2},{4,5},{5,4},{6,7},{7,6},{8,9},{9,8},{10,11... | collective-permute-start | bytes 5157896 | tf_op jit(solution)/shard_map/ppermute | solution.py:49
  432.6 44.3 %collective-permute-start.55 = (bf16[128,6716]{0,1:T(8,128)(2,1)}, bf16[128,6716]{0,1:T(8,128)(2,1)}, u32[]{:S(2)}, u32[]{:S(2)}) collective-permute-start(bf16[128,6716]{0,1:T(8,128)(2,1)} %collective-permute-done.47), channel_id=1, source_target_pairs={{0,1},{1,0},{2,3},{3,2},{4,5},{5,4},{6,7},{7,6},{8,9},{9,8},{10,11... | collective-permute-start | bytes 5157896 | tf_op jit(solution)/shard_map/ppermute | solution.py:49
  432.6 48.1 %collective-permute-start.4 = (bf16[128,6784]{1,0:T(8,128)(2,1)}, bf16[128,6784]{1,0:T(8,128)(2,1)}, u32[]{:S(2)}, u32[]{:S(2)}) collective-permute-start(bf16[128,6784]{1,0:T(8,128)(2,1)} %collective-permute-done.2), channel_id=1, source_target_pairs={{0,2},{2,0},{1,3},{3,1},{4,6},{6,4},{5,7},{7,5},{8,10},{10,8},{9,1... | collective-permute-start | bytes 5210120 | tf_op jit(solution)/shard_map/ppermute | solution.py:49
  436.8 48.4 %collective-permute-start.6 = (bf16[128,6784]{1,0:T(8,128)(2,1)}, bf16[128,6784]{1,0:T(8,128)(2,1)}, u32[]{:S(2)}, u32[]{:S(2)}) collective-permute-start(bf16[128,6784]{1,0:T(8,128)(2,1)} %all-gather.7.cloned.1.call-done), channel_id=1, source_target_pairs={{0,1},{1,0},{2,3},{3,2},{4,5},{5,4},{6,7},{7,6},{8,9},{9,8},{10,11... | collective-permute-start | bytes 5210120 | tf_op jit(solution)/shard_map/ppermute | solution.py:49
  468.8 58.6 %collective-permute-start.50 = (bf16[128,6784]{1,0:T(8,128)(2,1)}, bf16[128,6784]{1,0:T(8,128)(2,1)}, u32[]{:S(2)}, u32[]{:S(2)}) collective-permute-start(bf16[128,6784]{1,0:T(8,128)(2,1)} %all-gather.15.cloned.1.call-done), channel_id=1, source_target_pairs={{0,1},{1,0},{2,3},{3,2},{4,5},{5,4},{6,7},{7,6},{8,9},{9,8},{10,11... | collective-permute-start | bytes 5210120 | tf_op jit(solution)/shard_map/ppermute | solution.py:49
  472.6 120.0 %collective-permute-start.42 = (bf16[512,1024]{0,1:T(8,128)(2,1)}, bf16[512,1024]{0,1:T(8,128)(2,1)}, u32[]{:S(2)}, u32[]{:S(2)}) collective-permute-start(bf16[512,1024]{0,1:T(8,128)(2,1)} %collective-permute-done.38), channel_id=1, source_target_pairs={{0,1},{1,0},{2,3},{3,2},{4,5},{5,4},{6,7},{7,6},{8,9},{9,8},{10,11... | collective-permute-start | bytes 3145736 | tf_op jit(solution)/shard_map/ppermute | solution.py:49
  489.1 42.3 %collective-permute-start.52 = (bf16[128,6784]{1,0:T(8,128)(2,1)}, bf16[128,6784]{1,0:T(8,128)(2,1)S(1)}, u32[]{:S(2)}, u32[]{:S(2)}) collective-permute-start(bf16[128,6784]{1,0:T(8,128)(2,1)} %collective-permute-done.44), channel_id=1, source_target_pairs={{0,1},{1,0},{2,3},{3,2},{4,5},{5,4},{6,7},{7,6},{8,9},{9,8},{10,11... | collective-permute-start | bytes 5210120 | tf_op jit(solution)/shard_map/ppermute | solution.py:49
  533.6 61.3 %collective-permute-start.43 = (bf16[512,1024]{0,1:T(8,128)(2,1)}, bf16[512,1024]{0,1:T(8,128)(2,1)}, u32[]{:S(2)}, u32[]{:S(2)}) collective-permute-start(bf16[512,1024]{0,1:T(8,128)(2,1)} %collective-permute-done.39), channel_id=1, source_target_pairs={{0,1},{1,0},{2,3},{3,2},{4,5},{5,4},{6,7},{7,6},{8,9},{9,8},{10,11... | collective-permute-start | bytes 3145736 | tf_op jit(solution)/shard_map/ppermute | solution.py:49
  536.0 61.1 %collective-permute-start.36 = (bf16[128,4096]{1,0:T(8,128)(2,1)}, bf16[128,4096]{1,0:T(8,128)(2,1)}, u32[]{:S(2)}, u32[]{:S(2)}) collective-permute-start(bf16[128,4096]{1,0:T(8,128)(2,1)} %collective-permute-done.32), channel_id=1, source_target_pairs={{0,1},{1,0},{2,3},{3,2},{4,5},{5,4},{6,7},{7,6},{8,9},{9,8},{10,11... | collective-permute-start | bytes 3145736 | tf_op jit(solution)/shard_map/ppermute | solution.py:49
  783.7 112.6 %collective-permute-start.72 = (bf16[512,4096]{1,0:T(8,128)(2,1)}, bf16[512,4096]{1,0:T(8,128)(2,1)}, u32[]{:S(2)}, u32[]{:S(2)}) collective-permute-start(bf16[512,4096]{1,0:T(8,128)(2,1)} %slice.344), channel_id=1, source_target_pairs={{0,1},{1,0},{2,3},{3,2},{4,5},{5,4},{6,7},{7,6},{8,9},{9,8},{10,11... | collective-permute-start | bytes 12582920 | tf_op jit(solution)/shard_map/ppermute | solution.py:49
  834.5 49.3 %collective-permute-start.75 = (bf16[2048,1024]{1,0:T(8,128)(2,1)}, bf16[2048,1024]{1,0:T(8,128)(2,1)}, u32[]{:S(2)}, u32[]{:S(2)}) collective-permute-start(bf16[2048,1024]{1,0:T(8,128)(2,1)} %slice.350), channel_id=1, source_target_pairs={{0,1},{1,0},{2,3},{3,2},{4,5},{5,4},{6,7},{7,6},{8,9},{9,8},{10,11... | collective-permute-start | bytes 12582920 | tf_op jit(solution)/shard_map/ppermute | solution.py:49
  838.3 123.4 %collective-permute-start.81 = (bf16[512,6716]{0,1:T(8,128)(2,1)}, bf16[512,6716]{0,1:T(8,128)(2,1)}, u32[]{:S(2)}, u32[]{:S(2)}) collective-permute-start(bf16[512,6716]{0,1:T(8,128)(2,1)} %slice.364), channel_id=1, source_target_pairs={{0,1},{1,0},{2,3},{3,2},{4,5},{5,4},{6,7},{7,6},{8,9},{9,8},{10,11... | collective-permute-start | bytes 20631560 | tf_op jit(solution)/shard_map/ppermute | solution.py:49
  845.2 171.3 %collective-permute-start.78 = (bf16[512,6784]{1,0:T(8,128)(2,1)}, bf16[512,6784]{1,0:T(8,128)(2,1)}, u32[]{:S(2)}, u32[]{:S(2)}) collective-permute-start(bf16[512,6784]{1,0:T(8,128)(2,1)} %slice.358), channel_id=1, source_target_pairs={{0,1},{1,0},{2,3},{3,2},{4,5},{5,4},{6,7},{7,6},{8,9},{9,8},{10,11... | collective-permute-start | bytes 20840456 | tf_op jit(solution)/shard_map/ppermute | solution.py:49
  846.0 551.0 %reduce-scatter.21.cloned.1.call-start = ((), (), s32[]{:S(2)}) async-start(), calls=%async_computation.17 | async-start | bytes 1310720 | tf_op jit(solution)/shard_map/reduce_scatter | solution.py:115
  895.9 48.3 %collective-permute-start.76 = (bf16[2,512,1024]{1,2,0:T(8,128)(2,1)}, bf16[2,512,1024]{1,2,0:T(8,128)(2,1)}, u32[]{:S(2)}, u32[]{:S(2)}) collective-permute-start(bf16[2,512,1024]{1,2,0:T(8,128)(2,1)} %copy.229), channel_id=1, source_target_pairs={{0,4},{4,0},{1,5},{5,1},{2,6},{6,2},{3,7},{7,3},{8,12},{12,8},{9,1... | collective-permute-start | bytes 6291464 | tf_op jit(solution)/shard_map/ppermute | solution.py:49
  904.2 48.0 %collective-permute-start.73 = (bf16[2,128,4096]{2,1,0:T(8,128)(2,1)}, bf16[2,128,4096]{2,1,0:T(8,128)(2,1)}, u32[]{:S(2)}, u32[]{:S(2)}) collective-permute-start(bf16[2,128,4096]{2,1,0:T(8,128)(2,1)} %slice_bitcast_fusion), channel_id=1, source_target_pairs={{0,2},{2,0},{1,3},{3,1},{4,6},{6,4},{5,7},{7,5},{8,10},{10,8},{9,1... | collective-permute-start | bytes 6291464 | tf_op jit(solution)/shard_map/ppermute | solution.py:49
  909.7 45.9 %collective-permute-start.66 = (bf16[512,3200]{1,0:T(8,128)(2,1)}, bf16[512,3200]{1,0:T(8,128)(2,1)}, u32[]{:S(2)}, u32[]{:S(2)}) collective-permute-start(bf16[512,3200]{1,0:T(8,128)(2,1)} %slice.329), channel_id=1, source_target_pairs={{0,1},{1,0},{2,3},{3,2},{4,5},{5,4},{6,7},{7,6},{8,9},{9,8},{10,11... | collective-permute-start | bytes 9830408 | tf_op jit(solution)/shard_map/ppermute | solution.py:49
  944.2 167.4 %collective-permute-start.63 = (bf16[512,6716]{0,1:T(8,128)(2,1)}, bf16[512,6716]{0,1:T(8,128)(2,1)}, u32[]{:S(2)}, u32[]{:S(2)}) collective-permute-start(bf16[512,6716]{0,1:T(8,128)(2,1)} %slice.323), channel_id=1, source_target_pairs={{0,1},{1,0},{2,3},{3,2},{4,5},{5,4},{6,7},{7,6},{8,9},{9,8},{10,11... | collective-permute-start | bytes 20631560 | tf_op jit(solution)/shard_map/ppermute | solution.py:49
  952.2 213.7 %collective-permute-start.60 = (bf16[512,6784]{1,0:T(8,128)(2,1)}, bf16[512,6784]{1,0:T(8,128)(2,1)}, u32[]{:S(2)}, u32[]{:S(2)}) collective-permute-start(bf16[512,6784]{1,0:T(8,128)(2,1)} %slice.316), channel_id=1, source_target_pairs={{0,1},{1,0},{2,3},{3,2},{4,5},{5,4},{6,7},{7,6},{8,9},{9,8},{10,11... | collective-permute-start | bytes 20840456 | tf_op jit(solution)/shard_map/ppermute | solution.py:49
  955.6 59.0 %collective-permute-start.74 = (bf16[128,4096]{1,0:T(8,128)(2,1)}, bf16[128,4096]{1,0:T(8,128)(2,1)S(1)}, u32[]{:S(2)}, u32[]{:S(2)}) collective-permute-start(bf16[128,4096]{1,0:T(8,128)(2,1)} %slice_bitcast_fusion.12), channel_id=1, source_target_pairs={{0,4},{4,0},{1,5},{5,1},{2,6},{6,2},{3,7},{7,3},{8,12},{12,8},{9,1... | collective-permute-start | bytes 3145736 | tf_op jit(solution)/shard_map/ppermute | solution.py:49
  961.7 66.2 %collective-permute-start.77 = (bf16[512,1024]{0,1:T(8,128)(2,1)}, bf16[512,1024]{0,1:T(8,128)(2,1)}, u32[]{:S(2)}, u32[]{:S(2)}) collective-permute-start(bf16[512,1024]{0,1:T(8,128)(2,1)} %slice_bitcast_fusion.10), channel_id=1, source_target_pairs={{0,2},{2,0},{1,3},{3,1},{4,6},{6,4},{5,7},{7,5},{8,10},{10,8},{9,1... | collective-permute-start | bytes 3145736 | tf_op jit(solution)/shard_map/ppermute | solution.py:49
  1016.5 383.4 %reduce-scatter.27.cloned.1.call-start = ((), (), s32[]{:S(2)}) async-start(), calls=%async_computation.20 | async-start | bytes 1310720
  1016.5 158.8 %collective-permute-start.82 = (bf16[2,128,6716]{1,0,2:T(2,128)(2,1)}, bf16[2,128,6716]{1,0,2:T(2,128)(2,1)}, u32[]{:S(2)}, u32[]{:S(2)}) collective-permute-start(bf16[2,128,6716]{1,0,2:T(2,128)(2,1)} %bitcast.296), channel_id=1, source_target_pairs={{0,2},{2,0},{1,3},{3,1},{4,6},{6,4},{5,7},{7,5},{8,10},{10,8},{9,1... | collective-permute-start | bytes 10315784 | tf_op jit(solution)/shard_map/ppermute | solution.py:49
  1030.8 371.3 %reduce-scatter.17.cloned.1.call-start = ((), (), s32[]{:S(2)}) async-start(), calls=%async_computation.15 | async-start | bytes 1024000 | tf_op jit(solution)/shard_map/reduce_scatter | solution.py:115
  1054.5 55.8 %collective-permute-start.68 = (bf16[128,3200]{1,0:T(8,128)(2,1)S(1)}, bf16[128,3200]{1,0:T(8,128)(2,1)S(1)}, u32[]{:S(2)}, u32[]{:S(2)}) collective-permute-start(bf16[128,3200]{1,0:T(8,128)(2,1)S(1)} %slice_bitcast_fusion.14), channel_id=1, source_target_pairs={{0,2},{2,0},{1,3},{3,1},{4,6},{6,4},{5,7},{7,5},{8,10},{10,8},{9,1... | collective-permute-start | bytes 2457608 | tf_op jit(solution)/shard_map/ppermute | solution.py:49
  1062.7 119.0 %collective-permute-start.79 = (bf16[2,128,6784]{2,1,0:T(8,128)(2,1)}, bf16[2,128,6784]{2,1,0:T(8,128)(2,1)S(1)}, u32[]{:S(2)}, u32[]{:S(2)}) collective-permute-start(bf16[2,128,6784]{2,1,0:T(8,128)(2,1)} %bitcast.91), channel_id=1, source_target_pairs={{0,4},{4,0},{1,5},{5,1},{2,6},{6,2},{3,7},{7,3},{8,12},{12,8},{9,1... | collective-permute-start | bytes 10420232 | tf_op jit(solution)/shard_map/ppermute | solution.py:49
  1111.4 294.0 %reduce-scatter.29.cloned.1.call-start = ((), (), s32[]{:S(2)}) async-start(), calls=%async_computation.21 | async-start | bytes 2170880 | tf_op jit(solution)/shard_map/reduce_scatter | solution.py:115
  1164.2 115.7 %collective-permute-start.64 = (bf16[2,128,6716]{1,0,2:T(2,128)(2,1)}, bf16[2,128,6716]{1,0,2:T(2,128)(2,1)}, u32[]{:S(2)}, u32[]{:S(2)}) collective-permute-start(bf16[2,128,6716]{1,0,2:T(2,128)(2,1)} %bitcast.259), channel_id=1, source_target_pairs={{0,2},{2,0},{1,3},{3,1},{4,6},{6,4},{5,7},{7,5},{8,10},{10,8},{9,1... | collective-permute-start | bytes 10315784 | tf_op jit(solution)/shard_map/ppermute | solution.py:49
  1187.9 88.9 %collective-permute-start.80 = (bf16[128,6784]{1,0:T(8,128)(2,1)}, bf16[128,6784]{1,0:T(8,128)(2,1)}, u32[]{:S(2)}, u32[]{:S(2)}) collective-permute-start(bf16[128,6784]{1,0:T(8,128)(2,1)} %slice_bitcast_fusion.2), channel_id=1, source_target_pairs={{0,2},{2,0},{1,3},{3,1},{4,6},{6,4},{5,7},{7,5},{8,10},{10,8},{9,1... | collective-permute-start | bytes 5210120 | tf_op jit(solution)/shard_map/ppermute | solution.py:49
  1223.7 181.8 %reduce-scatter.23.cloned.1.call-start = ((), (), s32[]{:S(2)}) async-start(), calls=%async_computation.18 | async-start | bytes 2170880 | tf_op jit(solution)/shard_map/reduce_scatter | solution.py:115
  1230.2 78.4 %collective-permute-start.61 = (bf16[2,128,6784]{2,1,0:T(8,128)(2,1)}, bf16[2,128,6784]{2,1,0:T(8,128)(2,1)}, u32[]{:S(2)}, u32[]{:S(2)}) collective-permute-start(bf16[2,128,6784]{2,1,0:T(8,128)(2,1)} %bitcast.56), channel_id=1, source_target_pairs={{0,4},{4,0},{1,5},{5,1},{2,6},{6,2},{3,7},{7,3},{8,12},{12,8},{9,1... | collective-permute-start | bytes 10420232 | tf_op jit(solution)/shard_map/ppermute | solution.py:49
  1279.9 128.1 %reduce-scatter.25.cloned.1.call-start = ((), (), s32[]{:S(2)}) async-start(), calls=%async_computation.19 | async-start | bytes 2170880 | tf_op jit(solution)/shard_map/reduce_scatter | solution.py:115
  1284.8 57.1 %collective-permute-start.65 = (bf16[128,6716]{0,1:T(8,128)(2,1)S(1)}, bf16[128,6716]{0,1:T(8,128)(2,1)S(1)}, u32[]{:S(2)}, u32[]{:S(2)}) collective-permute-start(bf16[128,6716]{0,1:T(8,128)(2,1)S(1)} %slice_bitcast_fusion.8), channel_id=1, source_target_pairs={{0,4},{4,0},{1,5},{5,1},{2,6},{6,2},{3,7},{7,3},{8,12},{12,8},{9,1... | collective-permute-start | bytes 5157896 | tf_op jit(solution)/shard_map/ppermute | solution.py:49
  1312.9 58.6 %collective-permute-start.62 = (bf16[128,6784]{1,0:T(8,128)(2,1)}, bf16[128,6784]{1,0:T(8,128)(2,1)}, u32[]{:S(2)}, u32[]{:S(2)}) collective-permute-start(bf16[128,6784]{1,0:T(8,128)(2,1)} %slice_bitcast_fusion.4), channel_id=1, source_target_pairs={{0,2},{2,0},{1,3},{3,1},{4,6},{6,4},{5,7},{7,5},{8,10},{10,8},{9,1... | collective-permute-start | bytes 5210120 | tf_op jit(solution)/shard_map/ppermute | solution.py:49
  1347.4 75.1 %reduce-scatter.15.cloned.1.call-start = ((), (), s32[]{:S(2)}) async-start(), calls=%async_computation.14 | async-start | bytes 2170880 | tf_op jit(solution)/shard_map/reduce_scatter | solution.py:115
  (146 other events, 2525.9 us)
Sparse Core Ops, SparseCore 0:
  10.2 42.8 all-gather.12
  54.7 28.3 all-gather.10
  85.3 39.0 all-gather.8
  126.4 38.6 all-gather.16
  167.0 38.6 all-gather.6
  207.1 38.6 all-gather.14
  846.1 16.8 reduce-scatter.18
  1016.6 26.0 reduce-scatter.20
  1045.0 25.7 reduce-scatter.26
  1111.5 22.5 reduce-scatter.16
  1223.8 35.8 reduce-scatter.28
  1280.0 36.7 reduce-scatter.22
  1347.5 35.7 reduce-scatter.24
  1385.5 36.9 reduce-scatter.14

commit v2 on v1

--- a/solution.py
+++ b/solution.py
@@ -100,29 +100,52 @@
     )
 
 
-def scatter_rows(part, first, second):
-    half = part.shape[0] // 2
-    other = swap(part[half:], "c")
-    part = part[:half].astype(jnp.float32) + other.astype(jnp.float32)
-    part = part.astype(jnp.bfloat16).reshape((2, 2, half // 4, -1))
-    if first == "x":
-        part = part[0].astype(jnp.float32) + swap(part[1], "x").astype(jnp.float32)
-    else:
-        part = part[:, 0].astype(jnp.float32) + swap(part[:, 1], "y").astype(jnp.float32)
-    part = part.astype(jnp.bfloat16)
-    part = part[0].astype(jnp.float32) + swap(part[1], second).astype(jnp.float32)
-    part = part.astype(jnp.bfloat16)
-    return lax.psum_scatter(part, "h", scatter_dimension=0, tiled=True).astype(jnp.float32)
+def with_other_core(value):
+    return jnp.concatenate([value, swap(value, "c")], axis=0)
+
+
+def own_half(left):
+    half = left.shape[1] // 2
+    return jnp.concatenate([left[:, :half], swap(left[:, half:], "c")], axis=0)
+
+
+def sum_over_h(part):
+    n_h = lax.axis_size("h")
+    rows = part.shape[0] // n_h
+    at = lax.axis_index("h")
+    total = lax.dynamic_slice_in_dim(part, at * rows, rows, 0).astype(jnp.float32)
+    for step in range(1, n_h):
+        send = lax.dynamic_slice_in_dim(part, lax.rem(at + step, n_h) * rows, rows, 0)
+        ring = [(i, (i + step) % n_h) for i in range(n_h)]
+        total = total + lax.ppermute(send, "h", ring).astype(jnp.float32)
+    return total
+
+
+def scatter(left, right, first, second):
+    w = left.shape[1] // 4
+    near, by_y, by_x, far = (left[:, k * w : (k + 1) * w] for k in range(4))
+    one, two = (by_x, by_y) if first == "x" else (by_y, by_x)
+    got_far = swap(contract_rows(far, right).astype(jnp.bfloat16), first).astype(jnp.float32)
+    got_one = swap(contract_rows(one, right).astype(jnp.bfloat16), first).astype(jnp.float32)
+    got_two = swap((contract_rows(two, right) + got_far).astype(jnp.bfloat16), second)
+    part = contract_rows(near, right) + got_one + got_two.astype(jnp.float32)
+    return sum_over_h(part.astype(jnp.bfloat16))
 
 
 def scatter_columns(left, right):
     cut = -(-right.shape[1] // 256) * 128
-    left = relative(left, 1)
-    one = contract_rows(left, right[:, :cut]).astype(jnp.bfloat16)
-    two = contract_rows(left, right[:, cut:]).astype(jnp.bfloat16)
     return jnp.concatenate(
-        [scatter_rows(one, "x", "y"), scatter_rows(two, "y", "x")], axis=1
+        [scatter(left, right[:, :cut], "x", "y"), scatter(left, right[:, cut:], "y", "x")], axis=1
     ).T
+
+
+def scatter_vectors(part):
+    half = part.shape[0] // 2
+    part = part[:half] + swap(part[half:].astype(jnp.bfloat16), "c").astype(jnp.float32)
+    part = part[: half // 2] + swap(part[half // 2 :].astype(jnp.bfloat16), "x").astype(jnp.float32)
+    half = half // 2
+    part = part[: half // 2] + swap(part[half // 2 :].astype(jnp.bfloat16), "y").astype(jnp.float32)
+    return sum_over_h(part.astype(jnp.bfloat16))
 
 
 def gather_group(mine):
@@ -225,24 +248,24 @@
     act = jax.nn.gelu(hidden, approximate=False).astype(jnp.bfloat16)
     act_rel = relative(act, 1)
     h2 = h1 + matmul(act_rel, down_all)
-    hb = h2.astype(jnp.bfloat16)
-    logits = matmul(relative(hb, 1), dec_all).astype(jnp.bfloat16)
-    grad_dec = scatter_columns(hb, cotangent)
+    hb_rel = relative(h2.astype(jnp.bfloat16), 1)
+    logits = matmul(hb_rel, dec_all).astype(jnp.bfloat16)
+    grad_dec = scatter_columns(own_half(hb_rel), with_other_core(cotangent))
     dh2 = relative(contract_cols(cotangent, dec_all), 1)
     dfb = dh2.astype(jnp.bfloat16)
-    grad_down = contract_rows(act_rel, dfb)
+    grad_down = scatter(own_half(act_rel), with_other_core(dfb), "x", "y")
     d_act = relative(contract_cols(dfb, down_all), 1)
     slope = jax.vjp(lambda v: jax.nn.gelu(v, approximate=False), hidden)[1](d_act)[0]
     d_hidden = slope.astype(jnp.bfloat16)
-    grad_up = contract_rows(a2_rel, d_hidden)
+    grad_up = scatter(own_half(a2_rel), with_other_core(d_hidden), "y", "x")
     da2 = relative(contract_cols(d_hidden, up_all), 1)
     norm_pull = jax.vjp(layer_norm, h1, g2f, b2f)[1]
     dh1_norm, grad_gain_two, grad_shift_two = norm_pull(da2)
     dh1 = dh2 + dh1_norm
-    grad_down = from_owner(scatter_rows(grad_down.astype(jnp.bfloat16), "x", "y"), 1)
-    grad_up = from_owner(scatter_rows(grad_up.astype(jnp.bfloat16), "y", "x"), 1)
+    grad_down = from_owner(grad_down, 1)
+    grad_up = from_owner(grad_up, 1)
     dab = dh1.astype(jnp.bfloat16)
-    grad_out = contract_rows(attended_rel, dab)
+    grad_out = from_owner(scatter(own_half(attended_rel), with_other_core(dab), "y", "x"), 1)
     d_attended = relative(contract_cols(dab, out_all).astype(jnp.bfloat16), 1)
     d_attended = from_owner(d_attended, 1).reshape(rows, heads, head_width)
     probs = jnp.exp(scores_of() - log_total)
@@ -260,23 +283,20 @@
     d_kv = jnp.concatenate([d_keys.reshape(slots, width), d_values.reshape(slots, width)], axis=1)
     d_kv = scatter_group(d_kv)
     d_qkv = jnp.concatenate([d_query.reshape(rows, width), d_kv], axis=1).astype(jnp.bfloat16)
-    grad_qkv = contract_rows(a1_rel, d_qkv)
+    grad_qkv = scatter(own_half(a1_rel), with_other_core(d_qkv), "x", "y")
     da1 = relative(contract_cols(d_qkv, qkv_all), 1)
     first_pull = jax.vjp(layer_norm, h0, g1f, b1f)[1]
     dh0_norm, grad_gain_one, grad_shift_one = first_pull(da1)
     grad_vectors = jnp.stack([grad_gain_one, grad_shift_one, grad_gain_two, grad_shift_two], axis=1)
-    grad_vectors = jnp.pad(relative(grad_vectors, 0), ((0, 0), (0, 124)))
-    grad_qkv = jnp.concatenate([grad_qkv, grad_vectors], axis=1).astype(jnp.bfloat16)
-    grad_out = from_owner(scatter_rows(grad_out.astype(jnp.bfloat16), "y", "x"), 1)
-    grad_qkv = scatter_rows(grad_qkv, "x", "y")
+    grad_vectors = scatter_vectors(relative(grad_vectors, 0))
     grad_gain_one, grad_shift_one, grad_gain_two, grad_shift_two = (
-        grad_qkv[:, 3 * width + k] for k in range(4)
-    )
-    grad_qkv = grad_qkv[:, : 3 * width]
+        grad_vectors[:, k] for k in range(4)
+    )
     dh0b = (dh1 + dh0_norm).astype(jnp.bfloat16)
 
-    grad_enc = scatter_columns(dh0b, xb)
-    d_xb = matmul(relative(dh0b, 1), enc_all)
+    dh0b_rel = relative(dh0b, 1)
+    grad_enc = scatter_columns(own_half(dh0b_rel), with_other_core(xb))
+    d_xb = matmul(dh0b_rel, enc_all)
     counts_grad = d_xb * scale[:, None] / (1.0 + counts_f * scale[:, None])
     return (
         logits,

time: 1440 us -> 1510 us (1.049)
  local copies, waits for them, and re-layouts: 375 us -> 247 us
  waiting for transfers between devices: 535 us -> 631 us
  starting transfers between devices: 53.6 us -> 147 us
  matrix products: 209 us -> 284 us
  other arithmetic: 194 us -> 127 us
    ppermute x0 -> x27, waiting for transfers between devices: none -> 88.9 us  [sum_over_h(): total = total + lax.ppermute(send, 'h', ring).astype(jnp.float32)]
    convert_element_type x25 -> x4, other arithmetic: 92.6 us -> 4.69 us  [the longest x1 2.84 us: scatter(): return sum_over_h(part.astype(jnp.bfloat16))]
    slice x16 -> x2, local copies, waits for them, and re-layouts: 83.6 us -> 0.01 us  [scatter_vectors(): part[half // 2:].astype(jnp.bfloat16)]
    ppermute x0 -> x27, starting transfers between devices: none -> 81.4 us  [sum_over_h(): total = total + lax.ppermute(send, 'h', ring).astype(jnp.float32)]
    dot_general x8 -> x32, matrix products: 57.7 us -> 129 us  [contract_rows(): lax.dot_general(left, right, (((0,), (0,)), ((), ())), preferred_element_...]
    reshape x2, local copies, waits for them, and re-layouts: 29.4 us -> 1.41 us  [from_owner(): split = value.reshape(at[:axis] + (2, 2, 2, n_h, block) + at[axis + 1:])]
    ppermute x84 -> x99, waiting for transfers between devices: 422 us -> 448 us  [swap(): return lax.ppermute(value, axis, [(0, 1), (1, 0)])]
    unnamed x358 -> x382, local copies, waits for them, and re-layouts: 126 us -> 103 us
  transfers between devices with their start and end apart: 98 -> 132, of which waited for: 25 -> 39; matrix products, arithmetic and copies ran while one was open for 43% -> 42% of each run, Pallas kernels for 0% -> 0%
where the time goes in v2:
time: 1510 us; the launch traced here: 1500 us
  waiting for transfers between devices  631 us (42%)
  matrix products  284 us (19%)
  local copies, waits for them, and re-layouts  247 us (16%)
  starting transfers between devices  147 us (10%)
  other arithmetic  127 us (8%)
  blocking collectives  48 us (3%)
  between operations  17.8 us (1%)
    ppermute x99, waiting for transfers between devices, swap(): return lax.ppermute(value, axis, [(0, 1), (1, 0)])  448 us
    dot_general x32, matrix products, contract_rows(): lax.dot_general(left, right, (((0,), (0,)), ((), ())), preferred_element_...  129 us
    unnamed x382, local copies, waits for them, and re-layouts  103 us
    all_gather x6, waiting for transfers between devices, gather_parts(): own = lax.all_gather(shard, 'h', axis=0, tiled=True)  94 us
    ppermute x27, waiting for transfers between devices, sum_over_h(): total = total + lax.ppermute(send, 'h', ring).astype(jnp.float32)  88.9 us
    ppermute x27, starting transfers between devices, sum_over_h(): total = total + lax.ppermute(send, 'h', ring).astype(jnp.float32)  81.4 us
    dot_general x6, matrix products, matmul(): return jnp.dot(left, right, preferred_element_type=jnp.float32)  68.2 us
    ppermute x99, starting transfers between devices, swap(): return lax.ppermute(value, axis, [(0, 1), (1, 0)])  65.2 us
  transfers between devices with their start and end apart: 132, of which 39 were waited for; matrix products, arithmetic and copies ran while one was open for 42% of the time, Pallas kernels for 0%

profile of v2, /device:TPU:0, one launch (start us, length us, event | category | flops | bytes accessed | tf_op | source)
XLA Modules:
  0.0 1501.4 jit_solution(6575340309101319994)
XLA Ops:
  15.4 32.2 %all_gather.26 = bf16[128,3200]{1,0:T(8,128)(2,1)S(1)} all-gather(bf16[32,3200]{1,0:T(8,128)(2,1)S(1)} %fusion.80), channel_id=1, replica_groups=mesh['h'=4,'x'=2,'y'=2,'c'=2] {'h'}, dimensions={0}, use_global_device_ids=true | all-gather | bytes 1024000 | tf_op jit(solution)/shard_map/all_gather | solution.py:82
  51.0 15.8 %all_gather.27 = bf16[128,1024]{1,0:T(8,128)(2,1)} all-gather(bf16[32,1024]{1,0:T(8,128)(2,1)S(1)} %reshape.393), channel_id=1, replica_groups=mesh['h'=4,'x'=2,'y'=2,'c'=2] {'h'}, dimensions={0}, use_global_device_ids=true | all-gather | bytes 327680 | tf_op jit(solution)/shard_map/all_gather | solution.py:82
  70.9 8.0 constant_dynamic-update-slice_fusion.129
  78.9 6.6 log-plus-one_convert_fusion
  114.7 9.9 collective-permute-done.16
  141.6 23.7 %all-gather.17.cloned.1.call-done = bf16[128,6716]{1,0:T(8,128)(2,1)} async-done(((bf16[32,6716]{1,0:T(8,128)(2,1)}), bf16[128,6716]{1,0:T(8,128)(2,1)}) %all-gather.17.cloned.1.call-update) | async-done | bytes 1719312 | tf_op jit(solution)/shard_map/all_gather | solution.py:82
  169.1 36.9 %all-gather.7.cloned.1.call-done = bf16[128,6784]{1,0:T(8,128)(2,1)} async-done(((bf16[32,6784]{1,0:T(8,128)(2,1)}), bf16[128,6784]{1,0:T(8,128)(2,1)}) %all-gather.7.cloned.1.call-update) | async-done | bytes 1736720 | tf_op jit(solution)/shard_map/all_gather | solution.py:82
  212.6 33.4 %all-gather.15.cloned.1.call-done = bf16[128,6784]{1,0:T(8,128)(2,1)} async-done(((bf16[32,6784]{1,0:T(8,128)(2,1)}), bf16[128,6784]{1,0:T(8,128)(2,1)}) %all-gather.15.cloned.1.call-update) | async-done | bytes 1736720 | tf_op jit(solution)/shard_map/all_gather | solution.py:82
  268.5 21.7 %collective-permute-done.1 = bf16[128,6716]{0,1:T(8,128)(2,1)S(1)} collective-permute-done((bf16[128,6716]{0,1:T(8,128)(2,1)}, bf16[128,6716]{0,1:T(8,128)(2,1)S(1)}, u32[]{:S(2)}, u32[]{:S(2)}) %collective-permute-start.1) | collective-permute-done | bytes 1719328 | tf_op jit(solution)/shard_map/ppermute | solution.py:49
  313.4 13.8 collective-permute-done.45
  340.5 23.9 %collective-permute-done = bf16[128,6784]{1,0:T(8,128)(2,1)} collective-permute-done((bf16[128,6784]{1,0:T(8,128)(2,1)}, bf16[128,6784]{1,0:T(8,128)(2,1)}, u32[]{:S(2)}, u32[]{:S(2)}) %collective-permute-start) | collective-permute-done | bytes 1736736 | tf_op jit(solution)/shard_map/ppermute | solution.py:49
  373.5 26.9 %collective-permute-done.44 = bf16[128,6784]{1,0:T(8,128)(2,1)} collective-permute-done((bf16[128,6784]{1,0:T(8,128)(2,1)}, bf16[128,6784]{1,0:T(8,128)(2,1)}, u32[]{:S(2)}, u32[]{:S(2)}) %collective-permute-start.44) | collective-permute-done | bytes 1736736 | tf_op jit(solution)/shard_map/ppermute | solution.py:49
  405.9 34.1 %collective-permute-done.5 = bf16[128,6716]{0,1:T(8,128)(2,1)} collective-permute-done((bf16[128,6716]{0,1:T(8,128)(2,1)}, bf16[128,6716]{0,1:T(8,128)(2,1)}, u32[]{:S(2)}, u32[]{:S(2)}) %collective-permute-start.5) | collective-permute-done | bytes 1719328 | tf_op jit(solution)/shard_map/ppermute | solution.py:49
  460.4 14.9 collective-permute-done.49
  495.4 6.1 collective-permute-done.8
  506.1 35.7 %collective-permute-done.48 = bf16[128,6784]{1,0:T(8,128)(2,1)} collective-permute-done((bf16[128,6784]{1,0:T(8,128)(2,1)}, bf16[128,6784]{1,0:T(8,128)(2,1)}, u32[]{:S(2)}, u32[]{:S(2)}) %collective-permute-start.48) | collective-permute-done | bytes 1736736 | tf_op jit(solution)/shard_map/ppermute | solution.py:49
  553.9 5.3 pad_maximum_fusion
  559.2 6.6 fusion.19
  565.8 6.8 constant_dynamic-update-slice_fusion.128
  581.5 14.7 fusion.126
  604.2 4.6 fusion.42
  613.1 16.3 %fusion.127 = f32[1024,256]{0,1:T(8,128)S(1)} fusion(bf16[1024,13500]{1,0:T(8,128)(2,1)} %maximum_dynamic-update-slice_fusion.8, bf16[256,13500]{0,1:T(8,128)(2,1)} %param.19), kind=kOutput, calls=%fused_computation.521 | convolution fusion | flops 7077888000 | bytes 35608576 | tf_op jit(solution)/shard_map/dot_general | solution.py:39
  629.6 5.1 collective-permute-done.21
  639.8 5.9 fusion.128
  679.3 4.3 fusion.58
  695.9 15.5 %add_convert_fusion = (bf16[256,4096]{1,0:T(8,128)(2,1)}, f32[256,4096]{1,0:T(8,128)S(1)}, f32[256,4096]{1,0:T(8,128)S(1)}) fusion(f32[256,4096]{1,0:T(8,128)S(1)} %copy-done.86, bf16[256,1024]{1,0:T(8,128)(2,1)S(1)} %get-tuple-element.109, bf16[1024,4096]{1,0:T(8,128)(2,1)} %constant_dynamic-update-slice_fusion.56), kind=kOutput, calls=%fused_computation.86 | convolution fusion | flops 2222981120 | bytes 23592960 | tf_op jit(solution)/shard_map/dot_general | solution.py:45
  717.5 5.9 fusion.56
  742.0 14.5 multiply_reduce_fusion
  756.5 9.3 convert_bitcast_fusion
  765.8 7.9 multiply_convert_fusion
  780.0 6.9 fusion.57
  791.4 17.5 %convolution_convert_fusion = bf16[256,13500]{0,1:T(8,128)(2,1)} fusion(bf16[256,1024]{1,0:T(8,128)(2,1)S(1)} %get-tuple-element.77, bf16[1024,13500]{1,0:T(8,128)(2,1)} %maximum_dynamic-update-slice_fusion.8), kind=kOutput, calls=%fused_computation.1 | convolution fusion | flops 7081344000 | bytes 35084288 | tf_op jit(solution)/shard_map/dot_general | solution.py:45
  811.6 4.7 copy.167
  816.4 4.5 concatenate.256
  820.8 6.4 copy.168
  838.0 6.3 convolution_convert_fusion.1
  844.4 6.7 convolution_convert_fusion.3
  865.1 39.8 %collective-permute-done.85 = bf16[128,1024]{1,0:T(8,128)(2,1)S(1)} collective-permute-done((bf16[128,1024]{1,0:T(8,128)(2,1)S(1)}, bf16[128,1024]{1,0:T(8,128)(2,1)S(1)}, u32[]{:S(2)}, u32[]{:S(2)}) %collective-permute-start.85) | collective-permute-done | bytes 262176 | tf_op jit(solution)/shard_map/ppermute | solution.py:49
  913.5 36.3 %collective-permute-done.84 = bf16[128,1024]{1,0:T(8,128)(2,1)S(1)} collective-permute-done((bf16[128,1024]{1,0:T(8,128)(2,1)S(1)}, bf16[128,1024]{1,0:T(8,128)(2,1)S(1)}, u32[]{:S(2)}, u32[]{:S(2)}) %collective-permute-start.84) | collective-permute-done | bytes 262176 | tf_op jit(solution)/shard_map/ppermute | solution.py:49
  976.6 6.7 fusion.14
  987.1 10.0 collective-permute-done.115
  997.8 7.1 fusion.12
  1014.4 42.4 %collective-permute-done.107 = bf16[512,1024]{1,0:T(8,128)(2,1)S(1)} collective-permute-done((bf16[512,1024]{1,0:T(8,128)(2,1)}, bf16[512,1024]{1,0:T(8,128)(2,1)S(1)}, u32[]{:S(2)}, u32[]{:S(2)}) %collective-permute-start.107) | collective-permute-done | bytes 1048608 | tf_op jit(solution)/shard_map/ppermute | solution.py:49
  1074.9 22.2 %fusion = f32[256,13500]{0,1:T(8,128)} fusion(bf16[256,1024]{1,0:T(8,128)(2,1)S(1)} %get-tuple-element.57, bf16[1024,13500]{1,0:T(8,128)(2,1)} %maximum_dynamic-update-slice_fusion, bf16[256,13500]{0,1:T(8,128)(2,1)} %param.15, f32[256]{0:T(256)S(1)} %copy-done.100), kind=kOutput, calls=%fused_computation.8 | convolution fusion | flops 7095168000 | bytes 48909312 | tf_op jit(solution)/shard_map/dot_general | solution.py:45
  1105.1 4.4 fusion.26
  1142.0 6.5 collective-permute-done.110
  1154.3 6.4 fusion.7
  1162.8 19.7 %collective-permute-done.116 = bf16[128,6784]{1,0:T(8,128)(2,1)} collective-permute-done((bf16[128,6784]{1,0:T(8,128)(2,1)}, bf16[128,6784]{1,0:T(8,128)(2,1)}, u32[]{:S(2)}, u32[]{:S(2)}) %collective-permute-start.116) | collective-permute-done | bytes 1736736 | tf_op jit(solution)/shard_map/ppermute | solution.py:49
  1185.1 6.4 fusion.8
  1193.3 10.6 collective-permute-done.124
  1203.9 15.3 %collective-permute-start.117 = (bf16[32,6784]{1,0:T(8,128)(2,1)S(1)}, bf16[32,6784]{1,0:T(8,128)(2,1)S(1)}, u32[]{:S(2)}, u32[]{:S(2)}) collective-permute-start(bf16[32,6784]{1,0:T(8,128)(2,1)S(1)} %get-tuple-element.169), channel_id=1, source_target_pairs={{0,8},{8,16},{16,24},{24,0},{1,9},{9,17},{17,25},{25,1},{2,10},{10... | collective-permute-start | bytes 1302536 | tf_op jit(solution)/shard_map/ppermute | solution.py:120
  1220.9 17.6 %collective-permute-done.118 = bf16[32,6784]{1,0:T(8,128)(2,1)S(1)} collective-permute-done((bf16[32,6784]{1,0:T(8,128)(2,1)S(1)}, bf16[32,6784]{1,0:T(8,128)(2,1)S(1)}, u32[]{:S(2)}, u32[]{:S(2)}) %collective-permute-start.118) | collective-permute-done | bytes 434208 | tf_op jit(solution)/shard_map/ppermute | solution.py:120
  1251.6 12.0 collective-permute-start.102
  1268.3 10.6 collective-permute-start.101
  1289.9 6.6 fusion.13
  1296.5 19.7 %collective-permute-done.68 = bf16[128,6716]{0,1:T(8,128)(2,1)} collective-permute-done((bf16[128,6716]{0,1:T(8,128)(2,1)}, bf16[128,6716]{0,1:T(8,128)(2,1)}, u32[]{:S(2)}, u32[]{:S(2)}) %collective-permute-start.68) | collective-permute-done | bytes 1719328 | tf_op jit(solution)/shard_map/ppermute | solution.py:49
  1321.6 18.3 %collective-permute-done.76 = bf16[128,3072]{1,0:T(8,128)(2,1)} collective-permute-done((bf16[128,3072]{1,0:T(8,128)(2,1)}, bf16[128,3072]{1,0:T(8,128)(2,1)}, u32[]{:S(2)}, u32[]{:S(2)}) %collective-permute-start.76) | collective-permute-done | bytes 786464 | tf_op jit(solution)/shard_map/ppermute | solution.py:49
  1345.7 5.1 fusion.11
  1356.6 54.3 %collective-permute-done.70 = bf16[128,6716]{0,1:T(8,128)(2,1)} collective-permute-done((bf16[128,6716]{0,1:T(8,128)(2,1)}, bf16[128,6716]{0,1:T(8,128)(2,1)}, u32[]{:S(2)}, u32[]{:S(2)}) %collective-permute-start.70) | collective-permute-done | bytes 1719328 | tf_op jit(solution)/shard_map/ppermute | solution.py:49
  1413.6 5.5 fusion.9
  1421.3 6.4 fusion.10
  1431.7 19.4 %collective-permute-start.65 = (bf16[32,6784]{1,0:T(8,128)(2,1)S(1)}, bf16[32,6784]{1,0:T(8,128)(2,1)S(1)}, u32[]{:S(2)}, u32[]{:S(2)}) collective-permute-start(bf16[32,6784]{1,0:T(8,128)(2,1)S(1)} %get-tuple-element.175), channel_id=1, source_target_pairs={{0,8},{8,16},{16,24},{24,0},{1,9},{9,17},{17,25},{25,1},{2,10},{10... | collective-permute-start | bytes 1302536 | tf_op jit(solution)/shard_map/ppermute | solution.py:120
  1451.1 27.0 %collective-permute-done.72 = bf16[32,6716]{1,0:T(8,128)(2,1)S(1)} collective-permute-done((bf16[32,6716]{1,0:T(8,128)(2,1)S(1)}, bf16[32,6716]{1,0:T(8,128)(2,1)S(1)}, u32[]{:S(2)}, u32[]{:S(2)}) %collective-permute-start.72) | collective-permute-done | bytes 429856 | tf_op jit(solution)/shard_map/ppermute | solution.py:120
  1478.3 14.2 collective-permute-done.66
  (831 shorter events, 513.7 us)
Async XLA Ops:
  7.3 102.1 %all-gather.13.cloned.1.call-start = ((), (), s32[]{:S(2)}) async-start(), calls=%async_computation.3 | async-start | bytes 1310720 | tf_op jit(solution)/shard_map/all_gather | solution.py:82
  9.3 103.1 %all-gather.11.cloned.1.call-start = ((), (), s32[]{:S(2)}) async-start(), calls=%async_computation.2 | async-start | bytes 1310720 | tf_op jit(solution)/shard_map/all_gather | solution.py:82
  11.5 126.2 %all-gather.9.cloned.1.call-start = ((), (), s32[]{:S(2)}) async-start(), calls=%async_computation.1 | async-start | bytes 2170880 | tf_op jit(solution)/shard_map/all_gather | solution.py:82
  13.4 151.9 %all-gather.17.cloned.1.call-start = ((), (), s32[]{:S(2)}) async-start(), calls=%async_computation.5 | async-start | bytes 2170880 | tf_op jit(solution)/shard_map/all_gather | solution.py:82
  14.3 191.7 %all-gather.7.cloned.1.call-start = ((), (), s32[]{:S(2)}) async-start(), calls=%async_computation | async-start | bytes 2170880 | tf_op jit(solution)/shard_map/all_gather | solution.py:82
  15.1 230.9 %all-gather.15.cloned.1.call-start = ((), (), s32[]{:S(2)}) async-start(), calls=%async_computation.4 | async-start | bytes 2170880 | tf_op jit(solution)/shard_map/all_gather | solution.py:82
  47.6 57.3 %collective-permute-start.14 = (bf16[128,3200]{1,0:T(8,128)(2,1)S(1)}, bf16[128,3200]{1,0:T(8,128)(2,1)}, u32[]{:S(2)}, u32[]{:S(2)}) collective-permute-start(bf16[128,3200]{1,0:T(8,128)(2,1)S(1)} %all_gather.26), channel_id=1, source_target_pairs={{0,2},{2,0},{1,3},{3,1},{4,6},{6,4},{5,7},{7,5},{8,10},{10,8},{9,1... | collective-permute-start | bytes 2457608 | tf_op jit(solution)/shard_map/ppermute | solution.py:49
  48.9 54.4 %collective-permute-start.15 = (bf16[128,3200]{1,0:T(8,128)(2,1)S(1)}, bf16[128,3200]{1,0:T(8,128)(2,1)}, u32[]{:S(2)}, u32[]{:S(2)}) collective-permute-start(bf16[128,3200]{1,0:T(8,128)(2,1)S(1)} %all_gather.26), channel_id=1, source_target_pairs={{0,4},{4,0},{1,5},{5,1},{2,6},{6,2},{3,7},{7,3},{8,12},{12,8},{9,1... | collective-permute-start | bytes 2457608 | tf_op jit(solution)/shard_map/ppermute | solution.py:49
  109.4 100.0 %collective-permute-start.37 = (bf16[512,1024]{0,1:T(8,128)(2,1)}, bf16[512,1024]{0,1:T(8,128)(2,1)}, u32[]{:S(2)}, u32[]{:S(2)}) collective-permute-start(bf16[512,1024]{0,1:T(8,128)(2,1)} %all-gather.13.cloned.1.call-done), channel_id=1, source_target_pairs={{0,2},{2,0},{1,3},{3,1},{4,6},{6,4},{5,7},{7,5},{8,10},{10,8},{9,1... | collective-permute-start | bytes 3145736 | tf_op jit(solution)/shard_map/ppermute | solution.py:49
  124.6 84.9 %collective-permute-start.38 = (bf16[512,1024]{0,1:T(8,128)(2,1)}, bf16[512,1024]{0,1:T(8,128)(2,1)}, u32[]{:S(2)}, u32[]{:S(2)}) collective-permute-start(bf16[512,1024]{0,1:T(8,128)(2,1)} %all-gather.13.cloned.1.call-done), channel_id=1, source_target_pairs={{0,4},{4,0},{1,5},{5,1},{2,6},{6,2},{3,7},{7,3},{8,12},{12,8},{9,1... | collective-permute-start | bytes 3145736 | tf_op jit(solution)/shard_map/ppermute | solution.py:49
  126.8 84.2 %collective-permute-start.40 = (bf16[512,1024]{0,1:T(8,128)(2,1)}, bf16[512,1024]{0,1:T(8,128)(2,1)}, u32[]{:S(2)}, u32[]{:S(2)}) collective-permute-start(bf16[512,1024]{0,1:T(8,128)(2,1)} %all-gather.13.cloned.1.call-done), channel_id=1, source_target_pairs={{0,1},{1,0},{2,3},{3,2},{4,5},{5,4},{6,7},{7,6},{8,9},{9,8},{10,11... | collective-permute-start | bytes 3145736 | tf_op jit(solution)/shard_map/ppermute | solution.py:49
  130.4 80.7 %collective-permute-start.30 = (bf16[128,4096]{1,0:T(8,128)(2,1)}, bf16[128,4096]{1,0:T(8,128)(2,1)}, u32[]{:S(2)}, u32[]{:S(2)}) collective-permute-start(bf16[128,4096]{1,0:T(8,128)(2,1)} %all-gather.11.cloned.1.call-done), channel_id=1, source_target_pairs={{0,2},{2,0},{1,3},{3,1},{4,6},{6,4},{5,7},{7,5},{8,10},{10,8},{9,1... | collective-permute-start | bytes 3145736 | tf_op jit(solution)/shard_map/ppermute | solution.py:49
  133.2 116.4 %collective-permute-start.31 = (bf16[128,4096]{1,0:T(8,128)(2,1)}, bf16[128,4096]{1,0:T(8,128)(2,1)}, u32[]{:S(2)}, u32[]{:S(2)}) collective-permute-start(bf16[128,4096]{1,0:T(8,128)(2,1)} %all-gather.11.cloned.1.call-done), channel_id=1, source_target_pairs={{0,4},{4,0},{1,5},{5,1},{2,6},{6,2},{3,7},{7,3},{8,12},{12,8},{9,1... | collective-permute-start | bytes 3145736 | tf_op jit(solution)/shard_map/ppermute | solution.py:49
  209.5 47.7 %collective-permute-start.39 = (bf16[512,1024]{0,1:T(8,128)(2,1)}, bf16[512,1024]{0,1:T(8,128)(2,1)}, u32[]{:S(2)}, u32[]{:S(2)}) collective-permute-start(bf16[512,1024]{0,1:T(8,128)(2,1)} %collective-permute-done.38), channel_id=1, source_target_pairs={{0,2},{2,0},{1,3},{3,1},{4,6},{6,4},{5,7},{7,5},{8,10},{10,8},{9,1... | collective-permute-start | bytes 3145736 | tf_op jit(solution)/shard_map/ppermute | solution.py:49
  211.0 48.5 %collective-permute-start.41 = (bf16[512,1024]{0,1:T(8,128)(2,1)}, bf16[512,1024]{0,1:T(8,128)(2,1)}, u32[]{:S(2)}, u32[]{:S(2)}) collective-permute-start(bf16[512,1024]{0,1:T(8,128)(2,1)} %collective-permute-done.37), channel_id=1, source_target_pairs={{0,1},{1,0},{2,3},{3,2},{4,5},{5,4},{6,7},{7,6},{8,9},{9,8},{10,11... | collective-permute-start | bytes 3145736 | tf_op jit(solution)/shard_map/ppermute | solution.py:49
  211.2 48.8 %collective-permute-start.32 = (bf16[128,4096]{1,0:T(8,128)(2,1)}, bf16[128,4096]{1,0:T(8,128)(2,1)}, u32[]{:S(2)}, u32[]{:S(2)}) collective-permute-start(bf16[128,4096]{1,0:T(8,128)(2,1)} %collective-permute-done.30), channel_id=1, source_target_pairs={{0,4},{4,0},{1,5},{5,1},{2,6},{6,2},{3,7},{7,3},{8,12},{12,8},{9,1... | collective-permute-start | bytes 3145736 | tf_op jit(solution)/shard_map/ppermute | solution.py:49
  267.4 59.7 %collective-permute-start.45 = (bf16[128,6716]{0,1:T(8,128)(2,1)}, bf16[128,6716]{0,1:T(8,128)(2,1)}, u32[]{:S(2)}, u32[]{:S(2)}) collective-permute-start(bf16[128,6716]{0,1:T(8,128)(2,1)} %copy.147), channel_id=1, source_target_pairs={{0,2},{2,0},{1,3},{3,1},{4,6},{6,4},{5,7},{7,5},{8,10},{10,8},{9,1... | collective-permute-start | bytes 5157896 | tf_op jit(solution)/shard_map/ppermute | solution.py:49
  268.0 64.5 %collective-permute-start.47 = (bf16[128,6716]{0,1:T(8,128)(2,1)}, bf16[128,6716]{0,1:T(8,128)(2,1)}, u32[]{:S(2)}, u32[]{:S(2)}) collective-permute-start(bf16[128,6716]{0,1:T(8,128)(2,1)} %copy.147), channel_id=1, source_target_pairs={{0,4},{4,0},{1,5},{5,1},{2,6},{6,2},{3,7},{7,3},{8,12},{12,8},{9,1... | collective-permute-start | bytes 5157896 | tf_op jit(solution)/shard_map/ppermute | solution.py:49
  290.2 47.5 %collective-permute-start.51 = (bf16[128,6716]{0,1:T(8,128)(2,1)}, bf16[128,6716]{0,1:T(8,128)(2,1)}, u32[]{:S(2)}, u32[]{:S(2)}) collective-permute-start(bf16[128,6716]{0,1:T(8,128)(2,1)} %copy.147), channel_id=1, source_target_pairs={{0,1},{1,0},{2,3},{3,2},{4,5},{5,4},{6,7},{7,6},{8,9},{9,8},{10,11... | collective-permute-start | bytes 5157896 | tf_op jit(solution)/shard_map/ppermute | solution.py:49
  291.7 72.7 %collective-permute-start = (bf16[128,6784]{1,0:T(8,128)(2,1)}, bf16[128,6784]{1,0:T(8,128)(2,1)}, u32[]{:S(2)}, u32[]{:S(2)}) collective-permute-start(bf16[128,6784]{1,0:T(8,128)(2,1)} %all-gather.7.cloned.1.call-done), channel_id=1, source_target_pairs={{0,2},{2,0},{1,3},{3,1},{4,6},{6,4},{5,7},{7,5},{8,10},{10,8},{9,1... | collective-permute-start | bytes 5210120 | tf_op jit(solution)/shard_map/ppermute | solution.py:49
  302.4 67.5 %collective-permute-start.2 = (bf16[128,6784]{1,0:T(8,128)(2,1)}, bf16[128,6784]{1,0:T(8,128)(2,1)}, u32[]{:S(2)}, u32[]{:S(2)}) collective-permute-start(bf16[128,6784]{1,0:T(8,128)(2,1)} %all-gather.7.cloned.1.call-done), channel_id=1, source_target_pairs={{0,4},{4,0},{1,5},{5,1},{2,6},{6,2},{3,7},{7,3},{8,12},{12,8},{9,1... | collective-permute-start | bytes 5210120 | tf_op jit(solution)/shard_map/ppermute | solution.py:49
  327.2 73.3 %collective-permute-start.44 = (bf16[128,6784]{1,0:T(8,128)(2,1)}, bf16[128,6784]{1,0:T(8,128)(2,1)}, u32[]{:S(2)}, u32[]{:S(2)}) collective-permute-start(bf16[128,6784]{1,0:T(8,128)(2,1)} %all-gather.15.cloned.1.call-done), channel_id=1, source_target_pairs={{0,2},{2,0},{1,3},{3,1},{4,6},{6,4},{5,7},{7,5},{8,10},{10,8},{9,1... | collective-permute-start | bytes 5210120 | tf_op jit(solution)/shard_map/ppermute | solution.py:49
  332.4 71.5 %collective-permute-start.46 = (bf16[128,6784]{1,0:T(8,128)(2,1)}, bf16[128,6784]{1,0:T(8,128)(2,1)}, u32[]{:S(2)}, u32[]{:S(2)}) collective-permute-start(bf16[128,6784]{1,0:T(8,128)(2,1)} %all-gather.15.cloned.1.call-done), channel_id=1, source_target_pairs={{0,4},{4,0},{1,5},{5,1},{2,6},{6,2},{3,7},{7,3},{8,12},{12,8},{9,1... | collective-permute-start | bytes 5210120 | tf_op jit(solution)/shard_map/ppermute | solution.py:49
  337.7 66.7 %collective-permute-start.43 = (bf16[512,1024]{0,1:T(8,128)(2,1)}, bf16[512,1024]{0,1:T(8,128)(2,1)}, u32[]{:S(2)}, u32[]{:S(2)}) collective-permute-start(bf16[512,1024]{0,1:T(8,128)(2,1)} %collective-permute-done.39), channel_id=1, source_target_pairs={{0,1},{1,0},{2,3},{3,2},{4,5},{5,4},{6,7},{7,6},{8,9},{9,8},{10,11... | collective-permute-start | bytes 3145736 | tf_op jit(solution)/shard_map/ppermute | solution.py:49
  364.4 75.6 %collective-permute-start.5 = (bf16[128,6716]{0,1:T(8,128)(2,1)}, bf16[128,6716]{0,1:T(8,128)(2,1)}, u32[]{:S(2)}, u32[]{:S(2)}) collective-permute-start(bf16[128,6716]{0,1:T(8,128)(2,1)} %copy-done.41), channel_id=1, source_target_pairs={{0,4},{4,0},{1,5},{5,1},{2,6},{6,2},{3,7},{7,3},{8,12},{12,8},{9,1... | collective-permute-start | bytes 5157896 | tf_op jit(solution)/shard_map/ppermute | solution.py:49
  369.8 70.1 %collective-permute-start.9 = (bf16[128,6716]{0,1:T(8,128)(2,1)S(1)}, bf16[128,6716]{0,1:T(8,128)(2,1)S(1)}, u32[]{:S(2)}, u32[]{:S(2)}) collective-permute-start(bf16[128,6716]{0,1:T(8,128)(2,1)S(1)} %copy-done.42), channel_id=1, source_target_pairs={{0,1},{1,0},{2,3},{3,2},{4,5},{5,4},{6,7},{7,6},{8,9},{9,8},{10,11... | collective-permute-start | bytes 5157896 | tf_op jit(solution)/shard_map/ppermute | solution.py:49
  404.4 71.0 %collective-permute-start.49 = (bf16[128,6716]{0,1:T(8,128)(2,1)}, bf16[128,6716]{0,1:T(8,128)(2,1)}, u32[]{:S(2)}, u32[]{:S(2)}) collective-permute-start(bf16[128,6716]{0,1:T(8,128)(2,1)} %collective-permute-done.45), channel_id=1, source_target_pairs={{0,4},{4,0},{1,5},{5,1},{2,6},{6,2},{3,7},{7,3},{8,12},{12,8},{9,1... | collective-permute-start | bytes 5157896 | tf_op jit(solution)/shard_map/ppermute | solution.py:49
  405.9 73.3 %collective-permute-start.53 = (bf16[128,6716]{0,1:T(8,128)(2,1)}, bf16[128,6716]{0,1:T(8,128)(2,1)}, u32[]{:S(2)}, u32[]{:S(2)}) collective-permute-start(bf16[128,6716]{0,1:T(8,128)(2,1)} %collective-permute-done.45), channel_id=1, source_target_pairs={{0,1},{1,0},{2,3},{3,2},{4,5},{5,4},{6,7},{7,6},{8,9},{9,8},{10,11... | collective-permute-start | bytes 5157896 | tf_op jit(solution)/shard_map/ppermute | solution.py:49
  440.0 43.5 %collective-permute-start.55 = (bf16[128,6716]{0,1:T(8,128)(2,1)}, bf16[128,6716]{0,1:T(8,128)(2,1)}, u32[]{:S(2)}, u32[]{:S(2)}) collective-permute-start(bf16[128,6716]{0,1:T(8,128)(2,1)} %collective-permute-done.47), channel_id=1, source_target_pairs={{0,1},{1,0},{2,3},{3,2},{4,5},{5,4},{6,7},{7,6},{8,9},{9,8},{10,11... | collective-permute-start | bytes 5157896 | tf_op jit(solution)/shard_map/ppermute | solution.py:49
  440.0 47.3 %collective-permute-start.4 = (bf16[128,6784]{1,0:T(8,128)(2,1)}, bf16[128,6784]{1,0:T(8,128)(2,1)}, u32[]{:S(2)}, u32[]{:S(2)}) collective-permute-start(bf16[128,6784]{1,0:T(8,128)(2,1)} %collective-permute-done.2), channel_id=1, source_target_pairs={{0,2},{2,0},{1,3},{3,1},{4,6},{6,4},{5,7},{7,5},{8,10},{10,8},{9,1... | collective-permute-start | bytes 5210120 | tf_op jit(solution)/shard_map/ppermute | solution.py:49
  446.3 45.5 %collective-permute-start.6 = (bf16[128,6784]{1,0:T(8,128)(2,1)}, bf16[128,6784]{1,0:T(8,128)(2,1)}, u32[]{:S(2)}, u32[]{:S(2)}) collective-permute-start(bf16[128,6784]{1,0:T(8,128)(2,1)} %all-gather.7.cloned.1.call-done), channel_id=1, source_target_pairs={{0,1},{1,0},{2,3},{3,2},{4,5},{5,4},{6,7},{7,6},{8,9},{9,8},{10,11... | collective-permute-start | bytes 5210120 | tf_op jit(solution)/shard_map/ppermute | solution.py:49
  475.4 90.4 %collective-permute-start.113 = (bf16[256,13500]{0,1:T(8,128)(2,1)}, bf16[256,13500]{0,1:T(8,128)(2,1)}, u32[]{:S(2)}, u32[]{:S(2)}) collective-permute-start(bf16[256,13500]{0,1:T(8,128)(2,1)} %param.19), channel_id=1, source_target_pairs={{0,1},{1,0},{2,3},{3,2},{4,5},{5,4},{6,7},{7,6},{8,9},{9,8},{10,11... | collective-permute-start | bytes 20736008 | tf_op jit(solution)/shard_map/ppermute | solution.py:49
  479.2 74.7 %collective-permute-start.61 = (bf16[256,13500]{0,1:T(8,128)(2,1)}, bf16[256,13500]{0,1:T(8,128)(2,1)}, u32[]{:S(2)}, u32[]{:S(2)}) collective-permute-start(bf16[256,13500]{0,1:T(8,128)(2,1)} %log-plus-one_convert_fusion), channel_id=1, source_target_pairs={{0,1},{1,0},{2,3},{3,2},{4,5},{5,4},{6,7},{7,6},{8,9},{9,8},{10,11... | collective-permute-start | bytes 20736008 | tf_op jit(solution)/shard_map/ppermute | solution.py:49
  483.5 61.7 %collective-permute-start.50 = (bf16[128,6784]{1,0:T(8,128)(2,1)}, bf16[128,6784]{1,0:T(8,128)(2,1)}, u32[]{:S(2)}, u32[]{:S(2)}) collective-permute-start(bf16[128,6784]{1,0:T(8,128)(2,1)} %all-gather.15.cloned.1.call-done), channel_id=1, source_target_pairs={{0,1},{1,0},{2,3},{3,2},{4,5},{5,4},{6,7},{7,6},{8,9},{9,8},{10,11... | collective-permute-start | bytes 5210120 | tf_op jit(solution)/shard_map/ppermute | solution.py:49
  504.1 45.2 %collective-permute-start.52 = (bf16[128,6784]{1,0:T(8,128)(2,1)}, bf16[128,6784]{1,0:T(8,128)(2,1)S(1)}, u32[]{:S(2)}, u32[]{:S(2)}) collective-permute-start(bf16[128,6784]{1,0:T(8,128)(2,1)} %collective-permute-done.44), channel_id=1, source_target_pairs={{0,1},{1,0},{2,3},{3,2},{4,5},{5,4},{6,7},{7,6},{8,9},{9,8},{10,11... | collective-permute-start | bytes 5210120 | tf_op jit(solution)/shard_map/ppermute | solution.py:49
  553.9 55.8 %collective-permute-start.56 = (bf16[128,6784]{1,0:T(8,128)(2,1)}, bf16[128,6784]{1,0:T(8,128)(2,1)}, u32[]{:S(2)}, u32[]{:S(2)}) collective-permute-start(bf16[128,6784]{1,0:T(8,128)(2,1)} %collective-permute-done.48), channel_id=1, source_target_pairs={{0,1},{1,0},{2,3},{3,2},{4,5},{5,4},{6,7},{7,6},{8,9},{9,8},{10,11... | collective-permute-start | bytes 5210120 | tf_op jit(solution)/shard_map/ppermute | solution.py:49
  639.8 269.0 %collective-permute-start.105 = (bf16[256,1024]{1,0:T(8,128)(2,1)}, bf16[256,1024]{1,0:T(8,128)(2,1)}, u32[]{:S(2)}, u32[]{:S(2)}) collective-permute-start(bf16[256,1024]{1,0:T(8,128)(2,1)} %convert_element_type.434), channel_id=1, source_target_pairs={{0,1},{1,0},{2,3},{3,2},{4,5},{5,4},{6,7},{7,6},{8,9},{9,8},{10,11... | collective-permute-start | bytes 1572872 | tf_op jit(solution)/shard_map/ppermute | solution.py:49
  787.0 72.1 %collective-permute-start.83 = (bf16[256,1024]{1,0:T(8,128)(2,1)}, bf16[256,1024]{1,0:T(8,128)(2,1)}, u32[]{:S(2)}, u32[]{:S(2)}) collective-permute-start(bf16[256,1024]{1,0:T(8,128)(2,1)} %fusion.81), channel_id=1, source_target_pairs={{0,1},{1,0},{2,3},{3,2},{4,5},{5,4},{6,7},{7,6},{8,9},{9,8},{10,11... | collective-permute-start | bytes 1572872 | tf_op jit(solution)/shard_map/ppermute | solution.py:49
  830.3 153.0 %collective-permute-start.58 = (bf16[2,256,2048]{2,1,0:T(8,128)(2,1)}, bf16[2,256,2048]{2,1,0:T(8,128)(2,1)}, u32[]{:S(2)}, u32[]{:S(2)}) collective-permute-start(bf16[2,256,2048]{2,1,0:T(8,128)(2,1)} %fusion.49), channel_id=1, source_target_pairs={{0,1},{1,0},{2,3},{3,2},{4,5},{5,4},{6,7},{7,6},{8,9},{9,8},{10,11... | collective-permute-start | bytes 6291464 | tf_op jit(solution)/shard_map/ppermute | solution.py:49
  836.4 70.6 %collective-permute-start.104 = (bf16[256,2048]{1,0:T(8,128)(2,1)S(1)}, bf16[256,2048]{1,0:T(8,128)(2,1)S(1)}, u32[]{:S(2)}, u32[]{:S(2)}) collective-permute-start(bf16[256,2048]{1,0:T(8,128)(2,1)S(1)} %pad_maximum_fusion.9), channel_id=1, source_target_pairs={{0,1},{1,0},{2,3},{3,2},{4,5},{5,4},{6,7},{7,6},{8,9},{9,8},{10,11... | collective-permute-start | bytes 3145736 | tf_op jit(solution)/shard_map/ppermute | solution.py:49
  859.0 117.0 %collective-permute-start.121 = (bf16[128,6716]{0,1:T(8,128)(2,1)}, bf16[128,6716]{0,1:T(8,128)(2,1)}, u32[]{:S(2)}, u32[]{:S(2)}) collective-permute-start(bf16[128,6716]{0,1:T(8,128)(2,1)} %convolution_convert_fusion.1), channel_id=1, source_target_pairs={{0,2},{2,0},{1,3},{3,1},{4,6},{6,4},{5,7},{7,5},{8,10},{10,8},{9,1... | collective-permute-start | bytes 5157896 | tf_op jit(solution)/shard_map/ppermute | solution.py:49
  861.2 43.6 %collective-permute-start.85 = (bf16[128,1024]{1,0:T(8,128)(2,1)S(1)}, bf16[128,1024]{1,0:T(8,128)(2,1)S(1)}, u32[]{:S(2)}, u32[]{:S(2)}) collective-permute-start(bf16[128,1024]{1,0:T(8,128)(2,1)S(1)} %convolution_convert_fusion.16), channel_id=1, source_target_pairs={{0,2},{2,0},{1,3},{3,1},{4,6},{6,4},{5,7},{7,5},{8,10},{10,8},{9,1... | collective-permute-start | bytes 786440 | tf_op jit(solution)/shard_map/ppermute | solution.py:49
  904.9 65.9 %collective-permute-start.120 = (bf16[128,6716]{0,1:T(8,128)(2,1)}, bf16[128,6716]{0,1:T(8,128)(2,1)}, u32[]{:S(2)}, u32[]{:S(2)}) collective-permute-start(bf16[128,6716]{0,1:T(8,128)(2,1)} %convolution_convert_fusion.2), channel_id=1, source_target_pairs={{0,2},{2,0},{1,3},{3,1},{4,6},{6,4},{5,7},{7,5},{8,10},{10,8},{9,1... | collective-permute-start | bytes 5157896 | tf_op jit(solution)/shard_map/ppermute | solution.py:49
  970.8 190.1 %collective-permute-start.114 = (bf16[128,6784]{1,0:T(8,128)(2,1)}, bf16[128,6784]{1,0:T(8,128)(2,1)}, u32[]{:S(2)}, u32[]{:S(2)}) collective-permute-start(bf16[128,6784]{1,0:T(8,128)(2,1)} %convolution_convert_fusion.4), channel_id=1, source_target_pairs={{0,4},{4,0},{1,5},{5,1},{2,6},{6,2},{3,7},{7,3},{8,12},{12,8},{9,1... | collective-permute-start | bytes 5210120 | tf_op jit(solution)/shard_map/ppermute | solution.py:49
  976.0 80.7 %collective-permute-start.107 = (bf16[512,1024]{1,0:T(8,128)(2,1)}, bf16[512,1024]{1,0:T(8,128)(2,1)S(1)}, u32[]{:S(2)}, u32[]{:S(2)}) collective-permute-start(bf16[512,1024]{1,0:T(8,128)(2,1)} %convolution_convert_fusion.13), channel_id=1, source_target_pairs={{0,4},{4,0},{1,5},{5,1},{2,6},{6,2},{3,7},{7,3},{8,12},{12,8},{9,1... | collective-permute-start | bytes 3145736 | tf_op jit(solution)/shard_map/ppermute | solution.py:49
  983.2 114.0 %collective-permute-start.106 = (bf16[512,1024]{1,0:T(8,128)(2,1)}, bf16[512,1024]{1,0:T(8,128)(2,1)}, u32[]{:S(2)}, u32[]{:S(2)}) collective-permute-start(bf16[512,1024]{1,0:T(8,128)(2,1)} %convolution_convert_fusion.14), channel_id=1, source_target_pairs={{0,4},{4,0},{1,5},{5,1},{2,6},{6,2},{3,7},{7,3},{8,12},{12,8},{9,1... | collective-permute-start | bytes 3145736 | tf_op jit(solution)/shard_map/ppermute | solution.py:49
  997.2 63.3 %collective-permute-start.59 = (bf16[256,2048]{1,0:T(8,128)(2,1)S(1)}, bf16[256,2048]{1,0:T(8,128)(2,1)S(1)}, u32[]{:S(2)}, u32[]{:S(2)}) collective-permute-start(bf16[256,2048]{1,0:T(8,128)(2,1)S(1)} %dynamic-slice_bitcast_fusion), channel_id=1, source_target_pairs={{0,2},{2,0},{1,3},{3,1},{4,6},{6,4},{5,7},{7,5},{8,10},{10,8},{9,1... | collective-permute-start | bytes 3145736 | tf_op jit(solution)/shard_map/ppermute | solution.py:49
  1004.9 145.6 %collective-permute-start.122 = (bf16[128,6716]{0,1:T(8,128)(2,1)}, bf16[128,6716]{0,1:T(8,128)(2,1)}, u32[]{:S(2)}, u32[]{:S(2)}) collective-permute-start(bf16[128,6716]{0,1:T(8,128)(2,1)} %fusion.14), channel_id=1, source_target_pairs={{0,4},{4,0},{1,5},{5,1},{2,6},{6,2},{3,7},{7,3},{8,12},{12,8},{9,1... | collective-permute-start | bytes 5157896 | tf_op jit(solution)/shard_map/ppermute | solution.py:49
  1056.8 48.3 %collective-permute-start.99 = (bf16[128,4096]{1,0:T(8,128)(2,1)}, bf16[128,4096]{1,0:T(8,128)(2,1)}, u32[]{:S(2)}, u32[]{:S(2)}) collective-permute-start(bf16[128,4096]{1,0:T(8,128)(2,1)} %convolution_convert_fusion.9), channel_id=1, source_target_pairs={{0,2},{2,0},{1,3},{3,1},{4,6},{6,4},{5,7},{7,5},{8,10},{10,8},{9,1... | collective-permute-start | bytes 3145736 | tf_op jit(solution)/shard_map/ppermute | solution.py:49
  1148.5 93.7 %collective-permute-start.98 = (bf16[128,4096]{1,0:T(8,128)(2,1)}, bf16[128,4096]{1,0:T(8,128)(2,1)}, u32[]{:S(2)}, u32[]{:S(2)}) collective-permute-start(bf16[128,4096]{1,0:T(8,128)(2,1)} %convolution_convert_fusion.10), channel_id=1, source_target_pairs={{0,2},{2,0},{1,3},{3,1},{4,6},{6,4},{5,7},{7,5},{8,10},{10,8},{9,1... | collective-permute-start | bytes 3145736 | tf_op jit(solution)/shard_map/ppermute | solution.py:49
  1149.1 98.8 %collective-permute-start.75 = (bf16[256,3072]{1,0:T(8,128)(2,1)}, bf16[256,3072]{1,0:T(8,128)(2,1)}, u32[]{:S(2)}, u32[]{:S(2)}) collective-permute-start(bf16[256,3072]{1,0:T(8,128)(2,1)} %pad_maximum_fusion.6), channel_id=1, source_target_pairs={{0,1},{1,0},{2,3},{3,2},{4,5},{5,4},{6,7},{7,6},{8,9},{9,8},{10,11... | collective-permute-start | bytes 4718600 | tf_op jit(solution)/shard_map/ppermute | solution.py:49
  1238.6 49.9 %collective-permute-start.69 = (bf16[128,6716]{0,1:T(8,128)(2,1)}, bf16[128,6716]{0,1:T(8,128)(2,1)}, u32[]{:S(2)}, u32[]{:S(2)}) collective-permute-start(bf16[128,6716]{0,1:T(8,128)(2,1)} %convolution_convert_fusion.5), channel_id=1, source_target_pairs={{0,2},{2,0},{1,3},{3,1},{4,6},{6,4},{5,7},{7,5},{8,10},{10,8},{9,1... | collective-permute-start | bytes 5157896 | tf_op jit(solution)/shard_map/ppermute | solution.py:49
  1239.2 77.0 %collective-permute-start.68 = (bf16[128,6716]{0,1:T(8,128)(2,1)}, bf16[128,6716]{0,1:T(8,128)(2,1)}, u32[]{:S(2)}, u32[]{:S(2)}) collective-permute-start(bf16[128,6716]{0,1:T(8,128)(2,1)} %convolution_convert_fusion.6), channel_id=1, source_target_pairs={{0,2},{2,0},{1,3},{3,1},{4,6},{6,4},{5,7},{7,5},{8,10},{10,8},{9,1... | collective-permute-start | bytes 5157896 | tf_op jit(solution)/shard_map/ppermute | solution.py:49
  1281.9 63.5 %collective-permute-start.63 = (bf16[128,6784]{1,0:T(8,128)(2,1)}, bf16[128,6784]{1,0:T(8,128)(2,1)}, u32[]{:S(2)}, u32[]{:S(2)}) collective-permute-start(bf16[128,6784]{1,0:T(8,128)(2,1)} %convolution_convert_fusion.7), channel_id=1, source_target_pairs={{0,4},{4,0},{1,5},{5,1},{2,6},{6,2},{3,7},{7,3},{8,12},{12,8},{9,1... | collective-permute-start | bytes 5210120 | tf_op jit(solution)/shard_map/ppermute | solution.py:49
  1285.3 54.6 %collective-permute-start.76 = (bf16[128,3072]{1,0:T(8,128)(2,1)}, bf16[128,3072]{1,0:T(8,128)(2,1)}, u32[]{:S(2)}, u32[]{:S(2)}) collective-permute-start(bf16[128,3072]{1,0:T(8,128)(2,1)} %convolution_convert_fusion.12), channel_id=1, source_target_pairs={{0,4},{4,0},{1,5},{5,1},{2,6},{6,2},{3,7},{7,3},{8,12},{12,8},{9,1... | collective-permute-start | bytes 2359304 | tf_op jit(solution)/shard_map/ppermute | solution.py:49
  1285.9 54.0 %collective-permute-start.78 = (bf16[128,3072]{1,0:T(8,128)(2,1)}, bf16[128,3072]{1,0:T(8,128)(2,1)}, u32[]{:S(2)}, u32[]{:S(2)}) collective-permute-start(bf16[128,3072]{1,0:T(8,128)(2,1)} %fusion.47), channel_id=1, source_target_pairs={{0,2},{2,0},{1,3},{3,1},{4,6},{6,4},{5,7},{7,5},{8,10},{10,8},{9,1... | collective-permute-start | bytes 2359304 | tf_op jit(solution)/shard_map/ppermute | solution.py:49
  1288.5 132.8 %collective-permute-start.62 = (bf16[128,6784]{1,0:T(8,128)(2,1)}, bf16[128,6784]{1,0:T(8,128)(2,1)}, u32[]{:S(2)}, u32[]{:S(2)}) collective-permute-start(bf16[128,6784]{1,0:T(8,128)(2,1)} %convolution_convert_fusion.8), channel_id=1, source_target_pairs={{0,4},{4,0},{1,5},{5,1},{2,6},{6,2},{3,7},{7,3},{8,12},{12,8},{9,1... | collective-permute-start | bytes 5210120 | tf_op jit(solution)/shard_map/ppermute | solution.py:49
  1316.2 94.6 %collective-permute-start.70 = (bf16[128,6716]{0,1:T(8,128)(2,1)}, bf16[128,6716]{0,1:T(8,128)(2,1)}, u32[]{:S(2)}, u32[]{:S(2)}) collective-permute-start(bf16[128,6716]{0,1:T(8,128)(2,1)} %fusion.13), channel_id=1, source_target_pairs={{0,4},{4,0},{1,5},{5,1},{2,6},{6,2},{3,7},{7,3},{8,12},{12,8},{9,1... | collective-permute-start | bytes 5157896 | tf_op jit(solution)/shard_map/ppermute | solution.py:49
  1350.8 70.5 %collective-permute-start.64 = (bf16[128,6784]{1,0:T(8,128)(2,1)}, bf16[128,6784]{1,0:T(8,128)(2,1)}, u32[]{:S(2)}, u32[]{:S(2)}) collective-permute-start(bf16[128,6784]{1,0:T(8,128)(2,1)} %fusion.11), channel_id=1, source_target_pairs={{0,2},{2,0},{1,3},{3,1},{4,6},{6,4},{5,7},{7,5},{8,10},{10,8},{9,1... | collective-permute-start | bytes 5210120 | tf_op jit(solution)/shard_map/ppermute | solution.py:49
  1419.3 58.8 %collective-permute-start.72 = (bf16[32,6716]{1,0:T(8,128)(2,1)S(1)}, bf16[32,6716]{1,0:T(8,128)(2,1)S(1)}, u32[]{:S(2)}, u32[]{:S(2)}) collective-permute-start(bf16[32,6716]{1,0:T(8,128)(2,1)S(1)} %get-tuple-element.180), channel_id=1, source_target_pairs={{0,16},{8,24},{16,0},{24,8},{1,17},{9,25},{17,1},{25,9},{2,18},{10... | collective-permute-start | bytes 1289480 | tf_op jit(solution)/shard_map/ppermute | solution.py:120
  1421.0 57.1 %collective-permute-start.71 = (bf16[32,6716]{1,0:T(8,128)(2,1)S(1)}, bf16[32,6716]{1,0:T(8,128)(2,1)S(1)}, u32[]{:S(2)}, u32[]{:S(2)}) collective-permute-start(bf16[32,6716]{1,0:T(8,128)(2,1)S(1)} %get-tuple-element.178), channel_id=1, source_target_pairs={{0,8},{8,16},{16,24},{24,0},{1,9},{9,17},{17,25},{25,1},{2,10},{10... | collective-permute-start | bytes 1289480 | tf_op jit(solution)/shard_map/ppermute | solution.py:120
  1427.9 50.4 %collective-permute-start.67 = (bf16[32,6784]{1,0:T(8,128)(2,1)S(1)}, bf16[32,6784]{1,0:T(8,128)(2,1)S(1)}, u32[]{:S(2)}, u32[]{:S(2)}) collective-permute-start(bf16[32,6784]{1,0:T(8,128)(2,1)S(1)} %get-tuple-element.176), channel_id=1, source_target_pairs={{0,24},{8,0},{16,8},{24,16},{1,25},{9,1},{17,9},{25,17},{2,26},{10... | collective-permute-start | bytes 1302536 | tf_op jit(solution)/shard_map/ppermute | solution.py:120
  1431.4 61.1 %collective-permute-start.66 = (bf16[32,6784]{1,0:T(8,128)(2,1)S(1)}, bf16[32,6784]{1,0:T(8,128)(2,1)S(1)}, u32[]{:S(2)}, u32[]{:S(2)}) collective-permute-start(bf16[32,6784]{1,0:T(8,128)(2,1)S(1)} %get-tuple-element.177), channel_id=1, source_target_pairs={{0,16},{8,24},{16,0},{24,8},{1,17},{9,25},{17,1},{25,9},{2,18},{10... | collective-permute-start | bytes 1302536 | tf_op jit(solution)/shard_map/ppermute | solution.py:120
  1431.7 60.8 %collective-permute-start.65 = (bf16[32,6784]{1,0:T(8,128)(2,1)S(1)}, bf16[32,6784]{1,0:T(8,128)(2,1)S(1)}, u32[]{:S(2)}, u32[]{:S(2)}) collective-permute-start(bf16[32,6784]{1,0:T(8,128)(2,1)S(1)} %get-tuple-element.175), channel_id=1, source_target_pairs={{0,8},{8,16},{16,24},{24,0},{1,9},{9,17},{17,25},{25,1},{2,10},{10... | collective-permute-start | bytes 1302536 | tf_op jit(solution)/shard_map/ppermute | solution.py:120
  (198 other events, 3960.6 us)
Sparse Core Ops, SparseCore 0:
  10.2 42.8 all-gather.12
  54.7 28.7 all-gather.10
  85.7 38.9 all-gather.8
  126.6 38.6 all-gather.16
  167.3 38.6 all-gather.6
  207.4 38.6 all-gather.14

commit v3 on v2

--- a/solution.py
+++ b/solution.py
@@ -1,12 +1,17 @@
+import functools
 import math
 
 import jax
 import jax.numpy as jnp
 from jax import lax
+from jax.experimental import pallas as pl
+from jax.experimental.pallas import tpu as pltpu
 from jax.sharding import Mesh
 from jax.sharding import PartitionSpec as P
 
 HEADS = 16
+MESH = pl.DeviceIdType.MESH
+RING = 8
 
 
 eps = 1e-05
@@ -78,26 +83,316 @@
     return jnp.concatenate(parts, axis=axis)
 
 
-def gather_parts(shard, first, second):
-    own = lax.all_gather(shard, "h", axis=0, tiled=True)
-    one = swap(own, first)
-    two = swap(own, second)
-    both = swap(one, second)
-    four = [own, two, one, both] if first == "x" else [own, one, two, both]
-    return four + [swap(part, "c") for part in four]
-
-
-def gather_rows(shard, first, second):
-    return jnp.concatenate(gather_parts(shard, first, second), axis=0)
-
-
-def gather_columns(shard):
-    cut = -(-shard.shape[1] // 256) * 128
-    left = gather_parts(shard[:, :cut], "x", "y")
-    right = gather_parts(shard[:, cut:], "y", "x")
-    return jnp.concatenate(
-        [jnp.concatenate([a, b], axis=1) for a, b in zip(left, right)], axis=0
-    )
+def greet(peers):
+    barrier = pltpu.get_barrier_semaphore()
+    for peer in peers:
+        pl.semaphore_signal(barrier, inc=1, device_id=peer, device_id_type=MESH)
+    pl.semaphore_wait(barrier, len(peers))
+
+
+def gather_kernel(n_h, jobs, n_arrays, n_full, *refs):
+    shards, wholes = refs[:n_arrays], refs[n_arrays : 2 * n_arrays]
+    own_sem, h_send, h_recv, send, recv = refs[2 * n_arrays :]
+    h, x, y, c = (lax.axis_index(name) for name in ("h", "x", "y", "c"))
+    h = 0 if n_h == 1 else h
+    to_x, to_y, to_c = {"x": 1 - x}, {"y": 1 - y}, {"c": 1 - c}
+    greet([{"h": lax.rem(h + d, n_h)} for d in range(1, n_h)] + [to_x, to_y, to_c])
+
+    def rows_of(job, at):
+        array, low, high, _ = job
+        rows = shards[array].shape[0]
+        place = (pl.ds(at * rows, rows), pl.ds(low, high - low))
+        return wholes[array].at[(c, x, y, *place) if array < n_full else place]
+
+    def h_copy(j, d):
+        array, low, high, _ = jobs[j]
+        return pltpu.make_async_remote_copy(
+            src_ref=shards[array].at[:, pl.ds(low, high - low)],
+            dst_ref=rows_of(jobs[j], h),
+            send_sem=h_send.at[j, d - 1],
+            recv_sem=h_recv.at[j, d - 1],
+            device_id={"h": lax.rem(h + d, n_h)},
+            device_id_type=MESH,
+        )
+
+    def own_copy(j):
+        array, low, high, _ = jobs[j]
+        return pltpu.make_async_copy(
+            shards[array].at[:, pl.ds(low, high - low)], rows_of(jobs[j], h), own_sem.at[j]
+        )
+
+    def block_copy(j, k, block, to, columns):
+        view = wholes[jobs[j][0]].at[(*block, slice(None), pl.ds(columns[0], columns[1] - columns[0]))]
+        return pltpu.make_async_remote_copy(
+            src_ref=view,
+            dst_ref=view,
+            send_sem=send.at[j, k],
+            recv_sem=recv.at[j, k],
+            device_id=to,
+            device_id_type=MESH,
+        )
+
+    own, by_x, by_y, far = (c, x, y), (c, 1 - x, y), (c, x, 1 - y), (c, 1 - x, 1 - y)
+
+    def copy(j, k):
+        _, low, high, middle = jobs[j]
+        block, to, columns = [
+            (own, to_x, (low, high)),
+            (own, to_y, (low, high)),
+            (own, to_c, (low, high)),
+            (by_x, to_y, (low, middle)),
+            (by_y, to_x, (middle, high)),
+            (by_x, to_c, (low, high)),
+            (by_y, to_c, (low, high)),
+            (far, to_c, (low, high)),
+        ][k]
+        return block_copy(j, k, block, to, columns)
+
+    def start_h(j):
+        own_copy(j).start()
+        for d in range(1, n_h):
+            h_copy(j, d).start()
+
+    n = sum(array < n_full for array, *_ in jobs)
+    ahead = 2
+    for j in range(ahead):
+        start_h(j)
+    for step in range(n + 2):
+        if step < n:
+            own_copy(step).wait()
+            for d in range(1, n_h):
+                h_copy(step, d).wait_recv()
+            for k in (0, 1, 2):
+                copy(step, k).start()
+            if step + ahead < len(jobs):
+                start_h(step + ahead)
+        if 0 <= step - 1 < n:
+            for k in (0, 1):
+                copy(step - 1, k).wait_recv()
+            for k in (3, 4, 5, 6):
+                copy(step - 1, k).start()
+        if 0 <= step - 2 < n:
+            for k in (3, 4):
+                copy(step - 2, k).wait_recv()
+            copy(step - 2, 7).start()
+    for j in range(n + ahead, len(jobs)):
+        start_h(j)
+    for j in range(n, len(jobs)):
+        own_copy(j).wait()
+        for d in range(1, n_h):
+            h_copy(j, d).wait_recv()
+    for j in range(len(jobs)):
+        for d in range(1, n_h):
+            h_copy(j, d).wait_send()
+    for j in range(n):
+        for k in range(8):
+            copy(j, k).wait_send()
+        for k in (2, 5, 6, 7):
+            copy(j, k).wait_recv()
+
+
+def gather_all(shards, n_full, cuts, order, collective_id):
+    n_h = lax.axis_size("h")
+    if any(shard.shape[0] % 16 for shard in shards):
+        shards = [lax.all_gather(s, "h", axis=0, tiled=True) for s in shards]
+        n_h = 1
+    jobs = []
+    for array, piece in order:
+        low, high = cuts[array][piece], cuts[array][piece + 1]
+        jobs.append((array, low, high, low + (high - low) // 256 * 128))
+    n, others, dma = len(jobs), max(n_h - 1, 1), pltpu.SemaphoreType.DMA
+    shapes = [(n_h * s.shape[0], s.shape[1]) for s in shards]
+    return pl.pallas_call(
+        functools.partial(gather_kernel, n_h, jobs, len(shards), n_full),
+        out_shape=[
+            jax.ShapeDtypeStruct((2, 2, 2) + shape if k < n_full else shape, jnp.bfloat16)
+            for k, shape in enumerate(shapes)
+        ],
+        in_specs=[pl.BlockSpec(memory_space=pl.ANY)] * len(shards),
+        out_specs=[pl.BlockSpec(memory_space=pl.ANY)] * len(shards),
+        scratch_shapes=[dma((n,)), dma((n, others)), dma((n, others)), dma((n, 8)), dma((n, 8))],
+        compiler_params=pltpu.CompilerParams(collective_id=collective_id, has_side_effects=True),
+    )(*shards)
+
+
+def scatter_kernel(n_h, n, n_first, run, lefts, rights, more, out, right_buf, own, s1, r1, s2, r2, s3, r3,
+                   load_sem, send1, recv1, send2, recv2, send3, recv3):
+    h, x, y = (lax.axis_index(name) for name in ("h", "x", "y"))
+    to_x, to_y = {"x": 1 - x}, {"y": 1 - y}
+    w = s3.shape[1]
+    rows = w // n_h
+    f32, b16 = jnp.float32, jnp.bfloat16
+    greet([{"h": lax.rem(h + d, n_h)} for d in range(1, n_h)] + [to_x, to_y])
+
+    def load(i, source, k):
+        slot = lax.rem(i, 3)
+        return pltpu.make_async_copy(source.at[k], right_buf.at[slot], load_sem.at[slot])
+
+    def start_load(i):
+        @pl.when(i < n_first)
+        def _():
+            load(i, rights, i).start()
+
+        @pl.when((i >= n_first) & (i < n))
+        def _():
+            load(i, more, i - n_first).start()
+
+    def hop(i, source, target, send_sem, recv_sem, to):
+        slot = lax.rem(i, RING)
+        return pltpu.make_async_remote_copy(
+            src_ref=source.at[slot], dst_ref=target.at[i], send_sem=send_sem.at[slot],
+            recv_sem=recv_sem.at[i], device_id=to, device_id_type=MESH,
+        )
+
+    def first(i, odd):
+        return hop(i, s1, r1, send1, recv1, to_y if odd else to_x)
+
+    def second(i, odd):
+        return hop(i, s2, r2, send2, recv2, to_x if odd else to_y)
+
+    def third(i, d):
+        to = lax.rem(h + d, n_h)
+        slot = lax.rem(i, RING)
+        return pltpu.make_async_remote_copy(
+            src_ref=s3.at[slot, pl.ds(to * rows, rows)], dst_ref=r3.at[i, d - 1],
+            send_sem=send3.at[slot, d - 1], recv_sem=recv3.at[i, d - 1],
+            device_id={"h": to}, device_id_type=MESH,
+        )
+
+    def multiply(i, odd):
+        slot = lax.rem(i, RING)
+        load(i, rights, 0).wait()
+        pair = i // 2
+        left = lefts[pair - (pair + 1024 - run) // 1024 * (pair - run)]
+        right = right_buf[lax.rem(i, 3)]
+        start_load(i + 2)
+
+        @pl.when(i >= RING)
+        def _():
+            first(i - RING, odd).wait_send()
+
+        part = lax.dot_general(left, right, (((1,), (1,)), ((), ())), preferred_element_type=f32)
+        own[slot, :w] = part[:w]
+        if odd:
+            own[slot, w:] = part[2 * w : 3 * w]
+            s1[slot, :w] = part[w : 2 * w].astype(b16)
+            s1[slot, w:] = part[3 * w :].astype(b16)
+        else:
+            own[slot, w:] = part[w : 2 * w]
+            s1[slot] = part[2 * w :].astype(b16)
+        first(i, odd).start()
+
+    def pass_on(i, odd):
+        slot = lax.rem(i, RING)
+        first(i, odd).wait_recv()
+
+        @pl.when(i >= RING)
+        def _():
+            second(i - RING, odd).wait_send()
+
+        s2[slot] = (own[slot, w:] + r1[i, w:].astype(f32)).astype(b16)
+        second(i, odd).start()
+
+    def keep(i, odd):
+        slot = lax.rem(i, RING)
+        second(i, odd).wait_recv()
+        part = own[slot, :w] + r1[i, :w].astype(f32) + r2[i].astype(f32)
+        if n_h == 1:
+            out[i] = part.astype(b16)
+            return
+
+        @pl.when(i >= RING)
+        def _():
+            for d in range(1, n_h):
+                third(i - RING, d).wait_send()
+
+        s3[slot] = part.astype(b16)
+        for d in range(1, n_h):
+            third(i, d).start()
+
+    def finish(i, odd):
+        if n_h == 1:
+            return
+        total = s3[lax.rem(i, RING), pl.ds(h * rows, rows)].astype(f32)
+        for d in range(1, n_h):
+            third(i, d).wait_recv()
+            total = total + r3[i, d - 1].astype(f32)
+        out[i] = total
+
+    start_load(jnp.int32(0))
+    start_load(jnp.int32(1))
+    pairs = (n + 1) // 2
+
+    def step(p, carry):
+        for lag, stage in enumerate((multiply, pass_on, keep, finish)):
+            for odd in (0, 1):
+                i = 2 * (p - lag) + odd
+
+                @pl.when((i >= 0) & (i < n))
+                def _(stage=stage, i=i, odd=odd):
+                    stage(i, odd)
+
+        return carry
+
+    lax.fori_loop(0, pairs + 3, step, 0)
+    for i in range(max(n - RING, 0), n):
+        first(i, i % 2).wait_send()
+        second(i, i % 2).wait_send()
+        for d in range(1, n_h):
+            third(i, d).wait_send()
+
+
+def scatter_all(lefts, rights, more, collective_id):
+    n_first, m, cells = rights.shape
+    n = n_first + more.shape[0]
+    w = lefts.shape[1] // 4
+    n_h = lax.axis_size("h")
+    rows = w // n_h
+    inner_h = n_h if rows % 16 == 0 else 1
+    dma, bf16 = pltpu.SemaphoreType.DMA, jnp.bfloat16
+    vmem, hbm = pl.BlockSpec(memory_space=pltpu.VMEM), pl.BlockSpec(memory_space=pl.ANY)
+    others = max(inner_h - 1, 1)
+    part = pl.pallas_call(
+        functools.partial(scatter_kernel, inner_h, n, n_first, lefts.shape[0] - 1),
+        out_shape=(
+            jax.ShapeDtypeStruct((n, rows, m), jnp.float32)
+            if inner_h > 1
+            else jax.ShapeDtypeStruct((n, w, m), bf16)
+        ),
+        in_specs=[vmem, hbm, hbm],
+        out_specs=vmem,
+        scratch_shapes=[
+            pltpu.VMEM((3, m, cells), bf16),
+            pltpu.VMEM((RING, 2 * w, m), jnp.float32),
+            pltpu.VMEM((RING, 2 * w, m), bf16),
+            pltpu.VMEM((n, 2 * w, m), bf16),
+            pltpu.VMEM((RING, w, m), bf16),
+            pltpu.VMEM((n, w, m), bf16),
+            pltpu.VMEM((RING, w, m), bf16),
+            pltpu.VMEM((n, others, w // inner_h, m), bf16),
+            dma((3,)),
+            dma((RING,)),
+            dma((n,)),
+            dma((RING,)),
+            dma((n,)),
+            dma((RING, others)),
+            dma((n, others)),
+        ],
+        compiler_params=pltpu.CompilerParams(
+            collective_id=collective_id, has_side_effects=True, vmem_limit_bytes=60 * 2**20
+        ),
+    )(lefts, rights, more)
+    if inner_h > 1:
+        return part
+    return lax.psum_scatter(part, "h", scatter_dimension=1, tiled=True).astype(jnp.float32)
+
+
+def gather_dec(own):
+    by_x, by_y = swap(own, "x"), swap(own, "y")
+    middle = own.shape[1] // 256 * 128
+    far = [swap(by_x[:, :middle], "y"), swap(by_y[:, middle:], "x")]
+    four = [own, by_y, by_x, jnp.concatenate(far, axis=1)]
+    return jnp.concatenate(four + [swap(part, "c") for part in four], axis=0)
 
 
 def with_other_core(value):
@@ -171,6 +466,22 @@
     keep = lax.dynamic_index_in_dim(part, at_y, 0, False).astype(jnp.float32)
     send = lax.dynamic_index_in_dim(part, 1 - at_y, 0, False)
     return keep + swap(send, "y").astype(jnp.float32)
+
+
+def in_chunks(right):
+    n = -(-right.shape[0] // 512) * 512
+    return jnp.pad(right, ((0, n - right.shape[0]), (0, 0))).reshape(n // 512, 512, -1)
+
+
+def left_of(left, pieces):
+    left = own_half(relative(left, 1)).T
+    n_h = lax.axis_size("h")
+    left = left.reshape(4, n_h, pieces, -1, left.shape[1])
+    return left.transpose(2, 0, 1, 3, 4).reshape(pieces, -1, left.shape[-1])
+
+
+def right_of(right):
+    return in_chunks(with_other_core(right).T)
 
 
 def on_device(
@@ -198,29 +509,45 @@
     group_size = 4
     slots = rows * group_size
     scale = 10000.0 / library
+    genes = counts.shape[1]
+    padded = -(-genes // 128) * 128
     counts_f = counts.astype(jnp.float32)
-    xb = jnp.log1p(counts_f * scale[:, None]).astype(jnp.bfloat16)
+    xb = jnp.pad(counts.T, ((0, padded - genes), (0, 0))).astype(jnp.float32)
+    xb = jnp.log1p(xb * scale[None, :]).astype(jnp.bfloat16)
+    xb_both = in_chunks(jnp.concatenate([xb, swap(xb, "c")], axis=1))
     pe = by_owner(positions(coords, width), 1)
     ends = jnp.cumsum(lengths[0])
     place = jnp.arange(slots, dtype=jnp.int32)
     seg_all = jnp.sum((place[:, None] >= ends[None, :]).astype(jnp.int32), axis=1)
     seg_mine = lax.dynamic_slice_in_dim(seg_all, (lax.axis_index("y") * 2 + lax.axis_index("c")) * rows, rows)
     same = (seg_mine[:, None] == seg_all[None, :])[None]
-    enc_all = gather_columns(w_enc.T)
     vectors = jnp.stack([gain_one, shift_one, gain_two, shift_two], axis=1)
     vectors = jnp.pad(vectors, ((0, 0), (0, 124)))
-    qkv_all = gather_rows(jnp.concatenate([w_qkv, vectors], axis=1), "x", "y")
-    out_all = gather_rows(by_owner(w_out, 1), "y", "x")
-    up_all = gather_rows(by_owner(w_up, 1), "y", "x")
-    down_all = gather_rows(by_owner(w_down, 1), "x", "y")
-    dec_all = gather_columns(w_dec.T)
-    vectors = relative(qkv_all[:, 3 * width :].astype(jnp.float32), 0).T
+    pad = ((0, 0), (0, padded - genes))
+    quarter = -(-padded // 512) * 128
+    gene_cuts = [0, quarter, 2 * quarter, 3 * quarter, padded]
+    shards = [
+        jnp.pad(w_enc.T, pad),
+        jnp.concatenate([w_qkv, vectors], axis=1),
+        by_owner(w_out, 1),
+        by_owner(w_up, 1),
+        by_owner(w_down, 1),
+        jnp.pad(w_dec.T, pad),
+    ]
+    cuts = [gene_cuts, [0, width // 2 * 3, 3 * width + 128], [0, width]]
+    cuts += [[0, 2 * width, 4 * width], [0, width // 2, width], [0, padded]]
+    order = [(0, 0), (0, 1), (0, 2), (0, 3), (1, 0), (1, 1), (2, 0), (3, 0), (3, 1), (4, 0), (4, 1), (5, 0)]
+    gathered = gather_all(shards, 5, cuts, order, 0)
+    enc_all, qkv_all, out_all, up_all, down_all = (
+        w.reshape(-1, w.shape[-1]) for w in gathered[:5]
+    )
+    dec_all = gather_dec(gathered[5])
+    vectors = qkv_all[:, 3 * width :].astype(jnp.float32).T
     qkv_all = qkv_all[:, : 3 * width]
     g1f, b1f, g2f, b2f = vectors[0], vectors[1], vectors[2], vectors[3]
-    h0 = relative(contract_cols(xb, enc_all), 1) + pe
+    h0 = contract_cols(xb.T, enc_all) + pe
     a1 = layer_norm(h0, g1f, b1f).astype(jnp.bfloat16)
-    a1_rel = relative(a1, 1)
-    qkv = matmul(a1_rel, qkv_all).astype(jnp.bfloat16)
+    qkv = matmul(a1, qkv_all).astype(jnp.bfloat16)
     query = qkv[:, :width].reshape(rows, heads, head_width)
     kv_all = gather_group(qkv[:, width:])
     keys = kv_all[:, :width].reshape(slots, heads, head_width)
@@ -240,33 +567,26 @@
     probs_b = (expo / total).astype(jnp.bfloat16)
     attended = jnp.einsum("hqk,khd->qhd", probs_b, values, preferred_element_type=jnp.float32)
     attended_b = attended.reshape(rows, width).astype(jnp.bfloat16)
-    attended_rel = relative(by_owner(attended_b, 1), 1)
-    h1 = h0 + matmul(attended_rel, out_all)
+    attended_b = by_owner(attended_b, 1)
+    h1 = h0 + matmul(attended_b, out_all)
     a2 = layer_norm(h1, g2f, b2f).astype(jnp.bfloat16)
-    a2_rel = relative(a2, 1)
-    hidden = matmul(a2_rel, up_all)
+    hidden = matmul(a2, up_all)
     act = jax.nn.gelu(hidden, approximate=False).astype(jnp.bfloat16)
-    act_rel = relative(act, 1)
-    h2 = h1 + matmul(act_rel, down_all)
+    h2 = h1 + matmul(act, down_all)
     hb_rel = relative(h2.astype(jnp.bfloat16), 1)
-    logits = matmul(hb_rel, dec_all).astype(jnp.bfloat16)
+    logits = matmul(hb_rel, dec_all).astype(jnp.bfloat16)[:, :genes]
     grad_dec = scatter_columns(own_half(hb_rel), with_other_core(cotangent))
-    dh2 = relative(contract_cols(cotangent, dec_all), 1)
+    dh2 = relative(contract_cols(jnp.pad(cotangent, pad), dec_all), 1)
     dfb = dh2.astype(jnp.bfloat16)
-    grad_down = scatter(own_half(act_rel), with_other_core(dfb), "x", "y")
-    d_act = relative(contract_cols(dfb, down_all), 1)
+    d_act = contract_cols(dfb, down_all)
     slope = jax.vjp(lambda v: jax.nn.gelu(v, approximate=False), hidden)[1](d_act)[0]
     d_hidden = slope.astype(jnp.bfloat16)
-    grad_up = scatter(own_half(a2_rel), with_other_core(d_hidden), "y", "x")
-    da2 = relative(contract_cols(d_hidden, up_all), 1)
+    da2 = contract_cols(d_hidden, up_all)
     norm_pull = jax.vjp(layer_norm, h1, g2f, b2f)[1]
     dh1_norm, grad_gain_two, grad_shift_two = norm_pull(da2)
     dh1 = dh2 + dh1_norm
-    grad_down = from_owner(grad_down, 1)
-    grad_up = from_owner(grad_up, 1)
     dab = dh1.astype(jnp.bfloat16)
-    grad_out = from_owner(scatter(own_half(attended_rel), with_other_core(dab), "y", "x"), 1)
-    d_attended = relative(contract_cols(dab, out_all).astype(jnp.bfloat16), 1)
+    d_attended = contract_cols(dab, out_all).astype(jnp.bfloat16)
     d_attended = from_owner(d_attended, 1).reshape(rows, heads, head_width)
     probs = jnp.exp(scores_of() - log_total)
     probs_b = probs.astype(jnp.bfloat16)
@@ -283,8 +603,7 @@
     d_kv = jnp.concatenate([d_keys.reshape(slots, width), d_values.reshape(slots, width)], axis=1)
     d_kv = scatter_group(d_kv)
     d_qkv = jnp.concatenate([d_query.reshape(rows, width), d_kv], axis=1).astype(jnp.bfloat16)
-    grad_qkv = scatter(own_half(a1_rel), with_other_core(d_qkv), "x", "y")
-    da1 = relative(contract_cols(d_qkv, qkv_all), 1)
+    da1 = contract_cols(d_qkv, qkv_all)
     first_pull = jax.vjp(layer_norm, h0, g1f, b1f)[1]
     dh0_norm, grad_gain_one, grad_shift_one = first_pull(da1)
     grad_vectors = jnp.stack([grad_gain_one, grad_shift_one, grad_gain_two, grad_shift_two], axis=1)
@@ -294,9 +613,26 @@
     )
     dh0b = (dh1 + dh0_norm).astype(jnp.bfloat16)
 
-    dh0b_rel = relative(dh0b, 1)
-    grad_enc = scatter_columns(own_half(dh0b_rel), with_other_core(xb))
-    d_xb = matmul(dh0b_rel, enc_all)
+    lefts = [left_of(a1, 1)] * 3 + [left_of(attended_b, 1)] + [left_of(a2, 1)] * 4
+    lefts += [left_of(act, act.shape[1] // width), left_of(dh0b, 1)]
+    rights = [right_of(d_qkv), right_of(dab), right_of(d_hidden)] + [right_of(dfb)] * 4
+    grads = scatter_all(
+        jnp.concatenate(lefts, axis=0), jnp.concatenate(rights, axis=0), xb_both, 1
+    )
+    own_rows, m = grads.shape[1:]
+    ends = [0]
+    for columns in (3 * width, width, 4 * width, 4 * width):
+        ends.append(ends[-1] + columns // m)
+    grad_qkv, grad_out, grad_up, grad_down, grad_enc = (
+        grads[low:high] for low, high in zip(ends, ends[1:] + [grads.shape[0]])
+    )
+    grad_qkv, grad_out, grad_up, grad_enc = (
+        g.transpose(1, 0, 2).reshape(own_rows, -1) for g in (grad_qkv, grad_out, grad_up, grad_enc)
+    )
+    grad_down = grad_down.reshape(4, -1, own_rows, m).transpose(0, 2, 1, 3).reshape(4 * own_rows, -1)
+    grad_out, grad_up, grad_down = (from_owner(g, 1) for g in (grad_out, grad_up, grad_down))
+    grad_enc = grad_enc[:, :genes].T
+    d_xb = matmul(dh0b, enc_all)[:, :genes]
     counts_grad = d_xb * scale[:, None] / (1.0 + counts_f * scale[:, None])
     return (
         logits,

time: 1510 us -> 1170 us (0.77)
  Pallas kernels: 0 us -> 497 us
  waiting for transfers between devices: 631 us -> 175 us
  local copies, waits for them, and re-layouts: 247 us -> 142 us
  matrix products: 284 us -> 204 us
  starting transfers between devices: 147 us -> 70.7 us
  other arithmetic: 127 us -> 71.9 us
  blocking collectives: 48 us -> 0 us
    pallas_call x0 -> x2, Pallas kernels: none -> 497 us  [the longest x1 253 us: gather_all(): pl.pallas_call(functools.partial(gather_kernel, n_h, jobs, len(shards), n...]
    ppermute x99 -> x33, waiting for transfers between devices: 448 us -> 159 us  [swap(): return lax.ppermute(value, axis, [(0, 1), (1, 0)])]
    all_gather x6 -> x0, waiting for transfers between devices: 94 us -> none  [gather_parts(): own = lax.all_gather(shard, 'h', axis=0, tiled=True)]
    dot_general x32 -> x8, matrix products: 129 us -> 42.9 us  [contract_rows(): lax.dot_general(left, right, (((0,), (0,)), ((), ())), preferred_element_...]
    ppermute x27 -> x9, waiting for transfers between devices: 88.9 us -> 15.4 us  [sum_over_h(): total = total + lax.ppermute(send, 'h', ring).astype(jnp.float32)]
    ppermute x18 -> x2, local copies, waits for them, and re-layouts: 61.4 us -> 8.11 us  [swap(): return lax.ppermute(value, axis, [(0, 1), (1, 0)])]
    ppermute x99 -> x33, starting transfers between devices: 65.2 us -> 14.7 us  [swap(): return lax.ppermute(value, axis, [(0, 1), (1, 0)])]
    all_gather x2 -> x0, blocking collectives: 48 us -> none  [gather_parts(): own = lax.all_gather(shard, 'h', axis=0, tiled=True)]
  transfers between devices with their start and end apart: 132 -> 42, of which waited for: 39 -> 15; matrix products, arithmetic and copies ran while one was open for 42% -> 25% of each run, Pallas kernels for 0% -> 0%
where the time goes in v3:
time: 1170 us; the launch traced here: 1160 us
  Pallas kernels  497 us (42%)
  matrix products  204 us (17%)
  waiting for transfers between devices  175 us (15%)
  local copies, waits for them, and re-layouts  142 us (12%)
  other arithmetic  71.9 us (6%)
  starting transfers between devices  70.7 us (6%)
    pallas_call x1, Pallas kernels, gather_all(): pl.pallas_call(functools.partial(gather_kernel, n_h, jobs, len(shards), n...  253 us
    pallas_call x1, Pallas kernels, scatter_all(): pl.pallas_call(functools.partial(scatter_kernel, inner_h, n, n_first, lef...  244 us
    ppermute x33, waiting for transfers between devices, swap(): return lax.ppermute(value, axis, [(0, 1), (1, 0)])  159 us
    dot_general x6, matrix products, contract_cols(): lax.dot_general(left, right, (((1,), (1,)), ((), ())), preferred_element_...  63.2 us
    unnamed x186, local copies, waits for them, and re-layouts  58.8 us
    ppermute x9, starting transfers between devices, sum_over_h(): total = total + lax.ppermute(send, 'h', ring).astype(jnp.float32)  56 us
    dot_general x6, matrix products, matmul(): return jnp.dot(left, right, preferred_element_type=jnp.float32)  54.7 us
    dot_general x8, matrix products, contract_rows(): lax.dot_general(left, right, (((0,), (0,)), ((), ())), preferred_element_...  42.9 us
  transfers between devices with their start and end apart: 42, of which 15 were waited for; matrix products, arithmetic and copies ran while one was open for 25% of the time, Pallas kernels for 0%

profile of v3, /device:TPU:0, one launch (start us, length us, event | category | flops | bytes accessed | tf_op | source)
XLA Modules:
  0.0 1163.4 jit_solution(11870840778383606770)
XLA Ops:
  10.3 252.6 %shard_map.238 = (bf16[2,2,2,128,13568]{4,3,2,1,0:T(8,128)(2,1)}, bf16[2,2,2,128,3200]{4,3,2,1,0:T(8,128)(2,1)}, bf16[2,2,2,128,1024]{4,3,2,1,0:T(8,128)(2,1)}, ...) custom-call(bf16[32,13568]{1,0:T(8,128)(2,1)} %pad.24.refs_0_, ...), custom_call_target="tpu_custom_call" | custom-call | tf_op jit(solution)/shard_map/pallas_call | solution.py:205
  267.2 18.4 %fusion.91 = (f32[256]{0:T(256)S(1)}, f32[256,1024]{0,1:T(8,128)S(1)}) fusion(f32[256,1024]{0,1:T(8,128)S(1)} %bitcast.255, bf16[1024,13568]{1,0:T(8,128)(2,1)} %bitcast.286, f32[256]{0:T(256)S(1)} %broadcast_divide_fusion, bf16[13500,256]{1,0:T(8,128)(2,1)} %bitcast.233), kind=kOutput, calls=%fused_computation.318 | convolution fusion | flops 7124484096 | bytes 36798464 | tf_op jit(solution)/shard_map/dot_general | solution.py:44
  288.7 4.8 fusion.44
  296.3 9.9 log-plus-one_convert_fusion
  308.0 3.9 constant_dynamic-update-slice_fusion.15
  311.9 50.9 %collective-permute-done = bf16[256,2048]{1,0:T(8,128)(2,1)} collective-permute-done((bf16[256,2048]{1,0:T(8,128)(2,1)}, bf16[256,2048]{1,0:T(8,128)(2,1)}, u32[]{:S(2)}, u32[]{:S(2)}) %collective-permute-start) | collective-permute-done | bytes 1048608 | tf_op jit(solution)/shard_map/ppermute | solution.py:54
  364.6 6.8 constant_dynamic-update-slice_fusion.32
  374.0 2.5 fusion.88
  376.5 2.9 copy.166
  379.4 4.6 copy.164
  384.0 4.1 fusion.92
  388.1 3.8 fusion.7
  394.4 4.7 fusion.53
  399.2 2.6 fusion.93
  403.2 6.1 fusion.96
  411.8 2.9 slice.189
  418.2 3.9 constant_dynamic-update-slice_fusion.14
  422.1 4.0 constant_dynamic-update-slice_fusion.13
  426.1 28.9 %collective-permute-done.4 = bf16[128,6784]{1,0:T(8,128)(2,1)S(1)} collective-permute-done((bf16[128,6784]{1,0:T(8,128)(2,1)S(1)}, bf16[128,6784]{1,0:T(8,128)(2,1)S(1)}, u32[]{:S(2)}, u32[]{:S(2)}) %collective-permute-start.4) | collective-permute-done | bytes 1736736 | tf_op jit(solution)/shard_map/ppermute | solution.py:54
  460.2 4.0 constant_dynamic-update-slice_fusion.11
  464.2 6.8 constant_dynamic-update-slice_fusion.31
  473.0 4.0 constant_dynamic-update-slice_fusion.9
  477.0 12.5 %fusion.11 = bf16[13824,512]{1,0:T(8,128)(2,1)} fusion(bf16[13568,256]{1,0:T(8,128)(2,1)} %collective-permute-done.21, bf16[13568,256]{1,0:T(8,128)(2,1)S(1)} %bitcast.214), kind=kLoop, calls=%fused_computation.14 | loop fusion | flops 49545216 | bytes 28049408 | tf_op jit(solution)/shard_map/concatenate | solution.py:517
  491.5 14.6 %fusion.23 = f32[256,1024]{0,1:T(8,128)S(1)} fusion(bf16[1024,13568]{1,0:T(8,128)(2,1)} %constant_dynamic-update-slice_fusion.8, bf16[256,13500]{0,1:T(8,128)(2,1)} %param.19), kind=kOutput, calls=%fused_computation.35 | convolution fusion | flops 7113539584 | bytes 35747840 | tf_op jit(solution)/shard_map/dot_general | solution.py:44
  506.4 15.8 %add_convert_fusion = (bf16[256,4096]{1,0:T(8,128)(2,1)}, f32[256,4096]{1,0:T(8,128)}) fusion(f32[256,4096]{1,0:T(8,128)S(1)} %fusion.96, bf16[256,1024]{0,1:T(8,128)(2,1)S(1)} %convert_element_type.245, bf16[4096,1024]{1,0:T(8,128)(2,1)} %bitcast.288), kind=kOutput, calls=%fused_computation.64 | convolution fusion | flops 2222981120 | bytes 19398656 | tf_op jit(solution)/shard_map/dot_general | solution.py:44
  522.3 7.4 fusion.94
  534.1 14.5 %multiply_reduce_fusion = (f32[16,256]{1,0:T(8,128)S(1)}, f32[16,256,1024]{2,1,0:T(8,128)}) fusion(f32[16,256,1024]{2,1,0:T(8,128)} %copy-done, f32[16,256]{1,0:T(8,128)S(1)} %log_add_fusion, bf16[256,16,64]{0,2,1:T(8,128)(2,1)S(1)} %bitcast.235, bf16[1024,16,64]{0,2,1:T(8,128)(2,1)} %bitcast.225), kind=kOutput, calls=%fused_computation.7 | convolution fusion | flops 549449728 | bytes 36208640 | tf_op jit(solution)/shard_map/qhd,khd->hqk/dot_general | solution.py:593
  548.6 9.9 convert_bitcast_fusion
  558.6 10.4 multiply_convert_fusion
  568.9 7.1 fusion.52
  576.1 2.9 fusion.50
  581.6 3.4 fusion.51
  588.6 4.5 concatenate.137
  593.1 2.9 concatenate.136
  603.2 15.5 %fusion.97 = bf16[256,13568]{0,1:T(8,128)(2,1)S(1)} fusion(bf16[256,1024]{0,1:T(8,128)(2,1)} %copy-done.54, bf16[1024,13568]{1,0:T(8,128)(2,1)} %constant_dynamic-update-slice_fusion.8), kind=kOutput, calls=%fused_computation.324 | convolution fusion | flops 7113539584 | bytes 35258368 | tf_op jit(solution)/shard_map/dot_general | solution.py:50
  618.8 3.6 slice.267
  624.3 6.7 convolution_convert_fusion.3
  631.1 3.2 convolution_convert_fusion
  634.5 3.2 convolution_convert_fusion.1
  639.4 3.6 convolution_convert_fusion.2
  648.1 2.5 copy.184
  653.9 21.1 %collective-permute-done.37 = bf16[128,6716]{0,1:T(8,128)(2,1)} collective-permute-done((bf16[128,6716]{0,1:T(8,128)(2,1)}, bf16[128,6716]{0,1:T(8,128)(2,1)}, u32[]{:S(2)}, u32[]{:S(2)}) %collective-permute-start.37) | collective-permute-done | bytes 1719328 | tf_op jit(solution)/shard_map/ppermute | solution.py:54
  675.2 6.6 fusion.18
  681.8 29.0 %collective-permute-done.36 = bf16[128,6716]{0,1:T(8,128)(2,1)} collective-permute-done((bf16[128,6716]{0,1:T(8,128)(2,1)}, bf16[128,6716]{0,1:T(8,128)(2,1)}, u32[]{:S(2)}, u32[]{:S(2)}) %collective-permute-start.36) | collective-permute-done | bytes 1719328 | tf_op jit(solution)/shard_map/ppermute | solution.py:54
  711.1 4.2 copy.195
  715.3 2.8 fusion.38
  719.5 7.1 fusion.17
  726.6 4.7 maximum_bitcast_fusion
  731.3 6.5 copy.186
  737.8 5.6 collective-permute-done.11
  744.9 6.2 fusion.95
  755.6 22.3 %fusion.8 = f32[256,13500]{0,1:T(8,128)} fusion(bf16[256,1024]{0,1:T(8,128)(2,1)} %add_convert_fusion.1, bf16[1024,13568]{1,0:T(8,128)(2,1)} %bitcast.287, bf16[256,13500]{0,1:T(8,128)(2,1)} %param.15, f32[256]{0:T(256)S(1)} %copy-done.56), kind=kOutput, calls=%fused_computation.13 | convolution fusion | flops 7095168000 | bytes 49048576 | tf_op jit(solution)/shard_map/dot_general | solution.py:50
  782.2 2.9 collective-permute-done.24
  785.2 17.1 %collective-permute-start.25 = (bf16[32,4]{0,1:T(4,128)(2,1)S(1)}, bf16[32,4]{0,1:T(4,128)(2,1)S(1)}, u32[]{:S(2)}, u32[]{:S(2)}) collective-permute-start(bf16[32,4]{0,1:T(4,128)(2,1)S(1)} %get-tuple-element.166), channel_id=1, source_target_pairs={{0,8},{8,16},{16,24},{24,0},{1,9},{9,17},{17,25},{25,1},{2,10},{10... | collective-permute-start | bytes 776 | tf_op jit(solution)/shard_map/ppermute | solution.py:415
  802.3 3.4 collective-permute-start.26
  811.9 3.9 copy.197
  815.9 6.3 fusion.15
  827.8 16.1 %collective-permute-done.32 = bf16[128,6784]{1,0:T(8,128)(2,1)} collective-permute-done((bf16[128,6784]{1,0:T(8,128)(2,1)}, bf16[128,6784]{1,0:T(8,128)(2,1)}, u32[]{:S(2)}, u32[]{:S(2)}) %collective-permute-start.32) | collective-permute-done | bytes 1736736 | tf_op jit(solution)/shard_map/ppermute | solution.py:54
  843.9 6.3 fusion.16
  851.6 4.7 collective-permute-start.34
  856.3 24.2 %collective-permute-start.35 = (bf16[32,6784]{1,0:T(8,128)(2,1)S(1)}, bf16[32,6784]{1,0:T(8,128)(2,1)S(1)}, u32[]{:S(2)}, u32[]{:S(2)}) collective-permute-start(bf16[32,6784]{1,0:T(8,128)(2,1)S(1)} %get-tuple-element.103), channel_id=1, source_target_pairs={{0,24},{8,0},{16,8},{24,16},{1,25},{9,1},{17,9},{25,17},{2,26},{10... | collective-permute-start | bytes 1302536 | tf_op jit(solution)/shard_map/ppermute | solution.py:415
  880.6 11.5 collective-permute-done.34
  899.8 4.6 copy-done.4
  904.4 244.2 %shard_map.239 = f32[51,32,512]{2,1,0:T(8,128)} custom-call(bf16[13,512,512]{2,1,0:T(8,128)(2,1)} %fusion.63.lefts, bf16[24,512,512]{2,1,0:T(8,128)(2,1)} %copy-done.4, bf16[27,512,512]{2,1,0:T(8,128)(2,1)} %bitcast.212), custom_call_target="tpu_custom_call" | custom-call | tf_op jit(solution)/shard_map/pallas_call | solution.py:355
  (380 shorter events, 121.5 us)
Async XLA Ops:
  0.7 8.9 copy-start.44
  3.0 262.2 %copy-start.57 = (s32[2,256]{1,0:T(2,128)S(1)}, s32[2,256]{1,0:T(2,128)}, u32[]{:S(2)}) copy-start(s32[2,256]{1,0:T(2,128)} %param.17) | copy-start | bytes 6148
  3.0 262.2 %copy-start.58 = (f32[256]{0:T(256)S(1)}, f32[256]{0:T(256)}, u32[]{:S(2)}) copy-start(f32[256]{0:T(256)} %param.16) | copy-start | bytes 3076
  262.9 153.6 %collective-permute-start.2 = (bf16[128,13568]{1,0:T(8,128)(2,1)}, bf16[128,13568]{1,0:T(8,128)(2,1)}, u32[]{:S(2)}, u32[]{:S(2)}) collective-permute-start(bf16[128,13568]{1,0:T(8,128)(2,1)} %get-tuple-element.23), channel_id=1, source_target_pairs={{0,2},{2,0},{1,3},{3,1},{4,6},{6,4},{5,7},{7,5},{8,10},{10,8},{9,1... | collective-permute-start | bytes 10420232 | tf_op jit(solution)/shard_map/ppermute | solution.py:54
  264.4 147.5 %collective-permute-start.3 = (bf16[128,13568]{1,0:T(8,128)(2,1)}, bf16[128,13568]{1,0:T(8,128)(2,1)}, u32[]{:S(2)}, u32[]{:S(2)}) collective-permute-start(bf16[128,13568]{1,0:T(8,128)(2,1)} %get-tuple-element.23), channel_id=1, source_target_pairs={{0,4},{4,0},{1,5},{5,1},{2,6},{6,2},{3,7},{7,3},{8,12},{12,8},{9,1... | collective-permute-start | bytes 10420232 | tf_op jit(solution)/shard_map/ppermute | solution.py:54
  265.1 194.6 %collective-permute-start.6 = (bf16[128,13568]{1,0:T(8,128)(2,1)}, bf16[128,13568]{1,0:T(8,128)(2,1)}, u32[]{:S(2)}, u32[]{:S(2)}) collective-permute-start(bf16[128,13568]{1,0:T(8,128)(2,1)} %get-tuple-element.23), channel_id=1, source_target_pairs={{0,1},{1,0},{2,3},{3,2},{4,5},{5,4},{6,7},{7,6},{8,9},{9,8},{10,11... | collective-permute-start | bytes 10420232 | tf_op jit(solution)/shard_map/ppermute | solution.py:54
  265.2 31.1 %copy-start.55 = (f32[256]{0:T(256)}, f32[256]{0:T(256)S(1)}, u32[]{:S(2)}) copy-start(f32[256]{0:T(256)S(1)} %broadcast_divide_fusion) | copy-start | bytes 3076
  285.6 113.5 %copy-start.2 = (f32[256,1024]{0,1:T(8,128)}, f32[256,1024]{0,1:T(8,128)S(1)}, u32[]{:S(2)}) copy-start(f32[256,1024]{0,1:T(8,128)S(1)} %get-tuple-element.170) | copy-start | bytes 3145732
  295.9 66.9 %collective-permute-start = (bf16[256,2048]{1,0:T(8,128)(2,1)}, bf16[256,2048]{1,0:T(8,128)(2,1)}, u32[]{:S(2)}, u32[]{:S(2)}) collective-permute-start(bf16[256,2048]{1,0:T(8,128)(2,1)} %get-tuple-element.109), channel_id=1, source_target_pairs={{0,2},{2,0},{1,3},{3,1},{4,6},{6,4},{5,7},{7,5},{8,10},{10,8},{9,1... | collective-permute-start | bytes 3145736 | tf_op jit(solution)/shard_map/ppermute | solution.py:54
  296.3 9.9 slice-start.10
  364.3 7.2 collective-permute-start.1
  402.5 8.9 collective-permute-start.14
  403.0 6.4 collective-permute-start.12
  409.3 97.1 %copy-start.8 = (f32[256,4096]{1,0:T(8,128)}, f32[256,4096]{1,0:T(8,128)S(1)}, u32[]{:S(2)}) copy-start(f32[256,4096]{1,0:T(8,128)S(1)} %fusion.96) | copy-start | bytes 12582916
  409.4 1.6 collective-permute-start.13
  411.0 53.3 %collective-permute-start.29 = (bf16[256,13500]{0,1:T(8,128)(2,1)}, bf16[256,13500]{0,1:T(8,128)(2,1)}, u32[]{:S(2)}, u32[]{:S(2)}) collective-permute-start(bf16[256,13500]{0,1:T(8,128)(2,1)} %param.19), channel_id=1, source_target_pairs={{0,1},{1,0},{2,3},{3,2},{4,5},{5,4},{6,7},{7,6},{8,9},{9,8},{10,11... | collective-permute-start | bytes 20736008 | tf_op jit(solution)/shard_map/ppermute | solution.py:54
  411.4 65.5 %collective-permute-start.21 = (bf16[13568,256]{1,0:T(8,128)(2,1)S(1)}, bf16[13568,256]{1,0:T(8,128)(2,1)}, u32[]{:S(2)}, u32[]{:S(2)}) collective-permute-start(bf16[13568,256]{1,0:T(8,128)(2,1)S(1)} %bitcast.214), channel_id=1, source_target_pairs={{0,1},{1,0},{2,3},{3,2},{4,5},{5,4},{6,7},{7,6},{8,9},{9,8},{10,11... | collective-permute-start | bytes 20840456 | tf_op jit(solution)/shard_map/ppermute | solution.py:54
  411.8 10.3 copy-start.22
  414.7 40.2 %collective-permute-start.4 = (bf16[128,6784]{1,0:T(8,128)(2,1)S(1)}, bf16[128,6784]{1,0:T(8,128)(2,1)S(1)}, u32[]{:S(2)}, u32[]{:S(2)}) collective-permute-start(bf16[128,6784]{1,0:T(8,128)(2,1)S(1)} %slice.189), channel_id=1, source_target_pairs={{0,2},{2,0},{1,3},{3,1},{4,6},{6,4},{5,7},{7,5},{8,10},{10,8},{9,1... | collective-permute-start | bytes 5210120 | tf_op jit(solution)/shard_map/ppermute | solution.py:54
  418.1 40.0 %collective-permute-start.5 = (bf16[128,6784]{1,0:T(8,128)(2,1)S(1)}, bf16[128,6784]{1,0:T(8,128)(2,1)S(1)}, u32[]{:S(2)}, u32[]{:S(2)}) collective-permute-start(bf16[128,6784]{1,0:T(8,128)(2,1)S(1)} %slice.190), channel_id=1, source_target_pairs={{0,4},{4,0},{1,5},{5,1},{2,6},{6,2},{3,7},{7,3},{8,12},{12,8},{9,1... | collective-permute-start | bytes 5210120 | tf_op jit(solution)/shard_map/ppermute | solution.py:54
  455.0 16.1 %collective-permute-start.7 = (bf16[128,13568]{1,0:T(8,128)(2,1)}, bf16[128,13568]{1,0:T(8,128)(2,1)S(1)}, u32[]{:S(2)}, u32[]{:S(2)}) collective-permute-start(bf16[128,13568]{1,0:T(8,128)(2,1)} %collective-permute-done.2), channel_id=1, source_target_pairs={{0,1},{1,0},{2,3},{3,2},{4,5},{5,4},{6,7},{7,6},{8,9},{9,8},{10,11... | collective-permute-start | bytes 10420232 | tf_op jit(solution)/shard_map/ppermute | solution.py:54
  458.1 14.9 %collective-permute-start.8 = (bf16[128,13568]{1,0:T(8,128)(2,1)}, bf16[128,13568]{1,0:T(8,128)(2,1)}, u32[]{:S(2)}, u32[]{:S(2)}) collective-permute-start(bf16[128,13568]{1,0:T(8,128)(2,1)} %collective-permute-done.3), channel_id=1, source_target_pairs={{0,1},{1,0},{2,3},{3,2},{4,5},{5,4},{6,7},{7,6},{8,9},{9,8},{10,11... | collective-permute-start | bytes 10420232 | tf_op jit(solution)/shard_map/ppermute | solution.py:54
  459.7 29.8 %collective-permute-start.9 = (bf16[128,13568]{1,0:T(8,128)(2,1)S(1)}, bf16[128,13568]{1,0:T(8,128)(2,1)S(1)}, u32[]{:S(2)}, u32[]{:S(2)}) collective-permute-start(bf16[128,13568]{1,0:T(8,128)(2,1)S(1)} %pad_maximum_fusion.1), channel_id=1, source_target_pairs={{0,1},{1,0},{2,3},{3,2},{4,5},{5,4},{6,7},{7,6},{8,9},{9,8},{10,11... | collective-permute-start | bytes 10420232 | tf_op jit(solution)/shard_map/ppermute | solution.py:54
  506.3 25.6 %copy-start.11 = (f32[256,1024]{0,1:T(8,128)}, f32[256,1024]{0,1:T(8,128)S(1)}, u32[]{:S(2)}) copy-start(f32[256,1024]{0,1:T(8,128)S(1)} %dynamic-slice_dynamic-update-slice_fusion) | copy-start | bytes 3145732
  506.4 15.9 %copy-start.28 = (bf16[256,1024]{0,1:T(8,128)(2,1)}, bf16[256,1024]{0,1:T(8,128)(2,1)S(1)}, u32[]{:S(2)}) copy-start(bf16[256,1024]{0,1:T(8,128)(2,1)S(1)} %convert_element_type.245) | copy-start | bytes 1572868
  534.1 24.4 %slice-start = ((s8[16777216]{0:T(1024)(128)(4,1)}), s8[4194304]{0:T(1024)(128)(4,1)S(1)}, s32[]{:S(2)}) async-start(s8[16777216]{0:T(1024)(128)(4,1)} %bitcast.210), calls=%async_computation | async-start | bytes 8388608
  534.1 24.4 %slice-start.1 = ((s8[16777216]{0:T(1024)(128)(4,1)}), s8[4194304]{0:T(1024)(128)(4,1)S(1)}, s32[]{:S(2)}) async-start(s8[16777216]{0:T(1024)(128)(4,1)} %bitcast.210), calls=%async_computation.1 | async-start | bytes 8388608
  534.1 24.4 %slice-start.2 = ((s8[16777216]{0:T(1024)(128)(4,1)}), s8[4194304]{0:T(1024)(128)(4,1)S(1)}, s32[]{:S(2)}) async-start(s8[16777216]{0:T(1024)(128)(4,1)} %bitcast.210), calls=%async_computation.2 | async-start | bytes 8388608
  548.6 9.9 slice-start.3
  558.5 10.4 copy-start.6
  568.9 12.2 %slice-start.11 = ((s8[8388608]{0:T(1024)(128)(4,1)}), s8[4194304]{0:T(1024)(128)(4,1)S(1)}, s32[]{:S(2)}) async-start(s8[8388608]{0:T(1024)(128)(4,1)} %bitcast.289), calls=%async_computation.11 | async-start | bytes 8388608
  579.0 58.7 %collective-permute-start.20 = (bf16[256,1024]{0,1:T(8,128)(2,1)S(1)}, bf16[256,1024]{0,1:T(8,128)(2,1)}, u32[]{:S(2)}, u32[]{:S(2)}) collective-permute-start(bf16[256,1024]{0,1:T(8,128)(2,1)S(1)} %copy-done.29), channel_id=1, source_target_pairs={{0,1},{1,0},{2,3},{3,2},{4,5},{5,4},{6,7},{7,6},{8,9},{9,8},{10,11... | collective-permute-start | bytes 1572872 | tf_op jit(solution)/shard_map/ppermute | solution.py:54
  579.0 65.2 %collective-permute-start.18 = (bf16[256,1024]{0,1:T(8,128)(2,1)S(1)}, bf16[256,1024]{0,1:T(8,128)(2,1)}, u32[]{:S(2)}, u32[]{:S(2)}) collective-permute-start(bf16[256,1024]{0,1:T(8,128)(2,1)S(1)} %fusion.65), channel_id=1, source_target_pairs={{0,1},{1,0},{2,3},{3,2},{4,5},{5,4},{6,7},{7,6},{8,9},{9,8},{10,11... | collective-permute-start | bytes 1572872 | tf_op jit(solution)/shard_map/ppermute | solution.py:54
  588.6 33.9 %collective-permute-start.28 = (bf16[256,512]{0,1:T(8,128)(2,1)}, bf16[256,512]{0,1:T(8,128)(2,1)}, u32[]{:S(2)}, u32[]{:S(2)}) collective-permute-start(bf16[256,512]{0,1:T(8,128)(2,1)} %pad_maximum_fusion.14), channel_id=1, source_target_pairs={{0,1},{1,0},{2,3},{3,2},{4,5},{5,4},{6,7},{7,6},{8,9},{9,8},{10,11... | collective-permute-start | bytes 786440 | tf_op jit(solution)/shard_map/ppermute | solution.py:54
  600.0 115.3 %collective-permute-start.10 = (bf16[2,256,2048]{1,2,0:T(8,128)(2,1)}, bf16[2,256,2048]{1,2,0:T(8,128)(2,1)}, u32[]{:S(2)}, u32[]{:S(2)}) collective-permute-start(bf16[2,256,2048]{1,2,0:T(8,128)(2,1)} %dynamic-slice_bitcast_fusion), channel_id=1, source_target_pairs={{0,1},{1,0},{2,3},{3,2},{4,5},{5,4},{6,7},{7,6},{8,9},{9,8},{10,11... | collective-permute-start | bytes 6291464 | tf_op jit(solution)/shard_map/ppermute | solution.py:54
  602.7 43.7 %collective-permute-start.15 = (bf16[256,2048]{1,0:T(8,128)(2,1)}, bf16[256,2048]{1,0:T(8,128)(2,1)}, u32[]{:S(2)}, u32[]{:S(2)}) collective-permute-start(bf16[256,2048]{1,0:T(8,128)(2,1)} %pad_maximum_fusion.6), channel_id=1, source_target_pairs={{0,1},{1,0},{2,3},{3,2},{4,5},{5,4},{6,7},{7,6},{8,9},{9,8},{10,11... | collective-permute-start | bytes 3145736 | tf_op jit(solution)/shard_map/ppermute | solution.py:54
  618.8 12.2 %slice-start.6 = ((s8[13828096]{0:T(1024)(128)(4,1)}), s8[4194304]{0:T(1024)(128)(4,1)S(1)}, s32[]{:S(2)}) async-start(s8[13828096]{0:T(1024)(128)(4,1)} %bitcast.243), calls=%async_computation.6 | async-start | bytes 8388608
  618.8 12.2 %slice-start.7 = ((s8[13828096]{0:T(1024)(128)(4,1)}), s8[4194304]{0:T(1024)(128)(4,1)S(1)}, s32[]{:S(2)}) async-start(s8[13828096]{0:T(1024)(128)(4,1)} %bitcast.243), calls=%async_computation.7 | async-start | bytes 8388608
  624.3 15.1 %copy-start.38 = (bf16[512,512]{0,1:T(8,128)(2,1)}, bf16[512,512]{0,1:T(8,128)(2,1)S(1)}, u32[]{:S(2)}) copy-start(bf16[512,512]{0,1:T(8,128)(2,1)S(1)} %pad_maximum_fusion.9) | copy-start | bytes 1572868
  634.2 40.7 %collective-permute-start.37 = (bf16[128,6716]{0,1:T(8,128)(2,1)}, bf16[128,6716]{0,1:T(8,128)(2,1)}, u32[]{:S(2)}, u32[]{:S(2)}) collective-permute-start(bf16[128,6716]{0,1:T(8,128)(2,1)} %convolution_convert_fusion), channel_id=1, source_target_pairs={{0,2},{2,0},{1,3},{3,1},{4,6},{6,4},{5,7},{7,5},{8,10},{10,8},{9,1... | collective-permute-start | bytes 5157896 | tf_op jit(solution)/shard_map/ppermute | solution.py:54
  637.7 73.2 %collective-permute-start.36 = (bf16[128,6716]{0,1:T(8,128)(2,1)}, bf16[128,6716]{0,1:T(8,128)(2,1)}, u32[]{:S(2)}, u32[]{:S(2)}) collective-permute-start(bf16[128,6716]{0,1:T(8,128)(2,1)} %convolution_convert_fusion.1), channel_id=1, source_target_pairs={{0,2},{2,0},{1,3},{3,1},{4,6},{6,4},{5,7},{7,5},{8,10},{10,8},{9,1... | collective-permute-start | bytes 5157896 | tf_op jit(solution)/shard_map/ppermute | solution.py:54
  644.2 82.4 %collective-permute-start.19 = (bf16[256,4096]{1,0:T(8,128)(2,1)}, bf16[256,4096]{1,0:T(8,128)(2,1)}, u32[]{:S(2)}, u32[]{:S(2)}) collective-permute-start(bf16[256,4096]{1,0:T(8,128)(2,1)} %get-tuple-element.66), channel_id=1, source_target_pairs={{0,1},{1,0},{2,3},{3,2},{4,5},{5,4},{6,7},{7,6},{8,9},{9,8},{10,11... | collective-permute-start | bytes 6291464 | tf_op jit(solution)/shard_map/ppermute | solution.py:54
  646.4 73.0 %collective-permute-start.31 = (bf16[128,6784]{1,0:T(8,128)(2,1)}, bf16[128,6784]{1,0:T(8,128)(2,1)}, u32[]{:S(2)}, u32[]{:S(2)}) collective-permute-start(bf16[128,6784]{1,0:T(8,128)(2,1)} %convolution_convert_fusion.2), channel_id=1, source_target_pairs={{0,4},{4,0},{1,5},{5,1},{2,6},{6,2},{3,7},{7,3},{8,12},{12,8},{9,1... | collective-permute-start | bytes 5210120 | tf_op jit(solution)/shard_map/ppermute | solution.py:54
  674.9 150.3 %collective-permute-start.30 = (bf16[128,6784]{1,0:T(8,128)(2,1)}, bf16[128,6784]{1,0:T(8,128)(2,1)}, u32[]{:S(2)}, u32[]{:S(2)}) collective-permute-start(bf16[128,6784]{1,0:T(8,128)(2,1)} %convolution_convert_fusion.3), channel_id=1, source_target_pairs={{0,4},{4,0},{1,5},{5,1},{2,6},{6,2},{3,7},{7,3},{8,12},{12,8},{9,1... | collective-permute-start | bytes 5210120 | tf_op jit(solution)/shard_map/ppermute | solution.py:54
  710.9 101.1 %collective-permute-start.38 = (bf16[128,6716]{0,1:T(8,128)(2,1)}, bf16[128,6716]{0,1:T(8,128)(2,1)}, u32[]{:S(2)}, u32[]{:S(2)}) collective-permute-start(bf16[128,6716]{0,1:T(8,128)(2,1)} %fusion.18), channel_id=1, source_target_pairs={{0,4},{4,0},{1,5},{5,1},{2,6},{6,2},{3,7},{7,3},{8,12},{12,8},{9,1... | collective-permute-start | bytes 5157896 | tf_op jit(solution)/shard_map/ppermute | solution.py:54
  719.2 24.3 %collective-permute-start.11 = (bf16[256,2048]{0,1:T(8,128)(2,1)}, bf16[256,2048]{0,1:T(8,128)(2,1)}, u32[]{:S(2)}, u32[]{:S(2)}) collective-permute-start(bf16[256,2048]{0,1:T(8,128)(2,1)} %dynamic-slice_bitcast_fusion.1), channel_id=1, source_target_pairs={{0,2},{2,0},{1,3},{3,1},{4,6},{6,4},{5,7},{7,5},{8,10},{10,8},{9,1... | collective-permute-start | bytes 3145736 | tf_op jit(solution)/shard_map/ppermute | solution.py:54
  753.7 24.2 %collective-permute-start.22 = (bf16[512,4]{0,1:T(4,128)(2,1)S(1)}, bf16[512,4]{0,1:T(4,128)(2,1)S(1)}, u32[]{:S(2)}, u32[]{:S(2)}) collective-permute-start(bf16[512,4]{0,1:T(4,128)(2,1)S(1)} %pad_maximum_fusion.16), channel_id=1, source_target_pairs={{0,1},{1,0},{2,3},{3,2},{4,5},{5,4},{6,7},{7,6},{8,9},{9,8},{10,11... | collective-permute-start | bytes 12296 | tf_op jit(solution)/shard_map/ppermute | solution.py:54
  755.6 24.1 %copy-start.17 = (bf16[256,2048]{0,1:T(8,128)(2,1)S(1)}, bf16[256,2048]{0,1:T(8,128)(2,1)}, u32[]{:S(2)}) copy-start(bf16[256,2048]{0,1:T(8,128)(2,1)} %copy-done.16) | copy-start | bytes 3145732
  755.6 24.1 %copy-start.24 = (bf16[16,64,256]{2,1,0:T(8,128)(2,1)S(1)}, bf16[16,64,256]{2,1,0:T(8,128)(2,1)}, u32[]{:S(2)}) copy-start(bf16[16,64,256]{2,1,0:T(8,128)(2,1)} %fusion.52) | copy-start | bytes 1572868
  755.6 26.6 %copy-start.33 = (bf16[256,1024]{0,1:T(8,128)(2,1)S(1)}, bf16[256,1024]{0,1:T(8,128)(2,1)}, u32[]{:S(2)}) copy-start(bf16[256,1024]{0,1:T(8,128)(2,1)} %add_convert_fusion.1) | copy-start | bytes 1572868
  777.9 3.7 collective-permute-start.23
  781.5 3.6 collective-permute-start.24
  785.2 21.5 %collective-permute-start.25 = (bf16[32,4]{0,1:T(4,128)(2,1)S(1)}, bf16[32,4]{0,1:T(4,128)(2,1)S(1)}, u32[]{:S(2)}, u32[]{:S(2)}) collective-permute-start(bf16[32,4]{0,1:T(4,128)(2,1)S(1)} %get-tuple-element.166), channel_id=1, source_target_pairs={{0,8},{8,16},{16,24},{24,0},{1,9},{9,17},{17,25},{25,1},{2,10},{10... | collective-permute-start | bytes 776 | tf_op jit(solution)/shard_map/ppermute | solution.py:415
  802.3 5.1 collective-permute-start.26
  805.7 3.6 collective-permute-start.27
  806.7 37.2 %collective-permute-start.32 = (bf16[128,6784]{1,0:T(8,128)(2,1)}, bf16[128,6784]{1,0:T(8,128)(2,1)}, u32[]{:S(2)}, u32[]{:S(2)}) collective-permute-start(bf16[128,6784]{1,0:T(8,128)(2,1)} %fusion.17), channel_id=1, source_target_pairs={{0,2},{2,0},{1,3},{3,1},{4,6},{6,4},{5,7},{7,5},{8,10},{10,8},{9,1... | collective-permute-start | bytes 5210120 | tf_op jit(solution)/shard_map/ppermute | solution.py:54
  807.3 87.3 %collective-permute-start.17 = (bf16[256,3072]{0,1:T(8,128)(2,1)}, bf16[256,3072]{0,1:T(8,128)(2,1)}, u32[]{:S(2)}, u32[]{:S(2)}) collective-permute-start(bf16[256,3072]{0,1:T(8,128)(2,1)} %pad_maximum_fusion.4), channel_id=1, source_target_pairs={{0,1},{1,0},{2,3},{3,2},{4,5},{5,4},{6,7},{7,6},{8,9},{9,8},{10,11... | collective-permute-start | bytes 4718600 | tf_op jit(solution)/shard_map/ppermute | solution.py:54
  809.3 1.8 collective-permute-start.16
  822.3 29.3 %collective-permute-start.39 = (bf16[32,6716]{1,0:T(8,128)(2,1)S(1)}, bf16[32,6716]{1,0:T(8,128)(2,1)S(1)}, u32[]{:S(2)}, u32[]{:S(2)}) collective-permute-start(bf16[32,6716]{1,0:T(8,128)(2,1)S(1)} %get-tuple-element.105), channel_id=1, source_target_pairs={{0,8},{8,16},{16,24},{24,0},{1,9},{9,17},{17,25},{25,1},{2,10},{10... | collective-permute-start | bytes 1289480 | tf_op jit(solution)/shard_map/ppermute | solution.py:415
  823.5 32.8 %collective-permute-start.40 = (bf16[32,6716]{1,0:T(8,128)(2,1)S(1)}, bf16[32,6716]{1,0:T(8,128)(2,1)S(1)}, u32[]{:S(2)}, u32[]{:S(2)}) collective-permute-start(bf16[32,6716]{1,0:T(8,128)(2,1)S(1)} %get-tuple-element.107), channel_id=1, source_target_pairs={{0,16},{8,24},{16,0},{24,8},{1,17},{9,25},{17,1},{25,9},{2,18},{10... | collective-permute-start | bytes 1289480 | tf_op jit(solution)/shard_map/ppermute | solution.py:415
  825.3 55.2 %collective-permute-start.41 = (bf16[32,6716]{1,0:T(8,128)(2,1)S(1)}, bf16[32,6716]{1,0:T(8,128)(2,1)S(1)}, u32[]{:S(2)}, u32[]{:S(2)}) collective-permute-start(bf16[32,6716]{1,0:T(8,128)(2,1)S(1)} %get-tuple-element.106), channel_id=1, source_target_pairs={{0,24},{8,0},{16,8},{24,16},{1,25},{9,1},{17,9},{25,17},{2,26},{10... | collective-permute-start | bytes 1289480 | tf_op jit(solution)/shard_map/ppermute | solution.py:415
  850.4 30.3 %collective-permute-start.33 = (bf16[32,6784]{1,0:T(8,128)(2,1)S(1)}, bf16[32,6784]{1,0:T(8,128)(2,1)S(1)}, u32[]{:S(2)}, u32[]{:S(2)}) collective-permute-start(bf16[32,6784]{1,0:T(8,128)(2,1)S(1)} %get-tuple-element.102), channel_id=1, source_target_pairs={{0,8},{8,16},{16,24},{24,0},{1,9},{9,17},{17,25},{25,1},{2,10},{10... | collective-permute-start | bytes 1302536 | tf_op jit(solution)/shard_map/ppermute | solution.py:415
  851.6 40.6 %collective-permute-start.34 = (bf16[32,6784]{1,0:T(8,128)(2,1)S(1)}, bf16[32,6784]{1,0:T(8,128)(2,1)S(1)}, u32[]{:S(2)}, u32[]{:S(2)}) collective-permute-start(bf16[32,6784]{1,0:T(8,128)(2,1)S(1)} %get-tuple-element.104), channel_id=1, source_target_pairs={{0,16},{8,24},{16,0},{24,8},{1,17},{9,25},{17,1},{25,9},{2,18},{10... | collective-permute-start | bytes 1302536 | tf_op jit(solution)/shard_map/ppermute | solution.py:415
  856.3 36.8 %collective-permute-start.35 = (bf16[32,6784]{1,0:T(8,128)(2,1)S(1)}, bf16[32,6784]{1,0:T(8,128)(2,1)S(1)}, u32[]{:S(2)}, u32[]{:S(2)}) collective-permute-start(bf16[32,6784]{1,0:T(8,128)(2,1)S(1)} %get-tuple-element.103), channel_id=1, source_target_pairs={{0,24},{8,0},{16,8},{24,16},{1,25},{9,1},{17,9},{25,17},{2,26},{10... | collective-permute-start | bytes 1302536 | tf_op jit(solution)/shard_map/ppermute | solution.py:415
  (54 other events, 246.4 us)

commit v4 on v3

--- a/solution.py
+++ b/solution.py
@@ -12,6 +12,7 @@
 HEADS = 16
 MESH = pl.DeviceIdType.MESH
 RING = 8
+CHUNK = 256
 
 
 eps = 1e-05
@@ -215,27 +216,67 @@
     )(*shards)
 
 
-def scatter_kernel(n_h, n, n_first, run, lefts, rights, more, out, right_buf, own, s1, r1, s2, r2, s3, r3,
-                   load_sem, send1, recv1, send2, recv2, send3, recv3):
+def scatter_kernel(n_h, sections, run, n_weights, with_sum, *refs):
+    lefts, vector = refs[:2]
+    n_sections = len(sections)
+    rights = refs[2 : 2 + 2 * n_sections]
+    weights = refs[2 + 2 * n_sections : 2 + 2 * n_sections + n_weights]
+    rest = refs[2 + 2 * n_sections + n_weights :]
+    out, product = rest[:2]
+    total_out = rest[2] if with_sum else None
+    (right_buf, weight_buf, product_buf, own, s1, r1, s2, r2, s3, r3, load_sem, weight_sem, product_sem,
+     send1, recv1, send2, recv2, send3, recv3) = rest[3 if with_sum else 2 :]
     h, x, y = (lax.axis_index(name) for name in ("h", "x", "y"))
     to_x, to_y = {"x": 1 - x}, {"y": 1 - y}
     w = s3.shape[1]
     rows = w // n_h
     f32, b16 = jnp.float32, jnp.bfloat16
+    cells = vector.shape[0]
+    starts = [sum(sections[:k]) for k in range(n_sections)]
+    n = sum(sections)
+    begin = starts[-1]
     greet([{"h": lax.rem(h + d, n_h)} for d in range(1, n_h)] + [to_x, to_y])
 
-    def load(i, source, k):
+    def chunk_of(k):
+        return pl.ds(pl.multiple_of(k * CHUNK, CHUNK), CHUNK)
+
+    def loads(i, section, k):
         slot = lax.rem(i, 3)
-        return pltpu.make_async_copy(source.at[k], right_buf.at[slot], load_sem.at[slot])
-
-    def start_load(i):
-        @pl.when(i < n_first)
-        def _():
-            load(i, rights, i).start()
-
-        @pl.when((i >= n_first) & (i < n))
-        def _():
-            load(i, more, i - n_first).start()
+        return [
+            pltpu.make_async_copy(
+                rights[2 * section + half].at[chunk_of(k)],
+                right_buf.at[slot, :, pl.ds(half * cells, cells)],
+                load_sem.at[slot, half],
+            )
+            for half in (0, 1)
+        ]
+
+    def weight_loads(k):
+        slot = lax.rem(k, 3)
+        size = weights[0].shape[0]
+        return [
+            pltpu.make_async_copy(
+                weight.at[:, chunk_of(k)],
+                weight_buf.at[slot, pl.ds(part * size, size)],
+                weight_sem.at[slot, part],
+            )
+            for part, weight in enumerate(weights)
+        ]
+
+    def start_loads(i):
+        for section, (start, count) in enumerate(zip(starts, sections)):
+
+            @pl.when((i >= start) & (i < start + count))
+            def _(section=section, start=start):
+                for copy in loads(i, section, i - start):
+                    copy.start()
+                if section == n_sections - 1:
+                    for copy in weight_loads(i - start):
+                        copy.start()
+
+    def product_store(k):
+        slot = lax.rem(k, 2)
+        return pltpu.make_async_copy(product_buf.at[slot], product.at[chunk_of(k)], product_sem.at[slot])
 
     def hop(i, source, target, send_sem, recv_sem, to):
         slot = lax.rem(i, RING)
@@ -261,17 +302,17 @@
 
     def multiply(i, odd):
         slot = lax.rem(i, RING)
-        load(i, rights, 0).wait()
-        pair = i // 2
-        left = lefts[pair - (pair + 1024 - run) // 1024 * (pair - run)]
-        right = right_buf[lax.rem(i, 3)]
-        start_load(i + 2)
+        for copy in loads(i, 0, 0):
+            copy.wait()
+        two = i // 4
+        left = lefts[two - (two + 1024 - run) // 1024 * (two - run)]
+        right = right_buf.at[lax.rem(i, 3)]
 
         @pl.when(i >= RING)
         def _():
             first(i - RING, odd).wait_send()
 
-        part = lax.dot_general(left, right, (((1,), (1,)), ((), ())), preferred_element_type=f32)
+        part = lax.dot_general(left, right[...], (((1,), (1,)), ((), ())), preferred_element_type=f32)
         own[slot, :w] = part[:w]
         if odd:
             own[slot, w:] = part[2 * w : 3 * w]
@@ -282,6 +323,39 @@
             s1[slot] = part[2 * w :].astype(b16)
         first(i, odd).start()
 
+        def beside(k):
+            for copy in weight_loads(k):
+                copy.wait()
+            weight = weight_buf[lax.rem(k, 3)]
+
+            @pl.when(k >= 2)
+            def _():
+                product_store(k - 2).wait()
+
+            value = jnp.dot(vector[...], weight, preferred_element_type=f32)
+            product_buf[lax.rem(k, 2)] = value.T.astype(product_buf.dtype)
+            product_store(k).start()
+            if with_sum:
+                term = jnp.dot(weight, right[:, :cells], preferred_element_type=f32)
+
+                @pl.when(k == 0)
+                def _():
+                    total_out[...] = term
+
+                @pl.when(k > 0)
+                def _():
+                    total_out[...] += term
+
+        if begin == 0:
+            beside(i)
+        else:
+
+            @pl.when(i >= begin)
+            def _():
+                beside(i - begin)
+
+        start_loads(i + 2)
+
     def pass_on(i, odd):
         slot = lax.rem(i, RING)
         first(i, odd).wait_recv()
@@ -319,8 +393,8 @@
             total = total + r3[i, d - 1].astype(f32)
         out[i] = total
 
-    start_load(jnp.int32(0))
-    start_load(jnp.int32(1))
+    start_loads(jnp.int32(0))
+    start_loads(jnp.int32(1))
     pairs = (n + 1) // 2
 
     def step(p, carry):
@@ -340,37 +414,50 @@
         second(i, i % 2).wait_send()
         for d in range(1, n_h):
             third(i, d).wait_send()
-
-
-def scatter_all(lefts, rights, more, collective_id):
-    n_first, m, cells = rights.shape
-    n = n_first + more.shape[0]
+    for k in range(max(sections[-1] - 2, 0), sections[-1]):
+        product_store(k).wait()
+
+
+def scatter_all(lefts, rights, vector, weights, product_type, with_sum, collective_id):
+    sections = [own.shape[0] // CHUNK for own, _ in rights]
+    n, cells = sum(sections), vector.shape[0]
+    features = vector.shape[1]
     w = lefts.shape[1] // 4
     n_h = lax.axis_size("h")
     rows = w // n_h
     inner_h = n_h if rows % 16 == 0 else 1
-    dma, bf16 = pltpu.SemaphoreType.DMA, jnp.bfloat16
+    dma, bf16, f32 = pltpu.SemaphoreType.DMA, jnp.bfloat16, jnp.float32
     vmem, hbm = pl.BlockSpec(memory_space=pltpu.VMEM), pl.BlockSpec(memory_space=pl.ANY)
     others = max(inner_h - 1, 1)
-    part = pl.pallas_call(
-        functools.partial(scatter_kernel, inner_h, n, n_first, lefts.shape[0] - 1),
-        out_shape=(
-            jax.ShapeDtypeStruct((n, rows, m), jnp.float32)
-            if inner_h > 1
-            else jax.ShapeDtypeStruct((n, w, m), bf16)
+    part_shape = jax.ShapeDtypeStruct((n, rows, CHUNK), f32)
+    if inner_h == 1:
+        part_shape = jax.ShapeDtypeStruct((n, w, CHUNK), bf16)
+    out_shape = [part_shape, jax.ShapeDtypeStruct((sections[-1] * CHUNK, cells), product_type)]
+    out_specs = [vmem, hbm]
+    if with_sum:
+        out_shape.append(jax.ShapeDtypeStruct((features, cells), f32))
+        out_specs.append(vmem)
+    part, *more = pl.pallas_call(
+        functools.partial(
+            scatter_kernel, inner_h, sections, lefts.shape[0] - 1, len(weights), with_sum
         ),
-        in_specs=[vmem, hbm, hbm],
-        out_specs=vmem,
+        out_shape=out_shape,
+        in_specs=[vmem, vmem] + [hbm] * (2 * len(rights) + len(weights)),
+        out_specs=out_specs,
         scratch_shapes=[
-            pltpu.VMEM((3, m, cells), bf16),
-            pltpu.VMEM((RING, 2 * w, m), jnp.float32),
-            pltpu.VMEM((RING, 2 * w, m), bf16),
-            pltpu.VMEM((n, 2 * w, m), bf16),
-            pltpu.VMEM((RING, w, m), bf16),
-            pltpu.VMEM((n, w, m), bf16),
-            pltpu.VMEM((RING, w, m), bf16),
-            pltpu.VMEM((n, others, w // inner_h, m), bf16),
-            dma((3,)),
+            pltpu.VMEM((3, CHUNK, 2 * cells), bf16),
+            pltpu.VMEM((3, features, CHUNK), bf16),
+            pltpu.VMEM((2, CHUNK, cells), product_type),
+            pltpu.VMEM((RING, 2 * w, CHUNK), f32),
+            pltpu.VMEM((RING, 2 * w, CHUNK), bf16),
+            pltpu.VMEM((n, 2 * w, CHUNK), bf16),
+            pltpu.VMEM((RING, w, CHUNK), bf16),
+            pltpu.VMEM((n, w, CHUNK), bf16),
+            pltpu.VMEM((RING, w, CHUNK), bf16),
+            pltpu.VMEM((n, others, w // inner_h, CHUNK), bf16),
+            dma((3, 2)),
+            dma((3, len(weights))),
+            dma((2,)),
             dma((RING,)),
             dma((n,)),
             dma((RING,)),
@@ -381,22 +468,19 @@
         compiler_params=pltpu.CompilerParams(
             collective_id=collective_id, has_side_effects=True, vmem_limit_bytes=60 * 2**20
         ),
-    )(lefts, rights, more)
-    if inner_h > 1:
-        return part
-    return lax.psum_scatter(part, "h", scatter_dimension=1, tiled=True).astype(jnp.float32)
-
-
-def gather_dec(own):
-    by_x, by_y = swap(own, "x"), swap(own, "y")
+    )(lefts, vector, *(half for pair in rights for half in pair), *weights)
+    if inner_h == 1:
+        part = lax.psum_scatter(part, "h", scatter_dimension=1, tiled=True).astype(f32)
+    return part, *more
+
+
+def gather_dec(own, after):
+    by_x = swap(own, "x")
+    by_y = swap(lax.optimization_barrier((own, after))[0], "y")
     middle = own.shape[1] // 256 * 128
     far = [swap(by_x[:, :middle], "y"), swap(by_y[:, middle:], "x")]
     four = [own, by_y, by_x, jnp.concatenate(far, axis=1)]
-    return jnp.concatenate(four + [swap(part, "c") for part in four], axis=0)
-
-
-def with_other_core(value):
-    return jnp.concatenate([value, swap(value, "c")], axis=0)
+    return four + [swap(part, "c") for part in four]
 
 
 def own_half(left):
@@ -416,24 +500,6 @@
     return total
 
 
-def scatter(left, right, first, second):
-    w = left.shape[1] // 4
-    near, by_y, by_x, far = (left[:, k * w : (k + 1) * w] for k in range(4))
-    one, two = (by_x, by_y) if first == "x" else (by_y, by_x)
-    got_far = swap(contract_rows(far, right).astype(jnp.bfloat16), first).astype(jnp.float32)
-    got_one = swap(contract_rows(one, right).astype(jnp.bfloat16), first).astype(jnp.float32)
-    got_two = swap((contract_rows(two, right) + got_far).astype(jnp.bfloat16), second)
-    part = contract_rows(near, right) + got_one + got_two.astype(jnp.float32)
-    return sum_over_h(part.astype(jnp.bfloat16))
-
-
-def scatter_columns(left, right):
-    cut = -(-right.shape[1] // 256) * 128
-    return jnp.concatenate(
-        [scatter(left, right[:, :cut], "x", "y"), scatter(left, right[:, cut:], "y", "x")], axis=1
-    ).T
-
-
 def scatter_vectors(part):
     half = part.shape[0] // 2
     part = part[:half] + swap(part[half:].astype(jnp.bfloat16), "c").astype(jnp.float32)
@@ -445,7 +511,8 @@
 
 def gather_group(mine):
     at_y, at_c = lax.axis_index("y"), lax.axis_index("c")
-    pair = jnp.stack([mine, swap(mine, "y")])
+    by_y = swap(mine, "y")
+    pair = jnp.stack([mine, by_y])
     both = jnp.stack([pair, swap(pair, "c")])
     order = [
         lax.dynamic_index_in_dim(
@@ -454,7 +521,7 @@
         for y in range(2)
         for c in range(2)
     ]
-    return jnp.concatenate(order, axis=0)
+    return jnp.concatenate(order, axis=0), by_y
 
 
 def scatter_group(rows_all):
@@ -468,11 +535,6 @@
     return keep + swap(send, "y").astype(jnp.float32)
 
 
-def in_chunks(right):
-    n = -(-right.shape[0] // 512) * 512
-    return jnp.pad(right, ((0, n - right.shape[0]), (0, 0))).reshape(n // 512, 512, -1)
-
-
 def left_of(left, pieces):
     left = own_half(relative(left, 1)).T
     n_h = lax.axis_size("h")
@@ -480,8 +542,12 @@
     return left.transpose(2, 0, 1, 3, 4).reshape(pieces, -1, left.shape[-1])
 
 
-def right_of(right):
-    return in_chunks(with_other_core(right).T)
+def both_cores(right):
+    return right, swap(right, "c")
+
+
+def columns_of(chunks):
+    return chunks.transpose(1, 0, 2).reshape(chunks.shape[1], -1)
 
 
 def on_device(
@@ -514,7 +580,9 @@
     counts_f = counts.astype(jnp.float32)
     xb = jnp.pad(counts.T, ((0, padded - genes), (0, 0))).astype(jnp.float32)
     xb = jnp.log1p(xb * scale[None, :]).astype(jnp.bfloat16)
-    xb_both = in_chunks(jnp.concatenate([xb, swap(xb, "c")], axis=1))
+    xb_pair = both_cores(xb)
+    cot = jnp.pad(cotangent.T, ((0, padded - genes), (0, 0)))
+    cot_pair = both_cores(cot)
     pe = by_owner(positions(coords, width), 1)
     ends = jnp.cumsum(lengths[0])
     place = jnp.arange(slots, dtype=jnp.int32)
@@ -541,7 +609,6 @@
     enc_all, qkv_all, out_all, up_all, down_all = (
         w.reshape(-1, w.shape[-1]) for w in gathered[:5]
     )
-    dec_all = gather_dec(gathered[5])
     vectors = qkv_all[:, 3 * width :].astype(jnp.float32).T
     qkv_all = qkv_all[:, : 3 * width]
     g1f, b1f, g2f, b2f = vectors[0], vectors[1], vectors[2], vectors[3]
@@ -549,7 +616,8 @@
     a1 = layer_norm(h0, g1f, b1f).astype(jnp.bfloat16)
     qkv = matmul(a1, qkv_all).astype(jnp.bfloat16)
     query = qkv[:, :width].reshape(rows, heads, head_width)
-    kv_all = gather_group(qkv[:, width:])
+    kv_all, arrived = gather_group(qkv[:, width:])
+    dec_parts = gather_dec(gathered[5], arrived)
     keys = kv_all[:, :width].reshape(slots, heads, head_width)
     values = kv_all[:, width:].reshape(slots, heads, head_width)
 
@@ -573,10 +641,14 @@
     hidden = matmul(a2, up_all)
     act = jax.nn.gelu(hidden, approximate=False).astype(jnp.bfloat16)
     h2 = h1 + matmul(act, down_all)
-    hb_rel = relative(h2.astype(jnp.bfloat16), 1)
-    logits = matmul(hb_rel, dec_all).astype(jnp.bfloat16)[:, :genes]
-    grad_dec = scatter_columns(own_half(hb_rel), with_other_core(cotangent))
-    dh2 = relative(contract_cols(jnp.pad(cotangent, pad), dec_all), 1)
+    hb = h2.astype(jnp.bfloat16)
+    grad_dec, logits, dh2 = scatter_all(
+        left_of(hb, 1), [cot_pair], relative(hb, 1), dec_parts, jnp.bfloat16, True, 1
+    )
+    own_rows = grad_dec.shape[1]
+    grad_dec = columns_of(grad_dec)[:, :genes].T
+    logits = logits[:genes].T
+    dh2 = relative(dh2, 0).T
     dfb = dh2.astype(jnp.bfloat16)
     d_act = contract_cols(dfb, down_all)
     slope = jax.vjp(lambda v: jax.nn.gelu(v, approximate=False), hidden)[1](d_act)[0]
@@ -613,26 +685,32 @@
     )
     dh0b = (dh1 + dh0_norm).astype(jnp.bfloat16)
 
-    lefts = [left_of(a1, 1)] * 3 + [left_of(attended_b, 1)] + [left_of(a2, 1)] * 4
-    lefts += [left_of(act, act.shape[1] // width), left_of(dh0b, 1)]
-    rights = [right_of(d_qkv), right_of(dab), right_of(d_hidden)] + [right_of(dfb)] * 4
-    grads = scatter_all(
-        jnp.concatenate(lefts, axis=0), jnp.concatenate(rights, axis=0), xb_both, 1
-    )
-    own_rows, m = grads.shape[1:]
+    lefts = [left_of(a2, 1)] * 4 + [left_of(act, act.shape[1] // width)]
+    lefts += [left_of(attended_b, 1)] + [left_of(a1, 1)] * 3 + [left_of(dh0b, 1)]
+    rights = [d_hidden.T] + [dfb.T] * 4 + [dab.T]
+    grads, d_xb = scatter_all(
+        jnp.concatenate(lefts, axis=0),
+        [both_cores(jnp.concatenate(rights, axis=0)), both_cores(d_qkv.T), xb_pair],
+        dh0b,
+        [enc_all],
+        jnp.float32,
+        False,
+        2,
+    )
     ends = [0]
-    for columns in (3 * width, width, 4 * width, 4 * width):
-        ends.append(ends[-1] + columns // m)
-    grad_qkv, grad_out, grad_up, grad_down, grad_enc = (
+    for columns in (4 * width, 4 * width, width, 3 * width):
+        ends.append(ends[-1] + columns // CHUNK)
+    grad_up, grad_down, grad_out, grad_qkv, grad_enc = (
         grads[low:high] for low, high in zip(ends, ends[1:] + [grads.shape[0]])
     )
-    grad_qkv, grad_out, grad_up, grad_enc = (
-        g.transpose(1, 0, 2).reshape(own_rows, -1) for g in (grad_qkv, grad_out, grad_up, grad_enc)
-    )
-    grad_down = grad_down.reshape(4, -1, own_rows, m).transpose(0, 2, 1, 3).reshape(4 * own_rows, -1)
+    grad_up, grad_out, grad_qkv, grad_enc = (
+        columns_of(g) for g in (grad_up, grad_out, grad_qkv, grad_enc)
+    )
+    grad_down = grad_down.reshape(4, -1, own_rows, CHUNK).transpose(0, 2, 1, 3)
+    grad_down = grad_down.reshape(4 * own_rows, -1)
     grad_out, grad_up, grad_down = (from_owner(g, 1) for g in (grad_out, grad_up, grad_down))
     grad_enc = grad_enc[:, :genes].T
-    d_xb = matmul(dh0b, enc_all)[:, :genes]
+    d_xb = d_xb[:genes].T
     counts_grad = d_xb * scale[:, None] / (1.0 + counts_f * scale[:, None])
     return (
         logits,

time: 1170 us -> 1030 us (0.88)
  Pallas kernels: 497 us -> 637 us
  matrix products: 204 us -> 106 us
  waiting for transfers between devices: 175 us -> 107 us
  starting transfers between devices: 70.7 us -> 14.2 us
  local copies, waits for them, and re-layouts: 142 us -> 99.1 us
    pallas_call x1 -> x2, Pallas kernels: 244 us -> 384 us  [scatter_all(): pl.pallas_call(functools.partial(scatter_kernel, inner_h, sections, lefts...]
    ppermute x33 -> x25, waiting for transfers between devices: 159 us -> 102 us  [swap(): return lax.ppermute(value, axis, [(0, 1), (1, 0)])]
    ppermute x9 -> x3, starting transfers between devices: 56 us -> 2.05 us  [sum_over_h(): total = total + lax.ppermute(send, 'h', ring).astype(jnp.float32)]
    dot_general x8 -> x0, matrix products: 42.9 us -> none  [contract_rows(): lax.dot_general(left, right, (((0,), (0,)), ((), ())), preferred_element_...]
    dot_general x6 -> x4, matrix products: 54.7 us -> 27.5 us  [matmul(): return jnp.dot(left, right, preferred_element_type=jnp.float32)]
    unnamed x186 -> x189, local copies, waits for them, and re-layouts: 58.8 us -> 31.7 us
    concatenate x7 -> x2, other arithmetic: 19.6 us -> 1.57 us  [the longest x1 0.97 us: on_device(): jnp.concatenate(rights, axis=0)]
    dot_general x6 -> x5, matrix products: 63.2 us -> 46.8 us  [contract_cols(): lax.dot_general(left, right, (((1,), (1,)), ((), ())), preferred_element_...]
  transfers between devices with their start and end apart: 42 -> 28, of which waited for: 15 -> 11; matrix products, arithmetic and copies ran while one was open for 25% -> 19% of each run, Pallas kernels for 0% -> 15%
where the time goes in v4:
time: 1030 us
  Pallas kernels  637 us (62%)
  waiting for transfers between devices  107 us (10%)
  matrix products  106 us (10%)
  local copies, waits for them, and re-layouts  99.1 us (10%)
  other arithmetic  63 us (6%)
  starting transfers between devices  14.2 us (1%)
    pallas_call x2, Pallas kernels, scatter_all(): pl.pallas_call(functools.partial(scatter_kernel, inner_h, sections, lefts...  384 us
    pallas_call x1, Pallas kernels, gather_all(): pl.pallas_call(functools.partial(gather_kernel, n_h, jobs, len(shards), n...  253 us
    ppermute x25, waiting for transfers between devices, swap(): return lax.ppermute(value, axis, [(0, 1), (1, 0)])  102 us
    dot_general x5, matrix products, contract_cols(): lax.dot_general(left, right, (((1,), (1,)), ((), ())), preferred_element_...  46.8 us
    unnamed x189, local copies, waits for them, and re-layouts  31.7 us
    dot_general x4, matrix products, matmul(): return jnp.dot(left, right, preferred_element_type=jnp.float32)  27.5 us
  transfers between devices with their start and end apart: 28, of which 11 were waited for; matrix products, arithmetic and copies ran while one was open for 19% of the time, Pallas kernels for 15%

profile of v4, /device:TPU:0, one launch (start us, length us, event | category | flops | bytes accessed | tf_op | source)
XLA Modules:
  0.0 1029.0 jit_solution(5750014588195398311)
XLA Ops:
  1.6 2.1 pad.19.refs_0_
  3.7 2.1 pad.21.refs_5_
  11.1 1.9 multiply_sine_fusion.1
  13.1 252.6 %shard_map.238 = (bf16[2,2,2,128,13568]{4,3,2,1,0:T(8,128)(2,1)}, bf16[2,2,2,128,3200]{4,3,2,1,0:T(8,128)(2,1)}, bf16[2,2,2,128,1024]{4,3,2,1,0:T(8,128)(2,1)}, ...) custom-call(bf16[32,13568]{1,0:T(8,128)(2,1)} %pad.19.refs_0_, ...), custom_call_target="tpu_custom_call" | custom-call | tf_op jit(solution)/shard_map/pallas_call | solution.py:206
  265.7 18.4 %fusion.87 = (f32[256]{0:T(256)S(1)}, f32[256,1024]{0,1:T(8,128)S(1)}) fusion(f32[256,1024]{0,1:T(8,128)S(1)} %bitcast.337, bf16[1024,13568]{1,0:T(8,128)(2,1)} %bitcast.299, f32[256]{0:T(256)S(1)} %broadcast_divide_fusion, bf16[13500,256]{1,0:T(8,128)(2,1)} %bitcast.301), kind=kOutput, calls=%fused_computation.291 | convolution fusion | flops 7124484096 | bytes 36798464 | tf_op jit(solution)/shard_map/dot_general | solution.py:45
  287.2 5.0 fusion.39
  292.3 1.5 collective-permute-start
  293.8 23.7 %collective-permute-done = bf16[256,2048]{1,0:T(8,128)(2,1)S(1)} collective-permute-done((bf16[256,2048]{1,0:T(8,128)(2,1)S(1)}, bf16[256,2048]{1,0:T(8,128)(2,1)S(1)}, u32[]{:S(2)}, u32[]{:S(2)}) %collective-permute-start) | collective-permute-done | bytes 1048608 | tf_op jit(solution)/shard_map/ppermute | solution.py:55
  317.5 1.6 pad_maximum_fusion.1
  319.3 4.2 pad.22.refs_2_
  323.8 1.8 constant_dynamic-slice_fusion.26
  326.5 1.9 slice.160
  328.3 2.0 copy.145
  332.0 1.6 collective-permute-start.4
  333.6 2.7 fusion.54
  337.0 2.5 fusion.84
  339.4 3.0 copy.146
  342.5 4.6 copy.144
  347.1 4.1 fusion.88
  351.3 3.8 fusion
  355.2 2.4 copy-done
  357.6 4.3 fusion.50
  362.0 2.7 fusion.89
  365.2 16.5 %multiply_convert_fusion.2 = (bf16[256,4096]{0,1:T(8,128)(2,1)S(1)}, f32[256,4096]{0,1:T(8,128)}, f32[256,4096]{0,1:T(8,128)}) fusion(bf16[256,1024]{0,1:T(8,128)(2,1)S(1)} %add_convert_fusion.3, bf16[1024,4096]{1,0:T(8,128)(2,1)} %bitcast.371), kind=kOutput, calls=%fused_computation.60 | convolution fusion | flops 2215641088 | bytes 19398656 | tf_op jit(solution)/shard_map/dot_general | solution.py:51
  381.8 3.4 fusion.48
  385.1 11.8 %collective-permute-done.5.refs_6_ = bf16[128,13568]{1,0:T(8,128)(2,1)} collective-permute-done((bf16[128,13568]{1,0:T(8,128)(2,1)}, bf16[128,13568]{1,0:T(8,128)(2,1)}, u32[]{:S(2)}, u32[]{:S(2)}) %collective-permute-start.5) | collective-permute-done | bytes 3473440 | tf_op jit(solution)/shard_map/ppermute | solution.py:55
  397.0 1.6 slice.164
  398.5 1.8 collective-permute-start.6
  403.0 7.3 collective-permute-done.4.refs_5_
  410.3 1.6 slice.165
  411.9 1.9 collective-permute-start.7
  414.9 31.9 %collective-permute-done.6 = bf16[128,6784]{1,0:T(8,128)(2,1)S(1)} collective-permute-done((bf16[128,6784]{1,0:T(8,128)(2,1)S(1)}, bf16[128,6784]{1,0:T(8,128)(2,1)S(1)}, u32[]{:S(2)}, u32[]{:S(2)}) %collective-permute-start.6) | collective-permute-done | bytes 1736736 | tf_op jit(solution)/shard_map/ppermute | solution.py:55
  448.7 2.0 collective-permute-done.7
  453.1 8.2 log-plus-one_convert_fusion.refs_6_
  468.0 1.5 constant_dynamic-update-slice_fusion.13
  473.5 149.9 %shard_map.239 = (f32[53,32,256]{2,1,0:T(8,128)}, bf16[13568,256]{1,0:T(8,128)(2,1)}, f32[1024,256]{1,0:T(8,128)}) custom-call(bf16[1,512,512]{2,1,0:T(8,128)(2,1)} %maximum_bitcast_fusion.refs_0_, bf16[256,1024]{1,0:T(8,128)(2,1)} %copy.152.refs_1_, bf16[13568,256]{1,0:T(8,128)(2,1)} %pad.22.refs_2_, bf16[13568,256]{1,0:T(8,128)(2,1)} %collective-permute-done.3.refs_3_, ...), custom_call_target="tpu_custom_call" | custom-call | tf_op jit(solution)/shard_map/pallas_call | solution.py:440
  630.8 15.7 %fusion.44 = (bf16[9216,256]{1,0:T(8,128)(2,1)}, f32[256,4096]{0,1:T(8,128)S(1)}) fusion(f32[256,4096]{0,1:T(8,128)} %get-tuple-element.185, bf16[4096,1024]{1,0:T(8,128)(2,1)} %bitcast.373, f32[1024,256]{1,0:T(8,128)S(1)} %dynamic-slice_dynamic-update-slice_fusion), kind=kOutput, calls=%fused_computation.85 | convolution fusion | flops 2222981120 | bytes 19922944 | tf_op jit(solution)/shard_map/dot_general | solution.py:45
  646.6 8.3 fusion.90
  654.8 1.6 copy.156
  661.6 1.6 convolution_convert_fusion
  663.2 2.0 copy.157
  666.3 11.3 %multiply_reduce_fusion = (f32[16,256]{1,0:T(8,128)S(1)}, f32[16,256,1024]{2,1,0:T(8,128)}) fusion(f32[16,256,1024]{2,1,0:T(8,128)} %copy-done, f32[16,256]{1,0:T(8,128)S(1)} %log_add_fusion, bf16[256,16,64]{0,2,1:T(8,128)(2,1)S(1)} %bitcast.321, bf16[1024,16,64]{0,2,1:T(8,128)(2,1)S(1)} %bitcast.308), kind=kOutput, calls=%fused_computation.1 | convolution fusion | flops 549449728 | bytes 36208640 | tf_op jit(solution)/shard_map/qhd,khd->hqk/dot_general | solution.py:665
  677.6 7.7 convert_bitcast_fusion
  685.4 2.8 concatenate.128
  688.1 11.8 %multiply_convert_fusion = bf16[16,256,1024]{2,1,0:T(8,128)(2,1)S(1)} fusion(f32[16,256,1024]{2,1,0:T(8,128)} %get-tuple-element.189, f32[16,256,1024]{2,1,0:T(8,128)} %copy-done, f32[16,256]{1,0:T(8,128)S(1)} %get-tuple-element.188, f32[16,256]{1,0:T(8,128)S(1)} %log_add_fusion), kind=kLoop, calls=%fused_computation | loop fusion | flops 16777216 | bytes 41975808 | tf_op jit(solution)/shard_map/convert_element_type | solution.py:667
  700.0 3.4 copy-done.1
  703.4 1.6 fusion.47
  704.9 2.8 concatenate.127
  707.7 2.0 copy_dynamic-update-slice_fusion.1
  712.7 4.0 slice_bitcast_fusion
  719.6 2.7 fusion.49
  722.3 20.4 %collective-permute-done.17 = bf16[256,2048]{0,1:T(8,128)(2,1)S(1)} collective-permute-done((bf16[256,2048]{0,1:T(8,128)(2,1)S(1)}, bf16[256,2048]{0,1:T(8,128)(2,1)S(1)}, u32[]{:S(2)}, u32[]{:S(2)}) %collective-permute-start.17) | collective-permute-done | bytes 1048608 | tf_op jit(solution)/shard_map/ppermute | solution.py:55
  743.0 2.8 fusion.91
  745.9 1.6 copy.161
  750.2 1.5 collective-permute-start.23
  751.7 2.1 collective-permute-done.23
  754.6 2.8 collective-permute-done.24
  759.6 3.3 collective-permute-done.25
  762.9 2.0 copy.163.refs_1_
  765.0 1.5 collective-permute-done.27
  767.9 234.1 %shard_map.240 = (f32[101,32,256]{2,1,0:T(8,128)}, f32[13568,256]{1,0:T(8,128)}) custom-call(bf16[13,512,512]{2,1,0:T(8,128)(2,1)} %fusion.62.refs_0_, bf16[256,1024]{1,0:T(8,128)(2,1)} %copy.163.refs_1_, bf16[9216,256]{1,0:T(8,128)(2,1)} %get-tuple-element.76.refs_2_, bf16[9216,256]{1,0:T(8,128)(2,1)} %collective-permute-done.19.refs_3_, ...), custom_call_target="tpu_custom_call" | custom-call | tf_op jit(solution)/shard_map/pallas_call | solution.py:440
  1002.1 1.6 slice_bitcast_fusion.3
  1005.0 1.6 slice_bitcast_fusion.6
  1007.6 12.2 %bitcast_divide_fusion = f32[256,13500]{0,1:T(8,128)} fusion(bf16[256,13500]{0,1:T(8,128)(2,1)} %param.15, f32[13568,256]{1,0:T(8,128)} %get-tuple-element.33, f32[256]{0:T(256)S(1)} %copy-done.54), kind=kLoop, calls=%fused_computation.8 | loop fusion | flops 17280000 | bytes 34562048 | tf_op jit(solution)/shard_map/div | solution.py:714
  (335 shorter events, 69.4 us)
Async XLA Ops:
  0.7 8.4 copy-start.47
  0.7 9.6 copy-start.67
  0.7 9.6 copy-start.66
  0.7 9.6 copy-start.65
  0.7 9.6 copy-start.64
  0.7 9.7 copy-start.63
  0.7 9.7 copy-start.41
  10.4 442.7 %copy-start.53 = (f32[256]{0:T(256)}, f32[256]{0:T(256)S(1)}, u32[]{:S(2)}) copy-start(f32[256]{0:T(256)S(1)} %broadcast_divide_fusion) | copy-start | bytes 3076
  284.1 77.8 %copy-start.2 = (f32[256,1024]{0,1:T(8,128)}, f32[256,1024]{0,1:T(8,128)S(1)}, u32[]{:S(2)}) copy-start(f32[256,1024]{0,1:T(8,128)S(1)} %get-tuple-element.180) | copy-start | bytes 3145732
  284.2 8.0 copy-start.49
  284.4 7.8 copy-start.57
  286.2 78.7 %copy-start.45 = (f32[1,1024]{1,0:T(1,128)}, f32[1,1024]{1,0:T(1,128)S(1)}, u32[]{:S(2)}) copy-start(f32[1,1024]{1,0:T(1,128)S(1)} %get-tuple-element.152) | copy-start | bytes 12292
  286.8 32.5 %slice-start.4 = ((s8[6914048]{0:T(1024)(128)(4,1)}), s8[4194304]{0:T(1024)(128)(4,1)S(1)}, s32[]{:S(2)}) async-start(s8[6914048]{0:T(1024)(128)(4,1)} %bitcast.316), calls=%async_computation.4 | async-start | bytes 8388608
  287.2 32.1 %slice-start.5 = ((s8[6914048]{0:T(1024)(128)(4,1)}), s8[2719744]{0:T(1024)(128)(4,1)S(1)}, s32[]{:S(2)}) async-start(s8[6914048]{0:T(1024)(128)(4,1)} %bitcast.316), calls=%async_computation.5 | async-start | bytes 5439488
  292.2 26.9 %copy-start.20 = (bf16[256,3072]{1,0:T(8,128)(2,1)}, bf16[256,3072]{1,0:T(8,128)(2,1)S(1)}, u32[]{:S(2)}) copy-start(bf16[256,3072]{1,0:T(8,128)(2,1)S(1)} %fusion.39) | copy-start | bytes 4718596
  292.3 25.2 %collective-permute-start = (bf16[256,2048]{1,0:T(8,128)(2,1)S(1)}, bf16[256,2048]{1,0:T(8,128)(2,1)S(1)}, u32[]{:S(2)}, u32[]{:S(2)}) collective-permute-start(bf16[256,2048]{1,0:T(8,128)(2,1)S(1)} %get-tuple-element.119), channel_id=1, source_target_pairs={{0,2},{2,0},{1,3},{3,1},{4,6},{6,4},{5,7},{7,5},{8,10},{10,8},{9,1... | collective-permute-start | bytes 3145736 | tf_op jit(solution)/shard_map/ppermute | solution.py:55
  319.1 14.5 %collective-permute-start.1 = (bf16[2,256,2048]{2,1,0:T(8,128)(2,1)}, bf16[2,256,2048]{2,1,0:T(8,128)(2,1)}, u32[]{:S(2)}, u32[]{:S(2)}) collective-permute-start(bf16[2,256,2048]{2,1,0:T(8,128)(2,1)} %get-tuple-element.116), channel_id=1, source_target_pairs={{0,1},{1,0},{2,3},{3,2},{4,5},{5,4},{6,7},{7,6},{8,9},{9,8},{10,11... | collective-permute-start | bytes 6291464 | tf_op jit(solution)/shard_map/ppermute | solution.py:55
  319.1 77.9 %collective-permute-start.5 = (bf16[128,13568]{1,0:T(8,128)(2,1)}, bf16[128,13568]{1,0:T(8,128)(2,1)}, u32[]{:S(2)}, u32[]{:S(2)}) collective-permute-start(bf16[128,13568]{1,0:T(8,128)(2,1)} %get-tuple-element.30.refs_4_), channel_id=1, source_target_pairs={{0,4},{4,0},{1,5},{5,1},{2,6},{6,2},{3,7},{7,3},{8,12},{12,8},{9,1... | collective-permute-start | bytes 10420232 | tf_op jit(solution)/shard_map/ppermute | solution.py:55
  323.5 149.9 %collective-permute-start.3 = (bf16[13568,256]{1,0:T(8,128)(2,1)}, bf16[13568,256]{1,0:T(8,128)(2,1)}, u32[]{:S(2)}, u32[]{:S(2)}) collective-permute-start(bf16[13568,256]{1,0:T(8,128)(2,1)} %pad.22.refs_2_), channel_id=1, source_target_pairs={{0,1},{1,0},{2,3},{3,2},{4,5},{5,4},{6,7},{7,6},{8,9},{9,8},{10,11... | collective-permute-start | bytes 20840456 | tf_op jit(solution)/shard_map/ppermute | solution.py:55
  326.3 121.9 %collective-permute-start.15 = (bf16[256,512]{0,1:T(8,128)(2,1)}, bf16[256,512]{0,1:T(8,128)(2,1)S(1)}, u32[]{:S(2)}, u32[]{:S(2)}) collective-permute-start(bf16[256,512]{0,1:T(8,128)(2,1)} %pad_maximum_fusion.10), channel_id=1, source_target_pairs={{0,1},{1,0},{2,3},{3,2},{4,5},{5,4},{6,7},{7,6},{8,9},{9,8},{10,11... | collective-permute-start | bytes 786440 | tf_op jit(solution)/shard_map/ppermute | solution.py:55
  332.0 78.3 %collective-permute-start.4 = (bf16[128,13568]{1,0:T(8,128)(2,1)}, bf16[128,13568]{1,0:T(8,128)(2,1)}, u32[]{:S(2)}, u32[]{:S(2)}) collective-permute-start(bf16[128,13568]{1,0:T(8,128)(2,1)} %get-tuple-element.30.refs_4_), channel_id=1, source_target_pairs={{0,2},{2,0},{1,3},{3,1},{4,6},{6,4},{5,7},{7,5},{8,10},{10,8},{9,1... | collective-permute-start | bytes 10420232 | tf_op jit(solution)/shard_map/ppermute | solution.py:55
  342.5 8.8 copy-start.4
  362.0 19.8 %slice-start.10 = ((s8[8388608]{0:T(1024)(128)(4,1)}), s8[4194304]{0:T(1024)(128)(4,1)S(1)}, s32[]{:S(2)}) async-start(s8[8388608]{0:T(1024)(128)(4,1)} %bitcast.374), calls=%async_computation.10 | async-start | bytes 8388608
  364.7 17.1 %copy-start.51 = (f32[256]{0:T(256)}, f32[256]{0:T(256)S(1)}, u32[]{:S(2)}) copy-start(f32[256]{0:T(256)S(1)} %broadcast_multiply_fusion) | copy-start | bytes 3076
  364.9 16.9 %copy-start.61 = (f32[256]{0:T(256)}, f32[256]{0:T(256)S(1)}, u32[]{:S(2)}) copy-start(f32[256]{0:T(256)S(1)} %multiply_reduce_fusion.5) | copy-start | bytes 3076
  364.9 16.9 %copy-start.55 = (f32[256]{0:T(256)}, f32[256]{0:T(256)S(1)}, u32[]{:S(2)}) copy-start(f32[256]{0:T(256)S(1)} %fusion.73) | copy-start | bytes 3076
  365.2 16.5 %slice-start.11 = ((s8[8388608]{0:T(1024)(128)(4,1)}), s8[4194304]{0:T(1024)(128)(4,1)S(1)}, s32[]{:S(2)}) async-start(s8[8388608]{0:T(1024)(128)(4,1)} %bitcast.374), calls=%async_computation.11 | async-start | bytes 8388608
  398.5 48.3 %collective-permute-start.6 = (bf16[128,6784]{1,0:T(8,128)(2,1)S(1)}, bf16[128,6784]{1,0:T(8,128)(2,1)S(1)}, u32[]{:S(2)}, u32[]{:S(2)}) collective-permute-start(bf16[128,6784]{1,0:T(8,128)(2,1)S(1)} %slice.164), channel_id=1, source_target_pairs={{0,2},{2,0},{1,3},{3,1},{4,6},{6,4},{5,7},{7,5},{8,10},{10,8},{9,1... | collective-permute-start | bytes 5210120 | tf_op jit(solution)/shard_map/ppermute | solution.py:55
  411.9 38.8 %collective-permute-start.7 = (bf16[128,6784]{1,0:T(8,128)(2,1)S(1)}, bf16[128,6784]{1,0:T(8,128)(2,1)S(1)}, u32[]{:S(2)}, u32[]{:S(2)}) collective-permute-start(bf16[128,6784]{1,0:T(8,128)(2,1)S(1)} %slice.165), channel_id=1, source_target_pairs={{0,4},{4,0},{1,5},{5,1},{2,6},{6,2},{3,7},{7,3},{8,12},{12,8},{9,1... | collective-permute-start | bytes 5210120 | tf_op jit(solution)/shard_map/ppermute | solution.py:55
  413.8 38.2 %collective-permute-start.2 = (bf16[256,512]{0,1:T(8,128)(2,1)S(1)}, bf16[256,512]{0,1:T(8,128)(2,1)S(1)}, u32[]{:S(2)}, u32[]{:S(2)}) collective-permute-start(bf16[256,512]{0,1:T(8,128)(2,1)S(1)} %pad_maximum_fusion.7), channel_id=1, source_target_pairs={{0,1},{1,0},{2,3},{3,2},{4,5},{5,4},{6,7},{7,6},{8,9},{9,8},{10,11... | collective-permute-start | bytes 786440 | tf_op jit(solution)/shard_map/ppermute | solution.py:55
  413.9 39.2 %slice-start.2 = ((s8[6914048]{0:T(1024)(128)(4,1)}), s8[4194304]{0:T(1024)(128)(4,1)S(1)}, s32[]{:S(2)}) async-start(s8[6914048]{0:T(1024)(128)(4,1)} %bitcast.302), calls=%async_computation.2 | async-start | bytes 8388608
  414.9 38.3 %slice-start.3 = ((s8[6914048]{0:T(1024)(128)(4,1)}), s8[2719744]{0:T(1024)(128)(4,1)S(1)}, s32[]{:S(2)}) async-start(s8[6914048]{0:T(1024)(128)(4,1)} %bitcast.302), calls=%async_computation.3 | async-start | bytes 5439488
  446.8 6.2 collective-permute-start.13
  448.2 4.3 collective-permute-start.14
  450.7 1.9 collective-permute-start.12
  452.0 9.3 copy-start.26
  452.0 9.3 copy-start.37
  452.0 21.0 %collective-permute-start.8 = (bf16[128,13568]{1,0:T(8,128)(2,1)}, bf16[128,13568]{1,0:T(8,128)(2,1)}, u32[]{:S(2)}, u32[]{:S(2)}) collective-permute-start(bf16[128,13568]{1,0:T(8,128)(2,1)} %get-tuple-element.30.refs_4_), channel_id=1, source_target_pairs={{0,1},{1,0},{2,3},{3,2},{4,5},{5,4},{6,7},{7,6},{8,9},{9,8},{10,11... | collective-permute-start | bytes 10420232 | tf_op jit(solution)/shard_map/ppermute | solution.py:55
  452.5 8.8 copy-start.39
  452.5 20.9 %collective-permute-start.10 = (bf16[128,13568]{1,0:T(8,128)(2,1)}, bf16[128,13568]{1,0:T(8,128)(2,1)}, u32[]{:S(2)}, u32[]{:S(2)}) collective-permute-start(bf16[128,13568]{1,0:T(8,128)(2,1)} %collective-permute-done.5.refs_6_), channel_id=1, source_target_pairs={{0,1},{1,0},{2,3},{3,2},{4,5},{5,4},{6,7},{7,6},{8,9},{9,8},{10,11... | collective-permute-start | bytes 10420232 | tf_op jit(solution)/shard_map/ppermute | solution.py:55
  452.6 20.8 %collective-permute-start.9 = (bf16[128,13568]{1,0:T(8,128)(2,1)}, bf16[128,13568]{1,0:T(8,128)(2,1)}, u32[]{:S(2)}, u32[]{:S(2)}) collective-permute-start(bf16[128,13568]{1,0:T(8,128)(2,1)} %collective-permute-done.4.refs_5_), channel_id=1, source_target_pairs={{0,1},{1,0},{2,3},{3,2},{4,5},{5,4},{6,7},{7,6},{8,9},{9,8},{10,11... | collective-permute-start | bytes 10420232 | tf_op jit(solution)/shard_map/ppermute | solution.py:55
  453.0 8.3 copy-start.23
  453.0 20.5 %collective-permute-start.11 = (bf16[128,13568]{1,0:T(8,128)(2,1)}, bf16[128,13568]{1,0:T(8,128)(2,1)}, u32[]{:S(2)}, u32[]{:S(2)}) collective-permute-start(bf16[128,13568]{1,0:T(8,128)(2,1)} %constant_dynamic-update-slice_fusion.8.refs_7_), channel_id=1, source_target_pairs={{0,1},{1,0},{2,3},{3,2},{4,5},{5,4},{6,7},{7,6},{8,9},{9,8},{10,11... | collective-permute-start | bytes 10420232 | tf_op jit(solution)/shard_map/ppermute | solution.py:55
  473.0 294.9 %collective-permute-start.21 = (bf16[13568,256]{1,0:T(8,128)(2,1)}, bf16[13568,256]{1,0:T(8,128)(2,1)}, u32[]{:S(2)}, u32[]{:S(2)}) collective-permute-start(bf16[13568,256]{1,0:T(8,128)(2,1)} %log-plus-one_convert_fusion.refs_6_), channel_id=1, source_target_pairs={{0,1},{1,0},{2,3},{3,2},{4,5},{5,4},{6,7},{7,6},{8,9},{9,8},{10,11... | collective-permute-start | bytes 20840456 | tf_op jit(solution)/shard_map/ppermute | solution.py:55
  630.8 15.7 %copy-start.68 = (f32[256,4096]{0,1:T(8,128)S(1)}, f32[256,4096]{0,1:T(8,128)}, u32[]{:S(2)}) copy-start(f32[256,4096]{0,1:T(8,128)} %get-tuple-element.99) | copy-start | bytes 12582916
  630.8 15.7 %copy-start.69 = (f32[256,4096]{0,1:T(8,128)S(1)}, f32[256,4096]{0,1:T(8,128)}, u32[]{:S(2)}) copy-start(f32[256,4096]{0,1:T(8,128)} %get-tuple-element.185) | copy-start | bytes 12582916
  646.5 9.8 copy-start.46
  646.5 9.9 copy-start.52
  646.6 9.9 copy-start.56
  688.1 15.2 %copy-start.11 = (bf16[256,1024]{0,1:T(8,128)(2,1)S(1)}, bf16[256,1024]{0,1:T(8,128)(2,1)}, u32[]{:S(2)}) copy-start(bf16[256,1024]{0,1:T(8,128)(2,1)} %copy.145) | copy-start | bytes 1572868
  710.3 6.4 collective-permute-start.16
  710.4 57.5 %collective-permute-start.19 = (bf16[9216,256]{1,0:T(8,128)(2,1)}, bf16[9216,256]{1,0:T(8,128)(2,1)}, u32[]{:S(2)}, u32[]{:S(2)}) collective-permute-start(bf16[9216,256]{1,0:T(8,128)(2,1)} %get-tuple-element.76.refs_2_), channel_id=1, source_target_pairs={{0,1},{1,0},{2,3},{3,2},{4,5},{5,4},{6,7},{7,6},{8,9},{9,8},{10,11... | collective-permute-start | bytes 14155784 | tf_op jit(solution)/shard_map/ppermute | solution.py:55
  717.3 25.6 %slice-start.8 = ((s8[6553600]{0:T(1024)(128)(4,1)}), s8[4194304]{0:T(1024)(128)(4,1)S(1)}, s32[]{:S(2)}) async-start(s8[6553600]{0:T(1024)(128)(4,1)} %bitcast.359), calls=%async_computation.8 | async-start | bytes 8388608
  717.4 25.3 %collective-permute-start.17 = (bf16[256,2048]{0,1:T(8,128)(2,1)S(1)}, bf16[256,2048]{0,1:T(8,128)(2,1)S(1)}, u32[]{:S(2)}, u32[]{:S(2)}) collective-permute-start(bf16[256,2048]{0,1:T(8,128)(2,1)S(1)} %dynamic-slice_bitcast_fusion.1), channel_id=1, source_target_pairs={{0,2},{2,0},{1,3},{3,1},{4,6},{6,4},{5,7},{7,5},{8,10},{10,8},{9,1... | collective-permute-start | bytes 3145736 | tf_op jit(solution)/shard_map/ppermute | solution.py:55
  719.6 23.4 %slice-start.9 = ((s8[6553600]{0:T(1024)(128)(4,1)}), s8[2359296]{0:T(1024)(128)(4,1)S(1)}, s32[]{:S(2)}) async-start(s8[6553600]{0:T(1024)(128)(4,1)} %bitcast.359), calls=%async_computation.9 | async-start | bytes 4718592
  722.3 23.6 %copy-start.17 = (bf16[16,64,256]{2,1,0:T(8,128)(2,1)}, bf16[16,64,256]{2,1,0:T(8,128)(2,1)S(1)}, u32[]{:S(2)}) copy-start(bf16[16,64,256]{2,1,0:T(8,128)(2,1)S(1)} %fusion.49) | copy-start | bytes 1572868
  748.4 1.8 collective-permute-start.22
  750.1 17.8 %collective-permute-start.20 = (bf16[3072,256]{1,0:T(8,128)(2,1)}, bf16[3072,256]{1,0:T(8,128)(2,1)}, u32[]{:S(2)}, u32[]{:S(2)}) collective-permute-start(bf16[3072,256]{1,0:T(8,128)(2,1)} %fusion.59.refs_4_), channel_id=1, source_target_pairs={{0,1},{1,0},{2,3},{3,2},{4,5},{5,4},{6,7},{7,6},{8,9},{9,8},{10,11... | collective-permute-start | bytes 4718600 | tf_op jit(solution)/shard_map/ppermute | solution.py:55
  750.2 3.7 collective-permute-start.23
  753.9 3.6 collective-permute-start.24
  757.5 5.4 collective-permute-start.25
  758.3 6.7 collective-permute-start.26
  762.9 3.6 collective-permute-start.27
  765.0 2.1 collective-permute-start.18
  (46 other events, 169.0 us)

commit v5 on v4

--- a/solution.py
+++ b/solution.py
@@ -216,7 +216,7 @@
     )(*shards)
 
 
-def scatter_kernel(n_h, sections, run, n_weights, with_sum, *refs):
+def scatter_kernel(n_h, sections, left_starts, n_weights, with_sum, *refs):
     lefts, vector = refs[:2]
     n_sections = len(sections)
     rights = refs[2 : 2 + 2 * n_sections]
@@ -304,8 +304,7 @@
         slot = lax.rem(i, RING)
         for copy in loads(i, 0, 0):
             copy.wait()
-        two = i // 4
-        left = lefts[two - (two + 1024 - run) // 1024 * (two - run)]
+        left = lefts[sum((i + 1024 - start) // 1024 for start in left_starts[1:]) if left_starts[1:] else 0]
         right = right_buf.at[lax.rem(i, 3)]
 
         @pl.when(i >= RING)
@@ -418,7 +417,7 @@
         product_store(k).wait()
 
 
-def scatter_all(lefts, rights, vector, weights, product_type, with_sum, collective_id):
+def scatter_all(lefts, left_starts, rights, vector, weights, product_type, with_sum, collective_id):
     sections = [own.shape[0] // CHUNK for own, _ in rights]
     n, cells = sum(sections), vector.shape[0]
     features = vector.shape[1]
@@ -439,7 +438,7 @@
         out_specs.append(vmem)
     part, *more = pl.pallas_call(
         functools.partial(
-            scatter_kernel, inner_h, sections, lefts.shape[0] - 1, len(weights), with_sum
+            scatter_kernel, inner_h, sections, left_starts, len(weights), with_sum
         ),
         out_shape=out_shape,
         in_specs=[vmem, vmem] + [hbm] * (2 * len(rights) + len(weights)),
@@ -474,39 +473,13 @@
     return part, *more
 
 
-def gather_dec(own, after):
-    by_x = swap(own, "x")
-    by_y = swap(lax.optimization_barrier((own, after))[0], "y")
-    middle = own.shape[1] // 256 * 128
-    far = [swap(by_x[:, :middle], "y"), swap(by_y[:, middle:], "x")]
-    four = [own, by_y, by_x, jnp.concatenate(far, axis=1)]
-    return four + [swap(part, "c") for part in four]
+def after(value, first):
+    return lax.optimization_barrier((value, first))
 
 
 def own_half(left):
     half = left.shape[1] // 2
     return jnp.concatenate([left[:, :half], swap(left[:, half:], "c")], axis=0)
-
-
-def sum_over_h(part):
-    n_h = lax.axis_size("h")
-    rows = part.shape[0] // n_h
-    at = lax.axis_index("h")
-    total = lax.dynamic_slice_in_dim(part, at * rows, rows, 0).astype(jnp.float32)
-    for step in range(1, n_h):
-        send = lax.dynamic_slice_in_dim(part, lax.rem(at + step, n_h) * rows, rows, 0)
-        ring = [(i, (i + step) % n_h) for i in range(n_h)]
-        total = total + lax.ppermute(send, "h", ring).astype(jnp.float32)
-    return total
-
-
-def scatter_vectors(part):
-    half = part.shape[0] // 2
-    part = part[:half] + swap(part[half:].astype(jnp.bfloat16), "c").astype(jnp.float32)
-    part = part[: half // 2] + swap(part[half // 2 :].astype(jnp.bfloat16), "x").astype(jnp.float32)
-    half = half // 2
-    part = part[: half // 2] + swap(part[half // 2 :].astype(jnp.bfloat16), "y").astype(jnp.float32)
-    return sum_over_h(part.astype(jnp.bfloat16))
 
 
 def gather_group(mine):
@@ -617,7 +590,11 @@
     qkv = matmul(a1, qkv_all).astype(jnp.bfloat16)
     query = qkv[:, :width].reshape(rows, heads, head_width)
     kv_all, arrived = gather_group(qkv[:, width:])
-    dec_parts = gather_dec(gathered[5], arrived)
+    dec_own = gathered[5]
+    middle = dec_own.shape[1] // 256 * 128
+    query, by_x = after(query, swap(dec_own, "x"))
+    by_y = swap(after(dec_own, arrived)[0], "y")
+    far_left = swap(by_x[:, :middle], "y")
     keys = kv_all[:, :width].reshape(slots, heads, head_width)
     values = kv_all[:, width:].reshape(slots, heads, head_width)
 
@@ -635,15 +612,19 @@
     probs_b = (expo / total).astype(jnp.bfloat16)
     attended = jnp.einsum("hqk,khd->qhd", probs_b, values, preferred_element_type=jnp.float32)
     attended_b = attended.reshape(rows, width).astype(jnp.bfloat16)
-    attended_b = by_owner(attended_b, 1)
+    attended_b, by_y = after(by_owner(attended_b, 1), by_y)
+    far_right = swap(by_y[:, middle:], "x")
     h1 = h0 + matmul(attended_b, out_all)
     a2 = layer_norm(h1, g2f, b2f).astype(jnp.bfloat16)
     hidden = matmul(a2, up_all)
     act = jax.nn.gelu(hidden, approximate=False).astype(jnp.bfloat16)
+    act, far = after(act, (far_left, far_right))
+    dec_parts = [dec_own, by_y, by_x, jnp.concatenate(far, axis=1)]
+    dec_parts += [swap(part, "c") for part in dec_parts]
     h2 = h1 + matmul(act, down_all)
     hb = h2.astype(jnp.bfloat16)
     grad_dec, logits, dh2 = scatter_all(
-        left_of(hb, 1), [cot_pair], relative(hb, 1), dec_parts, jnp.bfloat16, True, 1
+        left_of(hb, 1), [0], [cot_pair], relative(hb, 1), dec_parts, jnp.bfloat16, True, 1
     )
     own_rows = grad_dec.shape[1]
     grad_dec = columns_of(grad_dec)[:, :genes].T
@@ -678,19 +659,20 @@
     da1 = contract_cols(d_qkv, qkv_all)
     first_pull = jax.vjp(layer_norm, h0, g1f, b1f)[1]
     dh0_norm, grad_gain_one, grad_shift_one = first_pull(da1)
-    grad_vectors = jnp.stack([grad_gain_one, grad_shift_one, grad_gain_two, grad_shift_two], axis=1)
-    grad_vectors = scatter_vectors(relative(grad_vectors, 0))
-    grad_gain_one, grad_shift_one, grad_gain_two, grad_shift_two = (
-        grad_vectors[:, k] for k in range(4)
-    )
+    vectors_b = jnp.stack([grad_gain_one, grad_shift_one, grad_gain_two, grad_shift_two])
+    vectors_b = jnp.pad(vectors_b, ((0, rows - 4), (0, 0))).astype(jnp.bfloat16)
+    unit = jnp.eye(rows, dtype=jnp.bfloat16)
     dh0b = (dh1 + dh0_norm).astype(jnp.bfloat16)
 
-    lefts = [left_of(a2, 1)] * 4 + [left_of(act, act.shape[1] // width)]
-    lefts += [left_of(attended_b, 1)] + [left_of(a1, 1)] * 3 + [left_of(dh0b, 1)]
+    lefts = [left_of(a2, 1), left_of(act, act.shape[1] // width), left_of(attended_b, 1)]
+    lefts += [left_of(a1, 1), left_of(vectors_b, 1), left_of(dh0b, 1)]
+    pieces = (4 * width,) + (width,) * 5 + (3 * width, rows)
+    left_starts = [sum(pieces[:k]) // CHUNK for k in range(len(pieces) + 1)]
     rights = [d_hidden.T] + [dfb.T] * 4 + [dab.T]
     grads, d_xb = scatter_all(
         jnp.concatenate(lefts, axis=0),
-        [both_cores(jnp.concatenate(rights, axis=0)), both_cores(d_qkv.T), xb_pair],
+        left_starts,
+        [both_cores(jnp.concatenate(rights, axis=0)), both_cores(d_qkv.T), (unit, unit), xb_pair],
         dh0b,
         [enc_all],
         jnp.float32,
@@ -698,13 +680,16 @@
         2,
     )
     ends = [0]
-    for columns in (4 * width, 4 * width, width, 3 * width):
+    for columns in (4 * width, 4 * width, width, 3 * width, rows):
         ends.append(ends[-1] + columns // CHUNK)
-    grad_up, grad_down, grad_out, grad_qkv, grad_enc = (
+    grad_up, grad_down, grad_out, grad_qkv, grad_vectors, grad_enc = (
         grads[low:high] for low, high in zip(ends, ends[1:] + [grads.shape[0]])
     )
     grad_up, grad_out, grad_qkv, grad_enc = (
         columns_of(g) for g in (grad_up, grad_out, grad_qkv, grad_enc)
+    )
+    grad_gain_one, grad_shift_one, grad_gain_two, grad_shift_two = (
+        grad_vectors[0, :, k] for k in range(4)
     )
     grad_down = grad_down.reshape(4, -1, own_rows, CHUNK).transpose(0, 2, 1, 3)
     grad_down = grad_down.reshape(4 * own_rows, -1)

time: 1030 us -> 1050 us (1.019)
    ppermute x25 -> x23, waiting for transfers between devices: 102 us -> 113 us  [swap(): return lax.ppermute(value, axis, [(0, 1), (1, 0)])]
    unnamed x189 -> x183, local copies, waits for them, and re-layouts: 31.7 us -> 33.7 us
  transfers between devices with their start and end apart: 28 -> 23, of which waited for: 11 -> 8; matrix products, arithmetic and copies ran while one was open for 19% -> 19% of each run, Pallas kernels for 15% -> 14%
where the time goes in v5:
time: 1050 us; the launch traced here: 1040 us
  Pallas kernels  637 us (61%)
  waiting for transfers between devices  113 us (11%)
  matrix products  110 us (10%)
  local copies, waits for them, and re-layouts  108 us (10%)
  other arithmetic  64.7 us (6%)
    pallas_call x2, Pallas kernels, scatter_all(): pl.pallas_call(functools.partial(scatter_kernel, inner_h, sections, left_...  384 us
    pallas_call x1, Pallas kernels, gather_all(): pl.pallas_call(functools.partial(gather_kernel, n_h, jobs, len(shards), n...  253 us
    ppermute x23, waiting for transfers between devices, swap(): return lax.ppermute(value, axis, [(0, 1), (1, 0)])  113 us
    dot_general x5, matrix products, contract_cols(): lax.dot_general(left, right, (((1,), (1,)), ((), ())), preferred_element_...  50.3 us
    unnamed x183, local copies, waits for them, and re-layouts  33.7 us
    dot_general x4, matrix products, matmul(): return jnp.dot(left, right, preferred_element_type=jnp.float32)  27.5 us
  transfers between devices with their start and end apart: 23, of which 8 were waited for; matrix products, arithmetic and copies ran while one was open for 19% of the time, Pallas kernels for 14%

profile of v5, /device:TPU:0, one launch (start us, length us, event | category | flops | bytes accessed | tf_op | source)
XLA Modules:
  0.0 1044.4 jit_solution(1528523258192948834)
XLA Ops:
  1.6 2.1 pad.24.refs_0_
  3.7 2.1 pad.26.refs_5_
  11.1 1.9 multiply_sine_fusion.1
  13.1 252.6 %shard_map.238 = (bf16[2,2,2,128,13568]{4,3,2,1,0:T(8,128)(2,1)}, bf16[2,2,2,128,3200]{4,3,2,1,0:T(8,128)(2,1)}, bf16[2,2,2,128,1024]{4,3,2,1,0:T(8,128)(2,1)}, ...) custom-call(bf16[32,13568]{1,0:T(8,128)(2,1)} %pad.24.refs_0_, ...), custom_call_target="tpu_custom_call" | custom-call | tf_op jit(solution)/shard_map/pallas_call | solution.py:206
  265.7 18.4 %fusion.86 = (f32[256]{0:T(256)S(1)}, f32[256,1024]{0,1:T(8,128)S(1)}) fusion(f32[256,1024]{0,1:T(8,128)S(1)} %bitcast.321, bf16[1024,13568]{1,0:T(8,128)(2,1)} %bitcast.283, f32[256]{0:T(256)S(1)} %broadcast_divide_fusion, bf16[13500,256]{1,0:T(8,128)(2,1)} %bitcast.285), kind=kOutput, calls=%fused_computation.275 | convolution fusion | flops 7124484096 | bytes 36798464 | tf_op jit(solution)/shard_map/dot_general | solution.py:45
  287.3 5.0 fusion.39
  294.7 22.9 %collective-permute-done = bf16[256,2048]{1,0:T(8,128)(2,1)S(1)} collective-permute-done((bf16[256,2048]{1,0:T(8,128)(2,1)S(1)}, bf16[256,2048]{1,0:T(8,128)(2,1)S(1)}, u32[]{:S(2)}, u32[]{:S(2)}) %collective-permute-start) | collective-permute-done | bytes 1048608 | tf_op jit(solution)/shard_map/ppermute | solution.py:55
  317.6 1.6 pad_maximum_fusion.1
  319.7 4.2 pad.27.refs_2_
  323.9 1.9 slice.147
  325.8 2.0 copy.153
  328.7 1.8 collective-permute-start.3
  330.6 2.7 fusion.54
  333.9 2.5 fusion.83
  336.4 3.0 copy.154
  339.5 4.6 copy.152
  344.1 27.2 %collective-permute-done.2.refs_6_ = bf16[128,13568]{1,0:T(8,128)(2,1)} collective-permute-done((bf16[128,13568]{1,0:T(8,128)(2,1)}, bf16[128,13568]{1,0:T(8,128)(2,1)}, u32[]{:S(2)}, u32[]{:S(2)}) %collective-permute-start.2) | collective-permute-done | bytes 3473440 | tf_op jit(solution)/shard_map/ppermute | solution.py:55
  371.3 1.6 slice.126
  373.0 4.1 fusion.87
  377.1 3.8 fusion
  381.0 2.4 copy-done
  383.4 4.3 fusion.50
  388.2 18.9 %collective-permute-done.3.refs_5_ = bf16[128,13568]{1,0:T(8,128)(2,1)} collective-permute-done((bf16[128,13568]{1,0:T(8,128)(2,1)}, bf16[128,13568]{1,0:T(8,128)(2,1)}, u32[]{:S(2)}, u32[]{:S(2)}) %collective-permute-start.3) | collective-permute-done | bytes 3473440 | tf_op jit(solution)/shard_map/ppermute | solution.py:55
  407.1 2.5 fusion.88
  409.8 1.7 slice.127
  412.2 16.7 %multiply_convert_fusion.2 = (bf16[256,4096]{0,1:T(8,128)(2,1)S(1)}, f32[256,4096]{0,1:T(8,128)}, f32[256,4096]{0,1:T(8,128)}) fusion(bf16[256,1024]{0,1:T(8,128)(2,1)S(1)} %add_convert_fusion.3, bf16[1024,4096]{1,0:T(8,128)(2,1)} %bitcast.349), kind=kOutput, calls=%fused_computation.60 | convolution fusion | flops 2215641088 | bytes 19398656 | tf_op jit(solution)/shard_map/dot_general | solution.py:51
  428.9 14.9 %collective-permute-done.4 = bf16[128,6784]{1,0:T(8,128)(2,1)S(1)} collective-permute-done((bf16[128,6784]{1,0:T(8,128)(2,1)S(1)}, bf16[128,6784]{1,0:T(8,128)(2,1)S(1)}, u32[]{:S(2)}, u32[]{:S(2)}) %collective-permute-start.4) | collective-permute-done | bytes 1736736 | tf_op jit(solution)/shard_map/ppermute | solution.py:55
  443.8 7.0 collective-permute-done.5
  450.8 3.4 fusion.48
  463.2 2.5 constant_dynamic-slice_fusion.30
  468.1 149.8 %shard_map.239 = (f32[53,32,256]{2,1,0:T(8,128)}, bf16[13568,256]{1,0:T(8,128)(2,1)}, f32[1024,256]{1,0:T(8,128)}) custom-call(bf16[1,512,512]{2,1,0:T(8,128)(2,1)} %maximum_bitcast_fusion.refs_0_, bf16[256,1024]{1,0:T(8,128)(2,1)} %copy.160.refs_1_, bf16[13568,256]{1,0:T(8,128)(2,1)} %pad.27.refs_2_, bf16[13568,256]{1,0:T(8,128)(2,1)} %collective-permute-done.7.refs_3_, ...), custom_call_target="tpu_custom_call" | custom-call | tf_op jit(solution)/shard_map/pallas_call | solution.py:439
  625.4 15.8 %fusion.44 = (bf16[9216,256]{1,0:T(8,128)(2,1)}, f32[256,4096]{0,1:T(8,128)S(1)}) fusion(f32[256,4096]{0,1:T(8,128)} %get-tuple-element.196, bf16[4096,1024]{1,0:T(8,128)(2,1)} %bitcast.351, f32[1024,256]{1,0:T(8,128)S(1)} %dynamic-slice_dynamic-update-slice_fusion), kind=kOutput, calls=%fused_computation.85 | convolution fusion | flops 2222981120 | bytes 19922944 | tf_op jit(solution)/shard_map/dot_general | solution.py:45
  641.2 8.8 fusion.89
  650.1 1.6 copy.164
  651.6 1.7 multiply_reduce_fusion.4
  659.5 1.6 convolution_convert_fusion
  661.0 2.0 copy.165
  664.2 11.6 %multiply_reduce_fusion = (f32[16,256]{1,0:T(8,128)}, f32[16,256,1024]{2,1,0:T(8,128)}) fusion(f32[16,256,1024]{2,1,0:T(8,128)} %copy-done, f32[16,256]{1,0:T(8,128)S(1)} %log_add_fusion, bf16[256,16,64]{0,2,1:T(8,128)(2,1)S(1)} %bitcast.305, bf16[1024,16,64]{0,2,1:T(8,128)(2,1)S(1)} %bitcast.292), kind=kOutput, calls=%fused_computation.1 | convolution fusion | flops 549449728 | bytes 36208640 | tf_op jit(solution)/shard_map/qhd,khd->hqk/dot_general | solution.py:646
  675.8 7.7 convert_bitcast_fusion
  683.5 2.8 concatenate.130
  686.3 11.9 %multiply_convert_fusion = bf16[16,256,1024]{2,1,0:T(8,128)(2,1)S(1)} fusion(f32[16,256,1024]{2,1,0:T(8,128)} %get-tuple-element.202, f32[16,256,1024]{2,1,0:T(8,128)} %copy-done, f32[16,256]{1,0:T(8,128)} %get-tuple-element.201, f32[16,256]{1,0:T(8,128)S(1)} %log_add_fusion), kind=kLoop, calls=%fused_computation | loop fusion | flops 16777216 | bytes 41975808 | tf_op jit(solution)/shard_map/convert_element_type | solution.py:648
  698.1 3.4 copy-done.1
  701.5 1.6 fusion.47
  703.1 2.9 concatenate.129
  706.0 2.0 copy_dynamic-update-slice_fusion.1
  708.1 2.0 copy_dynamic-update-slice_fusion
  710.1 1.6 dynamic-slice_bitcast_fusion
  711.8 8.0 log-plus-one_convert_fusion.refs_8_
  721.3 6.9 collective-permute-done.12
  729.3 1.5 pad_maximum_fusion.2
  733.7 1.7 copy-done.13
  735.4 2.1 fusion.16
  737.8 3.6 slice_bitcast_fusion
  741.8 1.7 slice-done.1
  744.1 2.7 fusion.49
  748.2 15.0 %collective-permute-done.17 = bf16[256,2048]{0,1:T(8,128)(2,1)S(1)} collective-permute-done((bf16[256,2048]{0,1:T(8,128)(2,1)S(1)}, bf16[256,2048]{0,1:T(8,128)(2,1)S(1)}, u32[]{:S(2)}, u32[]{:S(2)}) %collective-permute-start.17) | collective-permute-done | bytes 1048608 | tf_op jit(solution)/shard_map/ppermute | solution.py:55
  764.7 5.7 fusion.90
  770.4 1.6 copy.169
  775.5 2.8 slice_bitcast_fusion.1
  781.0 234.6 %shard_map.240 = (f32[102,32,256]{2,1,0:T(8,128)}, f32[13568,256]{1,0:T(8,128)}) custom-call(bf16[9,512,512]{2,1,0:T(8,128)(2,1)} %fusion.65.refs_0_, bf16[256,1024]{1,0:T(8,128)(2,1)} %copy.174.refs_1_, bf16[9216,256]{1,0:T(8,128)(2,1)} %get-tuple-element.94.refs_2_, bf16[9216,256]{1,0:T(8,128)(2,1)} %collective-permute-done.20.refs_3_, ...), custom_call_target="tpu_custom_call" | custom-call | tf_op jit(solution)/shard_map/pallas_call | solution.py:439
  1015.7 1.6 slice_bitcast_fusion.3
  1018.5 1.6 slice_bitcast_fusion.6
  1021.1 1.6 slice_reduce_fusion
  1022.8 12.2 %bitcast_divide_fusion = f32[256,13500]{0,1:T(8,128)} fusion(bf16[256,13500]{0,1:T(8,128)(2,1)} %param.15, f32[13568,256]{1,0:T(8,128)} %get-tuple-element.47, f32[256]{0:T(256)S(1)} %copy-done.51), kind=kLoop, calls=%fused_computation.8 | loop fusion | flops 17280000 | bytes 34562048 | tf_op jit(solution)/shard_map/div | solution.py:699
  (313 shorter events, 67.4 us)
Async XLA Ops:
  0.6 7.2 copy-start.36
  0.7 8.4 copy-start.45
  0.7 9.6 copy-start.66
  0.7 9.6 copy-start.65
  0.7 9.6 copy-start.64
  0.7 9.6 copy-start.63
  0.7 9.7 copy-start.62
  0.7 9.7 copy-start.39
  10.4 273.7 %copy-start.49 = (f32[256]{0:T(256)}, f32[256]{0:T(256)S(1)}, u32[]{:S(2)}) copy-start(f32[256]{0:T(256)S(1)} %broadcast_divide_fusion) | copy-start | bytes 3076
  284.2 122.9 %copy-start.2 = (f32[256,1024]{0,1:T(8,128)}, f32[256,1024]{0,1:T(8,128)S(1)}, u32[]{:S(2)}) copy-start(f32[256,1024]{0,1:T(8,128)S(1)} %get-tuple-element.191) | copy-start | bytes 3145732
  284.2 8.1 copy-start.46
  284.4 7.9 copy-start.53
  286.3 125.5 %copy-start.44 = (f32[1,1024]{1,0:T(1,128)}, f32[1,1024]{1,0:T(1,128)S(1)}, u32[]{:S(2)}) copy-start(f32[1,1024]{1,0:T(1,128)S(1)} %get-tuple-element.170) | copy-start | bytes 12292
  286.9 32.8 %slice-start.4 = ((s8[6914048]{0:T(1024)(128)(4,1)}), s8[4194304]{0:T(1024)(128)(4,1)S(1)}, s32[]{:S(2)}) async-start(s8[6914048]{0:T(1024)(128)(4,1)} %bitcast.300), calls=%async_computation.4 | async-start | bytes 8388608
  287.2 32.5 %slice-start.5 = ((s8[6914048]{0:T(1024)(128)(4,1)}), s8[2719744]{0:T(1024)(128)(4,1)S(1)}, s32[]{:S(2)}) async-start(s8[6914048]{0:T(1024)(128)(4,1)} %bitcast.300), calls=%async_computation.5 | async-start | bytes 5439488
  292.3 26.9 %copy-start.25 = (bf16[256,3072]{1,0:T(8,128)(2,1)}, bf16[256,3072]{1,0:T(8,128)(2,1)S(1)}, u32[]{:S(2)}) copy-start(bf16[256,3072]{1,0:T(8,128)(2,1)S(1)} %fusion.39) | copy-start | bytes 4718596
  292.4 25.2 %collective-permute-start = (bf16[256,2048]{1,0:T(8,128)(2,1)S(1)}, bf16[256,2048]{1,0:T(8,128)(2,1)S(1)}, u32[]{:S(2)}, u32[]{:S(2)}) collective-permute-start(bf16[256,2048]{1,0:T(8,128)(2,1)S(1)} %get-tuple-element.137), channel_id=1, source_target_pairs={{0,2},{2,0},{1,3},{3,1},{4,6},{6,4},{5,7},{7,5},{8,10},{10,8},{9,1... | collective-permute-start | bytes 3145736 | tf_op jit(solution)/shard_map/ppermute | solution.py:55
  293.9 77.4 %collective-permute-start.2 = (bf16[128,13568]{1,0:T(8,128)(2,1)}, bf16[128,13568]{1,0:T(8,128)(2,1)}, u32[]{:S(2)}, u32[]{:S(2)}) collective-permute-start(bf16[128,13568]{1,0:T(8,128)(2,1)} %get-tuple-element.35.refs_4_), channel_id=1, source_target_pairs={{0,4},{4,0},{1,5},{5,1},{2,6},{6,2},{3,7},{7,3},{8,12},{12,8},{9,1... | collective-permute-start | bytes 10420232 | tf_op jit(solution)/shard_map/ppermute | solution.py:55
  319.2 11.4 %collective-permute-start.1 = (bf16[2,256,2048]{2,1,0:T(8,128)(2,1)}, bf16[2,256,2048]{2,1,0:T(8,128)(2,1)}, u32[]{:S(2)}, u32[]{:S(2)}) collective-permute-start(bf16[2,256,2048]{2,1,0:T(8,128)(2,1)} %get-tuple-element.134), channel_id=1, source_target_pairs={{0,1},{1,0},{2,3},{3,2},{4,5},{5,4},{6,7},{7,6},{8,9},{9,8},{10,11... | collective-permute-start | bytes 6291464 | tf_op jit(solution)/shard_map/ppermute | solution.py:55
  319.2 148.4 %collective-permute-start.8 = (bf16[128,13568]{1,0:T(8,128)(2,1)}, bf16[128,13568]{1,0:T(8,128)(2,1)}, u32[]{:S(2)}, u32[]{:S(2)}) collective-permute-start(bf16[128,13568]{1,0:T(8,128)(2,1)} %get-tuple-element.35.refs_4_), channel_id=1, source_target_pairs={{0,1},{1,0},{2,3},{3,2},{4,5},{5,4},{6,7},{7,6},{8,9},{9,8},{10,11... | collective-permute-start | bytes 10420232 | tf_op jit(solution)/shard_map/ppermute | solution.py:55
  323.9 144.2 %collective-permute-start.7 = (bf16[13568,256]{1,0:T(8,128)(2,1)}, bf16[13568,256]{1,0:T(8,128)(2,1)}, u32[]{:S(2)}, u32[]{:S(2)}) collective-permute-start(bf16[13568,256]{1,0:T(8,128)(2,1)} %pad.27.refs_2_), channel_id=1, source_target_pairs={{0,1},{1,0},{2,3},{3,2},{4,5},{5,4},{6,7},{7,6},{8,9},{9,8},{10,11... | collective-permute-start | bytes 20840456 | tf_op jit(solution)/shard_map/ppermute | solution.py:55
  328.7 78.3 %collective-permute-start.3 = (bf16[128,13568]{1,0:T(8,128)(2,1)}, bf16[128,13568]{1,0:T(8,128)(2,1)}, u32[]{:S(2)}, u32[]{:S(2)}) collective-permute-start(bf16[128,13568]{1,0:T(8,128)(2,1)} %get-tuple-element.35.refs_4_), channel_id=1, source_target_pairs={{0,2},{2,0},{1,3},{3,1},{4,6},{6,4},{5,7},{7,5},{8,10},{10,8},{9,1... | collective-permute-start | bytes 10420232 | tf_op jit(solution)/shard_map/ppermute | solution.py:55
  339.5 37.6 %copy-start.4 = (bf16[1024,1024]{0,1:T(8,128)(2,1)}, bf16[1024,1024]{0,1:T(8,128)(2,1)S(1)}, u32[]{:S(2)}) copy-start(bf16[1024,1024]{0,1:T(8,128)(2,1)S(1)} %copy.154) | copy-start | bytes 6291460
  372.9 94.7 %collective-permute-start.10 = (bf16[128,13568]{1,0:T(8,128)(2,1)}, bf16[128,13568]{1,0:T(8,128)(2,1)}, u32[]{:S(2)}, u32[]{:S(2)}) collective-permute-start(bf16[128,13568]{1,0:T(8,128)(2,1)} %collective-permute-done.2.refs_6_), channel_id=1, source_target_pairs={{0,1},{1,0},{2,3},{3,2},{4,5},{5,4},{6,7},{7,6},{8,9},{9,8},{10,11... | collective-permute-start | bytes 10420232 | tf_op jit(solution)/shard_map/ppermute | solution.py:55
  387.8 21.8 %copy-start.14 = (bf16[256,4,2,2,2,32]{0,5,1,3,2,4:T(8,128)(2,1)}, bf16[256,4,2,2,2,32]{0,5,1,3,2,4:T(8,128)(2,1)S(1)}, u32[]{:S(2)}) copy-start(bf16[256,4,2,2,2,32]{0,5,1,3,2,4:T(8,128)(2,1)S(1)} %copy.155) | copy-start | bytes 1572868
  387.8 56.0 %collective-permute-start.4 = (bf16[128,6784]{1,0:T(8,128)(2,1)S(1)}, bf16[128,6784]{1,0:T(8,128)(2,1)S(1)}, u32[]{:S(2)}, u32[]{:S(2)}) collective-permute-start(bf16[128,6784]{1,0:T(8,128)(2,1)S(1)} %slice.126), channel_id=1, source_target_pairs={{0,2},{2,0},{1,3},{3,1},{4,6},{6,4},{5,7},{7,5},{8,10},{10,8},{9,1... | collective-permute-start | bytes 5210120 | tf_op jit(solution)/shard_map/ppermute | solution.py:55
  409.6 19.2 %copy-start.48 = (f32[256]{0:T(256)}, f32[256]{0:T(256)S(1)}, u32[]{:S(2)}) copy-start(f32[256]{0:T(256)S(1)} %broadcast_multiply_fusion) | copy-start | bytes 3076
  409.8 19.1 %copy-start.57 = (f32[256]{0:T(256)}, f32[256]{0:T(256)S(1)}, u32[]{:S(2)}) copy-start(f32[256]{0:T(256)S(1)} %multiply_reduce_fusion.5) | copy-start | bytes 3076
  409.8 19.1 %copy-start.52 = (f32[256]{0:T(256)}, f32[256]{0:T(256)S(1)}, u32[]{:S(2)}) copy-start(f32[256]{0:T(256)S(1)} %fusion.72) | copy-start | bytes 3076
  409.8 40.9 %slice-start.8 = ((s8[8388608]{0:T(1024)(128)(4,1)}), s8[4194304]{0:T(1024)(128)(4,1)S(1)}, s32[]{:S(2)}) async-start(s8[8388608]{0:T(1024)(128)(4,1)} %bitcast.352), calls=%async_computation.8 | async-start | bytes 8388608
  411.6 39.2 %collective-permute-start.5 = (bf16[128,6784]{1,0:T(8,128)(2,1)S(1)}, bf16[128,6784]{1,0:T(8,128)(2,1)S(1)}, u32[]{:S(2)}, u32[]{:S(2)}) collective-permute-start(bf16[128,6784]{1,0:T(8,128)(2,1)S(1)} %slice.127), channel_id=1, source_target_pairs={{0,4},{4,0},{1,5},{5,1},{2,6},{6,2},{3,7},{7,3},{8,12},{12,8},{9,1... | collective-permute-start | bytes 5210120 | tf_op jit(solution)/shard_map/ppermute | solution.py:55
  412.2 16.7 %copy-start.22 = (bf16[256,1024]{0,1:T(8,128)(2,1)}, bf16[256,1024]{0,1:T(8,128)(2,1)S(1)}, u32[]{:S(2)}) copy-start(bf16[256,1024]{0,1:T(8,128)(2,1)S(1)} %add_convert_fusion.3) | copy-start | bytes 1572868
  412.2 38.6 %slice-start.9 = ((s8[8388608]{0:T(1024)(128)(4,1)}), s8[4194304]{0:T(1024)(128)(4,1)S(1)}, s32[]{:S(2)}) async-start(s8[8388608]{0:T(1024)(128)(4,1)} %bitcast.352), calls=%async_computation.9 | async-start | bytes 8388608
  428.9 25.2 %copy-start.19 = (bf16[256,4096]{0,1:T(8,128)(2,1)}, bf16[256,4096]{0,1:T(8,128)(2,1)S(1)}, u32[]{:S(2)}) copy-start(bf16[256,4096]{0,1:T(8,128)(2,1)S(1)} %get-tuple-element.41) | copy-start | bytes 6291460
  443.8 24.4 %collective-permute-start.9 = (bf16[128,13568]{1,0:T(8,128)(2,1)}, bf16[128,13568]{1,0:T(8,128)(2,1)}, u32[]{:S(2)}, u32[]{:S(2)}) collective-permute-start(bf16[128,13568]{1,0:T(8,128)(2,1)} %collective-permute-done.3.refs_5_), channel_id=1, source_target_pairs={{0,1},{1,0},{2,3},{3,2},{4,5},{5,4},{6,7},{7,6},{8,9},{9,8},{10,11... | collective-permute-start | bytes 10420232 | tf_op jit(solution)/shard_map/ppermute | solution.py:55
  456.8 2.7 collective-permute-start.6
  460.3 7.8 collective-permute-start.11
  467.6 264.3 %collective-permute-start.15 = (bf16[256,512]{0,1:T(8,128)(2,1)}, bf16[256,512]{0,1:T(8,128)(2,1)}, u32[]{:S(2)}, u32[]{:S(2)}) collective-permute-start(bf16[256,512]{0,1:T(8,128)(2,1)} %pad_maximum_fusion.10), channel_id=1, source_target_pairs={{0,1},{1,0},{2,3},{3,2},{4,5},{5,4},{6,7},{7,6},{8,9},{9,8},{10,11... | collective-permute-start | bytes 786440 | tf_op jit(solution)/shard_map/ppermute | solution.py:55
  467.6 261.6 %collective-permute-start.13 = (bf16[256,2048]{0,1:T(8,128)(2,1)}, bf16[256,2048]{0,1:T(8,128)(2,1)}, u32[]{:S(2)}, u32[]{:S(2)}) collective-permute-start(bf16[256,2048]{0,1:T(8,128)(2,1)} %pad_maximum_fusion.5), channel_id=1, source_target_pairs={{0,1},{1,0},{2,3},{3,2},{4,5},{5,4},{6,7},{7,6},{8,9},{9,8},{10,11... | collective-permute-start | bytes 3145736 | tf_op jit(solution)/shard_map/ppermute | solution.py:55
  625.4 15.9 %copy-start.67 = (f32[256,4096]{0,1:T(8,128)S(1)}, f32[256,4096]{0,1:T(8,128)}, u32[]{:S(2)}) copy-start(f32[256,4096]{0,1:T(8,128)} %get-tuple-element.117) | copy-start | bytes 12582916
  625.4 15.9 %copy-start.68 = (f32[256,4096]{0,1:T(8,128)S(1)}, f32[256,4096]{0,1:T(8,128)}, u32[]{:S(2)}) copy-start(f32[256,4096]{0,1:T(8,128)} %get-tuple-element.196) | copy-start | bytes 12582916
  686.3 15.3 %copy-start.12 = (bf16[256,1024]{0,1:T(8,128)(2,1)S(1)}, bf16[256,1024]{0,1:T(8,128)(2,1)}, u32[]{:S(2)}) copy-start(bf16[256,1024]{0,1:T(8,128)(2,1)} %copy.153) | copy-start | bytes 1572868
  710.1 9.7 copy-start.6
  711.8 8.6 copy-start.23
  711.8 9.4 copy-start.15
  711.8 22.0 %collective-permute-start.16 = (bf16[2,256,2048]{1,2,0:T(8,128)(2,1)}, bf16[2,256,2048]{1,2,0:T(8,128)(2,1)}, u32[]{:S(2)}, u32[]{:S(2)}) collective-permute-start(bf16[2,256,2048]{1,2,0:T(8,128)(2,1)} %dynamic-slice_bitcast_fusion), channel_id=1, source_target_pairs={{0,1},{1,0},{2,3},{3,2},{4,5},{5,4},{6,7},{7,6},{8,9},{9,8},{10,11... | collective-permute-start | bytes 6291464 | tf_op jit(solution)/shard_map/ppermute | solution.py:55
  719.8 9.5 copy-start.26
  719.8 9.5 copy-start.27
  719.8 9.5 copy-start.28
  719.8 61.2 %collective-permute-start.22 = (bf16[13568,256]{1,0:T(8,128)(2,1)}, bf16[13568,256]{1,0:T(8,128)(2,1)}, u32[]{:S(2)}, u32[]{:S(2)}) collective-permute-start(bf16[13568,256]{1,0:T(8,128)(2,1)} %log-plus-one_convert_fusion.refs_8_), channel_id=1, source_target_pairs={{0,1},{1,0},{2,3},{3,2},{4,5},{5,4},{6,7},{7,6},{8,9},{9,8},{10,11... | collective-permute-start | bytes 20840456 | tf_op jit(solution)/shard_map/ppermute | solution.py:55
  720.4 7.7 collective-permute-start.12
  728.1 3.7 collective-permute-start.14
  729.3 8.5 slice-start.6
  731.1 6.6 slice-start.7
  733.3 47.8 %collective-permute-start.20 = (bf16[9216,256]{1,0:T(8,128)(2,1)}, bf16[9216,256]{1,0:T(8,128)(2,1)}, u32[]{:S(2)}, u32[]{:S(2)}) collective-permute-start(bf16[9216,256]{1,0:T(8,128)(2,1)} %get-tuple-element.94.refs_2_), channel_id=1, source_target_pairs={{0,1},{1,0},{2,3},{3,2},{4,5},{5,4},{6,7},{7,6},{8,9},{9,8},{10,11... | collective-permute-start | bytes 14155784 | tf_op jit(solution)/shard_map/ppermute | solution.py:55
  737.7 25.5 %collective-permute-start.17 = (bf16[256,2048]{0,1:T(8,128)(2,1)S(1)}, bf16[256,2048]{0,1:T(8,128)(2,1)S(1)}, u32[]{:S(2)}, u32[]{:S(2)}) collective-permute-start(bf16[256,2048]{0,1:T(8,128)(2,1)S(1)} %dynamic-slice_bitcast_fusion.1), channel_id=1, source_target_pairs={{0,2},{2,0},{1,3},{3,1},{4,6},{6,4},{5,7},{7,5},{8,10},{10,8},{9,1... | collective-permute-start | bytes 3145736 | tf_op jit(solution)/shard_map/ppermute | solution.py:55
  737.8 6.3 copy-start.5
  764.7 7.3 copy-start.3
  764.7 7.3 copy-start.43
  764.7 7.3 copy-start.47
  764.7 16.3 %collective-permute-start.21 = (bf16[3072,256]{1,0:T(8,128)(2,1)}, bf16[3072,256]{1,0:T(8,128)(2,1)}, u32[]{:S(2)}, u32[]{:S(2)}) collective-permute-start(bf16[3072,256]{1,0:T(8,128)(2,1)} %fusion.59.refs_4_), channel_id=1, source_target_pairs={{0,1},{1,0},{2,3},{3,2},{4,5},{5,4},{6,7},{7,6},{8,9},{9,8},{10,11... | collective-permute-start | bytes 4718600 | tf_op jit(solution)/shard_map/ppermute | solution.py:55
  774.5 5.6 collective-permute-start.19
  775.4 3.9 collective-permute-start.18
  1015.7 7.1 copy-start.51
  (38 other events, 139.0 us)

commit v6 on v5

--- a/solution.py
+++ b/solution.py
@@ -91,9 +91,8 @@
     pl.semaphore_wait(barrier, len(peers))
 
 
-def gather_kernel(n_h, jobs, n_arrays, n_full, *refs):
-    shards, wholes = refs[:n_arrays], refs[n_arrays : 2 * n_arrays]
-    own_sem, h_send, h_recv, send, recv = refs[2 * n_arrays :]
+def gather_kernel(n_h, jobs, n_full, shards, wholes, sems, between):
+    own_sem, h_send, h_recv, send, recv = sems
     h, x, y, c = (lax.axis_index(name) for name in ("h", "x", "y", "c"))
     h = 0 if n_h == 1 else h
     to_x, to_y, to_c = {"x": 1 - x}, {"y": 1 - y}, {"c": 1 - c}
@@ -153,6 +152,14 @@
         own_copy(j).start()
         for d in range(1, n_h):
             h_copy(j, d).start()
+
+    whole = set()
+
+    def landed(j):
+        if j not in whole:
+            whole.add(j)
+            for k in (2, 5, 6, 7):
+                copy(j, k).wait_recv()
 
     n = sum(array < n_full for array, *_ in jobs)
     ahead = 2
@@ -176,6 +183,7 @@
             for k in (3, 4):
                 copy(step - 2, k).wait_recv()
             copy(step - 2, 7).start()
+        between(step, landed)
     for j in range(n + ahead, len(jobs)):
         start_h(j)
     for j in range(n, len(jobs)):
@@ -188,11 +196,154 @@
     for j in range(n):
         for k in range(8):
             copy(j, k).wait_send()
-        for k in (2, 5, 6, 7):
-            copy(j, k).wait_recv()
-
-
-def gather_all(shards, n_full, cuts, order, collective_id):
+        landed(j)
+
+
+def front_kernel(n_h, jobs, n_arrays, n_full, *refs):
+    shards, (counts, tail, scale, pe) = refs[:n_arrays], refs[n_arrays : n_arrays + 4]
+    rest = refs[n_arrays + 4 :]
+    wholes, (xb, h0, a1, query, pairs) = rest[:n_arrays], rest[n_arrays : n_arrays + 5]
+    (count_buf, enc_buf, xb_buf, total, qkv_buf, mine, count_sem, enc_sem, xb_sem, qkv_sem, kv_sem,
+     kv_send, kv_recv, *sems) = rest[n_arrays + 5 :]
+    y, c = lax.axis_index("y"), lax.axis_index("c")
+    f32, b16 = jnp.float32, jnp.bfloat16
+    width = h0.shape[1]
+    n_chunks = xb.shape[0] // CHUNK
+    by_chunk = lambda k: pl.ds(pl.multiple_of(k * CHUNK, CHUNK), CHUNK)
+
+    def loads(k, last):
+        slot = lax.rem(k, 2)
+        source = tail if last else counts.at[by_chunk(k)]
+        return (
+            pltpu.make_async_copy(source, count_buf.at[slot], count_sem.at[slot]),
+            pltpu.make_async_copy(
+                wholes[0].at[:, :, :, :, by_chunk(k)], enc_buf.at[slot], enc_sem.at[slot]
+            ),
+        )
+
+    def store(k):
+        slot = lax.rem(k, 2)
+        return pltpu.make_async_copy(xb_buf.at[slot], xb.at[by_chunk(k)], xb_sem.at[slot])
+
+    def encode(k, first, last, low, high):
+        slot = lax.rem(k, 2)
+        for copy in loads(k, last):
+            copy.wait()
+        if not last:
+
+            @pl.when(k + 1 < (high - 1 if high == n_chunks else high))
+            def _():
+                for copy in loads(k + 1, False):
+                    copy.start()
+
+        @pl.when(k >= low + 2)
+        def _():
+            store(k - 2).wait()
+
+        value = jnp.log1p(count_buf[slot].astype(f32) * scale[...]).astype(b16)
+        xb_buf[slot] = value
+        store(k).start()
+        term = jnp.dot(enc_buf[slot].reshape(width, CHUNK), value, preferred_element_type=f32)
+        if first:
+
+            @pl.when(k == 0)
+            def _():
+                total[...] = pe[...] + term
+
+            @pl.when(k > 0)
+            def _():
+                total[...] += term
+
+        else:
+            total[...] += term
+
+    def encode_job(low, high):
+        low, high = low // CHUNK, high // CHUNK
+        stop = high - 1 if high == n_chunks else high
+        for copy in loads(jnp.int32(low), False):
+            copy.start()
+
+        def body(k, carry):
+            encode(k, low == 0, False, low, high)
+            return carry
+
+        lax.fori_loop(low, stop, body, 0)
+        if stop < high:
+            for copy in loads(jnp.int32(stop), True):
+                copy.start()
+            encode(jnp.int32(stop), False, True, low, high)
+        for k in range(max(low, high - 2), high):
+            store(jnp.int32(k)).wait()
+
+    def fetch_qkv():
+        return pltpu.make_async_copy(wholes[1], qkv_buf, qkv_sem.at[0])
+
+    def project():
+        fetch_qkv().wait()
+        vectors = qkv_buf[:, :, :, :, 3 * width :].reshape(width, 128).astype(f32)
+        value = total[...]
+        centred = value - jnp.mean(value, axis=0, keepdims=True)
+        variance = jnp.mean(centred * centred, axis=0, keepdims=True)
+        normed = centred * lax.rsqrt(variance + eps) * vectors[:, 0:1] + vectors[:, 1:2]
+        h0[...] = value.T
+        a1[...] = normed.T.astype(b16)
+
+        def tile(k):
+            weight = qkv_buf[:, :, :, :, by_chunk(k)].reshape(width, CHUNK)
+            return jnp.dot(a1[...], weight, preferred_element_type=f32).astype(b16)
+
+        def keys(k, carry):
+            mine[:, by_chunk(k)] = tile(k + width // CHUNK)
+            return carry
+
+        lax.fori_loop(0, 2 * width // CHUNK, keys, 0)
+        kv_own().start()
+        kv_copy(0).start()
+
+        def queries(k, carry):
+            query[:, by_chunk(k)] = tile(k)
+            return carry
+
+        lax.fori_loop(0, width // CHUNK, queries, 0)
+
+    def kv_own():
+        return pltpu.make_async_copy(mine, pairs.at[0, 0], kv_sem.at[0])
+
+    def kv_copy(k):
+        return pltpu.make_async_remote_copy(
+            src_ref=(mine, pairs.at[0])[k],
+            dst_ref=(pairs.at[0, 1], pairs.at[1])[k],
+            send_sem=kv_send.at[k],
+            recv_sem=kv_recv.at[k],
+            device_id=({"y": 1 - y}, {"c": 1 - c})[k],
+            device_id_type=MESH,
+        )
+
+    arrays = [array for array, *_ in jobs]
+    enc_jobs = [j for j, array in enumerate(arrays) if array == 0]
+    qkv_jobs = [j for j, array in enumerate(arrays) if array == 1]
+    at = max(qkv_jobs) + 3
+
+    def between(step, landed):
+        if step - 3 in enc_jobs:
+            landed(step - 3)
+            encode_job(*jobs[step - 3][1:3])
+        if step == at:
+            for j in qkv_jobs:
+                landed(j)
+            fetch_qkv().start()
+            project()
+        if step == at + 2:
+            kv_own().wait()
+            kv_copy(0).wait_recv()
+            kv_copy(1).start()
+
+    gather_kernel(n_h, jobs, n_full, shards, wholes, sems, between)
+    kv_copy(0).wait_send()
+    kv_copy(1).wait()
+
+
+def gather_all(shards, n_full, cuts, order, counts, scale, pe, collective_id):
     n_h = lax.axis_size("h")
     if any(shard.shape[0] % 16 for shard in shards):
         shards = [lax.all_gather(s, "h", axis=0, tiled=True) for s in shards]
@@ -203,17 +354,51 @@
         jobs.append((array, low, high, low + (high - low) // 256 * 128))
     n, others, dma = len(jobs), max(n_h - 1, 1), pltpu.SemaphoreType.DMA
     shapes = [(n_h * s.shape[0], s.shape[1]) for s in shards]
-    return pl.pallas_call(
-        functools.partial(gather_kernel, n_h, jobs, len(shards), n_full),
+    (genes, cells), width, padded = counts.shape, pe.shape[0], shards[0].shape[1]
+    tail = counts[genes // CHUNK * CHUNK :]
+    tail = jnp.pad(tail, ((0, CHUNK - tail.shape[0]), (0, 0)))
+    bf16, f32 = jnp.bfloat16, jnp.float32
+    vmem, hbm = pl.BlockSpec(memory_space=pltpu.VMEM), pl.BlockSpec(memory_space=pl.ANY)
+    out = pl.pallas_call(
+        functools.partial(front_kernel, n_h, jobs, len(shards), n_full),
         out_shape=[
-            jax.ShapeDtypeStruct((2, 2, 2) + shape if k < n_full else shape, jnp.bfloat16)
+            jax.ShapeDtypeStruct((2, 2, 2) + shape if k < n_full else shape, bf16)
             for k, shape in enumerate(shapes)
+        ]
+        + [
+            jax.ShapeDtypeStruct((padded, cells), bf16),
+            jax.ShapeDtypeStruct((cells, width), f32),
+            jax.ShapeDtypeStruct((cells, width), bf16),
+            jax.ShapeDtypeStruct((cells, width), bf16),
+            jax.ShapeDtypeStruct((2, 2, cells, 2 * width), bf16),
         ],
-        in_specs=[pl.BlockSpec(memory_space=pl.ANY)] * len(shards),
-        out_specs=[pl.BlockSpec(memory_space=pl.ANY)] * len(shards),
-        scratch_shapes=[dma((n,)), dma((n, others)), dma((n, others)), dma((n, 8)), dma((n, 8))],
-        compiler_params=pltpu.CompilerParams(collective_id=collective_id, has_side_effects=True),
-    )(*shards)
+        in_specs=[hbm] * (len(shards) + 2) + [vmem] * 2,
+        out_specs=[hbm] * (len(shards) + 1) + [vmem] * 3 + [hbm],
+        scratch_shapes=[
+            pltpu.VMEM((2, CHUNK, cells), bf16),
+            pltpu.VMEM((2, 2, 2, 2, width // 8, CHUNK), bf16),
+            pltpu.VMEM((2, CHUNK, cells), bf16),
+            pltpu.VMEM((width, cells), f32),
+            pltpu.VMEM((2, 2, 2, width // 8, shards[1].shape[1]), bf16),
+            pltpu.VMEM((cells, 2 * width), bf16),
+            dma((2,)),
+            dma((2,)),
+            dma((2,)),
+            dma((1,)),
+            dma((1,)),
+            dma((2,)),
+            dma((2,)),
+            dma((n,)),
+            dma((n, others)),
+            dma((n, others)),
+            dma((n, 8)),
+            dma((n, 8)),
+        ],
+        compiler_params=pltpu.CompilerParams(
+            collective_id=collective_id, has_side_effects=True, vmem_limit_bytes=60 * 2**20
+        ),
+    )(*shards, counts, tail, scale, pe)
+    return out[: len(shards)], *out[len(shards) :]
 
 
 def scatter_kernel(n_h, sections, left_starts, n_weights, with_sum, *refs):
@@ -473,39 +658,16 @@
     return part, *more
 
 
-def after(value, first):
-    return lax.optimization_barrier((value, first))
-
-
 def own_half(left):
     half = left.shape[1] // 2
     return jnp.concatenate([left[:, :half], swap(left[:, half:], "c")], axis=0)
 
 
-def gather_group(mine):
-    at_y, at_c = lax.axis_index("y"), lax.axis_index("c")
-    by_y = swap(mine, "y")
-    pair = jnp.stack([mine, by_y])
-    both = jnp.stack([pair, swap(pair, "c")])
-    order = [
-        lax.dynamic_index_in_dim(
-            lax.dynamic_index_in_dim(both, at_c ^ c, 0, False), at_y ^ y, 0, False
-        )
-        for y in range(2)
-        for c in range(2)
-    ]
-    return jnp.concatenate(order, axis=0), by_y
-
-
 def scatter_group(rows_all):
-    at_y, at_c = lax.axis_index("y"), lax.axis_index("c")
     part = rows_all.astype(jnp.bfloat16).reshape((2, 2, rows_all.shape[0] // 4, -1))
-    keep = lax.dynamic_index_in_dim(part, at_c, 1, False).astype(jnp.float32)
-    send = lax.dynamic_index_in_dim(part, 1 - at_c, 1, False)
-    part = (keep + swap(send, "c").astype(jnp.float32)).astype(jnp.bfloat16)
-    keep = lax.dynamic_index_in_dim(part, at_y, 0, False).astype(jnp.float32)
-    send = lax.dynamic_index_in_dim(part, 1 - at_y, 0, False)
-    return keep + swap(send, "y").astype(jnp.float32)
+    got = swap(part[1], "c").astype(jnp.float32)
+    part = (part[0].astype(jnp.float32) + got).astype(jnp.bfloat16)
+    return part[0].astype(jnp.float32) + swap(part[1], "y").astype(jnp.float32)
 
 
 def left_of(left, pieces):
@@ -549,23 +711,24 @@
     slots = rows * group_size
     scale = 10000.0 / library
     genes = counts.shape[1]
-    padded = -(-genes // 128) * 128
+    padded = -(-genes // CHUNK) * CHUNK
     counts_f = counts.astype(jnp.float32)
-    xb = jnp.pad(counts.T, ((0, padded - genes), (0, 0))).astype(jnp.float32)
-    xb = jnp.log1p(xb * scale[None, :]).astype(jnp.bfloat16)
-    xb_pair = both_cores(xb)
     cot = jnp.pad(cotangent.T, ((0, padded - genes), (0, 0)))
     cot_pair = both_cores(cot)
     pe = by_owner(positions(coords, width), 1)
     ends = jnp.cumsum(lengths[0])
-    place = jnp.arange(slots, dtype=jnp.int32)
+    group = [
+        (lax.axis_index("y") ^ by_y) * 2 + (lax.axis_index("c") ^ by_c)
+        for by_c in range(2)
+        for by_y in range(2)
+    ]
+    place = jnp.concatenate([at * rows + jnp.arange(rows, dtype=jnp.int32) for at in group])
     seg_all = jnp.sum((place[:, None] >= ends[None, :]).astype(jnp.int32), axis=1)
-    seg_mine = lax.dynamic_slice_in_dim(seg_all, (lax.axis_index("y") * 2 + lax.axis_index("c")) * rows, rows)
-    same = (seg_mine[:, None] == seg_all[None, :])[None]
+    same = (seg_all[:rows, None] == seg_all[None, :])[None]
     vectors = jnp.stack([gain_one, shift_one, gain_two, shift_two], axis=1)
     vectors = jnp.pad(vectors, ((0, 0), (0, 124)))
     pad = ((0, 0), (0, padded - genes))
-    quarter = -(-padded // 512) * 128
+    quarter = padded // CHUNK // 4 * CHUNK
     gene_cuts = [0, quarter, 2 * quarter, 3 * quarter, padded]
     shards = [
         jnp.pad(w_enc.T, pad),
@@ -578,23 +741,24 @@
     cuts = [gene_cuts, [0, width // 2 * 3, 3 * width + 128], [0, width]]
     cuts += [[0, 2 * width, 4 * width], [0, width // 2, width], [0, padded]]
     order = [(0, 0), (0, 1), (0, 2), (0, 3), (1, 0), (1, 1), (2, 0), (3, 0), (3, 1), (4, 0), (4, 1), (5, 0)]
-    gathered = gather_all(shards, 5, cuts, order, 0)
+    gathered, xb, h0, a1, query, kv_all = gather_all(
+        shards, 5, cuts, order, counts.T, scale[None, :], pe.T, 0
+    )
+    xb_pair = both_cores(xb)
     enc_all, qkv_all, out_all, up_all, down_all = (
         w.reshape(-1, w.shape[-1]) for w in gathered[:5]
     )
     vectors = qkv_all[:, 3 * width :].astype(jnp.float32).T
     qkv_all = qkv_all[:, : 3 * width]
     g1f, b1f, g2f, b2f = vectors[0], vectors[1], vectors[2], vectors[3]
-    h0 = contract_cols(xb.T, enc_all) + pe
-    a1 = layer_norm(h0, g1f, b1f).astype(jnp.bfloat16)
-    qkv = matmul(a1, qkv_all).astype(jnp.bfloat16)
-    query = qkv[:, :width].reshape(rows, heads, head_width)
-    kv_all, arrived = gather_group(qkv[:, width:])
+    query = query.reshape(rows, heads, head_width)
+    kv_all = kv_all.reshape(slots, -1)
     dec_own = gathered[5]
     middle = dec_own.shape[1] // 256 * 128
-    query, by_x = after(query, swap(dec_own, "x"))
-    by_y = swap(after(dec_own, arrived)[0], "y")
-    far_left = swap(by_x[:, :middle], "y")
+    by_x, by_y = swap(dec_own, "x"), swap(dec_own, "y")
+    far = (swap(by_x[:, :middle], "y"), swap(by_y[:, middle:], "x"))
+    dec_parts = [dec_own, by_y, by_x, jnp.concatenate(far, axis=1)]
+    dec_parts += [swap(part, "c") for part in dec_parts]
     keys = kv_all[:, :width].reshape(slots, heads, head_width)
     values = kv_all[:, width:].reshape(slots, heads, head_width)
 
@@ -612,15 +776,11 @@
     probs_b = (expo / total).astype(jnp.bfloat16)
     attended = jnp.einsum("hqk,khd->qhd", probs_b, values, preferred_element_type=jnp.float32)
     attended_b = attended.reshape(rows, width).astype(jnp.bfloat16)
-    attended_b, by_y = after(by_owner(attended_b, 1), by_y)
-    far_right = swap(by_y[:, middle:], "x")
+    attended_b = by_owner(attended_b, 1)
     h1 = h0 + matmul(attended_b, out_all)
     a2 = layer_norm(h1, g2f, b2f).astype(jnp.bfloat16)
     hidden = matmul(a2, up_all)
     act = jax.nn.gelu(hidden, approximate=False).astype(jnp.bfloat16)
-    act, far = after(act, (far_left, far_right))
-    dec_parts = [dec_own, by_y, by_x, jnp.concatenate(far, axis=1)]
-    dec_parts += [swap(part, "c") for part in dec_parts]
     h2 = h1 + matmul(act, down_all)
     hb = h2.astype(jnp.bfloat16)
     grad_dec, logits, dh2 = scatter_all(

time: 1050 us -> 1010 us (0.962)
  waiting for transfers between devices: 113 us -> 67.1 us
  Pallas kernels: 637 us -> 655 us
  matrix products: 110 us -> 92.9 us
    ppermute x23 -> x21, waiting for transfers between devices: 113 us -> 67.1 us  [swap(): return lax.ppermute(value, axis, [(0, 1), (1, 0)])]
    pallas_call x1, Pallas kernels: 253 us -> 285 us  [gather_all(): pl.pallas_call(functools.partial(front_kernel, n_h, jobs, len(shards), n_...]
    dot_general x5 -> x4, matrix products: 50.3 us -> 31.7 us  [contract_cols(): lax.dot_general(left, right, (((1,), (1,)), ((), ())), preferred_element_...]
    pallas_call x2, Pallas kernels: 384 us -> 370 us  [scatter_all(): pl.pallas_call(functools.partial(scatter_kernel, inner_h, sections, left_...]
    unnamed x183 -> x140, local copies, waits for them, and re-layouts: 33.7 us -> 24.5 us
    dot_general x4 -> x3, matrix products: 27.5 us -> 26.1 us  [matmul(): return jnp.dot(left, right, preferred_element_type=jnp.float32)]
  transfers between devices with their start and end apart: 23 -> 21, of which waited for: 8 -> 5; matrix products, arithmetic and copies ran while one was open for 19% -> 13% of each run, Pallas kernels for 14% -> 0%
where the time goes in v6:
time: 1010 us
  Pallas kernels  655 us (65%)
  local copies, waits for them, and re-layouts  118 us (12%)
  matrix products  92.9 us (9%)
  waiting for transfers between devices  67.1 us (7%)
  other arithmetic  60.1 us (6%)
  starting transfers between devices  10.3 us (1%)
    pallas_call x2, Pallas kernels, scatter_all(): pl.pallas_call(functools.partial(scatter_kernel, inner_h, sections, left_...  370 us
    pallas_call x1, Pallas kernels, gather_all(): pl.pallas_call(functools.partial(front_kernel, n_h, jobs, len(shards), n_...  285 us
    ppermute x21, waiting for transfers between devices, swap(): return lax.ppermute(value, axis, [(0, 1), (1, 0)])  67.1 us
    dot_general x4, matrix products, contract_cols(): lax.dot_general(left, right, (((1,), (1,)), ((), ())), preferred_element_...  31.7 us
    dot_general x3, matrix products, matmul(): return jnp.dot(left, right, preferred_element_type=jnp.float32)  26.1 us
    unnamed x140, local copies, waits for them, and re-layouts  24.5 us
  transfers between devices with their start and end apart: 21, of which 5 were waited for; matrix products, arithmetic and copies ran while one was open for 13% of the time, Pallas kernels for 0%

profile of v6, /device:TPU:0, one launch (start us, length us, event | category | flops | bytes accessed | tf_op | source)
XLA Modules:
  0.0 1005.8 jit_solution(5432508926937315745)
XLA Ops:
  4.4 2.1 pad.24.refs_0_
  6.6 2.1 pad.26.refs_5_
  13.9 1.9 multiply_sine_fusion.1
  16.9 284.6 %shard_map.238 = (bf16[2,2,2,128,13568]{4,3,2,1,0:T(8,128)(2,1)}, bf16[2,2,2,128,3200]{4,3,2,1,0:T(8,128)(2,1)}, bf16[2,2,2,128,1024]{4,3,2,1,0:T(8,128)(2,1)}, ...) custom-call(bf16[32,13568]{1,0:T(8,128)(2,1)} %pad.24.refs_0_, ...), custom_call_target="tpu_custom_call" | custom-call | tf_op jit(solution)/shard_map/pallas_call | solution.py:362
  301.6 2.1 collective-permute-start.2
  303.6 7.7 pad.28.refs_2_
  312.5 4.7 fusion.69
  317.2 2.9 copy.185
  320.4 4.6 copy.183
  325.2 3.0 fusion.72
  328.3 3.8 fusion
  332.1 2.4 copy-done
  334.6 4.6 fusion.45
  339.6 2.9 fusion.73
  345.1 16.4 %multiply_convert_fusion.2 = (bf16[256,4096]{0,1:T(8,128)(2,1)S(1)}, f32[256,4096]{0,1:T(8,128)}, f32[256,4096]{0,1:T(8,128)}) fusion(bf16[256,1024]{0,1:T(8,128)(2,1)S(1)} %add_convert_fusion.4, bf16[1024,4096]{1,0:T(8,128)(2,1)} %bitcast.339), kind=kOutput, calls=%fused_computation.49 | convolution fusion | flops 2215641088 | bytes 19398656 | tf_op jit(solution)/shard_map/dot_general | solution.py:51
  361.6 17.7 %collective-permute-done.3.refs_6_ = bf16[128,13568]{1,0:T(8,128)(2,1)} collective-permute-done((bf16[128,13568]{1,0:T(8,128)(2,1)}, bf16[128,13568]{1,0:T(8,128)(2,1)}, u32[]{:S(2)}, u32[]{:S(2)}) %collective-permute-start.3) | collective-permute-done | bytes 3473440 | tf_op jit(solution)/shard_map/ppermute | solution.py:55
  379.3 1.6 slice.163
  381.2 6.7 fusion.43
  388.0 1.6 slice.164
  389.6 1.8 collective-permute-start.5
  392.9 27.4 %collective-permute-done.4 = bf16[128,6784]{1,0:T(8,128)(2,1)S(1)} collective-permute-done((bf16[128,6784]{1,0:T(8,128)(2,1)S(1)}, bf16[128,6784]{1,0:T(8,128)(2,1)S(1)}, u32[]{:S(2)}, u32[]{:S(2)}) %collective-permute-start.4) | collective-permute-done | bytes 1736736 | tf_op jit(solution)/shard_map/ppermute | solution.py:55
  421.6 7.4 collective-permute-done.5
  431.5 2.0 copy.193.refs_1_
  435.6 1.7 maximum_bitcast_fusion.refs_0_
  437.3 3.1 collective-permute-done.9.refs_11_
  440.4 133.6 %shard_map.239 = (f32[53,32,256]{2,1,0:T(8,128)}, bf16[13568,256]{1,0:T(8,128)(2,1)}, f32[1024,256]{1,0:T(8,128)}) custom-call(bf16[1,512,512]{2,1,0:T(8,128)(2,1)} %maximum_bitcast_fusion.refs_0_, bf16[256,1024]{1,0:T(8,128)(2,1)} %copy.193.refs_1_, bf16[13568,256]{1,0:T(8,128)(2,1)} %pad.28.refs_2_, bf16[13568,256]{1,0:T(8,128)(2,1)} %collective-permute-done.1.refs_3_, ...), custom_call_target="tpu_custom_call" | custom-call | tf_op jit(solution)/shard_map/pallas_call | solution.py:624
  581.5 15.6 %fusion.39 = (bf16[9216,256]{1,0:T(8,128)(2,1)}, f32[256,4096]{0,1:T(8,128)S(1)}) fusion(f32[256,4096]{0,1:T(8,128)} %get-tuple-element.185, bf16[4096,1024]{1,0:T(8,128)(2,1)} %bitcast.342, f32[1024,256]{1,0:T(8,128)S(1)} %dynamic-slice_dynamic-update-slice_fusion), kind=kOutput, calls=%fused_computation.70 | convolution fusion | flops 2222981120 | bytes 19922944 | tf_op jit(solution)/shard_map/dot_general | solution.py:45
  597.1 8.8 fusion.74
  605.9 1.6 copy.206
  612.7 1.6 convolution_convert_fusion
  614.3 2.0 copy.207
  617.5 13.9 %multiply_reduce_fusion = (f32[16,256]{1,0:T(8,128)S(1)}, f32[16,256,1024]{2,1,0:T(8,128)}) fusion(f32[16,256,1024]{2,1,0:T(8,128)} %copy-done, f32[16,256]{1,0:T(8,128)S(1)} %log_add_fusion, bf16[256,16,64]{0,2,1:T(8,128)(2,1)S(1)} %bitcast.293, bf16[1024,16,64]{0,2,1:T(8,128)(2,1)S(1)} %bitcast.281), kind=kOutput, calls=%fused_computation.1 | convolution fusion | flops 549449728 | bytes 36208640 | tf_op jit(solution)/shard_map/qhd,khd->hqk/dot_general | solution.py:806
  631.4 9.3 fusion.40
  640.7 7.8 multiply_convert_fusion
  648.5 1.6 multiply_convert_fusion.1
  650.1 1.8 copy-done.1
  651.9 2.6 copy.209
  654.5 3.9 copy.210
  658.5 3.3 pad_maximum_fusion
  661.8 3.9 copy.211
  665.7 2.2 pad_maximum_fusion.4
  668.4 2.0 copy.195
  670.5 1.7 constant_dynamic-slice_fusion.15
  673.0 1.8 constant_dynamic-slice_fusion.23
  676.0 1.8 constant_dynamic-slice_fusion.39
  681.1 1.9 fusion.48
  682.9 1.6 pad_maximum_fusion.1
  684.8 1.5 constant_dynamic-update-slice_fusion.10
  686.3 1.8 fusion.49
  688.1 1.8 fusion.50
  689.9 2.9 copy.212
  692.8 3.3 add_convert_fusion
  696.3 2.7 collective-permute-start.15
  699.0 8.1 slice_bitcast_fusion
  707.2 2.7 fusion.44
  711.2 11.6 %collective-permute-done.15 = bf16[256,2048]{0,1:T(8,128)(2,1)S(1)} collective-permute-done((bf16[256,2048]{0,1:T(8,128)(2,1)S(1)}, bf16[256,2048]{0,1:T(8,128)(2,1)S(1)}, u32[]{:S(2)}, u32[]{:S(2)}) %collective-permute-start.15) | collective-permute-done | bytes 1048608 | tf_op jit(solution)/shard_map/ppermute | solution.py:55
  724.3 5.7 fusion.75
  730.0 1.6 copy.213
  735.1 2.8 slice_bitcast_fusion.1
  740.6 236.4 %shard_map.240 = (f32[102,32,256]{2,1,0:T(8,128)}, f32[13568,256]{1,0:T(8,128)}) custom-call(bf16[9,512,512]{2,1,0:T(8,128)(2,1)} %fusion.52.refs_0_, bf16[256,1024]{1,0:T(8,128)(2,1)} %copy.218.refs_1_, bf16[9216,256]{1,0:T(8,128)(2,1)} %get-tuple-element.90.refs_2_, bf16[9216,256]{1,0:T(8,128)(2,1)} %collective-permute-done.18.refs_3_, ...), custom_call_target="tpu_custom_call" | custom-call | tf_op jit(solution)/shard_map/pallas_call | solution.py:624
  977.0 1.6 slice_bitcast_fusion.3
  979.9 1.6 slice_bitcast_fusion.8
  982.5 1.7 slice_reduce_fusion
  984.2 12.2 %bitcast_divide_fusion = f32[256,13500]{0,1:T(8,128)} fusion(bf16[256,13500]{0,1:T(8,128)(2,1)} %param.15, f32[13568,256]{1,0:T(8,128)} %get-tuple-element.41, f32[256]{0:T(256)S(1)} %copy-done.40), kind=kLoop, calls=%fused_computation.7 | loop fusion | flops 17280000 | bytes 34562048 | tf_op jit(solution)/shard_map/div | solution.py:859
  (260 shorter events, 61.9 us)
Async XLA Ops:
  0.6 10.0 copy-start.28
  0.7 11.2 %copy-start.35 = (bf16[32,1024]{1,0:T(8,128)(2,1)S(1)}, bf16[32,1024]{1,0:T(8,128)(2,1)}, u32[]{:S(2)}) copy-start(bf16[32,1024]{1,0:T(8,128)(2,1)} %param.22) | copy-start | bytes 196612
  0.7 12.4 %copy-start.49 = (bf16[32]{0:T(256)(128)(2,1)S(1)}, bf16[32]{0:T(256)(128)(2,1)}, u32[]{:S(2)}) copy-start(bf16[32]{0:T(256)(128)(2,1)} %param.23) | copy-start | bytes 196
  0.7 12.4 %copy-start.48 = (bf16[32]{0:T(256)(128)(2,1)S(1)}, bf16[32]{0:T(256)(128)(2,1)}, u32[]{:S(2)}) copy-start(bf16[32]{0:T(256)(128)(2,1)} %param.24) | copy-start | bytes 196
  0.7 12.4 %copy-start.47 = (bf16[32]{0:T(256)(128)(2,1)S(1)}, bf16[32]{0:T(256)(128)(2,1)}, u32[]{:S(2)}) copy-start(bf16[32]{0:T(256)(128)(2,1)} %param.27) | copy-start | bytes 196
  0.7 12.4 %copy-start.46 = (bf16[32]{0:T(256)(128)(2,1)S(1)}, bf16[32]{0:T(256)(128)(2,1)}, u32[]{:S(2)}) copy-start(bf16[32]{0:T(256)(128)(2,1)} %param.28) | copy-start | bytes 196
  0.7 12.5 %copy-start.31 = (bf16[32,3072]{1,0:T(8,128)(2,1)S(1)}, bf16[32,3072]{1,0:T(8,128)(2,1)}, u32[]{:S(2)}) copy-start(bf16[32,3072]{1,0:T(8,128)(2,1)} %param.21) | copy-start | bytes 589828
  301.5 77.8 %collective-permute-start.3 = (bf16[128,13568]{1,0:T(8,128)(2,1)}, bf16[128,13568]{1,0:T(8,128)(2,1)}, u32[]{:S(2)}, u32[]{:S(2)}) collective-permute-start(bf16[128,13568]{1,0:T(8,128)(2,1)} %get-tuple-element.35.refs_4_), channel_id=1, source_target_pairs={{0,4},{4,0},{1,5},{5,1},{2,6},{6,2},{3,7},{7,3},{8,12},{12,8},{9,1... | collective-permute-start | bytes 10420232 | tf_op jit(solution)/shard_map/ppermute | solution.py:55
  301.6 86.4 %collective-permute-start.2 = (bf16[128,13568]{1,0:T(8,128)(2,1)}, bf16[128,13568]{1,0:T(8,128)(2,1)}, u32[]{:S(2)}, u32[]{:S(2)}) collective-permute-start(bf16[128,13568]{1,0:T(8,128)(2,1)} %get-tuple-element.35.refs_4_), channel_id=1, source_target_pairs={{0,2},{2,0},{1,3},{3,1},{4,6},{6,4},{5,7},{7,5},{8,10},{10,8},{9,1... | collective-permute-start | bytes 10420232 | tf_op jit(solution)/shard_map/ppermute | solution.py:55
  303.6 133.7 %collective-permute-start.6 = (bf16[128,13568]{1,0:T(8,128)(2,1)}, bf16[128,13568]{1,0:T(8,128)(2,1)}, u32[]{:S(2)}, u32[]{:S(2)}) collective-permute-start(bf16[128,13568]{1,0:T(8,128)(2,1)} %get-tuple-element.35.refs_4_), channel_id=1, source_target_pairs={{0,1},{1,0},{2,3},{3,2},{4,5},{5,4},{6,7},{7,6},{8,9},{9,8},{10,11... | collective-permute-start | bytes 10420232 | tf_op jit(solution)/shard_map/ppermute | solution.py:55
  311.4 126.0 %collective-permute-start.1 = (bf16[13568,256]{1,0:T(8,128)(2,1)}, bf16[13568,256]{1,0:T(8,128)(2,1)}, u32[]{:S(2)}, u32[]{:S(2)}) collective-permute-start(bf16[13568,256]{1,0:T(8,128)(2,1)} %pad.28.refs_2_), channel_id=1, source_target_pairs={{0,1},{1,0},{2,3},{3,2},{4,5},{5,4},{6,7},{7,6},{8,9},{9,8},{10,11... | collective-permute-start | bytes 20840456 | tf_op jit(solution)/shard_map/ppermute | solution.py:55
  320.1 8.1 copy-start.4
  320.4 7.9 copy-start.10
  328.3 6.3 copy-start
  328.3 6.3 copy-start.32
  328.3 6.3 copy-start.8
  332.1 7.1 copy-start.37
  334.6 4.7 copy-start.15
  339.3 4.5 copy-start.12
  339.6 5.3 copy-start.2
  342.6 19.0 %copy-start.38 = (f32[256]{0:T(256)}, f32[256]{0:T(256)S(1)}, u32[]{:S(2)}) copy-start(f32[256]{0:T(256)S(1)} %broadcast_multiply_fusion.1) | copy-start | bytes 3076
  344.9 16.7 %copy-start.17 = (bf16[256,1024]{0,1:T(8,128)(2,1)}, bf16[256,1024]{0,1:T(8,128)(2,1)S(1)}, u32[]{:S(2)}) copy-start(bf16[256,1024]{0,1:T(8,128)(2,1)S(1)} %add_convert_fusion.4) | copy-start | bytes 1572868
  380.9 39.4 %collective-permute-start.4 = (bf16[128,6784]{1,0:T(8,128)(2,1)S(1)}, bf16[128,6784]{1,0:T(8,128)(2,1)S(1)}, u32[]{:S(2)}, u32[]{:S(2)}) collective-permute-start(bf16[128,6784]{1,0:T(8,128)(2,1)S(1)} %slice.163), channel_id=1, source_target_pairs={{0,2},{2,0},{1,3},{3,1},{4,6},{6,4},{5,7},{7,5},{8,10},{10,8},{9,1... | collective-permute-start | bytes 5210120 | tf_op jit(solution)/shard_map/ppermute | solution.py:55
  389.6 39.4 %collective-permute-start.5 = (bf16[128,6784]{1,0:T(8,128)(2,1)S(1)}, bf16[128,6784]{1,0:T(8,128)(2,1)S(1)}, u32[]{:S(2)}, u32[]{:S(2)}) collective-permute-start(bf16[128,6784]{1,0:T(8,128)(2,1)S(1)} %slice.164), channel_id=1, source_target_pairs={{0,4},{4,0},{1,5},{5,1},{2,6},{6,2},{3,7},{7,3},{8,12},{12,8},{9,1... | collective-permute-start | bytes 5210120 | tf_op jit(solution)/shard_map/ppermute | solution.py:55
  392.8 37.5 %copy-start.19 = (bf16[256,1024]{0,1:T(8,128)(2,1)}, bf16[256,1024]{0,1:T(8,128)(2,1)S(1)}, u32[]{:S(2)}) copy-start(bf16[256,1024]{0,1:T(8,128)(2,1)S(1)} %get-tuple-element.96) | copy-start | bytes 1572868
  392.8 37.5 %collective-permute-start = (bf16[256,512]{0,1:T(8,128)(2,1)S(1)}, bf16[256,512]{0,1:T(8,128)(2,1)S(1)}, u32[]{:S(2)}, u32[]{:S(2)}) collective-permute-start(bf16[256,512]{0,1:T(8,128)(2,1)S(1)} %pad_maximum_fusion.6), channel_id=1, source_target_pairs={{0,1},{1,0},{2,3},{3,2},{4,5},{5,4},{6,7},{7,6},{8,9},{9,8},{10,11... | collective-permute-start | bytes 786440 | tf_op jit(solution)/shard_map/ppermute | solution.py:55
  420.3 17.0 %collective-permute-start.7 = (bf16[128,13568]{1,0:T(8,128)(2,1)}, bf16[128,13568]{1,0:T(8,128)(2,1)}, u32[]{:S(2)}, u32[]{:S(2)}) collective-permute-start(bf16[128,13568]{1,0:T(8,128)(2,1)} %collective-permute-done.2.refs_5_), channel_id=1, source_target_pairs={{0,1},{1,0},{2,3},{3,2},{4,5},{5,4},{6,7},{7,6},{8,9},{9,8},{10,11... | collective-permute-start | bytes 10420232 | tf_op jit(solution)/shard_map/ppermute | solution.py:55
  429.0 8.3 collective-permute-start.8
  431.0 9.4 collective-permute-start.9
  581.5 15.6 %copy-start.50 = (f32[256,4096]{0,1:T(8,128)S(1)}, f32[256,4096]{0,1:T(8,128)}, u32[]{:S(2)}) copy-start(f32[256,4096]{0,1:T(8,128)} %get-tuple-element.113) | copy-start | bytes 12582916
  581.5 15.6 %copy-start.51 = (f32[256,4096]{0,1:T(8,128)S(1)}, f32[256,4096]{0,1:T(8,128)}, u32[]{:S(2)}) copy-start(f32[256,4096]{0,1:T(8,128)} %get-tuple-element.185) | copy-start | bytes 12582916
  597.1 10.4 %copy-start.34 = (f32[1,1024]{1,0:T(1,128)S(1)}, f32[1,1024]{1,0:T(1,128)}, u32[]{:S(2)}) copy-start(f32[1,1024]{1,0:T(1,128)} %copy-done.33) | copy-start | bytes 12292
  597.1 10.4 %copy-start.39 = (f32[256]{0:T(256)S(1)}, f32[256]{0:T(256)}, u32[]{:S(2)}) copy-start(f32[256]{0:T(256)} %copy-done.38) | copy-start | bytes 3076
  597.1 10.4 %copy-start.42 = (f32[256]{0:T(256)S(1)}, f32[256]{0:T(256)}, u32[]{:S(2)}) copy-start(f32[256]{0:T(256)} %copy-done.41) | copy-start | bytes 3076
  608.3 4.5 copy-start.6
  608.3 4.4 copy-start.16
  611.8 5.6 copy-start.9
  617.4 23.3 %slice-start = ((s8[16777216]{0:T(1024)(128)(4,1)}), s8[4194304]{0:T(1024)(128)(4,1)S(1)}, s32[]{:S(2)}) async-start(s8[16777216]{0:T(1024)(128)(4,1)} %bitcast.270), calls=%async_computation | async-start | bytes 8388608
  617.4 23.3 %slice-start.1 = ((s8[16777216]{0:T(1024)(128)(4,1)}), s8[4194304]{0:T(1024)(128)(4,1)S(1)}, s32[]{:S(2)}) async-start(s8[16777216]{0:T(1024)(128)(4,1)} %bitcast.270), calls=%async_computation.1 | async-start | bytes 8388608
  617.5 23.2 %slice-start.2 = ((s8[16777216]{0:T(1024)(128)(4,1)}), s8[4194304]{0:T(1024)(128)(4,1)S(1)}, s32[]{:S(2)}) async-start(s8[16777216]{0:T(1024)(128)(4,1)} %bitcast.270), calls=%async_computation.2 | async-start | bytes 8388608
  631.4 9.3 slice-start.3
  640.7 7.8 copy-start.11
  648.5 3.4 copy-start.1
  665.7 27.1 %collective-permute-start.14 = (bf16[2,256,2048]{1,2,0:T(8,128)(2,1)}, bf16[2,256,2048]{1,2,0:T(8,128)(2,1)}, u32[]{:S(2)}, u32[]{:S(2)}) collective-permute-start(bf16[2,256,2048]{1,2,0:T(8,128)(2,1)} %copy.211), channel_id=1, source_target_pairs={{0,1},{1,0},{2,3},{3,2},{4,5},{5,4},{6,7},{7,6},{8,9},{9,8},{10,11... | collective-permute-start | bytes 6291464 | tf_op jit(solution)/shard_map/ppermute | solution.py:55
  667.9 15.0 %collective-permute-start.11 = (bf16[256,2048]{0,1:T(8,128)(2,1)}, bf16[256,2048]{0,1:T(8,128)(2,1)}, u32[]{:S(2)}, u32[]{:S(2)}) collective-permute-start(bf16[256,2048]{0,1:T(8,128)(2,1)} %pad_maximum_fusion.4), channel_id=1, source_target_pairs={{0,1},{1,0},{2,3},{3,2},{4,5},{5,4},{6,7},{7,6},{8,9},{9,8},{10,11... | collective-permute-start | bytes 3145736 | tf_op jit(solution)/shard_map/ppermute | solution.py:55
  673.0 15.2 %collective-permute-start.13 = (bf16[256,512]{0,1:T(8,128)(2,1)}, bf16[256,512]{0,1:T(8,128)(2,1)}, u32[]{:S(2)}, u32[]{:S(2)}) collective-permute-start(bf16[256,512]{0,1:T(8,128)(2,1)} %pad_maximum_fusion.9), channel_id=1, source_target_pairs={{0,1},{1,0},{2,3},{3,2},{4,5},{5,4},{6,7},{7,6},{8,9},{9,8},{10,11... | collective-permute-start | bytes 786440 | tf_op jit(solution)/shard_map/ppermute | solution.py:55
  675.4 10.8 %collective-permute-start.12 = (bf16[256,512]{0,1:T(8,128)(2,1)}, bf16[256,512]{0,1:T(8,128)(2,1)}, u32[]{:S(2)}, u32[]{:S(2)}) collective-permute-start(bf16[256,512]{0,1:T(8,128)(2,1)} %pad_maximum_fusion.8), channel_id=1, source_target_pairs={{0,1},{1,0},{2,3},{3,2},{4,5},{5,4},{6,7},{7,6},{8,9},{9,8},{10,11... | collective-permute-start | bytes 786440 | tf_op jit(solution)/shard_map/ppermute | solution.py:55
  678.4 2.0 collective-permute-start.10
  680.5 60.1 %collective-permute-start.20 = (bf16[13568,256]{1,0:T(8,128)(2,1)}, bf16[13568,256]{1,0:T(8,128)(2,1)}, u32[]{:S(2)}, u32[]{:S(2)}) collective-permute-start(bf16[13568,256]{1,0:T(8,128)(2,1)} %get-tuple-element.39.refs_8_), channel_id=1, source_target_pairs={{0,1},{1,0},{2,3},{3,2},{4,5},{5,4},{6,7},{7,6},{8,9},{9,8},{10,11... | collective-permute-start | bytes 20840456 | tf_op jit(solution)/shard_map/ppermute | solution.py:55
  684.5 3.6 copy-start.22
  684.6 3.6 copy-start.23
  692.8 47.8 %collective-permute-start.18 = (bf16[9216,256]{1,0:T(8,128)(2,1)}, bf16[9216,256]{1,0:T(8,128)(2,1)}, u32[]{:S(2)}, u32[]{:S(2)}) collective-permute-start(bf16[9216,256]{1,0:T(8,128)(2,1)} %get-tuple-element.90.refs_2_), channel_id=1, source_target_pairs={{0,1},{1,0},{2,3},{3,2},{4,5},{5,4},{6,7},{7,6},{8,9},{9,8},{10,11... | collective-permute-start | bytes 14155784 | tf_op jit(solution)/shard_map/ppermute | solution.py:55
  696.2 10.9 %slice-start.4 = ((s8[8388608]{0:T(1024)(128)(4,1)}), s8[4194304]{0:T(1024)(128)(4,1)S(1)}, s32[]{:S(2)}) async-start(s8[8388608]{0:T(1024)(128)(4,1)} %bitcast.272), calls=%async_computation.4 | async-start | bytes 8388608
  696.3 26.5 %collective-permute-start.15 = (bf16[256,2048]{0,1:T(8,128)(2,1)S(1)}, bf16[256,2048]{0,1:T(8,128)(2,1)S(1)}, u32[]{:S(2)}, u32[]{:S(2)}) collective-permute-start(bf16[256,2048]{0,1:T(8,128)(2,1)S(1)} %slice_bitcast_fusion.4), channel_id=1, source_target_pairs={{0,2},{2,0},{1,3},{3,1},{4,6},{6,4},{5,7},{7,5},{8,10},{10,8},{9,1... | collective-permute-start | bytes 3145736 | tf_op jit(solution)/shard_map/ppermute | solution.py:55
  699.0 8.2 slice-start.5
  699.0 8.2 copy-start.5
  724.3 7.3 copy-start.3
  724.3 7.3 copy-start.36
  724.3 16.3 %collective-permute-start.19 = (bf16[3072,256]{1,0:T(8,128)(2,1)}, bf16[3072,256]{1,0:T(8,128)(2,1)}, u32[]{:S(2)}, u32[]{:S(2)}) collective-permute-start(bf16[3072,256]{1,0:T(8,128)(2,1)} %fusion.46.refs_4_), channel_id=1, source_target_pairs={{0,1},{1,0},{2,3},{3,2},{4,5},{5,4},{6,7},{7,6},{8,9},{9,8},{10,11... | collective-permute-start | bytes 4718600 | tf_op jit(solution)/shard_map/ppermute | solution.py:55
  734.0 3.8 copy-start.14
  734.1 5.6 collective-permute-start.17
  734.9 3.9 collective-permute-start.16
  977.0 7.2 copy-start.40
  999.7 3.1 copy-start.20
  (15 other events, 23.9 us)

commit v7 on v6

--- a/solution.py
+++ b/solution.py
@@ -401,29 +401,18 @@
     return out[: len(shards)], *out[len(shards) :]
 
 
-def scatter_kernel(n_h, sections, left_starts, n_weights, with_sum, *refs):
-    lefts, vector = refs[:2]
-    n_sections = len(sections)
-    rights = refs[2 : 2 + 2 * n_sections]
-    weights = refs[2 + 2 * n_sections : 2 + 2 * n_sections + n_weights]
-    rest = refs[2 + 2 * n_sections + n_weights :]
-    out, product = rest[:2]
-    total_out = rest[2] if with_sum else None
-    (right_buf, weight_buf, product_buf, own, s1, r1, s2, r2, s3, r3, load_sem, weight_sem, product_sem,
-     send1, recv1, send2, recv2, send3, recv3) = rest[3 if with_sum else 2 :]
+def scatter_kernel(n_h, sections, left_starts, lefts, rights, out, scratch, peers, prefetch, beside, after):
+    (right_buf, own, s1, r1, s2, r2, s3, r3, load_sem, send1, recv1, send2, recv2, send3, recv3) = scratch
     h, x, y = (lax.axis_index(name) for name in ("h", "x", "y"))
     to_x, to_y = {"x": 1 - x}, {"y": 1 - y}
     w = s3.shape[1]
     rows = w // n_h
     f32, b16 = jnp.float32, jnp.bfloat16
-    cells = vector.shape[0]
+    n_sections = len(sections)
     starts = [sum(sections[:k]) for k in range(n_sections)]
     n = sum(sections)
-    begin = starts[-1]
-    greet([{"h": lax.rem(h + d, n_h)} for d in range(1, n_h)] + [to_x, to_y])
-
-    def chunk_of(k):
-        return pl.ds(pl.multiple_of(k * CHUNK, CHUNK), CHUNK)
+    cells = right_buf.shape[2] // 2
+    greet([{"h": lax.rem(h + d, n_h)} for d in range(1, n_h)] + [to_x, to_y] + peers)
 
     def loads(i, section, k):
         slot = lax.rem(i, 3)
@@ -435,6 +424,138 @@
             )
             for half in (0, 1)
         ]
+
+    def start_loads(i):
+        for section, (start, count) in enumerate(zip(starts, sections)):
+
+            @pl.when((i >= start) & (i < start + count))
+            def _(section=section, start=start):
+                for copy in loads(i, section, i - start):
+                    copy.start()
+                prefetch(section, i - start)
+
+    def hop(i, source, target, send_sem, recv_sem, to):
+        slot = lax.rem(i, RING)
+        return pltpu.make_async_remote_copy(
+            src_ref=source.at[slot], dst_ref=target.at[i], send_sem=send_sem.at[slot],
+            recv_sem=recv_sem.at[i], device_id=to, device_id_type=MESH,
+        )
+
+    def first(i, odd):
+        return hop(i, s1, r1, send1, recv1, to_y if odd else to_x)
+
+    def second(i, odd):
+        return hop(i, s2, r2, send2, recv2, to_x if odd else to_y)
+
+    def third(i, d):
+        to = lax.rem(h + d, n_h)
+        slot = lax.rem(i, RING)
+        return pltpu.make_async_remote_copy(
+            src_ref=s3.at[slot, pl.ds(to * rows, rows)], dst_ref=r3.at[i, d - 1],
+            send_sem=send3.at[slot, d - 1], recv_sem=recv3.at[i, d - 1],
+            device_id={"h": to}, device_id_type=MESH,
+        )
+
+    def multiply(i, odd):
+        slot = lax.rem(i, RING)
+        for copy in loads(i, 0, 0):
+            copy.wait()
+        left = lefts[sum((i + 1024 - start) // 1024 for start in left_starts[1:]) if left_starts[1:] else 0]
+        right = right_buf.at[lax.rem(i, 3)]
+
+        @pl.when(i >= RING)
+        def _():
+            first(i - RING, odd).wait_send()
+
+        part = lax.dot_general(left, right[...], (((1,), (1,)), ((), ())), preferred_element_type=f32)
+        own[slot, :w] = part[:w]
+        if odd:
+            own[slot, w:] = part[2 * w : 3 * w]
+            s1[slot, :w] = part[w : 2 * w].astype(b16)
+            s1[slot, w:] = part[3 * w :].astype(b16)
+        else:
+            own[slot, w:] = part[w : 2 * w]
+            s1[slot] = part[2 * w :].astype(b16)
+        first(i, odd).start()
+
+        beside(i, right, odd)
+        start_loads(i + 2)
+
+    def pass_on(i, odd):
+        slot = lax.rem(i, RING)
+        first(i, odd).wait_recv()
+
+        @pl.when(i >= RING)
+        def _():
+            second(i - RING, odd).wait_send()
+
+        s2[slot] = (own[slot, w:] + r1[i, w:].astype(f32)).astype(b16)
+        second(i, odd).start()
+
+    def keep(i, odd):
+        slot = lax.rem(i, RING)
+        second(i, odd).wait_recv()
+        part = own[slot, :w] + r1[i, :w].astype(f32) + r2[i].astype(f32)
+        if n_h == 1:
+            out[i] = part.astype(b16)
+            return
+
+        @pl.when(i >= RING)
+        def _():
+            for d in range(1, n_h):
+                third(i - RING, d).wait_send()
+
+        s3[slot] = part.astype(b16)
+        for d in range(1, n_h):
+            third(i, d).start()
+
+    def finish(i, odd):
+        if n_h == 1:
+            return
+        total = s3[lax.rem(i, RING), pl.ds(h * rows, rows)].astype(f32)
+        for d in range(1, n_h):
+            third(i, d).wait_recv()
+            total = total + r3[i, d - 1].astype(f32)
+        out[i] = total
+
+    start_loads(jnp.int32(0))
+    start_loads(jnp.int32(1))
+    pairs = (n + 1) // 2
+
+    def step(p, carry):
+        for lag, stage in enumerate((multiply, pass_on, keep, finish)):
+            for odd in (0, 1):
+                i = 2 * (p - lag) + odd
+
+                @pl.when((i >= 0) & (i < n))
+                def _(stage=stage, i=i, odd=odd):
+                    stage(i, odd)
+
+        after(p)
+        return carry
+
+    lax.fori_loop(0, pairs + 3, step, 0)
+    for i in range(max(n - RING, 0), n):
+        first(i, i % 2).wait_send()
+        second(i, i % 2).wait_send()
+        for d in range(1, n_h):
+            third(i, d).wait_send()
+
+
+def chunk_of(k):
+    return pl.ds(pl.multiple_of(k * CHUNK, CHUNK), CHUNK)
+
+
+def product_kernel(n_h, sections, left_starts, n_weights, with_sum, *refs):
+    lefts, vector = refs[:2]
+    n_rights = 2 * len(sections)
+    rights, weights = refs[2 : 2 + n_rights], refs[2 + n_rights : 2 + n_rights + n_weights]
+    rest = refs[2 + n_rights + n_weights :]
+    out, product = rest[:2]
+    total_out = rest[2] if with_sum else None
+    weight_buf, product_buf, weight_sem, product_sem, *scratch = rest[3 if with_sum else 2 :]
+    begin, count = sum(sections[:-1]), sections[-1]
+    cells = vector.shape[0]
 
     def weight_loads(k):
         slot = lax.rem(k, 3)
@@ -448,164 +569,144 @@
             for part, weight in enumerate(weights)
         ]
 
-    def start_loads(i):
-        for section, (start, count) in enumerate(zip(starts, sections)):
-
-            @pl.when((i >= start) & (i < start + count))
-            def _(section=section, start=start):
-                for copy in loads(i, section, i - start):
-                    copy.start()
-                if section == n_sections - 1:
-                    for copy in weight_loads(i - start):
-                        copy.start()
-
     def product_store(k):
         slot = lax.rem(k, 2)
         return pltpu.make_async_copy(product_buf.at[slot], product.at[chunk_of(k)], product_sem.at[slot])
 
-    def hop(i, source, target, send_sem, recv_sem, to):
-        slot = lax.rem(i, RING)
-        return pltpu.make_async_remote_copy(
-            src_ref=source.at[slot], dst_ref=target.at[i], send_sem=send_sem.at[slot],
-            recv_sem=recv_sem.at[i], device_id=to, device_id_type=MESH,
-        )
-
-    def first(i, odd):
-        return hop(i, s1, r1, send1, recv1, to_y if odd else to_x)
-
-    def second(i, odd):
-        return hop(i, s2, r2, send2, recv2, to_x if odd else to_y)
-
-    def third(i, d):
-        to = lax.rem(h + d, n_h)
-        slot = lax.rem(i, RING)
-        return pltpu.make_async_remote_copy(
-            src_ref=s3.at[slot, pl.ds(to * rows, rows)], dst_ref=r3.at[i, d - 1],
-            send_sem=send3.at[slot, d - 1], recv_sem=recv3.at[i, d - 1],
-            device_id={"h": to}, device_id_type=MESH,
-        )
-
-    def multiply(i, odd):
-        slot = lax.rem(i, RING)
-        for copy in loads(i, 0, 0):
+    def prefetch(section, k):
+        if section == len(sections) - 1:
+            for copy in weight_loads(k):
+                copy.start()
+
+    def multiply(k, right):
+        for copy in weight_loads(k):
             copy.wait()
-        left = lefts[sum((i + 1024 - start) // 1024 for start in left_starts[1:]) if left_starts[1:] else 0]
-        right = right_buf.at[lax.rem(i, 3)]
-
-        @pl.when(i >= RING)
+        weight = weight_buf[lax.rem(k, 3)]
+
+        @pl.when(k >= 2)
         def _():
-            first(i - RING, odd).wait_send()
-
-        part = lax.dot_general(left, right[...], (((1,), (1,)), ((), ())), preferred_element_type=f32)
-        own[slot, :w] = part[:w]
-        if odd:
-            own[slot, w:] = part[2 * w : 3 * w]
-            s1[slot, :w] = part[w : 2 * w].astype(b16)
-            s1[slot, w:] = part[3 * w :].astype(b16)
-        else:
-            own[slot, w:] = part[w : 2 * w]
-            s1[slot] = part[2 * w :].astype(b16)
-        first(i, odd).start()
-
-        def beside(k):
-            for copy in weight_loads(k):
-                copy.wait()
-            weight = weight_buf[lax.rem(k, 3)]
-
-            @pl.when(k >= 2)
+            product_store(k - 2).wait()
+
+        value = jnp.dot(vector[...], weight, preferred_element_type=jnp.float32)
+        product_buf[lax.rem(k, 2)] = value.T.astype(product_buf.dtype)
+        product_store(k).start()
+        if with_sum:
+            term = jnp.dot(weight, right[:, :cells], preferred_element_type=jnp.float32)
+
+            @pl.when(k == 0)
             def _():
-                product_store(k - 2).wait()
-
-            value = jnp.dot(vector[...], weight, preferred_element_type=f32)
-            product_buf[lax.rem(k, 2)] = value.T.astype(product_buf.dtype)
-            product_store(k).start()
-            if with_sum:
-                term = jnp.dot(weight, right[:, :cells], preferred_element_type=f32)
-
-                @pl.when(k == 0)
-                def _():
-                    total_out[...] = term
-
-                @pl.when(k > 0)
-                def _():
-                    total_out[...] += term
-
+                total_out[...] = term
+
+            @pl.when(k > 0)
+            def _():
+                total_out[...] += term
+
+    def beside(i, right, odd):
         if begin == 0:
-            beside(i)
+            multiply(i, right)
         else:
 
             @pl.when(i >= begin)
             def _():
-                beside(i - begin)
-
-        start_loads(i + 2)
-
-    def pass_on(i, odd):
-        slot = lax.rem(i, RING)
-        first(i, odd).wait_recv()
-
-        @pl.when(i >= RING)
+                multiply(i - begin, right)
+
+    scatter_kernel(
+        n_h, sections, left_starts, lefts, rights, out, scratch, [], prefetch, beside, lambda p: None
+    )
+    for k in range(max(count - 2, 0), count):
+        product_store(k).wait()
+
+
+def attention_kernel(n_h, sections, left_starts, scale, *refs):
+    lefts, query, pairs, d_out, log_total, seg_keys, seg_mine = refs[:7]
+    n_rights = 2 * len(sections)
+    rights = refs[7 : 7 + n_rights]
+    out, d_qkv, d_pairs, by_core, by_y, d_query, send, recv, *scratch = refs[7 + n_rights :]
+    y, c = lax.axis_index("y"), lax.axis_index("c")
+    f32, b16 = jnp.float32, jnp.bfloat16
+    cells, width = query.shape
+    slots = 4 * cells
+    n_pairs, head = width // 128, 64
+    into = (((1,), (1,)), ((), ()))
+
+    def backward(j, half):
+        lanes = pl.ds(pl.multiple_of(j * 128, 128), 128)
+        value_lanes = pl.ds(pl.multiple_of(width + j * 128, 128), 128)
+        side = slice(half * head, (half + 1) * head)
+        keys = pairs[:, :, :, lanes].reshape(slots, 128)[:, side]
+        values = pairs[:, :, :, value_lanes].reshape(slots, 128)[:, side]
+        mine, above = query[:, lanes][:, side], d_out[:, lanes][:, side]
+        scores = lax.dot_general(keys, mine, into, preferred_element_type=f32) * scale
+        scores = jnp.where(seg_keys[...] == seg_mine[...], scores, -1000000000.0)
+        probs = jnp.exp(scores - log_total[pl.ds(2 * j + half, 1), :])
+        d_probs = lax.dot_general(values, above, into, preferred_element_type=f32)
+        inner = jnp.sum(probs * d_probs, axis=0, keepdims=True)
+        d_scores = (probs * (d_probs - inner)).astype(b16)
+        d_keys = jnp.dot(d_scores, mine, preferred_element_type=f32) * scale
+        d_values = jnp.dot(probs.astype(b16), above, preferred_element_type=f32)
+        d_pairs[0, j, :, side] = d_keys.astype(b16)
+        d_pairs[1, j, :, side] = d_values.astype(b16)
+        turned = keys.astype(f32).T.astype(b16)
+        d_query[side] = jnp.dot(turned, d_scores, preferred_element_type=f32) * scale
+        if half:
+            d_qkv[:, lanes] = d_query[...].T.astype(b16)
+
+    def to_core():
+        return pltpu.make_async_remote_copy(
+            src_ref=d_pairs.at[:, :, pl.ds(2 * cells, 2 * cells)], dst_ref=by_core,
+            send_sem=send.at[0], recv_sem=recv.at[0], device_id={"c": 1 - c}, device_id_type=MESH,
+        )
+
+    def to_y():
+        return pltpu.make_async_remote_copy(
+            src_ref=d_pairs.at[:, :, pl.ds(cells, cells)], dst_ref=by_y,
+            send_sem=send.at[1], recv_sem=recv.at[1], device_id={"y": 1 - y}, device_id_type=MESH,
+        )
+
+    def beside(i, right, odd):
+        @pl.when(i < 2 * n_pairs)
         def _():
-            second(i - RING, odd).wait_send()
-
-        s2[slot] = (own[slot, w:] + r1[i, w:].astype(f32)).astype(b16)
-        second(i, odd).start()
-
-    def keep(i, odd):
-        slot = lax.rem(i, RING)
-        second(i, odd).wait_recv()
-        part = own[slot, :w] + r1[i, :w].astype(f32) + r2[i].astype(f32)
-        if n_h == 1:
-            out[i] = part.astype(b16)
-            return
-
-        @pl.when(i >= RING)
+            backward(i // 2, odd)
+
+    def after(p):
+        @pl.when(p == n_pairs)
         def _():
-            for d in range(1, n_h):
-                third(i - RING, d).wait_send()
-
-        s3[slot] = part.astype(b16)
-        for d in range(1, n_h):
-            third(i, d).start()
-
-    def finish(i, odd):
-        if n_h == 1:
-            return
-        total = s3[lax.rem(i, RING), pl.ds(h * rows, rows)].astype(f32)
-        for d in range(1, n_h):
-            third(i, d).wait_recv()
-            total = total + r3[i, d - 1].astype(f32)
-        out[i] = total
-
-    start_loads(jnp.int32(0))
-    start_loads(jnp.int32(1))
-    pairs = (n + 1) // 2
-
-    def step(p, carry):
-        for lag, stage in enumerate((multiply, pass_on, keep, finish)):
-            for odd in (0, 1):
-                i = 2 * (p - lag) + odd
-
-                @pl.when((i >= 0) & (i < n))
-                def _(stage=stage, i=i, odd=odd):
-                    stage(i, odd)
-
+            to_core().start()
+
+        @pl.when(p == n_pairs + 2)
+        def _():
+            to_core().wait_recv()
+
+            def add(j, carry):
+                for kind in (0, 1):
+                    total = d_pairs[kind, j, : 2 * cells].astype(f32) + by_core[kind, j].astype(f32)
+                    d_pairs[kind, j, : 2 * cells] = total.astype(b16)
+                return carry
+
+            lax.fori_loop(0, n_pairs, add, 0)
+            to_y().start()
+
+    scatter_kernel(
+        n_h, sections, left_starts, lefts, rights, out, scratch, [{"c": 1 - c}],
+        lambda section, k: None, beside, after,
+    )
+    to_y().wait_recv()
+
+    def add(j, carry):
+        for kind in (0, 1):
+            lanes = pl.ds(pl.multiple_of((kind + 1) * width + j * 128, 128), 128)
+            total = d_pairs[kind, j, :cells].astype(f32) + by_y[kind, j].astype(f32)
+            d_qkv[:, lanes] = total.astype(b16)
         return carry
 
-    lax.fori_loop(0, pairs + 3, step, 0)
-    for i in range(max(n - RING, 0), n):
-        first(i, i % 2).wait_send()
-        second(i, i % 2).wait_send()
-        for d in range(1, n_h):
-            third(i, d).wait_send()
-    for k in range(max(sections[-1] - 2, 0), sections[-1]):
-        product_store(k).wait()
-
-
-def scatter_all(lefts, left_starts, rights, vector, weights, product_type, with_sum, collective_id):
+    lax.fori_loop(0, n_pairs, add, 0)
+    to_core().wait_send()
+    to_y().wait_send()
+
+
+def scatter_call(kernel, lefts, rights, operands, more_operands, out_shapes, out_specs, scratch, collective_id):
     sections = [own.shape[0] // CHUNK for own, _ in rights]
-    n, cells = sum(sections), vector.shape[0]
-    features = vector.shape[1]
+    n, cells = sum(sections), rights[0][0].shape[1]
     w = lefts.shape[1] // 4
     n_h = lax.axis_size("h")
     rows = w // n_h
@@ -616,22 +717,14 @@
     part_shape = jax.ShapeDtypeStruct((n, rows, CHUNK), f32)
     if inner_h == 1:
         part_shape = jax.ShapeDtypeStruct((n, w, CHUNK), bf16)
-    out_shape = [part_shape, jax.ShapeDtypeStruct((sections[-1] * CHUNK, cells), product_type)]
-    out_specs = [vmem, hbm]
-    if with_sum:
-        out_shape.append(jax.ShapeDtypeStruct((features, cells), f32))
-        out_specs.append(vmem)
     part, *more = pl.pallas_call(
-        functools.partial(
-            scatter_kernel, inner_h, sections, left_starts, len(weights), with_sum
-        ),
-        out_shape=out_shape,
-        in_specs=[vmem, vmem] + [hbm] * (2 * len(rights) + len(weights)),
-        out_specs=out_specs,
-        scratch_shapes=[
+        functools.partial(kernel, inner_h, sections),
+        out_shape=[part_shape] + out_shapes,
+        in_specs=[vmem] * (1 + len(operands)) + [hbm] * (2 * len(rights) + len(more_operands)),
+        out_specs=[vmem] + out_specs,
+        scratch_shapes=scratch
+        + [
             pltpu.VMEM((3, CHUNK, 2 * cells), bf16),
-            pltpu.VMEM((3, features, CHUNK), bf16),
-            pltpu.VMEM((2, CHUNK, cells), product_type),
             pltpu.VMEM((RING, 2 * w, CHUNK), f32),
             pltpu.VMEM((RING, 2 * w, CHUNK), bf16),
             pltpu.VMEM((n, 2 * w, CHUNK), bf16),
@@ -640,8 +733,6 @@
             pltpu.VMEM((RING, w, CHUNK), bf16),
             pltpu.VMEM((n, others, w // inner_h, CHUNK), bf16),
             dma((3, 2)),
-            dma((3, len(weights))),
-            dma((2,)),
             dma((RING,)),
             dma((n,)),
             dma((RING,)),
@@ -652,22 +743,69 @@
         compiler_params=pltpu.CompilerParams(
             collective_id=collective_id, has_side_effects=True, vmem_limit_bytes=60 * 2**20
         ),
-    )(lefts, vector, *(half for pair in rights for half in pair), *weights)
+    )(lefts, *operands, *(half for pair in rights for half in pair), *more_operands)
     if inner_h == 1:
         part = lax.psum_scatter(part, "h", scatter_dimension=1, tiled=True).astype(f32)
     return part, *more
 
 
+def scatter_product(lefts, left_starts, rights, vector, weights, product_type, with_sum, collective_id):
+    (cells, features), columns = vector.shape, rights[-1][0].shape[0]
+    dma = pltpu.SemaphoreType.DMA
+    vmem, hbm = pl.BlockSpec(memory_space=pltpu.VMEM), pl.BlockSpec(memory_space=pl.ANY)
+
+    def kernel(n_h, sections, *refs):
+        product_kernel(n_h, sections, left_starts, len(weights), with_sum, *refs)
+
+    return scatter_call(
+        kernel,
+        lefts,
+        rights,
+        [vector],
+        weights,
+        [jax.ShapeDtypeStruct((columns, cells), product_type)]
+        + [jax.ShapeDtypeStruct((features, cells), jnp.float32)] * with_sum,
+        [hbm] + [vmem] * with_sum,
+        [
+            pltpu.VMEM((3, features, CHUNK), jnp.bfloat16),
+            pltpu.VMEM((2, CHUNK, cells), product_type),
+            dma((3, len(weights))),
+            dma((2,)),
+        ],
+        collective_id,
+    )
+
+
+def scatter_attention(lefts, left_starts, rights, query, pairs, d_out, log_total, seg, scale, collective_id):
+    cells, width = query.shape
+    bf16, vmem = jnp.bfloat16, pl.BlockSpec(memory_space=pltpu.VMEM)
+
+    def kernel(n_h, sections, *refs):
+        attention_kernel(n_h, sections, left_starts, scale, *refs)
+
+    return scatter_call(
+        kernel,
+        lefts,
+        rights,
+        [query, pairs, d_out, log_total, seg[:, None], seg[None, :cells]],
+        [],
+        [jax.ShapeDtypeStruct((cells, 3 * width), bf16)],
+        [vmem],
+        [
+            pltpu.VMEM((2, width // 128, 4 * cells, 128), bf16),
+            pltpu.VMEM((2, width // 128, 2 * cells, 128), bf16),
+            pltpu.VMEM((2, width // 128, cells, 128), bf16),
+            pltpu.VMEM((128, cells), jnp.float32),
+            pltpu.SemaphoreType.DMA((2,)),
+            pltpu.SemaphoreType.DMA((2,)),
+        ],
+        collective_id,
+    )
+
+
 def own_half(left):
     half = left.shape[1] // 2
     return jnp.concatenate([left[:, :half], swap(left[:, half:], "c")], axis=0)
-
-
-def scatter_group(rows_all):
-    part = rows_all.astype(jnp.bfloat16).reshape((2, 2, rows_all.shape[0] // 4, -1))
-    got = swap(part[1], "c").astype(jnp.float32)
-    part = (part[0].astype(jnp.float32) + got).astype(jnp.bfloat16)
-    return part[0].astype(jnp.float32) + swap(part[1], "y").astype(jnp.float32)
 
 
 def left_of(left, pieces):
@@ -751,6 +889,7 @@
     vectors = qkv_all[:, 3 * width :].astype(jnp.float32).T
     qkv_all = qkv_all[:, : 3 * width]
     g1f, b1f, g2f, b2f = vectors[0], vectors[1], vectors[2], vectors[3]
+    kv_pairs, query_b = kv_all, query
     query = query.reshape(rows, heads, head_width)
     kv_all = kv_all.reshape(slots, -1)
     dec_own = gathered[5]
@@ -783,7 +922,7 @@
     act = jax.nn.gelu(hidden, approximate=False).astype(jnp.bfloat16)
     h2 = h1 + matmul(act, down_all)
     hb = h2.astype(jnp.bfloat16)
-    grad_dec, logits, dh2 = scatter_all(
+    grad_dec, logits, dh2 = scatter_product(
         left_of(hb, 1), [0], [cot_pair], relative(hb, 1), dec_parts, jnp.bfloat16, True, 1
     )
     own_rows = grad_dec.shape[1]
@@ -800,22 +939,30 @@
     dh1 = dh2 + dh1_norm
     dab = dh1.astype(jnp.bfloat16)
     d_attended = contract_cols(dab, out_all).astype(jnp.bfloat16)
-    d_attended = from_owner(d_attended, 1).reshape(rows, heads, head_width)
-    probs = jnp.exp(scores_of() - log_total)
-    probs_b = probs.astype(jnp.bfloat16)
-    d_probs = jnp.einsum("qhd,khd->hqk", d_attended, values, preferred_element_type=jnp.float32)
-    inner = jnp.sum(probs * d_probs, axis=-1, keepdims=True)
-    d_scores = (probs * (d_probs - inner)).astype(jnp.bfloat16)
-    d_query = (
-        jnp.einsum("hqk,khd->qhd", d_scores, keys, preferred_element_type=jnp.float32) * att_scale
-    )
-    d_keys = (
-        jnp.einsum("hqk,qhd->khd", d_scores, query, preferred_element_type=jnp.float32) * att_scale
-    )
-    d_values = jnp.einsum("hqk,qhd->khd", probs_b, d_attended, preferred_element_type=jnp.float32)
-    d_kv = jnp.concatenate([d_keys.reshape(slots, width), d_values.reshape(slots, width)], axis=1)
-    d_kv = scatter_group(d_kv)
-    d_qkv = jnp.concatenate([d_query.reshape(rows, width), d_kv], axis=1).astype(jnp.bfloat16)
+    d_attended = from_owner(d_attended, 1)
+    lefts = [left_of(a2, 1), left_of(act, act.shape[1] // width), left_of(attended_b, 1)]
+    pieces = (4 * width,) + (width,) * 4
+    rights = [d_hidden.T] + [dfb.T] * 4 + [dab.T]
+    grads, d_qkv = scatter_attention(
+        jnp.concatenate(lefts, axis=0),
+        [sum(pieces[:k]) // CHUNK for k in range(len(pieces) + 1)],
+        [both_cores(jnp.concatenate(rights, axis=0))],
+        query_b,
+        kv_pairs,
+        d_attended,
+        log_total[:, :, 0],
+        seg_all,
+        att_scale,
+        2,
+    )
+    ends = [0]
+    for columns in (4 * width, 4 * width, width):
+        ends.append(ends[-1] + columns // CHUNK)
+    grad_up, grad_down, grad_out = (grads[low:high] for low, high in zip(ends, ends[1:]))
+    grad_up, grad_out = columns_of(grad_up), columns_of(grad_out)
+    grad_down = grad_down.reshape(4, -1, own_rows, CHUNK).transpose(0, 2, 1, 3)
+    grad_down = grad_down.reshape(4 * own_rows, -1)
+    grad_out, grad_up, grad_down = (from_owner(g, 1) for g in (grad_out, grad_up, grad_down))
     da1 = contract_cols(d_qkv, qkv_all)
     first_pull = jax.vjp(layer_norm, h0, g1f, b1f)[1]
     dh0_norm, grad_gain_one, grad_shift_one = first_pull(da1)
@@ -824,36 +971,27 @@
     unit = jnp.eye(rows, dtype=jnp.bfloat16)
     dh0b = (dh1 + dh0_norm).astype(jnp.bfloat16)
 
-    lefts = [left_of(a2, 1), left_of(act, act.shape[1] // width), left_of(attended_b, 1)]
-    lefts += [left_of(a1, 1), left_of(vectors_b, 1), left_of(dh0b, 1)]
-    pieces = (4 * width,) + (width,) * 5 + (3 * width, rows)
-    left_starts = [sum(pieces[:k]) // CHUNK for k in range(len(pieces) + 1)]
-    rights = [d_hidden.T] + [dfb.T] * 4 + [dab.T]
-    grads, d_xb = scatter_all(
+    lefts = [left_of(a1, 1), left_of(vectors_b, 1), left_of(dh0b, 1)]
+    grads, d_xb = scatter_product(
         jnp.concatenate(lefts, axis=0),
-        left_starts,
-        [both_cores(jnp.concatenate(rights, axis=0)), both_cores(d_qkv.T), (unit, unit), xb_pair],
+        [0, 3 * width // CHUNK, (3 * width + rows) // CHUNK],
+        [both_cores(d_qkv.T), (unit, unit), xb_pair],
         dh0b,
         [enc_all],
         jnp.float32,
         False,
-        2,
+        3,
     )
     ends = [0]
-    for columns in (4 * width, 4 * width, width, 3 * width, rows):
+    for columns in (3 * width, rows):
         ends.append(ends[-1] + columns // CHUNK)
-    grad_up, grad_down, grad_out, grad_qkv, grad_vectors, grad_enc = (
+    grad_qkv, grad_vectors, grad_enc = (
         grads[low:high] for low, high in zip(ends, ends[1:] + [grads.shape[0]])
     )
-    grad_up, grad_out, grad_qkv, grad_enc = (
-        columns_of(g) for g in (grad_up, grad_out, grad_qkv, grad_enc)
-    )
+    grad_qkv, grad_enc = columns_of(grad_qkv), columns_of(grad_enc)
     grad_gain_one, grad_shift_one, grad_gain_two, grad_shift_two = (
         grad_vectors[0, :, k] for k in range(4)
     )
-    grad_down = grad_down.reshape(4, -1, own_rows, CHUNK).transpose(0, 2, 1, 3)
-    grad_down = grad_down.reshape(4 * own_rows, -1)
-    grad_out, grad_up, grad_down = (from_owner(g, 1) for g in (grad_out, grad_up, grad_down))
     grad_enc = grad_enc[:, :genes].T
     d_xb = d_xb[:genes].T
     counts_grad = d_xb * scale[:, None] / (1.0 + counts_f * scale[:, None])

time: 1010 us -> 961 us (0.951)
  Pallas kernels: 655 us -> 695 us
  matrix products: 92.9 us -> 66.1 us
  local copies, waits for them, and re-layouts: 118 us -> 93.4 us
  other arithmetic: 60.1 us -> 41.3 us
  waiting for transfers between devices: 67.1 us -> 48.7 us
    pallas_call x2 -> x3, Pallas kernels: 370 us -> 411 us  [scatter_call(): pl.pallas_call(functools.partial(kernel, inner_h, sections), out_shape=[p...]
    dot_general x4 -> x0, matrix products: 27.5 us -> none  [the longest x1 13.9 us: on_device(): jnp.einsum('qhd,khd->hqk', d_attended, values, preferred_element_type=jnp...]
    ppermute x21 -> x19, waiting for transfers between devices: 67.1 us -> 48.7 us  [swap(): return lax.ppermute(value, axis, [(0, 1), (1, 0)])]
    convert_element_type x2 -> x1, other arithmetic: 11.1 us -> 0.07 us  [on_device(): dfb = dh2.astype(jnp.bfloat16)]
    unnamed x140 -> x112, local copies, waits for them, and re-layouts: 24.5 us -> 17 us
  transfers between devices with their start and end apart: 21 -> 19, of which waited for: 5 -> 5; matrix products, arithmetic and copies ran while one was open for 13% -> 17% of each run, Pallas kernels for 0% -> 27%
where the time goes in v7:
time: 961 us; the launch traced here: 955 us
  Pallas kernels  695 us (72%)
  local copies, waits for them, and re-layouts  93.4 us (10%)
  matrix products  66.1 us (7%)
  waiting for transfers between devices  48.7 us (5%)
  other arithmetic  41.3 us (4%)
    pallas_call x3, Pallas kernels, scatter_call(): pl.pallas_call(functools.partial(kernel, inner_h, sections), out_shape=[p...  411 us
    pallas_call x1, Pallas kernels, gather_all(): pl.pallas_call(functools.partial(front_kernel, n_h, jobs, len(shards), n_...  285 us
    ppermute x19, waiting for transfers between devices, swap(): return lax.ppermute(value, axis, [(0, 1), (1, 0)])  48.7 us
    dot_general x4, matrix products, contract_cols(): lax.dot_general(left, right, (((1,), (1,)), ((), ())), preferred_element_...  32.2 us
    dot_general x3, matrix products, matmul(): return jnp.dot(left, right, preferred_element_type=jnp.float32)  23.4 us
  transfers between devices with their start and end apart: 19, of which 5 were waited for; matrix products, arithmetic and copies ran while one was open for 17% of the time, Pallas kernels for 27%

profile of v7, /device:TPU:0, one launch (start us, length us, event | category | flops | bytes accessed | tf_op | source)
XLA Modules:
  0.0 954.6 jit_solution(2925695519048327623)
XLA Ops:
  2.5 1.3 broadcast_divide_fusion
  4.4 2.1 pad.24.refs_0_
  6.5 2.1 pad.26.refs_5_
  8.7 1.1 copy.219
  13.9 1.9 multiply_sine_fusion.1
  15.8 1.1 pad_maximum_fusion.3
  16.9 284.6 %shard_map.238 = (bf16[2,2,2,128,13568]{4,3,2,1,0:T(8,128)(2,1)}, bf16[2,2,2,128,3200]{4,3,2,1,0:T(8,128)(2,1)}, bf16[2,2,2,128,1024]{4,3,2,1,0:T(8,128)(2,1)}, ...) custom-call(bf16[32,13568]{1,0:T(8,128)(2,1)} %pad.24.refs_0_, ...), custom_call_target="tpu_custom_call" | custom-call | tf_op jit(solution)/shard_map/pallas_call | solution.py:362
  301.6 2.1 collective-permute-start.2
  303.6 1.8 constant_dynamic-slice_fusion.47
  306.1 7.7 pad.28.refs_2_
  315.5 4.0 fusion.61
  319.6 4.0 copy.225
  323.8 2.6 copy.222
  326.6 4.5 fusion
  331.1 4.4 fusion.1
  335.5 6.0 fusion.36
  341.5 1.1 copy.226
  343.8 1.0 slice.143
  345.8 16.1 %multiply_convert_fusion = (bf16[256,4096]{0,1:T(8,128)(2,1)S(1)}, f32[256,4096]{0,1:T(8,128)}, f32[256,4096]{0,1:T(8,128)}) fusion(bf16[256,1024]{1,0:T(8,128)(2,1)S(1)} %add_convert_fusion.3, bf16[1024,4096]{1,0:T(8,128)(2,1)} %bitcast.285), kind=kOutput, calls=%fused_computation.40 | convolution fusion | flops 2215641088 | bytes 19398656 | tf_op jit(solution)/shard_map/dot_general | solution.py:51
  361.9 6.5 fusion.35
  369.1 10.2 %collective-permute-done.3.refs_6_ = bf16[128,13568]{1,0:T(8,128)(2,1)} collective-permute-done((bf16[128,13568]{1,0:T(8,128)(2,1)}, bf16[128,13568]{1,0:T(8,128)(2,1)}, u32[]{:S(2)}, u32[]{:S(2)}) %collective-permute-start.3) | collective-permute-done | bytes 3473440 | tf_op jit(solution)/shard_map/ppermute | solution.py:55
  379.3 2.8 slice.146
  386.0 2.8 slice.147
  388.8 1.7 collective-permute-start.5
  392.2 0.9 constant_dynamic-slice_fusion.31
  393.2 28.5 %collective-permute-done.4 = bf16[128,6784]{1,0:T(8,128)(2,1)} collective-permute-done((bf16[128,6784]{1,0:T(8,128)(2,1)}, bf16[128,6784]{1,0:T(8,128)(2,1)}, u32[]{:S(2)}, u32[]{:S(2)}) %collective-permute-start.4) | collective-permute-done | bytes 1736736 | tf_op jit(solution)/shard_map/ppermute | solution.py:55
  421.7 2.8 constant_dynamic-update-slice_fusion.9
  425.0 4.4 collective-permute-done.5
  429.4 2.8 constant_dynamic-update-slice_fusion.8.refs_7_
  433.6 1.0 copy-done.13
  436.6 1.3 log_add_fusion.refs_4_
  437.9 1.1 maximum_bitcast_fusion
  439.0 1.0 copy.230.refs_0_
  440.0 1.1 maximum_bitcast_fusion.2
  441.3 1.8 maximum_bitcast_fusion.1
  443.1 1.0 maximum_bitcast_fusion.3
  444.2 1.6 pad_maximum_fusion.1
  446.0 2.0 pad_maximum_fusion.refs_0_
  448.8 5.0 collective-permute-done.9.refs_11_
  453.8 134.7 %shard_map.239 = (f32[53,32,256]{2,1,0:T(8,128)}, bf16[13568,256]{1,0:T(8,128)(2,1)}, f32[1024,256]{1,0:T(8,128)}) custom-call(bf16[1,512,512]{2,1,0:T(8,128)(2,1)} %copy.230.refs_0_, bf16[256,1024]{1,0:T(8,128)(2,1)} %copy-done.14, bf16[13568,256]{1,0:T(8,128)(2,1)} %pad.28.refs_2_, bf16[13568,256]{1,0:T(8,128)(2,1)} %collective-permute-done.1.refs_3_, ...), custom_call_target="tpu_custom_call" | custom-call | tf_op jit(solution)/shard_map/pallas_call | solution.py:720
  588.4 1.6 copy.233
  591.3 16.6 %fusion.34 = (bf16[9216,256]{1,0:T(8,128)(2,1)}, f32[256,4096]{0,1:T(8,128)}) fusion(f32[256,4096]{0,1:T(8,128)} %get-tuple-element.197, bf16[4096,1024]{1,0:T(8,128)(2,1)} %bitcast.233, f32[1024,256]{0,1:T(8,128)S(1)} %dynamic-slice_dynamic-update-slice_fusion), kind=kOutput, calls=%fused_computation.58 | convolution fusion | flops 2222981120 | bytes 19922944 | tf_op jit(solution)/shard_map/dot_general | solution.py:45
  611.5 9.5 multiply_reduce_fusion.1
  622.6 1.6 copy.268
  624.2 1.3 slice_bitcast_fusion.1
  626.5 1.0 copy.251.refs_3_
  627.5 6.8 slice_bitcast_fusion
  634.4 120.1 %shard_map.240 = (f32[36,32,256]{2,1,0:T(8,128)}, bf16[256,3072]{1,0:T(8,128)(2,1)}) custom-call(bf16[6,512,512]{2,1,0:T(8,128)(2,1)} %pad_maximum_fusion.refs_0_, bf16[256,1024]{1,0:T(8,128)(2,1)} %get-tuple-element.32.refs_1_, bf16[2,2,256,2048]{3,2,1,0:T(8,128)(2,1)} %get-tuple-element.31.refs_2_, bf16[256,1024]{1,0:T(8,128)(2,1)} %copy.251.refs_3_, ...), custom_call_target="tpu_custom_call" | custom-call | tf_op jit(solution)/shard_map/pallas_call | solution.py:720
  754.5 2.8 copy.252
  757.3 5.4 multiply_reduce_fusion.2
  767.3 0.9 reshape_reshape.11
  769.1 1.0 copy.262
  770.1 1.4 copy.257
  772.0 1.2 reshape.432
  774.8 1.3 reshape.431
  776.1 1.0 maximum_bitcast_fusion.4
  777.2 1.0 maximum_bitcast_fusion.5
  778.4 1.6 copy.253.refs_0_
  779.9 155.8 %shard_map.241 = (f32[66,32,256]{2,1,0:T(8,128)}, f32[13568,256]{1,0:T(8,128)}) custom-call(bf16[3,512,512]{2,1,0:T(8,128)(2,1)} %copy.253.refs_0_, bf16[256,1024]{1,0:T(8,128)(2,1)} %copy-done.7, bf16[3072,256]{1,0:T(8,128)(2,1)} %bitcast.66.refs_2_, bf16[3072,256]{1,0:T(8,128)(2,1)} %collective-permute-done.17.refs_3_, ...), custom_call_target="tpu_custom_call" | custom-call | tf_op jit(solution)/shard_map/pallas_call | solution.py:720
  935.8 1.6 slice_bitcast_fusion.3
  937.4 1.0 slice_bitcast_fusion.5
  938.4 1.6 slice_reduce_fusion.1
  940.0 12.2 %bitcast_divide_fusion = f32[256,13500]{0,1:T(8,128)} fusion(bf16[256,13500]{0,1:T(8,128)(2,1)} %param.15, f32[13568,256]{1,0:T(8,128)} %get-tuple-element.44, f32[256]{0:T(256)S(1)} %copy-done.25), kind=kLoop, calls=%fused_computation.4 | loop fusion | flops 17280000 | bytes 34562048 | tf_op jit(solution)/shard_map/div | solution.py:997
  952.3 1.3 slice_bitcast_fusion.2
  (220 shorter events, 38.2 us)
Async XLA Ops:
  0.6 10.0 %copy-start.17 = (bf16[32,4096]{1,0:T(8,128)(2,1)S(1)}, bf16[32,4096]{1,0:T(8,128)(2,1)}, u32[]{:S(2)}) copy-start(bf16[32,4096]{1,0:T(8,128)(2,1)} %param.25) | copy-start | bytes 786436
  0.7 11.2 %copy-start.21 = (bf16[32,1024]{1,0:T(8,128)(2,1)S(1)}, bf16[32,1024]{1,0:T(8,128)(2,1)}, u32[]{:S(2)}) copy-start(bf16[32,1024]{1,0:T(8,128)(2,1)} %param.22) | copy-start | bytes 196612
  0.7 12.4 %copy-start.42 = (bf16[32]{0:T(256)(128)(2,1)S(1)}, bf16[32]{0:T(256)(128)(2,1)}, u32[]{:S(2)}) copy-start(bf16[32]{0:T(256)(128)(2,1)} %param.23) | copy-start | bytes 196
  0.7 12.4 %copy-start.41 = (bf16[32]{0:T(256)(128)(2,1)S(1)}, bf16[32]{0:T(256)(128)(2,1)}, u32[]{:S(2)}) copy-start(bf16[32]{0:T(256)(128)(2,1)} %param.24) | copy-start | bytes 196
  0.7 12.4 %copy-start.40 = (bf16[32]{0:T(256)(128)(2,1)S(1)}, bf16[32]{0:T(256)(128)(2,1)}, u32[]{:S(2)}) copy-start(bf16[32]{0:T(256)(128)(2,1)} %param.27) | copy-start | bytes 196
  0.7 12.4 %copy-start.39 = (bf16[32]{0:T(256)(128)(2,1)S(1)}, bf16[32]{0:T(256)(128)(2,1)}, u32[]{:S(2)}) copy-start(bf16[32]{0:T(256)(128)(2,1)} %param.28) | copy-start | bytes 196
  0.7 12.5 %copy-start.20 = (bf16[32,3072]{1,0:T(8,128)(2,1)S(1)}, bf16[32,3072]{1,0:T(8,128)(2,1)}, u32[]{:S(2)}) copy-start(bf16[32,3072]{1,0:T(8,128)(2,1)} %param.21) | copy-start | bytes 589828
  301.5 77.8 %collective-permute-start.3 = (bf16[128,13568]{1,0:T(8,128)(2,1)}, bf16[128,13568]{1,0:T(8,128)(2,1)}, u32[]{:S(2)}, u32[]{:S(2)}) collective-permute-start(bf16[128,13568]{1,0:T(8,128)(2,1)} %get-tuple-element.37.refs_4_), channel_id=1, source_target_pairs={{0,4},{4,0},{1,5},{5,1},{2,6},{6,2},{3,7},{7,3},{8,12},{12,8},{9,1... | collective-permute-start | bytes 10420232 | tf_op jit(solution)/shard_map/ppermute | solution.py:55
  301.6 84.4 %collective-permute-start.2 = (bf16[128,13568]{1,0:T(8,128)(2,1)}, bf16[128,13568]{1,0:T(8,128)(2,1)}, u32[]{:S(2)}, u32[]{:S(2)}) collective-permute-start(bf16[128,13568]{1,0:T(8,128)(2,1)} %get-tuple-element.37.refs_4_), channel_id=1, source_target_pairs={{0,2},{2,0},{1,3},{3,1},{4,6},{6,4},{5,7},{7,5},{8,10},{10,8},{9,1... | collective-permute-start | bytes 10420232 | tf_op jit(solution)/shard_map/ppermute | solution.py:55
  306.1 118.4 %collective-permute-start.10 = (bf16[256,512]{1,0:T(8,128)(2,1)}, bf16[256,512]{1,0:T(8,128)(2,1)}, u32[]{:S(2)}, u32[]{:S(2)}) collective-permute-start(bf16[256,512]{1,0:T(8,128)(2,1)} %pad_maximum_fusion.6), channel_id=1, source_target_pairs={{0,1},{1,0},{2,3},{3,2},{4,5},{5,4},{6,7},{7,6},{8,9},{9,8},{10,11... | collective-permute-start | bytes 786440 | tf_op jit(solution)/shard_map/ppermute | solution.py:55
  313.9 135.0 %collective-permute-start.1 = (bf16[13568,256]{1,0:T(8,128)(2,1)}, bf16[13568,256]{1,0:T(8,128)(2,1)}, u32[]{:S(2)}, u32[]{:S(2)}) collective-permute-start(bf16[13568,256]{1,0:T(8,128)(2,1)} %pad.28.refs_2_), channel_id=1, source_target_pairs={{0,1},{1,0},{2,3},{3,2},{4,5},{5,4},{6,7},{7,6},{8,9},{9,8},{10,11... | collective-permute-start | bytes 20840456 | tf_op jit(solution)/shard_map/ppermute | solution.py:55
  315.4 4.2 copy-start.8
  315.5 10.8 %copy-start.29 = (s32[256]{0:T(256)}, s32[256]{0:T(256)S(1)}, u32[]{:S(2)}) copy-start(s32[256]{0:T(256)S(1)} %slice_reduce_fusion) | copy-start | bytes 3076
  319.6 4.0 copy-start.9
  331.1 4.4 copy-start.10
  335.4 6.1 copy-start.22
  335.5 7.2 copy-start
  335.5 7.2 copy-start.3
  343.5 18.4 %copy-start.27 = (f32[256]{0:T(256)}, f32[256]{0:T(256)S(1)}, u32[]{:S(2)}) copy-start(f32[256]{0:T(256)S(1)} %broadcast_multiply_fusion.1) | copy-start | bytes 3076
  343.7 18.2 %copy-start.34 = (f32[256]{0:T(256)}, f32[256]{0:T(256)S(1)}, u32[]{:S(2)}) copy-start(f32[256]{0:T(256)S(1)} %multiply_reduce_fusion.5) | copy-start | bytes 3076
  343.7 18.2 %copy-start.30 = (f32[256]{0:T(256)}, f32[256]{0:T(256)S(1)}, u32[]{:S(2)}) copy-start(f32[256]{0:T(256)S(1)} %fusion.50) | copy-start | bytes 3076
  345.5 16.4 %copy-start.23 = (f32[1,1024]{1,0:T(1,128)}, f32[1,1024]{1,0:T(1,128)S(1)}, u32[]{:S(2)}) copy-start(f32[1,1024]{1,0:T(1,128)S(1)} %get-tuple-element.168) | copy-start | bytes 12292
  361.9 6.5 copy-start.1
  382.1 39.7 %collective-permute-start.4 = (bf16[128,6784]{1,0:T(8,128)(2,1)}, bf16[128,6784]{1,0:T(8,128)(2,1)}, u32[]{:S(2)}, u32[]{:S(2)}) collective-permute-start(bf16[128,6784]{1,0:T(8,128)(2,1)} %slice.146), channel_id=1, source_target_pairs={{0,2},{2,0},{1,3},{3,1},{4,6},{6,4},{5,7},{7,5},{8,10},{10,8},{9,1... | collective-permute-start | bytes 5210120 | tf_op jit(solution)/shard_map/ppermute | solution.py:55
  384.5 0.8 copy-start.14
  386.0 46.3 %collective-permute-start = (bf16[256,512]{1,0:T(8,128)(2,1)}, bf16[256,512]{1,0:T(8,128)(2,1)}, u32[]{:S(2)}, u32[]{:S(2)}) collective-permute-start(bf16[256,512]{1,0:T(8,128)(2,1)} %pad_maximum_fusion.5), channel_id=1, source_target_pairs={{0,1},{1,0},{2,3},{3,2},{4,5},{5,4},{6,7},{7,6},{8,9},{9,8},{10,11... | collective-permute-start | bytes 786440 | tf_op jit(solution)/shard_map/ppermute | solution.py:55
  388.8 40.6 %collective-permute-start.5 = (bf16[128,6784]{1,0:T(8,128)(2,1)}, bf16[128,6784]{1,0:T(8,128)(2,1)}, u32[]{:S(2)}, u32[]{:S(2)}) collective-permute-start(bf16[128,6784]{1,0:T(8,128)(2,1)} %slice.147), channel_id=1, source_target_pairs={{0,4},{4,0},{1,5},{5,1},{2,6},{6,2},{3,7},{7,3},{8,12},{12,8},{9,1... | collective-permute-start | bytes 5210120 | tf_op jit(solution)/shard_map/ppermute | solution.py:55
  390.5 1.7 copy-start.2
  421.7 11.6 %collective-permute-start.12 = (bf16[256,2048]{0,1:T(8,128)(2,1)S(1)}, bf16[256,2048]{0,1:T(8,128)(2,1)S(1)}, u32[]{:S(2)}, u32[]{:S(2)}) collective-permute-start(bf16[256,2048]{0,1:T(8,128)(2,1)S(1)} %pad_maximum_fusion.4), channel_id=1, source_target_pairs={{0,1},{1,0},{2,3},{3,2},{4,5},{5,4},{6,7},{7,6},{8,9},{9,8},{10,11... | collective-permute-start | bytes 3145736 | tf_op jit(solution)/shard_map/ppermute | solution.py:55
  424.5 8.2 collective-permute-start.11
  429.4 3.4 collective-permute-start.13
  432.3 15.8 %collective-permute-start.6 = (bf16[128,13568]{1,0:T(8,128)(2,1)}, bf16[128,13568]{1,0:T(8,128)(2,1)}, u32[]{:S(2)}, u32[]{:S(2)}) collective-permute-start(bf16[128,13568]{1,0:T(8,128)(2,1)} %get-tuple-element.37.refs_4_), channel_id=1, source_target_pairs={{0,1},{1,0},{2,3},{3,2},{4,5},{5,4},{6,7},{7,6},{8,9},{9,8},{10,11... | collective-permute-start | bytes 10420232 | tf_op jit(solution)/shard_map/ppermute | solution.py:55
  432.8 0.7 copy-start.19
  432.8 15.4 %collective-permute-start.7 = (bf16[128,13568]{1,0:T(8,128)(2,1)}, bf16[128,13568]{1,0:T(8,128)(2,1)}, u32[]{:S(2)}, u32[]{:S(2)}) collective-permute-start(bf16[128,13568]{1,0:T(8,128)(2,1)} %collective-permute-done.2.refs_5_), channel_id=1, source_target_pairs={{0,1},{1,0},{2,3},{3,2},{4,5},{5,4},{6,7},{7,6},{8,9},{9,8},{10,11... | collective-permute-start | bytes 10420232 | tf_op jit(solution)/shard_map/ppermute | solution.py:55
  432.9 0.7 copy-start.18
  432.9 15.9 %collective-permute-start.8 = (bf16[128,13568]{1,0:T(8,128)(2,1)}, bf16[128,13568]{1,0:T(8,128)(2,1)}, u32[]{:S(2)}, u32[]{:S(2)}) collective-permute-start(bf16[128,13568]{1,0:T(8,128)(2,1)} %collective-permute-done.3.refs_6_), channel_id=1, source_target_pairs={{0,1},{1,0},{2,3},{3,2},{4,5},{5,4},{6,7},{7,6},{8,9},{9,8},{10,11... | collective-permute-start | bytes 10420232 | tf_op jit(solution)/shard_map/ppermute | solution.py:55
  433.6 1.0 copy-start.13
  434.5 19.2 %collective-permute-start.9 = (bf16[128,13568]{1,0:T(8,128)(2,1)}, bf16[128,13568]{1,0:T(8,128)(2,1)}, u32[]{:S(2)}, u32[]{:S(2)}) collective-permute-start(bf16[128,13568]{1,0:T(8,128)(2,1)} %constant_dynamic-update-slice_fusion.8.refs_7_), channel_id=1, source_target_pairs={{0,1},{1,0},{2,3},{3,2},{4,5},{5,4},{6,7},{7,6},{8,9},{9,8},{10,11... | collective-permute-start | bytes 10420232 | tf_op jit(solution)/shard_map/ppermute | solution.py:55
  435.8 2.1 copy-start.32
  436.0 1.9 copy-start.36
  448.1 331.9 %collective-permute-start.18 = (bf16[13568,256]{1,0:T(8,128)(2,1)}, bf16[13568,256]{1,0:T(8,128)(2,1)}, u32[]{:S(2)}, u32[]{:S(2)}) collective-permute-start(bf16[13568,256]{1,0:T(8,128)(2,1)} %get-tuple-element.42.refs_6_), channel_id=1, source_target_pairs={{0,1},{1,0},{2,3},{3,2},{4,5},{5,4},{6,7},{7,6},{8,9},{9,8},{10,11... | collective-permute-start | bytes 20840456 | tf_op jit(solution)/shard_map/ppermute | solution.py:55
  590.3 1.0 copy-start.5
  607.9 3.6 copy-start.24
  607.9 3.6 copy-start.28
  607.9 3.6 copy-start.31
  608.1 3.3 copy-start.43
  611.4 9.5 copy-start.35
  611.4 9.9 %copy-start.6 = (f32[1024,256]{0,1:T(8,128)S(1)}, f32[1024,256]{0,1:T(8,128)}, u32[]{:S(2)}) copy-start(f32[1024,256]{0,1:T(8,128)} %copy-done.5) | copy-start | bytes 3145732
  621.8 3.7 copy-start.4
  622.6 11.8 %collective-permute-start.14 = (bf16[9216,256]{1,0:T(8,128)(2,1)}, bf16[9216,256]{1,0:T(8,128)(2,1)}, u32[]{:S(2)}, u32[]{:S(2)}) collective-permute-start(bf16[9216,256]{1,0:T(8,128)(2,1)} %constant_dynamic-update-slice_fusion.10.refs_7_), channel_id=1, source_target_pairs={{0,1},{1,0},{2,3},{3,2},{4,5},{5,4},{6,7},{7,6},{8,9},{9,8},{10,11... | collective-permute-start | bytes 14155784 | tf_op jit(solution)/shard_map/ppermute | solution.py:55
  634.4 122.9 %copy-start.26 = (f32[1,1024]{1,0:T(1,128)S(1)}, f32[1,1024]{1,0:T(1,128)}, u32[]{:S(2)}) copy-start(f32[1,1024]{1,0:T(1,128)} %get-tuple-element.166) | copy-start | bytes 12292
  634.4 122.9 %copy-start.33 = (f32[256]{0:T(256)S(1)}, f32[256]{0:T(256)}, u32[]{:S(2)}) copy-start(f32[256]{0:T(256)} %copy-done.32) | copy-start | bytes 3076
  634.4 122.9 %copy-start.38 = (f32[256]{0:T(256)S(1)}, f32[256]{0:T(256)}, u32[]{:S(2)}) copy-start(f32[256]{0:T(256)} %fusion.51) | copy-start | bytes 3076
  757.3 6.9 copy-start.37
  762.9 3.5 copy-start.12
  763.7 12.5 %collective-permute-start.15 = (bf16[256,512]{1,0:T(8,128)(2,1)}, bf16[256,512]{1,0:T(8,128)(2,1)}, u32[]{:S(2)}, u32[]{:S(2)}) collective-permute-start(bf16[256,512]{1,0:T(8,128)(2,1)} %pad_maximum_fusion.9), channel_id=1, source_target_pairs={{0,1},{1,0},{2,3},{3,2},{4,5},{5,4},{6,7},{7,6},{8,9},{9,8},{10,11... | collective-permute-start | bytes 786440 | tf_op jit(solution)/shard_map/ppermute | solution.py:55
  763.7 16.3 %collective-permute-start.17 = (bf16[3072,256]{1,0:T(8,128)(2,1)}, bf16[3072,256]{1,0:T(8,128)(2,1)}, u32[]{:S(2)}, u32[]{:S(2)}) collective-permute-start(bf16[3072,256]{1,0:T(8,128)(2,1)} %bitcast.66.refs_2_), channel_id=1, source_target_pairs={{0,1},{1,0},{2,3},{3,2},{4,5},{5,4},{6,7},{7,6},{8,9},{9,8},{10,11... | collective-permute-start | bytes 4718600 | tf_op jit(solution)/shard_map/ppermute | solution.py:55
  764.8 4.2 copy-start.7
  766.4 10.7 %collective-permute-start.16 = (bf16[256,512]{1,0:T(8,128)(2,1)}, bf16[256,512]{1,0:T(8,128)(2,1)}, u32[]{:S(2)}, u32[]{:S(2)}) collective-permute-start(bf16[256,512]{1,0:T(8,128)(2,1)} %pad_maximum_fusion.10), channel_id=1, source_target_pairs={{0,1},{1,0},{2,3},{3,2},{4,5},{5,4},{6,7},{7,6},{8,9},{9,8},{10,11... | collective-permute-start | bytes 786440 | tf_op jit(solution)/shard_map/ppermute | solution.py:55
  770.1 7.1 copy-start.15
  770.1 7.1 copy-start.16
  771.5 6.7 copy-start.11
  935.8 4.2 copy-start.25

commit v8 on v7

--- a/solution.py
+++ b/solution.py
@@ -162,9 +162,8 @@
                 copy(j, k).wait_recv()
 
     n = sum(array < n_full for array, *_ in jobs)
-    ahead = 2
-    for j in range(ahead):
-        start_h(j)
+    start_h(0)
+    start_h(1)
     for step in range(n + 2):
         if step < n:
             own_copy(step).wait()
@@ -172,8 +171,11 @@
                 h_copy(step, d).wait_recv()
             for k in (0, 1, 2):
                 copy(step, k).start()
-            if step + ahead < len(jobs):
-                start_h(step + ahead)
+            for j in (2, 3) if step == 0 else (step + 3,):
+                if j < n:
+                    start_h(j)
+            if 0 < step and n + step - 1 < len(jobs):
+                start_h(n + step - 1)
         if 0 <= step - 1 < n:
             for k in (0, 1):
                 copy(step - 1, k).wait_recv()
@@ -184,8 +186,6 @@
                 copy(step - 2, k).wait_recv()
             copy(step - 2, 7).start()
         between(step, landed)
-    for j in range(n + ahead, len(jobs)):
-        start_h(j)
     for j in range(n, len(jobs)):
         own_copy(j).wait()
         for d in range(1, n_h):
@@ -401,7 +401,7 @@
     return out[: len(shards)], *out[len(shards) :]
 
 
-def scatter_kernel(n_h, sections, left_starts, lefts, rights, out, scratch, peers, prefetch, beside, after):
+def scatter_kernel(n_h, sections, periods, left_starts, lefts, rights, out, scratch, peers, prefetch, beside, after):
     (right_buf, own, s1, r1, s2, r2, s3, r3, load_sem, send1, recv1, send2, recv2, send3, recv3) = scratch
     h, x, y = (lax.axis_index(name) for name in ("h", "x", "y"))
     to_x, to_y = {"x": 1 - x}, {"y": 1 - y}
@@ -430,7 +430,7 @@
 
             @pl.when((i >= start) & (i < start + count))
             def _(section=section, start=start):
-                for copy in loads(i, section, i - start):
+                for copy in loads(i, section, lax.rem(i - start, periods[section])):
                     copy.start()
                 prefetch(section, i - start)
 
@@ -546,7 +546,7 @@
     return pl.ds(pl.multiple_of(k * CHUNK, CHUNK), CHUNK)
 
 
-def product_kernel(n_h, sections, left_starts, n_weights, with_sum, *refs):
+def product_kernel(n_h, sections, periods, left_starts, n_weights, with_sum, *refs):
     lefts, vector = refs[:2]
     n_rights = 2 * len(sections)
     rights, weights = refs[2 : 2 + n_rights], refs[2 + n_rights : 2 + n_rights + n_weights]
@@ -611,13 +611,13 @@
                 multiply(i - begin, right)
 
     scatter_kernel(
-        n_h, sections, left_starts, lefts, rights, out, scratch, [], prefetch, beside, lambda p: None
+        n_h, sections, periods, left_starts, lefts, rights, out, scratch, [], prefetch, beside, lambda p: None
     )
     for k in range(max(count - 2, 0), count):
         product_store(k).wait()
 
 
-def attention_kernel(n_h, sections, left_starts, scale, *refs):
+def attention_kernel(n_h, sections, periods, left_starts, scale, *refs):
     lefts, query, pairs, d_out, log_total, seg_keys, seg_mine = refs[:7]
     n_rights = 2 * len(sections)
     rights = refs[7 : 7 + n_rights]
@@ -663,17 +663,22 @@
             send_sem=send.at[1], recv_sem=recv.at[1], device_id={"y": 1 - y}, device_id_type=MESH,
         )
 
+    both = n_pairs // 2
+
     def beside(i, right, odd):
-        @pl.when(i < 2 * n_pairs)
+        p = i // 2
+        late = (p + 1024 - both) // 1024
+
+        @pl.when((p < both) | ((p < 3 * both) & (lax.rem(p, 2) == odd)))
         def _():
-            backward(i // 2, odd)
+            backward(p - late * (p - both // 2 - p // 2), odd)
 
     def after(p):
-        @pl.when(p == n_pairs)
+        @pl.when(p == 3 * both)
         def _():
             to_core().start()
 
-        @pl.when(p == n_pairs + 2)
+        @pl.when(p == 3 * both + 2)
         def _():
             to_core().wait_recv()
 
@@ -687,7 +692,7 @@
             to_y().start()
 
     scatter_kernel(
-        n_h, sections, left_starts, lefts, rights, out, scratch, [{"c": 1 - c}],
+        n_h, sections, periods, left_starts, lefts, rights, out, scratch, [{"c": 1 - c}],
         lambda section, k: None, beside, after,
     )
     to_y().wait_recv()
@@ -705,7 +710,8 @@
 
 
 def scatter_call(kernel, lefts, rights, operands, more_operands, out_shapes, out_specs, scratch, collective_id):
-    sections = [own.shape[0] // CHUNK for own, _ in rights]
+    periods = [own.shape[0] // CHUNK for own, *_ in rights]
+    sections = [period * times for period, (*_, times) in zip(periods, rights)]
     n, cells = sum(sections), rights[0][0].shape[1]
     w = lefts.shape[1] // 4
     n_h = lax.axis_size("h")
@@ -718,7 +724,7 @@
     if inner_h == 1:
         part_shape = jax.ShapeDtypeStruct((n, w, CHUNK), bf16)
     part, *more = pl.pallas_call(
-        functools.partial(kernel, inner_h, sections),
+        functools.partial(kernel, inner_h, sections, periods),
         out_shape=[part_shape] + out_shapes,
         in_specs=[vmem] * (1 + len(operands)) + [hbm] * (2 * len(rights) + len(more_operands)),
         out_specs=[vmem] + out_specs,
@@ -743,7 +749,7 @@
         compiler_params=pltpu.CompilerParams(
             collective_id=collective_id, has_side_effects=True, vmem_limit_bytes=60 * 2**20
         ),
-    )(lefts, *operands, *(half for pair in rights for half in pair), *more_operands)
+    )(lefts, *operands, *(half for pair in rights for half in pair[:2]), *more_operands)
     if inner_h == 1:
         part = lax.psum_scatter(part, "h", scatter_dimension=1, tiled=True).astype(f32)
     return part, *more
@@ -754,8 +760,8 @@
     dma = pltpu.SemaphoreType.DMA
     vmem, hbm = pl.BlockSpec(memory_space=pltpu.VMEM), pl.BlockSpec(memory_space=pl.ANY)
 
-    def kernel(n_h, sections, *refs):
-        product_kernel(n_h, sections, left_starts, len(weights), with_sum, *refs)
+    def kernel(n_h, sections, periods, *refs):
+        product_kernel(n_h, sections, periods, left_starts, len(weights), with_sum, *refs)
 
     return scatter_call(
         kernel,
@@ -780,8 +786,8 @@
     cells, width = query.shape
     bf16, vmem = jnp.bfloat16, pl.BlockSpec(memory_space=pltpu.VMEM)
 
-    def kernel(n_h, sections, *refs):
-        attention_kernel(n_h, sections, left_starts, scale, *refs)
+    def kernel(n_h, sections, periods, *refs):
+        attention_kernel(n_h, sections, periods, left_starts, scale, *refs)
 
     return scatter_call(
         kernel,
@@ -815,8 +821,8 @@
     return left.transpose(2, 0, 1, 3, 4).reshape(pieces, -1, left.shape[-1])
 
 
-def both_cores(right):
-    return right, swap(right, "c")
+def both_cores(right, times=1):
+    return right, swap(right, "c"), times
 
 
 def columns_of(chunks):
@@ -877,8 +883,10 @@
         jnp.pad(w_dec.T, pad),
     ]
     cuts = [gene_cuts, [0, width // 2 * 3, 3 * width + 128], [0, width]]
-    cuts += [[0, 2 * width, 4 * width], [0, width // 2, width], [0, padded]]
-    order = [(0, 0), (0, 1), (0, 2), (0, 3), (1, 0), (1, 1), (2, 0), (3, 0), (3, 1), (4, 0), (4, 1), (5, 0)]
+    cuts += [[0, 2 * width, 4 * width], [0, width // 2, width]]
+    cuts += [[k * (padded // 1024) * 128 for k in range(8)] + [padded]]
+    order = [(0, 0), (0, 1), (0, 2), (0, 3), (1, 0), (1, 1), (2, 0), (3, 0), (3, 1), (4, 0), (4, 1)]
+    order += [(5, piece) for piece in range(8)]
     gathered, xb, h0, a1, query, kv_all = gather_all(
         shards, 5, cuts, order, counts.T, scale[None, :], pe.T, 0
     )
@@ -919,7 +927,10 @@
     h1 = h0 + matmul(attended_b, out_all)
     a2 = layer_norm(h1, g2f, b2f).astype(jnp.bfloat16)
     hidden = matmul(a2, up_all)
-    act = jax.nn.gelu(hidden, approximate=False).astype(jnp.bfloat16)
+    act, pull = jax.vjp(lambda v: jax.nn.gelu(v, approximate=False), hidden)
+    act, slope = lax.optimization_barrier(
+        (act.astype(jnp.bfloat16), pull(jnp.ones_like(hidden))[0])
+    )
     h2 = h1 + matmul(act, down_all)
     hb = h2.astype(jnp.bfloat16)
     grad_dec, logits, dh2 = scatter_product(
@@ -931,8 +942,7 @@
     dh2 = relative(dh2, 0).T
     dfb = dh2.astype(jnp.bfloat16)
     d_act = contract_cols(dfb, down_all)
-    slope = jax.vjp(lambda v: jax.nn.gelu(v, approximate=False), hidden)[1](d_act)[0]
-    d_hidden = slope.astype(jnp.bfloat16)
+    d_hidden = (d_act * slope).astype(jnp.bfloat16)
     da2 = contract_cols(d_hidden, up_all)
     norm_pull = jax.vjp(layer_norm, h1, g2f, b2f)[1]
     dh1_norm, grad_gain_two, grad_shift_two = norm_pull(da2)
@@ -942,11 +952,11 @@
     d_attended = from_owner(d_attended, 1)
     lefts = [left_of(a2, 1), left_of(act, act.shape[1] // width), left_of(attended_b, 1)]
     pieces = (4 * width,) + (width,) * 4
-    rights = [d_hidden.T] + [dfb.T] * 4 + [dab.T]
+    rights = [both_cores(d_hidden.T), both_cores(dfb.T, 4), both_cores(dab.T)]
     grads, d_qkv = scatter_attention(
         jnp.concatenate(lefts, axis=0),
         [sum(pieces[:k]) // CHUNK for k in range(len(pieces) + 1)],
-        [both_cores(jnp.concatenate(rights, axis=0))],
+        rights,
         query_b,
         kv_pairs,
         d_attended,
@@ -975,7 +985,7 @@
     grads, d_xb = scatter_product(
         jnp.concatenate(lefts, axis=0),
         [0, 3 * width // CHUNK, (3 * width + rows) // CHUNK],
-        [both_cores(d_qkv.T), (unit, unit), xb_pair],
+        [both_cores(d_qkv.T), (unit, unit, 1), xb_pair],
         dh0b,
         [enc_all],
         jnp.float32,

time: 961 us -> 967 us (level)
  Pallas kernels: 695 us -> 710 us
    pallas_call x3, Pallas kernels: 411 us -> 423 us  [scatter_call(): pl.pallas_call(functools.partial(kernel, inner_h, sections, periods), out...]
    ppermute x19 -> x21, waiting for transfers between devices: 48.7 us -> 47 us  [swap(): return lax.ppermute(value, axis, [(0, 1), (1, 0)])]
  transfers between devices with their start and end apart: 19 -> 21, of which waited for: 5 -> 5; matrix products, arithmetic and copies ran while one was open for 17% -> 16% of each run, Pallas kernels for 27% -> 28%
where the time goes in v8:
time: 967 us; the launch traced here: 960 us
  Pallas kernels  710 us (73%)
  local copies, waits for them, and re-layouts  93.7 us (10%)
  matrix products  56.5 us (6%)
  waiting for transfers between devices  47 us (5%)
  other arithmetic  42.8 us (4%)
    pallas_call x3, Pallas kernels, scatter_call(): pl.pallas_call(functools.partial(kernel, inner_h, sections, periods), out...  423 us
    pallas_call x1, Pallas kernels, gather_all(): pl.pallas_call(functools.partial(front_kernel, n_h, jobs, len(shards), n_...  286 us
    ppermute x21, waiting for transfers between devices, swap(): return lax.ppermute(value, axis, [(0, 1), (1, 0)])  47 us
    dot_general x4, matrix products, contract_cols(): lax.dot_general(left, right, (((1,), (1,)), ((), ())), preferred_element_...  22.9 us
    dot_general x3, matrix products, matmul(): return jnp.dot(left, right, preferred_element_type=jnp.float32)  22.5 us
  transfers between devices with their start and end apart: 21, of which 5 were waited for; matrix products, arithmetic and copies ran while one was open for 16% of the time, Pallas kernels for 28%

profile of v8, /device:TPU:0, one launch (start us, length us, event | category | flops | bytes accessed | tf_op | source)
XLA Modules:
  0.0 960.1 jit_solution(14031166718745315511)
XLA Ops:
  2.5 1.3 broadcast_divide_fusion
  4.4 2.1 pad.24.refs_0_
  6.6 2.1 pad.26.refs_5_
  8.7 1.1 copy.211
  13.9 1.9 multiply_sine_fusion.1
  15.8 1.1 pad_maximum_fusion.3
  16.9 286.4 %shard_map.238 = (bf16[2,2,2,128,13568]{4,3,2,1,0:T(8,128)(2,1)}, bf16[2,2,2,128,3200]{4,3,2,1,0:T(8,128)(2,1)}, bf16[2,2,2,128,1024]{4,3,2,1,0:T(8,128)(2,1)}, ...) custom-call(bf16[32,13568]{1,0:T(8,128)(2,1)} %pad.24.refs_0_, ...), custom_call_target="tpu_custom_call" | custom-call | tf_op jit(solution)/shard_map/pallas_call | solution.py:362
  303.3 1.2 collective-permute-start.3
  305.4 1.8 constant_dynamic-slice_fusion.47
  307.9 7.7 pad.28.refs_2_
  318.0 4.0 fusion.34
  321.9 4.0 copy.217
  326.2 2.6 copy.214
  328.9 4.5 fusion
  333.4 4.4 fusion.1
  337.8 6.6 fusion.13
  348.3 15.9 %multiply_add_fusion = (f32[256,4096]{0,1:T(8,128)}, f32[256,4096]{0,1:T(8,128)S(1)}, f32[256,4096]{0,1:T(8,128)S(1)}) fusion(bf16[256,1024]{1,0:T(8,128)(2,1)S(1)} %add_convert_fusion.1, bf16[1024,4096]{1,0:T(8,128)(2,1)} %bitcast.215), kind=kOutput, calls=%fused_computation.14 | convolution fusion | flops 2218786816 | bytes 21495808 | tf_op jit(solution)/shard_map/dot_general | solution.py:51
  364.9 5.7 fusion.12
  371.3 9.8 %collective-permute-done.3.refs_6_ = bf16[128,13568]{1,0:T(8,128)(2,1)} collective-permute-done((bf16[128,13568]{1,0:T(8,128)(2,1)}, bf16[128,13568]{1,0:T(8,128)(2,1)}, u32[]{:S(2)}, u32[]{:S(2)}) %collective-permute-start.3) | collective-permute-done | bytes 3473440 | tf_op jit(solution)/shard_map/ppermute | solution.py:55
  381.1 2.8 slice.146
  383.8 1.1 collective-permute-start.4
  388.6 2.8 slice.147
  392.3 1.8 constant_dynamic-slice_fusion.39
  394.1 1.8 constant_dynamic-slice_fusion.23
  397.0 26.5 %collective-permute-done.4 = bf16[128,6784]{1,0:T(8,128)(2,1)} collective-permute-done((bf16[128,6784]{1,0:T(8,128)(2,1)}, bf16[128,6784]{1,0:T(8,128)(2,1)}, u32[]{:S(2)}, u32[]{:S(2)}) %collective-permute-start.4) | collective-permute-done | bytes 1736736 | tf_op jit(solution)/shard_map/ppermute | solution.py:55
  423.5 2.8 constant_dynamic-update-slice_fusion.9
  426.8 5.1 collective-permute-done.5
  432.0 2.8 constant_dynamic-update-slice_fusion.8.refs_7_
  439.2 1.3 log_add_fusion.refs_4_
  440.5 1.1 maximum_bitcast_fusion
  441.6 1.0 copy.223.refs_0_
  442.6 1.1 maximum_bitcast_fusion.2
  443.9 1.8 maximum_bitcast_fusion.1
  445.7 1.0 maximum_bitcast_fusion.3
  446.8 1.6 pad_maximum_fusion.1
  448.6 2.1 pad_maximum_fusion.refs_0_
  451.4 5.0 collective-permute-done.9.refs_11_
  456.3 145.3 %shard_map.239 = (f32[53,32,256]{2,1,0:T(8,128)}, bf16[13568,256]{1,0:T(8,128)(2,1)}, f32[1024,256]{1,0:T(8,128)}) custom-call(bf16[1,512,512]{2,1,0:T(8,128)(2,1)} %copy.223.refs_0_, bf16[256,1024]{1,0:T(8,128)(2,1)} %copy-done.12, bf16[13568,256]{1,0:T(8,128)(2,1)} %pad.28.refs_2_, bf16[13568,256]{1,0:T(8,128)(2,1)} %collective-permute-done.1.refs_3_, ...), custom_call_target="tpu_custom_call" | custom-call | tf_op jit(solution)/shard_map/pallas_call | solution.py:726
  601.6 1.6 copy.226
  603.6 8.4 fusion.5
  612.0 6.8 multiply_reduce_fusion.1
  620.8 3.1 slice_bitcast_fusion
  624.0 1.3 slice_bitcast_fusion.1
  625.3 2.0 copy.240.refs_11_
  628.3 2.3 convolution_convert_fusion
  630.7 1.0 copy.235
  631.7 1.1 copy.236
  632.8 1.0 copy.237.refs_3_
  633.8 2.0 copy.241.refs_12_
  635.8 2.0 copy.239.refs_10_
  637.9 120.5 %shard_map.240 = (f32[36,32,256]{2,1,0:T(8,128)}, bf16[256,3072]{1,0:T(8,128)(2,1)}) custom-call(bf16[6,512,512]{2,1,0:T(8,128)(2,1)} %pad_maximum_fusion.refs_0_, bf16[256,1024]{1,0:T(8,128)(2,1)} %get-tuple-element.34.refs_1_, bf16[2,2,256,2048]{3,2,1,0:T(8,128)(2,1)} %get-tuple-element.33.refs_2_, bf16[256,1024]{1,0:T(8,128)(2,1)} %copy.237.refs_3_, ...), custom_call_target="tpu_custom_call" | custom-call | tf_op jit(solution)/shard_map/pallas_call | solution.py:726
  758.4 2.6 copy.242
  761.0 5.4 multiply_reduce_fusion.2
  773.8 1.4 copy.247
  775.7 1.2 reshape.432
  778.5 1.3 reshape.431
  780.9 1.0 maximum_bitcast_fusion.5
  782.1 1.6 copy.243.refs_0_
  783.6 157.6 %shard_map.241 = (f32[66,32,256]{2,1,0:T(8,128)}, f32[13568,256]{1,0:T(8,128)}) custom-call(bf16[3,512,512]{2,1,0:T(8,128)(2,1)} %copy.243.refs_0_, bf16[256,1024]{1,0:T(8,128)(2,1)} %copy-done.3, bf16[3072,256]{1,0:T(8,128)(2,1)} %bitcast.64.refs_2_, bf16[3072,256]{1,0:T(8,128)(2,1)} %collective-permute-done.19.refs_3_, ...), custom_call_target="tpu_custom_call" | custom-call | tf_op jit(solution)/shard_map/pallas_call | solution.py:726
  941.3 1.6 slice_bitcast_fusion.3
  942.9 1.0 slice_bitcast_fusion.5
  943.9 1.6 slice_reduce_fusion.1
  945.5 12.2 %bitcast_divide_fusion = f32[256,13500]{0,1:T(8,128)} fusion(bf16[256,13500]{0,1:T(8,128)(2,1)} %param.15, f32[13568,256]{1,0:T(8,128)} %get-tuple-element.48, f32[256]{0:T(256)S(1)} %copy-done.23), kind=kLoop, calls=%fused_computation.4 | loop fusion | flops 17280000 | bytes 34562048 | tf_op jit(solution)/shard_map/div | solution.py:1007
  957.8 1.3 slice_bitcast_fusion.2
  (221 shorter events, 41.6 us)
Async XLA Ops:
  0.6 10.0 %copy-start.15 = (bf16[32,4096]{1,0:T(8,128)(2,1)S(1)}, bf16[32,4096]{1,0:T(8,128)(2,1)}, u32[]{:S(2)}) copy-start(bf16[32,4096]{1,0:T(8,128)(2,1)} %param.25) | copy-start | bytes 786436
  0.7 11.2 %copy-start.19 = (bf16[32,1024]{1,0:T(8,128)(2,1)S(1)}, bf16[32,1024]{1,0:T(8,128)(2,1)}, u32[]{:S(2)}) copy-start(bf16[32,1024]{1,0:T(8,128)(2,1)} %param.22) | copy-start | bytes 196612
  0.7 12.4 %copy-start.40 = (bf16[32]{0:T(256)(128)(2,1)S(1)}, bf16[32]{0:T(256)(128)(2,1)}, u32[]{:S(2)}) copy-start(bf16[32]{0:T(256)(128)(2,1)} %param.23) | copy-start | bytes 196
  0.7 12.4 %copy-start.39 = (bf16[32]{0:T(256)(128)(2,1)S(1)}, bf16[32]{0:T(256)(128)(2,1)}, u32[]{:S(2)}) copy-start(bf16[32]{0:T(256)(128)(2,1)} %param.24) | copy-start | bytes 196
  0.7 12.4 %copy-start.38 = (bf16[32]{0:T(256)(128)(2,1)S(1)}, bf16[32]{0:T(256)(128)(2,1)}, u32[]{:S(2)}) copy-start(bf16[32]{0:T(256)(128)(2,1)} %param.27) | copy-start | bytes 196
  0.7 12.4 %copy-start.37 = (bf16[32]{0:T(256)(128)(2,1)S(1)}, bf16[32]{0:T(256)(128)(2,1)}, u32[]{:S(2)}) copy-start(bf16[32]{0:T(256)(128)(2,1)} %param.28) | copy-start | bytes 196
  0.7 12.5 %copy-start.18 = (bf16[32,3072]{1,0:T(8,128)(2,1)S(1)}, bf16[32,3072]{1,0:T(8,128)(2,1)}, u32[]{:S(2)}) copy-start(bf16[32,3072]{1,0:T(8,128)(2,1)} %param.21) | copy-start | bytes 589828
  303.3 77.8 %collective-permute-start.3 = (bf16[128,13568]{1,0:T(8,128)(2,1)}, bf16[128,13568]{1,0:T(8,128)(2,1)}, u32[]{:S(2)}, u32[]{:S(2)}) collective-permute-start(bf16[128,13568]{1,0:T(8,128)(2,1)} %get-tuple-element.40.refs_4_), channel_id=1, source_target_pairs={{0,4},{4,0},{1,5},{5,1},{2,6},{6,2},{3,7},{7,3},{8,12},{12,8},{9,1... | collective-permute-start | bytes 10420232 | tf_op jit(solution)/shard_map/ppermute | solution.py:55
  304.5 84.1 %collective-permute-start.2 = (bf16[128,13568]{1,0:T(8,128)(2,1)}, bf16[128,13568]{1,0:T(8,128)(2,1)}, u32[]{:S(2)}, u32[]{:S(2)}) collective-permute-start(bf16[128,13568]{1,0:T(8,128)(2,1)} %get-tuple-element.40.refs_4_), channel_id=1, source_target_pairs={{0,2},{2,0},{1,3},{3,1},{4,6},{6,4},{5,7},{7,5},{8,10},{10,8},{9,1... | collective-permute-start | bytes 10420232 | tf_op jit(solution)/shard_map/ppermute | solution.py:55
  307.9 118.4 %collective-permute-start.10 = (bf16[256,512]{1,0:T(8,128)(2,1)}, bf16[256,512]{1,0:T(8,128)(2,1)}, u32[]{:S(2)}, u32[]{:S(2)}) collective-permute-start(bf16[256,512]{1,0:T(8,128)(2,1)} %pad_maximum_fusion.6), channel_id=1, source_target_pairs={{0,1},{1,0},{2,3},{3,2},{4,5},{5,4},{6,7},{7,6},{8,9},{9,8},{10,11... | collective-permute-start | bytes 786440 | tf_op jit(solution)/shard_map/ppermute | solution.py:55
  315.6 135.7 %collective-permute-start.1 = (bf16[13568,256]{1,0:T(8,128)(2,1)}, bf16[13568,256]{1,0:T(8,128)(2,1)}, u32[]{:S(2)}, u32[]{:S(2)}) collective-permute-start(bf16[13568,256]{1,0:T(8,128)(2,1)} %pad.28.refs_2_), channel_id=1, source_target_pairs={{0,1},{1,0},{2,3},{3,2},{4,5},{5,4},{6,7},{7,6},{8,9},{9,8},{10,11... | collective-permute-start | bytes 20840456 | tf_op jit(solution)/shard_map/ppermute | solution.py:55
  317.2 0.8 copy-start.5
  317.3 11.4 %copy-start.27 = (s32[256]{0:T(256)}, s32[256]{0:T(256)S(1)}, u32[]{:S(2)}) copy-start(s32[256]{0:T(256)S(1)} %slice_reduce_fusion) | copy-start | bytes 3076
  321.9 4.0 copy-start.6
  337.8 6.7 copy-start.20
  337.8 6.7 copy-start
  337.8 6.7 copy-start.2
  344.5 0.9 copy-start.4
  345.4 18.8 %copy-start.25 = (f32[256]{0:T(256)}, f32[256]{0:T(256)S(1)}, u32[]{:S(2)}) copy-start(f32[256]{0:T(256)S(1)} %broadcast_multiply_fusion.1) | copy-start | bytes 3076
  345.7 0.6 copy-start.32
  345.7 18.6 %copy-start.28 = (f32[256]{0:T(256)}, f32[256]{0:T(256)S(1)}, u32[]{:S(2)}) copy-start(f32[256]{0:T(256)S(1)} %fusion.26) | copy-start | bytes 3076
  348.0 16.2 %copy-start.21 = (f32[1,1024]{1,0:T(1,128)}, f32[1,1024]{1,0:T(1,128)S(1)}, u32[]{:S(2)}) copy-start(f32[1,1024]{1,0:T(1,128)S(1)} %get-tuple-element.172) | copy-start | bytes 12292
  348.3 16.0 %copy-start.7 = (bf16[256,1024]{1,0:T(8,128)(2,1)}, bf16[256,1024]{1,0:T(8,128)(2,1)S(1)}, u32[]{:S(2)}) copy-start(bf16[256,1024]{1,0:T(8,128)(2,1)S(1)} %add_convert_fusion.1) | copy-start | bytes 1572868
  383.8 39.7 %collective-permute-start.4 = (bf16[128,6784]{1,0:T(8,128)(2,1)}, bf16[128,6784]{1,0:T(8,128)(2,1)}, u32[]{:S(2)}, u32[]{:S(2)}) collective-permute-start(bf16[128,6784]{1,0:T(8,128)(2,1)} %slice.146), channel_id=1, source_target_pairs={{0,2},{2,0},{1,3},{3,1},{4,6},{6,4},{5,7},{7,5},{8,10},{10,8},{9,1... | collective-permute-start | bytes 5210120 | tf_op jit(solution)/shard_map/ppermute | solution.py:55
  387.0 0.8 copy-start.12
  388.6 46.3 %collective-permute-start = (bf16[256,512]{1,0:T(8,128)(2,1)}, bf16[256,512]{1,0:T(8,128)(2,1)}, u32[]{:S(2)}, u32[]{:S(2)}) collective-permute-start(bf16[256,512]{1,0:T(8,128)(2,1)} %pad_maximum_fusion.5), channel_id=1, source_target_pairs={{0,1},{1,0},{2,3},{3,2},{4,5},{5,4},{6,7},{7,6},{8,9},{9,8},{10,11... | collective-permute-start | bytes 786440 | tf_op jit(solution)/shard_map/ppermute | solution.py:55
  391.3 40.6 %collective-permute-start.5 = (bf16[128,6784]{1,0:T(8,128)(2,1)}, bf16[128,6784]{1,0:T(8,128)(2,1)}, u32[]{:S(2)}, u32[]{:S(2)}) collective-permute-start(bf16[128,6784]{1,0:T(8,128)(2,1)} %slice.147), channel_id=1, source_target_pairs={{0,4},{4,0},{1,5},{5,1},{2,6},{6,2},{3,7},{7,3},{8,12},{12,8},{9,1... | collective-permute-start | bytes 5210120 | tf_op jit(solution)/shard_map/ppermute | solution.py:55
  396.9 40.6 %copy-start.1 = (f32[256,1024]{1,0:T(8,128)S(1)}, f32[256,1024]{1,0:T(8,128)}, u32[]{:S(2)}) copy-start(f32[256,1024]{1,0:T(8,128)} %get-tuple-element.32) | copy-start | bytes 3145732
  423.5 12.3 %collective-permute-start.12 = (bf16[256,2048]{0,1:T(8,128)(2,1)S(1)}, bf16[256,2048]{0,1:T(8,128)(2,1)S(1)}, u32[]{:S(2)}, u32[]{:S(2)}) collective-permute-start(bf16[256,2048]{0,1:T(8,128)(2,1)S(1)} %pad_maximum_fusion.4), channel_id=1, source_target_pairs={{0,1},{1,0},{2,3},{3,2},{4,5},{5,4},{6,7},{7,6},{8,9},{9,8},{10,11... | collective-permute-start | bytes 3145736 | tf_op jit(solution)/shard_map/ppermute | solution.py:55
  426.3 9.0 collective-permute-start.11
  432.0 3.4 collective-permute-start.13
  434.8 15.9 %collective-permute-start.6 = (bf16[128,13568]{1,0:T(8,128)(2,1)}, bf16[128,13568]{1,0:T(8,128)(2,1)}, u32[]{:S(2)}, u32[]{:S(2)}) collective-permute-start(bf16[128,13568]{1,0:T(8,128)(2,1)} %get-tuple-element.40.refs_4_), channel_id=1, source_target_pairs={{0,1},{1,0},{2,3},{3,2},{4,5},{5,4},{6,7},{7,6},{8,9},{9,8},{10,11... | collective-permute-start | bytes 10420232 | tf_op jit(solution)/shard_map/ppermute | solution.py:55
  435.3 0.7 copy-start.17
  435.3 15.5 %collective-permute-start.7 = (bf16[128,13568]{1,0:T(8,128)(2,1)}, bf16[128,13568]{1,0:T(8,128)(2,1)}, u32[]{:S(2)}, u32[]{:S(2)}) collective-permute-start(bf16[128,13568]{1,0:T(8,128)(2,1)} %collective-permute-done.2.refs_5_), channel_id=1, source_target_pairs={{0,1},{1,0},{2,3},{3,2},{4,5},{5,4},{6,7},{7,6},{8,9},{9,8},{10,11... | collective-permute-start | bytes 10420232 | tf_op jit(solution)/shard_map/ppermute | solution.py:55
  435.4 0.7 copy-start.16
  435.4 15.9 %collective-permute-start.8 = (bf16[128,13568]{1,0:T(8,128)(2,1)}, bf16[128,13568]{1,0:T(8,128)(2,1)}, u32[]{:S(2)}, u32[]{:S(2)}) collective-permute-start(bf16[128,13568]{1,0:T(8,128)(2,1)} %collective-permute-done.3.refs_6_), channel_id=1, source_target_pairs={{0,1},{1,0},{2,3},{3,2},{4,5},{5,4},{6,7},{7,6},{8,9},{9,8},{10,11... | collective-permute-start | bytes 10420232 | tf_op jit(solution)/shard_map/ppermute | solution.py:55
  436.1 1.0 copy-start.11
  437.1 19.2 %collective-permute-start.9 = (bf16[128,13568]{1,0:T(8,128)(2,1)}, bf16[128,13568]{1,0:T(8,128)(2,1)}, u32[]{:S(2)}, u32[]{:S(2)}) collective-permute-start(bf16[128,13568]{1,0:T(8,128)(2,1)} %constant_dynamic-update-slice_fusion.8.refs_7_), channel_id=1, source_target_pairs={{0,1},{1,0},{2,3},{3,2},{4,5},{5,4},{6,7},{7,6},{8,9},{9,8},{10,11... | collective-permute-start | bytes 10420232 | tf_op jit(solution)/shard_map/ppermute | solution.py:55
  438.3 2.2 copy-start.30
  438.6 1.9 copy-start.34
  450.7 332.9 %collective-permute-start.20 = (bf16[13568,256]{1,0:T(8,128)(2,1)}, bf16[13568,256]{1,0:T(8,128)(2,1)}, u32[]{:S(2)}, u32[]{:S(2)}) collective-permute-start(bf16[13568,256]{1,0:T(8,128)(2,1)} %get-tuple-element.46.refs_6_), channel_id=1, source_target_pairs={{0,1},{1,0},{2,3},{3,2},{4,5},{5,4},{6,7},{7,6},{8,9},{9,8},{10,11... | collective-permute-start | bytes 20840456 | tf_op jit(solution)/shard_map/ppermute | solution.py:55
  603.5 8.5 copy-start.22
  603.5 8.5 copy-start.26
  603.5 8.5 copy-start.29
  603.6 17.2 %slice-start = ((s8[6946816]{0:T(1024)(128)(4,1)}), s8[4194304]{0:T(1024)(128)(4,1)S(1)}, s32[]{:S(2)}) async-start(s8[6946816]{0:T(1024)(128)(4,1)} %bitcast.172), calls=%async_computation | async-start | bytes 8388608
  612.0 6.8 copy-start.33
  612.0 8.7 slice-start.1
  620.2 13.6 %collective-permute-start.16 = (bf16[1024,256]{0,1:T(8,128)(2,1)}, bf16[1024,256]{0,1:T(8,128)(2,1)}, u32[]{:S(2)}, u32[]{:S(2)}) collective-permute-start(bf16[1024,256]{0,1:T(8,128)(2,1)} %get-tuple-element.112), channel_id=1, source_target_pairs={{0,1},{1,0},{2,3},{3,2},{4,5},{5,4},{6,7},{7,6},{8,9},{9,8},{10,11... | collective-permute-start | bytes 1572872 | tf_op jit(solution)/shard_map/ppermute | solution.py:55
  620.2 17.6 %collective-permute-start.14 = (bf16[4096,256]{1,0:T(8,128)(2,1)}, bf16[4096,256]{1,0:T(8,128)(2,1)}, u32[]{:S(2)}, u32[]{:S(2)}) collective-permute-start(bf16[4096,256]{1,0:T(8,128)(2,1)} %bitcast.57.refs_7_), channel_id=1, source_target_pairs={{0,1},{1,0},{2,3},{3,2},{4,5},{5,4},{6,7},{7,6},{8,9},{9,8},{10,11... | collective-permute-start | bytes 6291464 | tf_op jit(solution)/shard_map/ppermute | solution.py:55
  620.7 15.1 %collective-permute-start.15 = (bf16[1024,256]{0,1:T(8,128)(2,1)S(1)}, bf16[1024,256]{0,1:T(8,128)(2,1)}, u32[]{:S(2)}, u32[]{:S(2)}) collective-permute-start(bf16[1024,256]{0,1:T(8,128)(2,1)S(1)} %convert_element_type.116), channel_id=1, source_target_pairs={{0,1},{1,0},{2,3},{3,2},{4,5},{5,4},{6,7},{7,6},{8,9},{9,8},{10,11... | collective-permute-start | bytes 1572872 | tf_op jit(solution)/shard_map/ppermute | solution.py:55
  620.7 3.1 copy-start.9
  637.9 123.1 %copy-start.24 = (f32[1,1024]{1,0:T(1,128)S(1)}, f32[1,1024]{1,0:T(1,128)}, u32[]{:S(2)}) copy-start(f32[1,1024]{1,0:T(1,128)} %get-tuple-element.170) | copy-start | bytes 12292
  637.9 123.1 %copy-start.31 = (f32[256]{0:T(256)S(1)}, f32[256]{0:T(256)}, u32[]{:S(2)}) copy-start(f32[256]{0:T(256)} %copy-done.30) | copy-start | bytes 3076
  637.9 123.1 %copy-start.36 = (f32[256]{0:T(256)S(1)}, f32[256]{0:T(256)}, u32[]{:S(2)}) copy-start(f32[256]{0:T(256)} %fusion.27) | copy-start | bytes 3076
  761.0 6.9 copy-start.35
  766.6 3.5 copy-start.10
  767.4 12.5 %collective-permute-start.17 = (bf16[256,512]{1,0:T(8,128)(2,1)}, bf16[256,512]{1,0:T(8,128)(2,1)}, u32[]{:S(2)}, u32[]{:S(2)}) collective-permute-start(bf16[256,512]{1,0:T(8,128)(2,1)} %pad_maximum_fusion.9), channel_id=1, source_target_pairs={{0,1},{1,0},{2,3},{3,2},{4,5},{5,4},{6,7},{7,6},{8,9},{9,8},{10,11... | collective-permute-start | bytes 786440 | tf_op jit(solution)/shard_map/ppermute | solution.py:55
  767.4 16.3 %collective-permute-start.19 = (bf16[3072,256]{1,0:T(8,128)(2,1)}, bf16[3072,256]{1,0:T(8,128)(2,1)}, u32[]{:S(2)}, u32[]{:S(2)}) collective-permute-start(bf16[3072,256]{1,0:T(8,128)(2,1)} %bitcast.64.refs_2_), channel_id=1, source_target_pairs={{0,1},{1,0},{2,3},{3,2},{4,5},{5,4},{6,7},{7,6},{8,9},{9,8},{10,11... | collective-permute-start | bytes 4718600 | tf_op jit(solution)/shard_map/ppermute | solution.py:55
  768.5 4.2 copy-start.3
  770.1 10.7 %collective-permute-start.18 = (bf16[256,512]{1,0:T(8,128)(2,1)}, bf16[256,512]{1,0:T(8,128)(2,1)}, u32[]{:S(2)}, u32[]{:S(2)}) collective-permute-start(bf16[256,512]{1,0:T(8,128)(2,1)} %pad_maximum_fusion.10), channel_id=1, source_target_pairs={{0,1},{1,0},{2,3},{3,2},{4,5},{5,4},{6,7},{7,6},{8,9},{9,8},{10,11... | collective-permute-start | bytes 786440 | tf_op jit(solution)/shard_map/ppermute | solution.py:55
  773.8 7.1 copy-start.13
  773.8 7.1 copy-start.14
  775.2 6.7 copy-start.8
  941.3 4.2 copy-start.23

commit v9 on v8

--- a/solution.py
+++ b/solution.py
@@ -162,8 +162,9 @@
                 copy(j, k).wait_recv()
 
     n = sum(array < n_full for array, *_ in jobs)
-    start_h(0)
-    start_h(1)
+    ahead = 2
+    for j in range(ahead):
+        start_h(j)
     for step in range(n + 2):
         if step < n:
             own_copy(step).wait()
@@ -171,11 +172,8 @@
                 h_copy(step, d).wait_recv()
             for k in (0, 1, 2):
                 copy(step, k).start()
-            for j in (2, 3) if step == 0 else (step + 3,):
-                if j < n:
-                    start_h(j)
-            if 0 < step and n + step - 1 < len(jobs):
-                start_h(n + step - 1)
+            if step + ahead < len(jobs):
+                start_h(step + ahead)
         if 0 <= step - 1 < n:
             for k in (0, 1):
                 copy(step - 1, k).wait_recv()
@@ -351,7 +349,7 @@
     jobs = []
     for array, piece in order:
         low, high = cuts[array][piece], cuts[array][piece + 1]
-        jobs.append((array, low, high, low + (high - low) // 256 * 128))
+        jobs.append((array, low, high, low + (high - low) * 5 // 12 // 128 * 128))
     n, others, dma = len(jobs), max(n_h - 1, 1), pltpu.SemaphoreType.DMA
     shapes = [(n_h * s.shape[0], s.shape[1]) for s in shards]
     (genes, cells), width, padded = counts.shape, pe.shape[0], shards[0].shape[1]
@@ -401,18 +399,21 @@
     return out[: len(shards)], *out[len(shards) :]
 
 
-def scatter_kernel(n_h, sections, periods, left_starts, lefts, rights, out, scratch, peers, prefetch, beside, after):
-    (right_buf, own, s1, r1, s2, r2, s3, r3, load_sem, send1, recv1, send2, recv2, send3, recv3) = scratch
+def scatter_kernel(
+    n_h, sections, periods, left_starts, leaning, lefts, rights, out, scratch, peers, prefetch, beside, after
+):
+    (right_buf, part, own, s1, r1, s2, r2, s3, r3, own_h, s1_h, r1_h, s2_h, r2_h, s3_h, r3_h, load_sem, send1, recv1,
+     send2, recv2, send3, recv3, send1_h, recv1_h, send2_h, recv2_h, send3_h, recv3_h) = scratch
     h, x, y = (lax.axis_index(name) for name in ("h", "x", "y"))
     to_x, to_y = {"x": 1 - x}, {"y": 1 - y}
     w = s3.shape[1]
     rows = w // n_h
     f32, b16 = jnp.float32, jnp.bfloat16
-    n_sections = len(sections)
-    starts = [sum(sections[:k]) for k in range(n_sections)]
+    starts = [sum(sections[:k]) for k in range(len(sections))]
     n = sum(sections)
     cells = right_buf.shape[2] // 2
-    greet([{"h": lax.rem(h + d, n_h)} for d in range(1, n_h)] + [to_x, to_y] + peers)
+    others = range(1, n_h)
+    greet([{"h": lax.rem(h + d, n_h)} for d in others] + [to_x, to_y] + peers)
 
     def loads(i, section, k):
         slot = lax.rem(i, 3)
@@ -434,112 +435,186 @@
                     copy.start()
                 prefetch(section, i - start)
 
-    def hop(i, source, target, send_sem, recv_sem, to):
-        slot = lax.rem(i, RING)
-        return pltpu.make_async_remote_copy(
-            src_ref=source.at[slot], dst_ref=target.at[i], send_sem=send_sem.at[slot],
-            recv_sem=recv_sem.at[i], device_id=to, device_id_type=MESH,
-        )
-
-    def first(i, odd):
-        return hop(i, s1, r1, send1, recv1, to_y if odd else to_x)
-
-    def second(i, odd):
-        return hop(i, s2, r2, send2, recv2, to_x if odd else to_y)
-
-    def third(i, d):
-        to = lax.rem(h + d, n_h)
-        slot = lax.rem(i, RING)
-        return pltpu.make_async_remote_copy(
-            src_ref=s3.at[slot, pl.ds(to * rows, rows)], dst_ref=r3.at[i, d - 1],
-            send_sem=send3.at[slot, d - 1], recv_sem=recv3.at[i, d - 1],
-            device_id={"h": to}, device_id_type=MESH,
-        )
-
     def multiply(i, odd):
-        slot = lax.rem(i, RING)
         for copy in loads(i, 0, 0):
             copy.wait()
         left = lefts[sum((i + 1024 - start) // 1024 for start in left_starts[1:]) if left_starts[1:] else 0]
         right = right_buf.at[lax.rem(i, 3)]
-
-        @pl.when(i >= RING)
-        def _():
-            first(i - RING, odd).wait_send()
-
-        part = lax.dot_general(left, right[...], (((1,), (1,)), ((), ())), preferred_element_type=f32)
-        own[slot, :w] = part[:w]
-        if odd:
-            own[slot, w:] = part[2 * w : 3 * w]
-            s1[slot, :w] = part[w : 2 * w].astype(b16)
-            s1[slot, w:] = part[3 * w :].astype(b16)
-        else:
-            own[slot, w:] = part[w : 2 * w]
-            s1[slot] = part[2 * w :].astype(b16)
-        first(i, odd).start()
-
-        beside(i, right, odd)
-        start_loads(i + 2)
-
-    def pass_on(i, odd):
-        slot = lax.rem(i, RING)
-        first(i, odd).wait_recv()
-
-        @pl.when(i >= RING)
-        def _():
-            second(i - RING, odd).wait_send()
-
-        s2[slot] = (own[slot, w:] + r1[i, w:].astype(f32)).astype(b16)
-        second(i, odd).start()
-
-    def keep(i, odd):
-        slot = lax.rem(i, RING)
-        second(i, odd).wait_recv()
-        part = own[slot, :w] + r1[i, :w].astype(f32) + r2[i].astype(f32)
-        if n_h == 1:
-            out[i] = part.astype(b16)
-            return
-
-        @pl.when(i >= RING)
-        def _():
-            for d in range(1, n_h):
-                third(i - RING, d).wait_send()
-
-        s3[slot] = part.astype(b16)
-        for d in range(1, n_h):
-            third(i, d).start()
-
-    def finish(i, odd):
-        if n_h == 1:
-            return
-        total = s3[lax.rem(i, RING), pl.ds(h * rows, rows)].astype(f32)
-        for d in range(1, n_h):
-            third(i, d).wait_recv()
-            total = total + r3[i, d - 1].astype(f32)
-        out[i] = total
+        part[...] = lax.dot_general(left, right[...], (((1,), (1,)), ((), ())), preferred_element_type=f32)
+
+    def remote(source, target, send_sem, recv_sem, to):
+        return pltpu.make_async_remote_copy(
+            src_ref=source, dst_ref=target, send_sem=send_sem, recv_sem=recv_sem, device_id=to, device_id_type=MESH
+        )
+
+    class Links:
+        def first(k, i, by_y):
+            slot = lax.rem(k, RING)
+            return remote(s1.at[slot], r1.at[i], send1.at[slot], recv1.at[i], to_y if by_y else to_x)
+
+        def second(k, i, by_y):
+            slot = lax.rem(k, RING)
+            return remote(s2.at[slot], r2.at[i], send2.at[slot], recv2.at[i], to_x if by_y else to_y)
+
+        def third(k, i, d):
+            slot, to = lax.rem(k, RING), lax.rem(h + d, n_h)
+            return remote(
+                s3.at[slot, pl.ds(to * rows, rows)], r3.at[i, d - 1], send3.at[slot, d - 1], recv3.at[i, d - 1], {"h": to}
+            )
+
+        def start(k, i, by_y):
+            slot = lax.rem(k, RING)
+
+            @pl.when(k >= RING)
+            def _():
+                Links.first(k, i, by_y).wait_send()
+
+            own[slot, :w] = part[:w]
+            if by_y:
+                own[slot, w:] = part[2 * w : 3 * w]
+                s1[slot, :w] = part[w : 2 * w].astype(b16)
+                s1[slot, w:] = part[3 * w :].astype(b16)
+            else:
+                own[slot, w:] = part[w : 2 * w]
+                s1[slot] = part[2 * w :].astype(b16)
+            Links.first(k, i, by_y).start()
+
+        def pass_on(k, i, by_y):
+            slot = lax.rem(k, RING)
+            Links.first(k, i, by_y).wait_recv()
+
+            @pl.when(k >= RING)
+            def _():
+                Links.second(k, i, by_y).wait_send()
+
+            s2[slot] = (own[slot, w:] + r1[i, w:].astype(f32)).astype(b16)
+            Links.second(k, i, by_y).start()
+
+        def keep(k, i, by_y):
+            slot = lax.rem(k, RING)
+            Links.second(k, i, by_y).wait_recv()
+            total = own[slot, :w] + r1[i, :w].astype(f32) + r2[i].astype(f32)
+            if n_h == 1:
+                out[i] = total.astype(b16)
+                return
+
+            @pl.when(k >= RING)
+            def _():
+                for d in others:
+                    Links.third(k, i, d).wait_send()
+
+            s3[slot] = total.astype(b16)
+            for d in others:
+                Links.third(k, i, d).start()
+
+        def finish(k, i, by_y):
+            if n_h == 1:
+                return
+            total = s3[lax.rem(k, RING), pl.ds(h * rows, rows)].astype(f32)
+            for d in others:
+                Links.third(k, i, d).wait_recv()
+                total = total + r3[i, d - 1].astype(f32)
+            out[i] = total
+
+    class Along:
+        def first(k, d):
+            to = lax.rem(h + d, n_h)
+            return remote(s1_h.at[k, :, to], r1_h.at[k, d - 1], send1_h.at[k, d - 1], recv1_h.at[k, d - 1], {"h": to})
+
+        def second(k, by_y):
+            return remote(s2_h.at[k], r2_h.at[k], send2_h.at[k], recv2_h.at[k], to_y if by_y else to_x)
+
+        def third(k, by_y):
+            return remote(s3_h.at[k], r3_h.at[k], send3_h.at[k], recv3_h.at[k], to_x if by_y else to_y)
+
+        def start(k, i, by_y):
+            for block in range(4):
+                s1_h[k, block] = part[block * w : (block + 1) * w].reshape(n_h, rows, CHUNK).astype(b16)
+                own_h[k, block] = part[pl.ds(block * w + h * rows, rows)]
+            for d in others:
+                Along.first(k, d).start()
+
+        def pass_on(k, i, by_y):
+            for d in others:
+                Along.first(k, d).wait_recv()
+
+            def total(block):
+                return own_h[k, block] + sum(r1_h[k, d - 1, block].astype(f32) for d in others)
+
+            mine, away = ((0, 2), (1, 3)) if by_y else ((0, 1), (2, 3))
+            for place, block in enumerate(away):
+                s2_h[k, place] = total(block).astype(b16)
+            Along.second(k, by_y).start()
+            for place, block in enumerate(mine):
+                own_h[k, place] = total(block)
+
+        def keep(k, i, by_y):
+            Along.second(k, by_y).wait_recv()
+            s3_h[k] = (own_h[k, 1] + r2_h[k, 1].astype(f32)).astype(b16)
+            Along.third(k, by_y).start()
+
+        def finish(k, i, by_y):
+            Along.third(k, by_y).wait_recv()
+            out[i] = own_h[k, 0] + r2_h[k, 0].astype(f32) + r3_h[k].astype(f32)
+
+    pairs = (n + 1) // 2
+    along = s1_h.shape[0] // 2 if n_h > 1 else 0
+    stages = ("start", "pass_on", "keep", "finish")
+
+    def step(p, carry):
+        for lag, stage in enumerate(stages):
+            q = p - lag
+            turn = q // 8
+            is_along = (lax.rem(q, 8) == 7) & (q < 8 * along)
+            for odd in (0, 1):
+                i = 2 * q + odd
+                here = (i >= 0) & (i < n)
+                if lag == 0:
+
+                    @pl.when(here)
+                    def _(i=i, odd=odd):
+                        multiply(i, odd)
+
+                k = i - 2 * turn if along else i
+                leans = (lax.rem(q, 2) == 0) if leaning else False
+                ways = [(0, here & ~is_along)] if not odd else [(1, here & ~is_along)]
+                if odd and leaning:
+                    ways = [(0, here & ~is_along & leans), (1, here & ~is_along & ~leans)]
+                for by_y, when in ways:
+
+                    @pl.when(when)
+                    def _(k=k, i=i, by_y=by_y, stage=stage):
+                        getattr(Links, stage)(k, i, by_y)
+
+                if along:
+
+                    @pl.when(here & is_along)
+                    def _(i=i, odd=odd, turn=turn, stage=stage):
+                        getattr(Along, stage)(2 * turn + odd, i, odd)
+
+                if lag == 0:
+
+                    @pl.when(here)
+                    def _(i=i, odd=odd):
+                        beside(i, right_buf.at[lax.rem(i, 3)], odd)
+                        start_loads(i + 2)
+
+        after(p)
+        return carry
 
     start_loads(jnp.int32(0))
     start_loads(jnp.int32(1))
-    pairs = (n + 1) // 2
-
-    def step(p, carry):
-        for lag, stage in enumerate((multiply, pass_on, keep, finish)):
-            for odd in (0, 1):
-                i = 2 * (p - lag) + odd
-
-                @pl.when((i >= 0) & (i < n))
-                def _(stage=stage, i=i, odd=odd):
-                    stage(i, odd)
-
-        after(p)
-        return carry
-
     lax.fori_loop(0, pairs + 3, step, 0)
-    for i in range(max(n - RING, 0), n):
-        first(i, i % 2).wait_send()
-        second(i, i % 2).wait_send()
-        for d in range(1, n_h):
-            third(i, d).wait_send()
+    for k in range(max(n - 2 * along - RING, 0), n - 2 * along):
+        Links.first(k, 0, 0).wait_send()
+        Links.second(k, 0, 0).wait_send()
+        for d in others:
+            Links.third(k, 0, d).wait_send()
+    for k in range(2 * along):
+        for d in others:
+            Along.first(k, d).wait_send()
+        Along.second(k, 0).wait_send()
+        Along.third(k, 0).wait_send()
 
 
 def chunk_of(k):
@@ -611,7 +686,7 @@
                 multiply(i - begin, right)
 
     scatter_kernel(
-        n_h, sections, periods, left_starts, lefts, rights, out, scratch, [], prefetch, beside, lambda p: None
+        n_h, sections, periods, left_starts, False, lefts, rights, out, scratch, [], prefetch, beside, lambda p: None
     )
     for k in range(max(count - 2, 0), count):
         product_store(k).wait()
@@ -663,22 +738,18 @@
             send_sem=send.at[1], recv_sem=recv.at[1], device_id={"y": 1 - y}, device_id_type=MESH,
         )
 
-    both = n_pairs // 2
-
     def beside(i, right, odd):
-        p = i // 2
-        late = (p + 1024 - both) // 1024
-
-        @pl.when((p < both) | ((p < 3 * both) & (lax.rem(p, 2) == odd)))
+        @pl.when(i < n_pairs)
         def _():
-            backward(p - late * (p - both // 2 - p // 2), odd)
+            backward(i, 0)
+            backward(i, 1)
 
     def after(p):
-        @pl.when(p == 3 * both)
+        @pl.when(p == n_pairs // 2)
         def _():
             to_core().start()
 
-        @pl.when(p == 3 * both + 2)
+        @pl.when(p == n_pairs // 2 + 2)
         def _():
             to_core().wait_recv()
 
@@ -692,7 +763,7 @@
             to_y().start()
 
     scatter_kernel(
-        n_h, sections, periods, left_starts, lefts, rights, out, scratch, [{"c": 1 - c}],
+        n_h, sections, periods, left_starts, True, lefts, rights, out, scratch, [{"c": 1 - c}],
         lambda section, k: None, beside, after,
     )
     to_y().wait_recv()
@@ -719,7 +790,7 @@
     inner_h = n_h if rows % 16 == 0 else 1
     dma, bf16, f32 = pltpu.SemaphoreType.DMA, jnp.bfloat16, jnp.float32
     vmem, hbm = pl.BlockSpec(memory_space=pltpu.VMEM), pl.BlockSpec(memory_space=pl.ANY)
-    others = max(inner_h - 1, 1)
+    others, along = max(inner_h - 1, 1), max(2 * (n // 16), 2)
     part_shape = jax.ShapeDtypeStruct((n, rows, CHUNK), f32)
     if inner_h == 1:
         part_shape = jax.ShapeDtypeStruct((n, w, CHUNK), bf16)
@@ -731,6 +802,7 @@
         scratch_shapes=scratch
         + [
             pltpu.VMEM((3, CHUNK, 2 * cells), bf16),
+            pltpu.VMEM((4 * w, CHUNK), f32),
             pltpu.VMEM((RING, 2 * w, CHUNK), f32),
             pltpu.VMEM((RING, 2 * w, CHUNK), bf16),
             pltpu.VMEM((n, 2 * w, CHUNK), bf16),
@@ -738,6 +810,13 @@
             pltpu.VMEM((n, w, CHUNK), bf16),
             pltpu.VMEM((RING, w, CHUNK), bf16),
             pltpu.VMEM((n, others, w // inner_h, CHUNK), bf16),
+            pltpu.VMEM((along, 4, rows, CHUNK), f32),
+            pltpu.VMEM((along, 4, inner_h, w // inner_h, CHUNK), bf16),
+            pltpu.VMEM((along, others, 4, rows, CHUNK), bf16),
+            pltpu.VMEM((along, 2, rows, CHUNK), bf16),
+            pltpu.VMEM((along, 2, rows, CHUNK), bf16),
+            pltpu.VMEM((along, rows, CHUNK), bf16),
+            pltpu.VMEM((along, rows, CHUNK), bf16),
             dma((3, 2)),
             dma((RING,)),
             dma((n,)),
@@ -745,6 +824,12 @@
             dma((n,)),
             dma((RING, others)),
             dma((n, others)),
+            dma((along, others)),
+            dma((along, others)),
+            dma((along,)),
+            dma((along,)),
+            dma((along,)),
+            dma((along,)),
         ],
         compiler_params=pltpu.CompilerParams(
             collective_id=collective_id, has_side_effects=True, vmem_limit_bytes=60 * 2**20
@@ -884,9 +969,8 @@
     ]
     cuts = [gene_cuts, [0, width // 2 * 3, 3 * width + 128], [0, width]]
     cuts += [[0, 2 * width, 4 * width], [0, width // 2, width]]
-    cuts += [[k * (padded // 1024) * 128 for k in range(8)] + [padded]]
-    order = [(0, 0), (0, 1), (0, 2), (0, 3), (1, 0), (1, 1), (2, 0), (3, 0), (3, 1), (4, 0), (4, 1)]
-    order += [(5, piece) for piece in range(8)]
+    cuts += [[0, padded]]
+    order = [(0, 0), (0, 1), (0, 2), (0, 3), (1, 0), (1, 1), (2, 0), (3, 0), (3, 1), (4, 0), (4, 1), (5, 0)]
     gathered, xb, h0, a1, query, kv_all = gather_all(
         shards, 5, cuts, order, counts.T, scale[None, :], pe.T, 0
     )

time: 967 us -> 1020 us (1.055)
  Pallas kernels: 710 us -> 767 us
    pallas_call x3, Pallas kernels: 423 us -> 481 us  [scatter_call(): pl.pallas_call(functools.partial(kernel, inner_h, sections, periods), out...]
  transfers between devices with their start and end apart: 21 -> 21, of which waited for: 5 -> 5; matrix products, arithmetic and copies ran while one was open for 16% -> 15% of each run, Pallas kernels for 28% -> 29%
where the time goes in v9:
time: 1020 us
  Pallas kernels  767 us (75%)
  local copies, waits for them, and re-layouts  93.9 us (9%)
  matrix products  56.5 us (6%)
  waiting for transfers between devices  46.5 us (5%)
  other arithmetic  42.8 us (4%)
    pallas_call x3, Pallas kernels, scatter_call(): pl.pallas_call(functools.partial(kernel, inner_h, sections, periods), out...  481 us
    pallas_call x1, Pallas kernels, gather_all(): pl.pallas_call(functools.partial(front_kernel, n_h, jobs, len(shards), n_...  286 us
    ppermute x21, waiting for transfers between devices, swap(): return lax.ppermute(value, axis, [(0, 1), (1, 0)])  46.5 us
    dot_general x4, matrix products, contract_cols(): lax.dot_general(left, right, (((1,), (1,)), ((), ())), preferred_element_...  22.9 us
    dot_general x3, matrix products, matmul(): return jnp.dot(left, right, preferred_element_type=jnp.float32)  22.5 us
  transfers between devices with their start and end apart: 21, of which 5 were waited for; matrix products, arithmetic and copies ran while one was open for 15% of the time, Pallas kernels for 29%

profile of v9, /device:TPU:0, one launch (start us, length us, event | category | flops | bytes accessed | tf_op | source)
XLA Modules:
  0.0 1018.2 jit_solution(6289022068507669594)
XLA Ops:
  2.5 1.3 broadcast_divide_fusion
  4.4 2.1 pad.24.refs_0_
  6.6 2.1 pad.26.refs_5_
  8.7 1.1 copy.211
  13.9 1.9 multiply_sine_fusion.1
  15.8 1.1 pad_maximum_fusion.3
  16.9 286.1 %shard_map.238 = (bf16[2,2,2,128,13568]{4,3,2,1,0:T(8,128)(2,1)}, bf16[2,2,2,128,3200]{4,3,2,1,0:T(8,128)(2,1)}, bf16[2,2,2,128,1024]{4,3,2,1,0:T(8,128)(2,1)}, ...) custom-call(bf16[32,13568]{1,0:T(8,128)(2,1)} %pad.24.refs_0_, ...), custom_call_target="tpu_custom_call" | custom-call | tf_op jit(solution)/shard_map/pallas_call | solution.py:360
  303.0 3.2 collective-permute-start.3
  306.2 1.8 constant_dynamic-slice_fusion.47
  308.7 7.7 pad.28.refs_2_
  318.7 4.0 fusion.34
  322.7 4.0 copy.217
  326.9 2.6 copy.214
  329.7 4.5 fusion
  334.1 4.4 fusion.1
  338.6 6.6 fusion.13
  349.0 15.9 %multiply_add_fusion = (f32[256,4096]{0,1:T(8,128)}, f32[256,4096]{0,1:T(8,128)S(1)}, f32[256,4096]{0,1:T(8,128)S(1)}) fusion(bf16[256,1024]{1,0:T(8,128)(2,1)S(1)} %add_convert_fusion.1, bf16[1024,4096]{1,0:T(8,128)(2,1)} %bitcast.215), kind=kOutput, calls=%fused_computation.14 | convolution fusion | flops 2218786816 | bytes 21495808 | tf_op jit(solution)/shard_map/dot_general | solution.py:51
  365.6 5.7 fusion.12
  372.0 10.1 collective-permute-done.3.refs_6_
  382.1 2.8 slice.146
  388.5 2.8 slice.147
  391.3 1.7 collective-permute-start.5
  393.0 1.8 constant_dynamic-slice_fusion.39
  394.9 1.8 constant_dynamic-slice_fusion.23
  397.7 27.1 %collective-permute-done.4 = bf16[128,6784]{1,0:T(8,128)(2,1)} collective-permute-done((bf16[128,6784]{1,0:T(8,128)(2,1)}, bf16[128,6784]{1,0:T(8,128)(2,1)}, u32[]{:S(2)}, u32[]{:S(2)}) %collective-permute-start.4) | collective-permute-done | bytes 1736736 | tf_op jit(solution)/shard_map/ppermute | solution.py:55
  424.8 2.8 constant_dynamic-update-slice_fusion.9
  428.1 3.8 collective-permute-done.5
  431.9 2.8 constant_dynamic-update-slice_fusion.8.refs_7_
  439.1 1.3 log_add_fusion.refs_4_
  440.5 1.1 maximum_bitcast_fusion
  441.5 1.0 copy.223.refs_0_
  442.5 1.1 maximum_bitcast_fusion.2
  443.8 1.8 maximum_bitcast_fusion.1
  445.7 1.0 maximum_bitcast_fusion.3
  446.7 1.6 pad_maximum_fusion.1
  448.6 2.1 pad_maximum_fusion.refs_0_
  451.3 5.0 collective-permute-done.9.refs_11_
  456.3 161.6 %shard_map.239 = (f32[53,32,256]{2,1,0:T(8,128)}, bf16[13568,256]{1,0:T(8,128)(2,1)}, f32[1024,256]{1,0:T(8,128)}) custom-call(bf16[1,512,512]{2,1,0:T(8,128)(2,1)} %copy.223.refs_0_, bf16[256,1024]{1,0:T(8,128)(2,1)} %copy-done.12, bf16[13568,256]{1,0:T(8,128)(2,1)} %pad.28.refs_2_, bf16[13568,256]{1,0:T(8,128)(2,1)} %collective-permute-done.1.refs_3_, ...), custom_call_target="tpu_custom_call" | custom-call | tf_op jit(solution)/shard_map/pallas_call | solution.py:797
  617.9 1.6 copy.226
  619.9 8.4 fusion.5
  628.3 6.8 multiply_reduce_fusion.1
  637.1 3.1 slice_bitcast_fusion
  640.3 1.3 slice_bitcast_fusion.1
  641.6 2.0 copy.240.refs_11_
  644.6 2.3 convolution_convert_fusion
  647.0 1.0 copy.235
  648.0 1.1 copy.236
  649.1 1.0 copy.237.refs_3_
  650.1 2.0 copy.241.refs_12_
  652.1 2.0 copy.239.refs_10_
  654.2 131.1 %shard_map.240 = (f32[36,32,256]{2,1,0:T(8,128)}, bf16[256,3072]{1,0:T(8,128)(2,1)}) custom-call(bf16[6,512,512]{2,1,0:T(8,128)(2,1)} %pad_maximum_fusion.refs_0_, bf16[256,1024]{1,0:T(8,128)(2,1)} %get-tuple-element.34.refs_1_, bf16[2,2,256,2048]{3,2,1,0:T(8,128)(2,1)} %get-tuple-element.33.refs_2_, bf16[256,1024]{1,0:T(8,128)(2,1)} %copy.237.refs_3_, ...), custom_call_target="tpu_custom_call" | custom-call | tf_op jit(solution)/shard_map/pallas_call | solution.py:797
  785.3 2.6 copy.242
  787.9 5.4 multiply_reduce_fusion.2
  798.9 1.0 copy.250
  800.9 1.4 copy.247
  802.9 1.2 reshape.432
  805.7 1.3 reshape.431
  809.2 1.6 copy.243.refs_0_
  810.8 188.5 %shard_map.241 = (f32[66,32,256]{2,1,0:T(8,128)}, f32[13568,256]{1,0:T(8,128)}) custom-call(bf16[3,512,512]{2,1,0:T(8,128)(2,1)} %copy.243.refs_0_, bf16[256,1024]{1,0:T(8,128)(2,1)} %copy-done.3, bf16[3072,256]{1,0:T(8,128)(2,1)} %bitcast.64.refs_2_, bf16[3072,256]{1,0:T(8,128)(2,1)} %collective-permute-done.19.refs_3_, ...), custom_call_target="tpu_custom_call" | custom-call | tf_op jit(solution)/shard_map/pallas_call | solution.py:797
  999.3 1.6 slice_bitcast_fusion.3
  1000.9 1.0 slice_bitcast_fusion.5
  1002.0 1.6 slice_reduce_fusion.1
  1003.6 12.2 %bitcast_divide_fusion = f32[256,13500]{0,1:T(8,128)} fusion(bf16[256,13500]{0,1:T(8,128)(2,1)} %param.15, f32[13568,256]{1,0:T(8,128)} %get-tuple-element.48, f32[256]{0:T(256)S(1)} %copy-done.23), kind=kLoop, calls=%fused_computation.4 | loop fusion | flops 17280000 | bytes 34562048 | tf_op jit(solution)/shard_map/div | solution.py:1091
  1015.9 1.3 slice_bitcast_fusion.2
  (221 shorter events, 39.9 us)
Async XLA Ops:
  0.6 10.0 copy-start.15
  0.7 11.2 %copy-start.19 = (bf16[32,1024]{1,0:T(8,128)(2,1)S(1)}, bf16[32,1024]{1,0:T(8,128)(2,1)}, u32[]{:S(2)}) copy-start(bf16[32,1024]{1,0:T(8,128)(2,1)} %param.22) | copy-start | bytes 196612
  0.7 12.4 %copy-start.40 = (bf16[32]{0:T(256)(128)(2,1)S(1)}, bf16[32]{0:T(256)(128)(2,1)}, u32[]{:S(2)}) copy-start(bf16[32]{0:T(256)(128)(2,1)} %param.23) | copy-start | bytes 196
  0.7 12.4 %copy-start.39 = (bf16[32]{0:T(256)(128)(2,1)S(1)}, bf16[32]{0:T(256)(128)(2,1)}, u32[]{:S(2)}) copy-start(bf16[32]{0:T(256)(128)(2,1)} %param.24) | copy-start | bytes 196
  0.7 12.4 %copy-start.38 = (bf16[32]{0:T(256)(128)(2,1)S(1)}, bf16[32]{0:T(256)(128)(2,1)}, u32[]{:S(2)}) copy-start(bf16[32]{0:T(256)(128)(2,1)} %param.27) | copy-start | bytes 196
  0.7 12.4 %copy-start.37 = (bf16[32]{0:T(256)(128)(2,1)S(1)}, bf16[32]{0:T(256)(128)(2,1)}, u32[]{:S(2)}) copy-start(bf16[32]{0:T(256)(128)(2,1)} %param.28) | copy-start | bytes 196
  0.7 12.5 %copy-start.18 = (bf16[32,3072]{1,0:T(8,128)(2,1)S(1)}, bf16[32,3072]{1,0:T(8,128)(2,1)}, u32[]{:S(2)}) copy-start(bf16[32,3072]{1,0:T(8,128)(2,1)} %param.21) | copy-start | bytes 589828
  303.0 79.1 %collective-permute-start.3 = (bf16[128,13568]{1,0:T(8,128)(2,1)}, bf16[128,13568]{1,0:T(8,128)(2,1)}, u32[]{:S(2)}, u32[]{:S(2)}) collective-permute-start(bf16[128,13568]{1,0:T(8,128)(2,1)} %get-tuple-element.40.refs_4_), channel_id=1, source_target_pairs={{0,4},{4,0},{1,5},{5,1},{2,6},{6,2},{3,7},{7,3},{8,12},{12,8},{9,1... | collective-permute-start | bytes 10420232 | tf_op jit(solution)/shard_map/ppermute | solution.py:55
  306.2 82.4 %collective-permute-start.2 = (bf16[128,13568]{1,0:T(8,128)(2,1)}, bf16[128,13568]{1,0:T(8,128)(2,1)}, u32[]{:S(2)}, u32[]{:S(2)}) collective-permute-start(bf16[128,13568]{1,0:T(8,128)(2,1)} %get-tuple-element.40.refs_4_), channel_id=1, source_target_pairs={{0,2},{2,0},{1,3},{3,1},{4,6},{6,4},{5,7},{7,5},{8,10},{10,8},{9,1... | collective-permute-start | bytes 10420232 | tf_op jit(solution)/shard_map/ppermute | solution.py:55
  308.6 119.0 %collective-permute-start.10 = (bf16[256,512]{1,0:T(8,128)(2,1)}, bf16[256,512]{1,0:T(8,128)(2,1)}, u32[]{:S(2)}, u32[]{:S(2)}) collective-permute-start(bf16[256,512]{1,0:T(8,128)(2,1)} %pad_maximum_fusion.6), channel_id=1, source_target_pairs={{0,1},{1,0},{2,3},{3,2},{4,5},{5,4},{6,7},{7,6},{8,9},{9,8},{10,11... | collective-permute-start | bytes 786440 | tf_op jit(solution)/shard_map/ppermute | solution.py:55
  316.4 134.9 %collective-permute-start.1 = (bf16[13568,256]{1,0:T(8,128)(2,1)}, bf16[13568,256]{1,0:T(8,128)(2,1)}, u32[]{:S(2)}, u32[]{:S(2)}) collective-permute-start(bf16[13568,256]{1,0:T(8,128)(2,1)} %pad.28.refs_2_), channel_id=1, source_target_pairs={{0,1},{1,0},{2,3},{3,2},{4,5},{5,4},{6,7},{7,6},{8,9},{9,8},{10,11... | collective-permute-start | bytes 20840456 | tf_op jit(solution)/shard_map/ppermute | solution.py:55
  317.9 0.8 copy-start.5
  318.0 11.4 %copy-start.27 = (s32[256]{0:T(256)}, s32[256]{0:T(256)S(1)}, u32[]{:S(2)}) copy-start(s32[256]{0:T(256)S(1)} %slice_reduce_fusion) | copy-start | bytes 3076
  322.7 4.0 copy-start.6
  338.5 6.7 copy-start.20
  338.5 6.7 copy-start
  338.6 6.7 copy-start.2
  345.3 0.9 copy-start.4
  346.1 18.8 %copy-start.25 = (f32[256]{0:T(256)}, f32[256]{0:T(256)S(1)}, u32[]{:S(2)}) copy-start(f32[256]{0:T(256)S(1)} %broadcast_multiply_fusion.1) | copy-start | bytes 3076
  346.4 0.6 copy-start.32
  346.4 18.6 %copy-start.28 = (f32[256]{0:T(256)}, f32[256]{0:T(256)S(1)}, u32[]{:S(2)}) copy-start(f32[256]{0:T(256)S(1)} %fusion.26) | copy-start | bytes 3076
  348.8 16.2 %copy-start.21 = (f32[1,1024]{1,0:T(1,128)}, f32[1,1024]{1,0:T(1,128)S(1)}, u32[]{:S(2)}) copy-start(f32[1,1024]{1,0:T(1,128)S(1)} %get-tuple-element.172) | copy-start | bytes 12292
  349.0 16.0 %copy-start.7 = (bf16[256,1024]{1,0:T(8,128)(2,1)}, bf16[256,1024]{1,0:T(8,128)(2,1)S(1)}, u32[]{:S(2)}) copy-start(bf16[256,1024]{1,0:T(8,128)(2,1)S(1)} %add_convert_fusion.1) | copy-start | bytes 1572868
  384.9 39.9 %collective-permute-start.4 = (bf16[128,6784]{1,0:T(8,128)(2,1)}, bf16[128,6784]{1,0:T(8,128)(2,1)}, u32[]{:S(2)}, u32[]{:S(2)}) collective-permute-start(bf16[128,6784]{1,0:T(8,128)(2,1)} %slice.146), channel_id=1, source_target_pairs={{0,2},{2,0},{1,3},{3,1},{4,6},{6,4},{5,7},{7,5},{8,10},{10,8},{9,1... | collective-permute-start | bytes 5210120 | tf_op jit(solution)/shard_map/ppermute | solution.py:55
  387.0 0.8 copy-start.12
  388.5 46.3 %collective-permute-start = (bf16[256,512]{1,0:T(8,128)(2,1)}, bf16[256,512]{1,0:T(8,128)(2,1)}, u32[]{:S(2)}, u32[]{:S(2)}) collective-permute-start(bf16[256,512]{1,0:T(8,128)(2,1)} %pad_maximum_fusion.5), channel_id=1, source_target_pairs={{0,1},{1,0},{2,3},{3,2},{4,5},{5,4},{6,7},{7,6},{8,9},{9,8},{10,11... | collective-permute-start | bytes 786440 | tf_op jit(solution)/shard_map/ppermute | solution.py:55
  391.3 40.6 %collective-permute-start.5 = (bf16[128,6784]{1,0:T(8,128)(2,1)}, bf16[128,6784]{1,0:T(8,128)(2,1)}, u32[]{:S(2)}, u32[]{:S(2)}) collective-permute-start(bf16[128,6784]{1,0:T(8,128)(2,1)} %slice.147), channel_id=1, source_target_pairs={{0,4},{4,0},{1,5},{5,1},{2,6},{6,2},{3,7},{7,3},{8,12},{12,8},{9,1... | collective-permute-start | bytes 5210120 | tf_op jit(solution)/shard_map/ppermute | solution.py:55
  397.7 39.8 %copy-start.1 = (f32[256,1024]{1,0:T(8,128)S(1)}, f32[256,1024]{1,0:T(8,128)}, u32[]{:S(2)}) copy-start(f32[256,1024]{1,0:T(8,128)} %get-tuple-element.32) | copy-start | bytes 3145732
  424.8 11.0 %collective-permute-start.12 = (bf16[256,2048]{0,1:T(8,128)(2,1)S(1)}, bf16[256,2048]{0,1:T(8,128)(2,1)S(1)}, u32[]{:S(2)}, u32[]{:S(2)}) collective-permute-start(bf16[256,2048]{0,1:T(8,128)(2,1)S(1)} %pad_maximum_fusion.4), channel_id=1, source_target_pairs={{0,1},{1,0},{2,3},{3,2},{4,5},{5,4},{6,7},{7,6},{8,9},{9,8},{10,11... | collective-permute-start | bytes 3145736 | tf_op jit(solution)/shard_map/ppermute | solution.py:55
  427.6 7.7 collective-permute-start.11
  431.9 3.4 collective-permute-start.13
  434.8 15.9 %collective-permute-start.6 = (bf16[128,13568]{1,0:T(8,128)(2,1)}, bf16[128,13568]{1,0:T(8,128)(2,1)}, u32[]{:S(2)}, u32[]{:S(2)}) collective-permute-start(bf16[128,13568]{1,0:T(8,128)(2,1)} %get-tuple-element.40.refs_4_), channel_id=1, source_target_pairs={{0,1},{1,0},{2,3},{3,2},{4,5},{5,4},{6,7},{7,6},{8,9},{9,8},{10,11... | collective-permute-start | bytes 10420232 | tf_op jit(solution)/shard_map/ppermute | solution.py:55
  435.3 0.7 copy-start.17
  435.3 15.5 %collective-permute-start.7 = (bf16[128,13568]{1,0:T(8,128)(2,1)}, bf16[128,13568]{1,0:T(8,128)(2,1)}, u32[]{:S(2)}, u32[]{:S(2)}) collective-permute-start(bf16[128,13568]{1,0:T(8,128)(2,1)} %collective-permute-done.2.refs_5_), channel_id=1, source_target_pairs={{0,1},{1,0},{2,3},{3,2},{4,5},{5,4},{6,7},{7,6},{8,9},{9,8},{10,11... | collective-permute-start | bytes 10420232 | tf_op jit(solution)/shard_map/ppermute | solution.py:55
  435.4 0.7 copy-start.16
  435.4 15.9 %collective-permute-start.8 = (bf16[128,13568]{1,0:T(8,128)(2,1)}, bf16[128,13568]{1,0:T(8,128)(2,1)}, u32[]{:S(2)}, u32[]{:S(2)}) collective-permute-start(bf16[128,13568]{1,0:T(8,128)(2,1)} %collective-permute-done.3.refs_6_), channel_id=1, source_target_pairs={{0,1},{1,0},{2,3},{3,2},{4,5},{5,4},{6,7},{7,6},{8,9},{9,8},{10,11... | collective-permute-start | bytes 10420232 | tf_op jit(solution)/shard_map/ppermute | solution.py:55
  436.1 1.0 copy-start.11
  437.0 19.2 %collective-permute-start.9 = (bf16[128,13568]{1,0:T(8,128)(2,1)}, bf16[128,13568]{1,0:T(8,128)(2,1)}, u32[]{:S(2)}, u32[]{:S(2)}) collective-permute-start(bf16[128,13568]{1,0:T(8,128)(2,1)} %constant_dynamic-update-slice_fusion.8.refs_7_), channel_id=1, source_target_pairs={{0,1},{1,0},{2,3},{3,2},{4,5},{5,4},{6,7},{7,6},{8,9},{9,8},{10,11... | collective-permute-start | bytes 10420232 | tf_op jit(solution)/shard_map/ppermute | solution.py:55
  438.3 2.2 copy-start.30
  438.5 1.9 copy-start.34
  450.7 360.1 %collective-permute-start.20 = (bf16[13568,256]{1,0:T(8,128)(2,1)}, bf16[13568,256]{1,0:T(8,128)(2,1)}, u32[]{:S(2)}, u32[]{:S(2)}) collective-permute-start(bf16[13568,256]{1,0:T(8,128)(2,1)} %get-tuple-element.46.refs_6_), channel_id=1, source_target_pairs={{0,1},{1,0},{2,3},{3,2},{4,5},{5,4},{6,7},{7,6},{8,9},{9,8},{10,11... | collective-permute-start | bytes 20840456 | tf_op jit(solution)/shard_map/ppermute | solution.py:55
  619.8 8.5 copy-start.22
  619.8 8.5 copy-start.26
  619.8 8.5 copy-start.29
  619.8 17.2 %slice-start = ((s8[6946816]{0:T(1024)(128)(4,1)}), s8[4194304]{0:T(1024)(128)(4,1)S(1)}, s32[]{:S(2)}) async-start(s8[6946816]{0:T(1024)(128)(4,1)} %bitcast.172), calls=%async_computation | async-start | bytes 8388608
  628.3 6.8 copy-start.33
  628.3 8.7 slice-start.1
  636.5 13.6 %collective-permute-start.16 = (bf16[1024,256]{0,1:T(8,128)(2,1)}, bf16[1024,256]{0,1:T(8,128)(2,1)}, u32[]{:S(2)}, u32[]{:S(2)}) collective-permute-start(bf16[1024,256]{0,1:T(8,128)(2,1)} %get-tuple-element.112), channel_id=1, source_target_pairs={{0,1},{1,0},{2,3},{3,2},{4,5},{5,4},{6,7},{7,6},{8,9},{9,8},{10,11... | collective-permute-start | bytes 1572872 | tf_op jit(solution)/shard_map/ppermute | solution.py:55
  636.5 17.7 %collective-permute-start.14 = (bf16[4096,256]{1,0:T(8,128)(2,1)}, bf16[4096,256]{1,0:T(8,128)(2,1)}, u32[]{:S(2)}, u32[]{:S(2)}) collective-permute-start(bf16[4096,256]{1,0:T(8,128)(2,1)} %bitcast.57.refs_7_), channel_id=1, source_target_pairs={{0,1},{1,0},{2,3},{3,2},{4,5},{5,4},{6,7},{7,6},{8,9},{9,8},{10,11... | collective-permute-start | bytes 6291464 | tf_op jit(solution)/shard_map/ppermute | solution.py:55
  637.0 15.1 %collective-permute-start.15 = (bf16[1024,256]{0,1:T(8,128)(2,1)S(1)}, bf16[1024,256]{0,1:T(8,128)(2,1)}, u32[]{:S(2)}, u32[]{:S(2)}) collective-permute-start(bf16[1024,256]{0,1:T(8,128)(2,1)S(1)} %convert_element_type.116), channel_id=1, source_target_pairs={{0,1},{1,0},{2,3},{3,2},{4,5},{5,4},{6,7},{7,6},{8,9},{9,8},{10,11... | collective-permute-start | bytes 1572872 | tf_op jit(solution)/shard_map/ppermute | solution.py:55
  637.0 3.1 copy-start.9
  654.2 133.7 %copy-start.24 = (f32[1,1024]{1,0:T(1,128)S(1)}, f32[1,1024]{1,0:T(1,128)}, u32[]{:S(2)}) copy-start(f32[1,1024]{1,0:T(1,128)} %get-tuple-element.170) | copy-start | bytes 12292
  654.2 133.7 %copy-start.31 = (f32[256]{0:T(256)S(1)}, f32[256]{0:T(256)}, u32[]{:S(2)}) copy-start(f32[256]{0:T(256)} %copy-done.30) | copy-start | bytes 3076
  654.2 133.7 %copy-start.36 = (f32[256]{0:T(256)S(1)}, f32[256]{0:T(256)}, u32[]{:S(2)}) copy-start(f32[256]{0:T(256)} %fusion.27) | copy-start | bytes 3076
  787.9 6.9 copy-start.35
  793.5 3.5 copy-start.10
  794.3 12.7 %collective-permute-start.17 = (bf16[256,512]{1,0:T(8,128)(2,1)}, bf16[256,512]{1,0:T(8,128)(2,1)}, u32[]{:S(2)}, u32[]{:S(2)}) collective-permute-start(bf16[256,512]{1,0:T(8,128)(2,1)} %pad_maximum_fusion.9), channel_id=1, source_target_pairs={{0,1},{1,0},{2,3},{3,2},{4,5},{5,4},{6,7},{7,6},{8,9},{9,8},{10,11... | collective-permute-start | bytes 786440 | tf_op jit(solution)/shard_map/ppermute | solution.py:55
  794.3 16.5 %collective-permute-start.19 = (bf16[3072,256]{1,0:T(8,128)(2,1)}, bf16[3072,256]{1,0:T(8,128)(2,1)}, u32[]{:S(2)}, u32[]{:S(2)}) collective-permute-start(bf16[3072,256]{1,0:T(8,128)(2,1)} %bitcast.64.refs_2_), channel_id=1, source_target_pairs={{0,1},{1,0},{2,3},{3,2},{4,5},{5,4},{6,7},{7,6},{8,9},{9,8},{10,11... | collective-permute-start | bytes 4718600 | tf_op jit(solution)/shard_map/ppermute | solution.py:55
  795.4 4.5 copy-start.3
  797.0 11.0 %collective-permute-start.18 = (bf16[256,512]{1,0:T(8,128)(2,1)}, bf16[256,512]{1,0:T(8,128)(2,1)}, u32[]{:S(2)}, u32[]{:S(2)}) collective-permute-start(bf16[256,512]{1,0:T(8,128)(2,1)} %pad_maximum_fusion.10), channel_id=1, source_target_pairs={{0,1},{1,0},{2,3},{3,2},{4,5},{5,4},{6,7},{7,6},{8,9},{9,8},{10,11... | collective-permute-start | bytes 786440 | tf_op jit(solution)/shard_map/ppermute | solution.py:55
  800.9 7.1 copy-start.13
  800.9 7.1 copy-start.14
  802.3 6.7 copy-start.8
  999.3 4.2 copy-start.23

commit v10 on v8

--- a/solution.py
+++ b/solution.py
@@ -162,8 +162,9 @@
                 copy(j, k).wait_recv()
 
     n = sum(array < n_full for array, *_ in jobs)
-    start_h(0)
-    start_h(1)
+    ahead = 2
+    for j in range(ahead):
+        start_h(j)
     for step in range(n + 2):
         if step < n:
             own_copy(step).wait()
@@ -171,11 +172,8 @@
                 h_copy(step, d).wait_recv()
             for k in (0, 1, 2):
                 copy(step, k).start()
-            for j in (2, 3) if step == 0 else (step + 3,):
-                if j < n:
-                    start_h(j)
-            if 0 < step and n + step - 1 < len(jobs):
-                start_h(n + step - 1)
+            if step + ahead < len(jobs):
+                start_h(step + ahead)
         if 0 <= step - 1 < n:
             for k in (0, 1):
                 copy(step - 1, k).wait_recv()
@@ -618,11 +616,12 @@
 
 
 def attention_kernel(n_h, sections, periods, left_starts, scale, *refs):
-    lefts, query, pairs, d_out, log_total, seg_keys, seg_mine = refs[:7]
+    lefts, query, pairs, d_out, log_total, seg_keys, seg_mine, h0, dh1, vectors, left_one = refs[:11]
     n_rights = 2 * len(sections)
-    rights = refs[7 : 7 + n_rights]
-    out, d_qkv, d_pairs, by_core, by_y, d_query, send, recv, *scratch = refs[7 + n_rights :]
-    y, c = lax.axis_index("y"), lax.axis_index("c")
+    rights, weight = refs[11 : 11 + n_rights], refs[11 + n_rights]
+    (out, turned_own, turned_other, lefts_next, dh0b, d_qkv, d_pairs, by_core, by_y, d_query, weight_buf, turned,
+     da1, vector_rows, send_left, got_left, send, recv, local, *scratch) = refs[12 + n_rights :]
+    x, y, c = (lax.axis_index(name) for name in ("x", "y", "c"))
     f32, b16 = jnp.float32, jnp.bfloat16
     cells, width = query.shape
     slots = 4 * cells
@@ -663,50 +662,121 @@
             send_sem=send.at[1], recv_sem=recv.at[1], device_id={"y": 1 - y}, device_id_type=MESH,
         )
 
-    both = n_pairs // 2
-
     def beside(i, right, odd):
-        p = i // 2
-        late = (p + 1024 - both) // 1024
-
-        @pl.when((p < both) | ((p < 3 * both) & (lax.rem(p, 2) == odd)))
+        @pl.when(i < 2 * n_pairs)
         def _():
-            backward(p - late * (p - both // 2 - p // 2), odd)
+            backward(i // 2, odd)
+
+    def fetch_weight():
+        return pltpu.make_async_copy(weight, weight_buf, local.at[0])
+
+    def keep_turned():
+        return pltpu.make_async_copy(turned, turned_own, local.at[1])
+
+    def send_turned():
+        return pltpu.make_async_remote_copy(
+            src_ref=turned, dst_ref=turned_other,
+            send_sem=send.at[2], recv_sem=recv.at[2], device_id={"c": 1 - c}, device_id_type=MESH,
+        )
+
+    def to_other_left():
+        return pltpu.make_async_remote_copy(
+            src_ref=send_left, dst_ref=got_left,
+            send_sem=send.at[3], recv_sem=recv.at[3], device_id={"c": 1 - c}, device_id_type=MESH,
+        )
+
+    def share():
+        to_core().wait_recv()
+
+        def add(j, carry):
+            for kind in (0, 1):
+                total = d_pairs[kind, j, : 2 * cells].astype(f32) + by_core[kind, j].astype(f32)
+                d_pairs[kind, j, : 2 * cells] = total.astype(b16)
+            return carry
+
+        lax.fori_loop(0, n_pairs, add, 0)
+        to_y().start()
+
+    def collect():
+        to_y().wait_recv()
+
+        def add(j, carry):
+            for kind in (0, 1):
+                lanes = pl.ds(pl.multiple_of((kind + 1) * width + j * 128, 128), 128)
+                total = d_pairs[kind, j, :cells].astype(f32) + by_y[kind, j].astype(f32)
+                d_qkv[:, lanes] = total.astype(b16)
+            return carry
+
+        lax.fori_loop(0, n_pairs, add, 0)
+
+    def turn():
+        def tile(k, carry):
+            turned[chunk_of(k)] = d_qkv[:, chunk_of(k)].astype(f32).T.astype(b16)
+            return carry
+
+        lax.fori_loop(0, 3 * width // CHUNK, tile, 0)
+        keep_turned().start()
+        send_turned().start()
+
+    def project():
+        fetch_weight().wait()
+        for k in range(4):
+            rows = weight_buf[k // 2, k % 2].reshape(width // 4, -1)[:, : 3 * width]
+            da1[:, k * width // 4 : (k + 1) * width // 4] = lax.dot_general(
+                d_qkv[...], rows, into, preferred_element_type=f32
+            )
+
+    def norm():
+        value, above = h0[...], da1[...]
+        centred = value - jnp.mean(value, axis=1, keepdims=True)
+        inverse = lax.rsqrt(jnp.mean(centred * centred, axis=1, keepdims=True) + eps)
+        normed = centred * inverse
+        vector_rows[...] = jnp.zeros_like(vector_rows)
+        vector_rows[0:1] = jnp.sum(above * normed, axis=0, keepdims=True)
+        vector_rows[1:2] = jnp.sum(above, axis=0, keepdims=True)
+        vector_rows[2:4] = vectors[1:3]
+        above = above * vectors[0:1]
+        inner = jnp.mean(above * normed, axis=1, keepdims=True)
+        below = inverse * (above - jnp.mean(above, axis=1, keepdims=True) - normed * inner)
+        dh0b[...] = (dh1[...] + below).astype(b16)
+
+    def halves():
+        for kind, source in enumerate((vector_rows, dh0b)):
+            for part in range(8):
+                eighth = (
+                    lax.rem(c + part // 4, 2) * 4 + lax.rem(x + part // 2 % 2, 2) * 2 + lax.rem(y + part % 2, 2)
+                )
+                lanes = pl.ds(pl.multiple_of(eighth * (width // 8), width // 8), width // 8)
+                block = source[:, lanes].astype(f32).T.astype(b16)
+                rows = slice(part % 4 * (width // 8), (part % 4 + 1) * (width // 8))
+                if part < 4:
+                    lefts_next[1 + kind, rows, :cells] = block
+                else:
+                    send_left[kind, rows] = block
+        to_other_left().start()
 
     def after(p):
-        @pl.when(p == 3 * both)
-        def _():
-            to_core().start()
-
-        @pl.when(p == 3 * both + 2)
-        def _():
-            to_core().wait_recv()
-
-            def add(j, carry):
-                for kind in (0, 1):
-                    total = d_pairs[kind, j, : 2 * cells].astype(f32) + by_core[kind, j].astype(f32)
-                    d_pairs[kind, j, : 2 * cells] = total.astype(b16)
-                return carry
-
-            lax.fori_loop(0, n_pairs, add, 0)
-            to_y().start()
-
+        plan = {0: lambda: fetch_weight().start(), n_pairs: lambda: to_core().start(), n_pairs + 2: share}
+        plan.update(zip(range(n_chunk_pairs - 2, n_chunk_pairs + 3), (collect, turn, project, norm, halves)))
+        for when, action in plan.items():
+
+            @pl.when(p == when)
+            def _(action=action):
+                action()
+
+    n_chunk_pairs = (sum(sections) + 1) // 2
     scatter_kernel(
         n_h, sections, periods, left_starts, lefts, rights, out, scratch, [{"c": 1 - c}],
         lambda section, k: None, beside, after,
     )
-    to_y().wait_recv()
-
-    def add(j, carry):
-        for kind in (0, 1):
-            lanes = pl.ds(pl.multiple_of((kind + 1) * width + j * 128, 128), 128)
-            total = d_pairs[kind, j, :cells].astype(f32) + by_y[kind, j].astype(f32)
-            d_qkv[:, lanes] = total.astype(b16)
-        return carry
-
-    lax.fori_loop(0, n_pairs, add, 0)
-    to_core().wait_send()
-    to_y().wait_send()
+    lefts_next[0] = left_one[...]
+    to_other_left().wait_recv()
+    for kind in (0, 1):
+        lefts_next[1 + kind, :, cells:] = got_left[kind]
+    keep_turned().wait()
+    send_turned().wait()
+    for copy in (to_core(), to_y(), to_other_left()):
+        copy.wait_send()
 
 
 def scatter_call(kernel, lefts, rights, operands, more_operands, out_shapes, out_specs, scratch, collective_id):
@@ -782,9 +852,10 @@
     )
 
 
-def scatter_attention(lefts, left_starts, rights, query, pairs, d_out, log_total, seg, scale, collective_id):
-    cells, width = query.shape
-    bf16, vmem = jnp.bfloat16, pl.BlockSpec(memory_space=pltpu.VMEM)
+def scatter_attention(lefts, left_starts, rights, operands, weight, scale, collective_id):
+    cells, width = operands[0].shape
+    bf16, f32, dma = jnp.bfloat16, jnp.float32, pltpu.SemaphoreType.DMA
+    vmem, hbm = pl.BlockSpec(memory_space=pltpu.VMEM), pl.BlockSpec(memory_space=pl.ANY)
 
     def kernel(n_h, sections, periods, *refs):
         attention_kernel(n_h, sections, periods, left_starts, scale, *refs)
@@ -793,17 +864,30 @@
         kernel,
         lefts,
         rights,
-        [query, pairs, d_out, log_total, seg[:, None], seg[None, :cells]],
-        [],
-        [jax.ShapeDtypeStruct((cells, 3 * width), bf16)],
-        [vmem],
+        operands,
+        [weight],
         [
+            jax.ShapeDtypeStruct((3 * width, cells), bf16),
+            jax.ShapeDtypeStruct((3 * width, cells), bf16),
+            jax.ShapeDtypeStruct((3,) + lefts.shape[1:], bf16),
+            jax.ShapeDtypeStruct((cells, width), bf16),
+        ],
+        [hbm, hbm, vmem, vmem],
+        [
+            pltpu.VMEM((cells, 3 * width), bf16),
             pltpu.VMEM((2, width // 128, 4 * cells, 128), bf16),
             pltpu.VMEM((2, width // 128, 2 * cells, 128), bf16),
             pltpu.VMEM((2, width // 128, cells, 128), bf16),
-            pltpu.VMEM((128, cells), jnp.float32),
-            pltpu.SemaphoreType.DMA((2,)),
-            pltpu.SemaphoreType.DMA((2,)),
+            pltpu.VMEM((128, cells), f32),
+            pltpu.VMEM(weight.shape, bf16),
+            pltpu.VMEM((3 * width, cells), bf16),
+            pltpu.VMEM((cells, width), f32),
+            pltpu.VMEM((cells, width), f32),
+            pltpu.VMEM((2, width // 2, cells), bf16),
+            pltpu.VMEM((2, width // 2, cells), bf16),
+            dma((4,)),
+            dma((4,)),
+            dma((2,)),
         ],
         collective_id,
     )
@@ -884,9 +968,8 @@
     ]
     cuts = [gene_cuts, [0, width // 2 * 3, 3 * width + 128], [0, width]]
     cuts += [[0, 2 * width, 4 * width], [0, width // 2, width]]
-    cuts += [[k * (padded // 1024) * 128 for k in range(8)] + [padded]]
-    order = [(0, 0), (0, 1), (0, 2), (0, 3), (1, 0), (1, 1), (2, 0), (3, 0), (3, 1), (4, 0), (4, 1)]
-    order += [(5, piece) for piece in range(8)]
+    cuts += [[0, padded]]
+    order = [(0, 0), (0, 1), (0, 2), (0, 3), (1, 0), (1, 1), (2, 0), (3, 0), (3, 1), (4, 0), (4, 1), (5, 0)]
     gathered, xb, h0, a1, query, kv_all = gather_all(
         shards, 5, cuts, order, counts.T, scale[None, :], pe.T, 0
     )
@@ -895,7 +978,6 @@
         w.reshape(-1, w.shape[-1]) for w in gathered[:5]
     )
     vectors = qkv_all[:, 3 * width :].astype(jnp.float32).T
-    qkv_all = qkv_all[:, : 3 * width]
     g1f, b1f, g2f, b2f = vectors[0], vectors[1], vectors[2], vectors[3]
     kv_pairs, query_b = kv_all, query
     query = query.reshape(rows, heads, head_width)
@@ -953,15 +1035,14 @@
     lefts = [left_of(a2, 1), left_of(act, act.shape[1] // width), left_of(attended_b, 1)]
     pieces = (4 * width,) + (width,) * 4
     rights = [both_cores(d_hidden.T), both_cores(dfb.T, 4), both_cores(dab.T)]
-    grads, d_qkv = scatter_attention(
+    operands = [query_b, kv_pairs, d_attended, log_total[:, :, 0], seg_all[:, None], seg_all[None, :rows], h0, dh1]
+    operands += [jnp.pad(jnp.stack([g1f, grad_gain_two, grad_shift_two]), ((0, 5), (0, 0))), left_of(a1, 1)[0]]
+    grads, d_qkv, d_qkv_other, lefts, dh0b = scatter_attention(
         jnp.concatenate(lefts, axis=0),
         [sum(pieces[:k]) // CHUNK for k in range(len(pieces) + 1)],
         rights,
-        query_b,
-        kv_pairs,
-        d_attended,
-        log_total[:, :, 0],
-        seg_all,
+        operands,
+        gathered[1],
         att_scale,
         2,
     )
@@ -973,19 +1054,11 @@
     grad_down = grad_down.reshape(4, -1, own_rows, CHUNK).transpose(0, 2, 1, 3)
     grad_down = grad_down.reshape(4 * own_rows, -1)
     grad_out, grad_up, grad_down = (from_owner(g, 1) for g in (grad_out, grad_up, grad_down))
-    da1 = contract_cols(d_qkv, qkv_all)
-    first_pull = jax.vjp(layer_norm, h0, g1f, b1f)[1]
-    dh0_norm, grad_gain_one, grad_shift_one = first_pull(da1)
-    vectors_b = jnp.stack([grad_gain_one, grad_shift_one, grad_gain_two, grad_shift_two])
-    vectors_b = jnp.pad(vectors_b, ((0, rows - 4), (0, 0))).astype(jnp.bfloat16)
     unit = jnp.eye(rows, dtype=jnp.bfloat16)
-    dh0b = (dh1 + dh0_norm).astype(jnp.bfloat16)
-
-    lefts = [left_of(a1, 1), left_of(vectors_b, 1), left_of(dh0b, 1)]
     grads, d_xb = scatter_product(
-        jnp.concatenate(lefts, axis=0),
+        lefts,
         [0, 3 * width // CHUNK, (3 * width + rows) // CHUNK],
-        [both_cores(d_qkv.T), (unit, unit, 1), xb_pair],
+        [(d_qkv, d_qkv_other, 1), (unit, unit, 1), xb_pair],
         dh0b,
         [enc_all],
         jnp.float32,

time: 967 us -> 946 us (0.978)
  Pallas kernels: 710 us -> 699 us
    unnamed x106 -> x98, local copies, waits for them, and re-layouts: 14 us -> 21.4 us
    dot_general x4 -> x3, matrix products: 22.9 us -> 17.2 us  [contract_cols(): lax.dot_general(left, right, (((1,), (1,)), ((), ())), preferred_element_...]
    ppermute x21 -> x18, waiting for transfers between devices: 47 us -> 42.4 us  [swap(): return lax.ppermute(value, axis, [(0, 1), (1, 0)])]
  transfers between devices with their start and end apart: 21 -> 18, of which waited for: 5 -> 5; matrix products, arithmetic and copies ran while one was open for 16% -> 15% of each run, Pallas kernels for 28% -> 27%
where the time goes in v10:
time: 946 us; the launch traced here: 939 us
  Pallas kernels  699 us (74%)
  local copies, waits for them, and re-layouts  95.3 us (10%)
  matrix products  53.3 us (6%)
  waiting for transfers between devices  42.4 us (4%)
  other arithmetic  39.1 us (4%)
    pallas_call x3, Pallas kernels, scatter_call(): pl.pallas_call(functools.partial(kernel, inner_h, sections, periods), out...  415 us
    pallas_call x1, Pallas kernels, gather_all(): pl.pallas_call(functools.partial(front_kernel, n_h, jobs, len(shards), n_...  285 us
    ppermute x18, waiting for transfers between devices, swap(): return lax.ppermute(value, axis, [(0, 1), (1, 0)])  42.4 us
    dot_general x3, matrix products, matmul(): return jnp.dot(left, right, preferred_element_type=jnp.float32)  25 us
    unnamed x98, local copies, waits for them, and re-layouts  21.4 us
  transfers between devices with their start and end apart: 18, of which 5 were waited for; matrix products, arithmetic and copies ran while one was open for 15% of the time, Pallas kernels for 27%

profile of v10, /device:TPU:0, one launch (start us, length us, event | category | flops | bytes accessed | tf_op | source)
XLA Modules:
  0.0 939.3 jit_solution(12068972726828991955)
XLA Ops:
  2.5 1.3 broadcast_divide_fusion
  4.4 2.1 pad.23.refs_0_
  6.6 2.1 pad.25.refs_5_
  8.7 1.1 copy.208
  13.9 1.9 multiply_sine_fusion.1
  15.8 1.1 pad_maximum_fusion.2
  16.9 284.6 %shard_map.238 = (bf16[2,2,2,128,13568]{4,3,2,1,0:T(8,128)(2,1)}, bf16[2,2,2,128,3200]{4,3,2,1,0:T(8,128)(2,1)}, bf16[2,2,2,128,1024]{4,3,2,1,0:T(8,128)(2,1)}, ...) custom-call(bf16[32,13568]{1,0:T(8,128)(2,1)} %pad.23.refs_0_, ...), custom_call_target="tpu_custom_call" | custom-call | tf_op jit(solution)/shard_map/pallas_call | solution.py:360
  301.6 2.1 collective-permute-start.2
  303.7 1.2 copy.230
  306.4 7.7 pad.27.refs_2_
  316.5 4.0 fusion.23
  320.4 4.0 copy.214
  324.6 2.6 copy.211
  327.4 4.5 fusion
  331.9 4.4 fusion.1
  336.3 6.6 fusion.11
  343.8 1.3 copy.216
  345.1 2.3 fusion.26
  348.2 1.0 slice.131
  350.3 15.9 %multiply_add_fusion = (f32[256,4096]{0,1:T(8,128)}, f32[256,4096]{0,1:T(8,128)S(1)}, f32[256,4096]{0,1:T(8,128)S(1)}) fusion(bf16[256,1024]{0,1:T(8,128)(2,1)S(1)} %add_convert_fusion, bf16[1024,4096]{1,0:T(8,128)(2,1)} %bitcast.202), kind=kOutput, calls=%fused_computation.12 | convolution fusion | flops 2218786816 | bytes 21495808 | tf_op jit(solution)/shard_map/dot_general | solution.py:51
  366.9 6.7 fusion.10
  374.3 4.9 collective-permute-done.3.refs_6_
  379.3 2.8 slice.134
  387.6 2.8 slice.135
  390.4 1.7 collective-permute-start.5
  392.2 1.8 constant_dynamic-slice_fusion.31
  394.0 1.8 constant_dynamic-slice_fusion.15
  395.8 1.0 constant_dynamic-slice_fusion.23
  396.9 24.8 %collective-permute-done.4 = bf16[128,6784]{1,0:T(8,128)(2,1)} collective-permute-done((bf16[128,6784]{1,0:T(8,128)(2,1)}, bf16[128,6784]{1,0:T(8,128)(2,1)}, u32[]{:S(2)}, u32[]{:S(2)}) %collective-permute-start.4) | collective-permute-done | bytes 1736736 | tf_op jit(solution)/shard_map/ppermute | solution.py:55
  421.7 2.8 constant_dynamic-update-slice_fusion.9
  425.1 5.9 collective-permute-done.5
  431.1 2.8 constant_dynamic-update-slice_fusion.8.refs_7_
  435.0 1.0 copy-done.12
  436.0 2.1 copy.223.refs_1_
  438.8 1.3 log_add_fusion.refs_4_
  440.2 1.8 maximum_bitcast_fusion.3.refs_10_
  442.0 1.8 maximum_bitcast_fusion.refs_0_
  443.7 1.0 maximum_bitcast_fusion.1
  444.8 1.1 maximum_bitcast_fusion.2
  446.3 2.1 pad_maximum_fusion.refs_0_
  448.8 1.6 collective-permute-done.8.refs_10_
  450.5 5.0 collective-permute-done.9.refs_11_
  455.4 134.5 %shard_map.239 = (f32[53,32,256]{2,1,0:T(8,128)}, bf16[13568,256]{1,0:T(8,128)(2,1)}, f32[1024,256]{1,0:T(8,128)}) custom-call(bf16[1,512,512]{2,1,0:T(8,128)(2,1)} %maximum_bitcast_fusion.refs_0_, bf16[256,1024]{1,0:T(8,128)(2,1)} %copy.223.refs_1_, bf16[13568,256]{1,0:T(8,128)(2,1)} %pad.27.refs_2_, bf16[13568,256]{1,0:T(8,128)(2,1)} %collective-permute-done.1.refs_3_, ...), custom_call_target="tpu_custom_call" | custom-call | tf_op jit(solution)/shard_map/pallas_call | solution.py:796
  598.2 8.2 fusion.3
  606.4 7.4 fusion.27
  613.8 1.6 copy.226
  616.2 1.5 convert_bitcast_fusion.1
  618.3 6.8 slice_bitcast_fusion
  625.2 1.3 slice_bitcast_fusion.1
  626.8 1.3 copy.239.refs_8_
  628.1 1.6 convolution_convert_fusion
  629.7 1.2 copy.227
  631.0 1.0 copy.238.refs_3_
  632.6 123.6 %shard_map.240 = (f32[36,32,256]{2,1,0:T(8,128)}, bf16[3072,256]{1,0:T(8,128)(2,1)}, bf16[3072,256]{1,0:T(8,128)(2,1)}, bf16[3,512,512]{2,1,0:T(8,128)(2,1)}, bf16[256,1024]{1,0:T(8,128)(2,1)}) custom-call(bf16[6,512,512]{2,1,0:T(8,128)(2,1)} %pad_maximum_fusion.refs_0_, bf16[256,1024]{1,0:T(8,128)(2,1)} %get-tuple-element.37.refs_1_, ...), custom_call_target="tpu_custom_call" | custom-call | tf_op jit(solution)/shard_map/pallas_call | solution.py:796
  756.3 156.7 %shard_map.241 = (f32[66,32,256]{2,1,0:T(8,128)}, f32[13568,256]{1,0:T(8,128)}) custom-call(bf16[3,512,512]{2,1,0:T(8,128)(2,1)} %get-tuple-element.48.refs_0_, bf16[256,1024]{1,0:T(8,128)(2,1)} %get-tuple-element.49.refs_1_, bf16[3072,256]{1,0:T(8,128)(2,1)} %get-tuple-element.50.refs_2_, bf16[3072,256]{1,0:T(8,128)(2,1)} %get-tuple-element.51.refs_3_, ...), custom_call_target="tpu_custom_call" | custom-call | tf_op jit(solution)/shard_map/pallas_call | solution.py:796
  913.0 1.7 slice_bitcast_fusion.3
  914.7 1.0 slice_bitcast_fusion.5
  915.8 1.7 slice_reduce_fusion.1
  917.5 12.2 %bitcast_divide_fusion = f32[256,13500]{0,1:T(8,128)} fusion(bf16[256,13500]{0,1:T(8,128)(2,1)} %param.15, f32[13568,256]{1,0:T(8,128)} %get-tuple-element.54, f32[256]{0:T(256)S(1)} %copy-done.28), kind=kLoop, calls=%fused_computation.4 | loop fusion | flops 17280000 | bytes 34562048 | tf_op jit(solution)/shard_map/div | solution.py:1080
  929.8 1.3 slice_bitcast_fusion.2
  932.9 1.0 copy.246
  934.0 1.0 copy.248
  935.8 1.2 reshape.396
  937.7 1.3 reshape.395
  (183 shorter events, 37.1 us)
Async XLA Ops:
  0.6 10.0 %copy-start.18 = (bf16[32,4096]{1,0:T(8,128)(2,1)S(1)}, bf16[32,4096]{1,0:T(8,128)(2,1)}, u32[]{:S(2)}) copy-start(bf16[32,4096]{1,0:T(8,128)(2,1)} %param.25) | copy-start | bytes 786436
  0.7 11.2 %copy-start.24 = (bf16[32,1024]{1,0:T(8,128)(2,1)S(1)}, bf16[32,1024]{1,0:T(8,128)(2,1)}, u32[]{:S(2)}) copy-start(bf16[32,1024]{1,0:T(8,128)(2,1)} %param.22) | copy-start | bytes 196612
  0.7 12.4 %copy-start.38 = (bf16[32]{0:T(256)(128)(2,1)S(1)}, bf16[32]{0:T(256)(128)(2,1)}, u32[]{:S(2)}) copy-start(bf16[32]{0:T(256)(128)(2,1)} %param.23) | copy-start | bytes 196
  0.7 12.4 %copy-start.37 = (bf16[32]{0:T(256)(128)(2,1)S(1)}, bf16[32]{0:T(256)(128)(2,1)}, u32[]{:S(2)}) copy-start(bf16[32]{0:T(256)(128)(2,1)} %param.24) | copy-start | bytes 196
  0.7 12.4 %copy-start.36 = (bf16[32]{0:T(256)(128)(2,1)S(1)}, bf16[32]{0:T(256)(128)(2,1)}, u32[]{:S(2)}) copy-start(bf16[32]{0:T(256)(128)(2,1)} %param.27) | copy-start | bytes 196
  0.7 12.4 %copy-start.35 = (bf16[32]{0:T(256)(128)(2,1)S(1)}, bf16[32]{0:T(256)(128)(2,1)}, u32[]{:S(2)}) copy-start(bf16[32]{0:T(256)(128)(2,1)} %param.28) | copy-start | bytes 196
  0.7 12.5 %copy-start.21 = (bf16[32,3072]{1,0:T(8,128)(2,1)S(1)}, bf16[32,3072]{1,0:T(8,128)(2,1)}, u32[]{:S(2)}) copy-start(bf16[32,3072]{1,0:T(8,128)(2,1)} %param.21) | copy-start | bytes 589828
  301.5 77.8 %collective-permute-start.3 = (bf16[128,13568]{1,0:T(8,128)(2,1)}, bf16[128,13568]{1,0:T(8,128)(2,1)}, u32[]{:S(2)}, u32[]{:S(2)}) collective-permute-start(bf16[128,13568]{1,0:T(8,128)(2,1)} %get-tuple-element.43.refs_4_), channel_id=1, source_target_pairs={{0,4},{4,0},{1,5},{5,1},{2,6},{6,2},{3,7},{7,3},{8,12},{12,8},{9,1... | collective-permute-start | bytes 10420232 | tf_op jit(solution)/shard_map/ppermute | solution.py:55
  301.6 86.1 %collective-permute-start.2 = (bf16[128,13568]{1,0:T(8,128)(2,1)}, bf16[128,13568]{1,0:T(8,128)(2,1)}, u32[]{:S(2)}, u32[]{:S(2)}) collective-permute-start(bf16[128,13568]{1,0:T(8,128)(2,1)} %get-tuple-element.43.refs_4_), channel_id=1, source_target_pairs={{0,2},{2,0},{1,3},{3,1},{4,6},{6,4},{5,7},{7,5},{8,10},{10,8},{9,1... | collective-permute-start | bytes 10420232 | tf_op jit(solution)/shard_map/ppermute | solution.py:55
  306.4 118.1 %collective-permute-start.13 = (bf16[256,512]{0,1:T(8,128)(2,1)}, bf16[256,512]{0,1:T(8,128)(2,1)}, u32[]{:S(2)}, u32[]{:S(2)}) collective-permute-start(bf16[256,512]{0,1:T(8,128)(2,1)} %pad_maximum_fusion.7), channel_id=1, source_target_pairs={{0,1},{1,0},{2,3},{3,2},{4,5},{5,4},{6,7},{7,6},{8,9},{9,8},{10,11... | collective-permute-start | bytes 786440 | tf_op jit(solution)/shard_map/ppermute | solution.py:55
  314.1 136.3 %collective-permute-start.1 = (bf16[13568,256]{1,0:T(8,128)(2,1)}, bf16[13568,256]{1,0:T(8,128)(2,1)}, u32[]{:S(2)}, u32[]{:S(2)}) collective-permute-start(bf16[13568,256]{1,0:T(8,128)(2,1)} %pad.27.refs_2_), channel_id=1, source_target_pairs={{0,1},{1,0},{2,3},{3,2},{4,5},{5,4},{6,7},{7,6},{8,9},{9,8},{10,11... | collective-permute-start | bytes 20840456 | tf_op jit(solution)/shard_map/ppermute | solution.py:55
  315.7 0.8 copy-start.4
  315.8 11.4 %copy-start.32 = (s32[256]{0:T(256)}, s32[256]{0:T(256)S(1)}, u32[]{:S(2)}) copy-start(s32[256]{0:T(256)S(1)} %slice_reduce_fusion) | copy-start | bytes 3076
  320.4 4.0 copy-start.5
  336.3 6.7 copy-start.25
  336.3 7.5 copy-start.3
  336.3 8.8 copy-start.1
  347.5 18.8 %copy-start.26 = (f32[256]{0:T(256)}, f32[256]{0:T(256)S(1)}, u32[]{:S(2)}) copy-start(f32[256]{0:T(256)S(1)} %broadcast_multiply_fusion) | copy-start | bytes 3076
  347.7 0.5 copy-start.33
  347.7 18.6 %copy-start.29 = (f32[256]{0:T(256)}, f32[256]{0:T(256)S(1)}, u32[]{:S(2)}) copy-start(f32[256]{0:T(256)S(1)} %fusion.17) | copy-start | bytes 3076
  350.0 16.3 %copy-start.22 = (f32[1,1024]{1,0:T(1,128)}, f32[1,1024]{1,0:T(1,128)S(1)}, u32[]{:S(2)}) copy-start(f32[1,1024]{1,0:T(1,128)S(1)} %get-tuple-element.154) | copy-start | bytes 12292
  350.3 16.0 %copy-start.6 = (bf16[256,1024]{0,1:T(8,128)(2,1)}, bf16[256,1024]{0,1:T(8,128)(2,1)S(1)}, u32[]{:S(2)}) copy-start(bf16[256,1024]{0,1:T(8,128)(2,1)S(1)} %add_convert_fusion) | copy-start | bytes 1572868
  382.1 39.7 %collective-permute-start.4 = (bf16[128,6784]{1,0:T(8,128)(2,1)}, bf16[128,6784]{1,0:T(8,128)(2,1)}, u32[]{:S(2)}, u32[]{:S(2)}) collective-permute-start(bf16[128,6784]{1,0:T(8,128)(2,1)} %slice.134), channel_id=1, source_target_pairs={{0,2},{2,0},{1,3},{3,1},{4,6},{6,4},{5,7},{7,5},{8,10},{10,8},{9,1... | collective-permute-start | bytes 5210120 | tf_op jit(solution)/shard_map/ppermute | solution.py:55
  387.6 46.3 %collective-permute-start = (bf16[256,512]{0,1:T(8,128)(2,1)}, bf16[256,512]{0,1:T(8,128)(2,1)}, u32[]{:S(2)}, u32[]{:S(2)}) collective-permute-start(bf16[256,512]{0,1:T(8,128)(2,1)} %pad_maximum_fusion.4), channel_id=1, source_target_pairs={{0,1},{1,0},{2,3},{3,2},{4,5},{5,4},{6,7},{7,6},{8,9},{9,8},{10,11... | collective-permute-start | bytes 786440 | tf_op jit(solution)/shard_map/ppermute | solution.py:55
  390.4 40.6 %collective-permute-start.5 = (bf16[128,6784]{1,0:T(8,128)(2,1)}, bf16[128,6784]{1,0:T(8,128)(2,1)}, u32[]{:S(2)}, u32[]{:S(2)}) collective-permute-start(bf16[128,6784]{1,0:T(8,128)(2,1)} %slice.135), channel_id=1, source_target_pairs={{0,4},{4,0},{1,5},{5,1},{2,6},{6,2},{3,7},{7,3},{8,12},{12,8},{9,1... | collective-permute-start | bytes 5210120 | tf_op jit(solution)/shard_map/ppermute | solution.py:55
  396.9 43.3 %copy-start.14 = (bf16[256,128]{0,1:T(8,128)(2,1)S(1)}, bf16[256,128]{0,1:T(8,128)(2,1)}, u32[]{:S(2)}) copy-start(bf16[256,128]{0,1:T(8,128)(2,1)} %get-tuple-element.150) | copy-start | bytes 196612
  396.9 43.3 %copy-start.15 = (bf16[256,128]{0,1:T(8,128)(2,1)S(1)}, bf16[256,128]{0,1:T(8,128)(2,1)}, u32[]{:S(2)}) copy-start(bf16[256,128]{0,1:T(8,128)(2,1)} %get-tuple-element.151) | copy-start | bytes 196612
  396.9 45.1 %copy-start.16 = (bf16[256,128]{0,1:T(8,128)(2,1)S(1)}, bf16[256,128]{0,1:T(8,128)(2,1)}, u32[]{:S(2)}) copy-start(bf16[256,128]{0,1:T(8,128)(2,1)} %get-tuple-element.129) | copy-start | bytes 196612
  396.9 45.1 %copy-start.17 = (bf16[256,128]{0,1:T(8,128)(2,1)S(1)}, bf16[256,128]{0,1:T(8,128)(2,1)}, u32[]{:S(2)}) copy-start(bf16[256,128]{0,1:T(8,128)(2,1)} %get-tuple-element.127) | copy-start | bytes 196612
  421.7 13.2 %collective-permute-start.11 = (bf16[256,2048]{0,1:T(8,128)(2,1)S(1)}, bf16[256,2048]{0,1:T(8,128)(2,1)S(1)}, u32[]{:S(2)}, u32[]{:S(2)}) collective-permute-start(bf16[256,2048]{0,1:T(8,128)(2,1)S(1)} %pad_maximum_fusion.3), channel_id=1, source_target_pairs={{0,1},{1,0},{2,3},{3,2},{4,5},{5,4},{6,7},{7,6},{8,9},{9,8},{10,11... | collective-permute-start | bytes 3145736 | tf_op jit(solution)/shard_map/ppermute | solution.py:55
  424.5 21.3 %copy-start.9 = (bf16[256,512]{0,1:T(8,128)(2,1)S(1)}, bf16[256,512]{0,1:T(8,128)(2,1)}, u32[]{:S(2)}) copy-start(bf16[256,512]{0,1:T(8,128)(2,1)} %get-tuple-element.139) | copy-start | bytes 786436
  424.5 21.3 %copy-start.10 = (bf16[256,512]{0,1:T(8,128)(2,1)S(1)}, bf16[256,512]{0,1:T(8,128)(2,1)}, u32[]{:S(2)}) copy-start(bf16[256,512]{0,1:T(8,128)(2,1)} %get-tuple-element.140) | copy-start | bytes 786436
  424.5 21.3 %copy-start.11 = (bf16[256,512]{0,1:T(8,128)(2,1)S(1)}, bf16[256,512]{0,1:T(8,128)(2,1)}, u32[]{:S(2)}) copy-start(bf16[256,512]{0,1:T(8,128)(2,1)} %get-tuple-element.141) | copy-start | bytes 786436
  424.5 9.9 %collective-permute-start.10 = (bf16[256,512]{0,1:T(8,128)(2,1)S(1)}, bf16[256,512]{0,1:T(8,128)(2,1)S(1)}, u32[]{:S(2)}, u32[]{:S(2)}) collective-permute-start(bf16[256,512]{0,1:T(8,128)(2,1)S(1)} %pad_maximum_fusion.5), channel_id=1, source_target_pairs={{0,1},{1,0},{2,3},{3,2},{4,5},{5,4},{6,7},{7,6},{8,9},{9,8},{10,11... | collective-permute-start | bytes 786440 | tf_op jit(solution)/shard_map/ppermute | solution.py:55
  431.1 3.5 collective-permute-start.12
  433.9 14.5 %collective-permute-start.6 = (bf16[128,13568]{1,0:T(8,128)(2,1)}, bf16[128,13568]{1,0:T(8,128)(2,1)}, u32[]{:S(2)}, u32[]{:S(2)}) collective-permute-start(bf16[128,13568]{1,0:T(8,128)(2,1)} %get-tuple-element.43.refs_4_), channel_id=1, source_target_pairs={{0,1},{1,0},{2,3},{3,2},{4,5},{5,4},{6,7},{7,6},{8,9},{9,8},{10,11... | collective-permute-start | bytes 10420232 | tf_op jit(solution)/shard_map/ppermute | solution.py:55
  434.4 1.6 copy-start.19
  434.4 14.4 %collective-permute-start.7 = (bf16[128,13568]{1,0:T(8,128)(2,1)}, bf16[128,13568]{1,0:T(8,128)(2,1)}, u32[]{:S(2)}, u32[]{:S(2)}) collective-permute-start(bf16[128,13568]{1,0:T(8,128)(2,1)} %collective-permute-done.2.refs_5_), channel_id=1, source_target_pairs={{0,1},{1,0},{2,3},{3,2},{4,5},{5,4},{6,7},{7,6},{8,9},{9,8},{10,11... | collective-permute-start | bytes 10420232 | tf_op jit(solution)/shard_map/ppermute | solution.py:55
  434.5 1.5 copy-start.20
  434.5 15.9 %collective-permute-start.8 = (bf16[128,13568]{1,0:T(8,128)(2,1)}, bf16[128,13568]{1,0:T(8,128)(2,1)}, u32[]{:S(2)}, u32[]{:S(2)}) collective-permute-start(bf16[128,13568]{1,0:T(8,128)(2,1)} %collective-permute-done.3.refs_6_), channel_id=1, source_target_pairs={{0,1},{1,0},{2,3},{3,2},{4,5},{5,4},{6,7},{7,6},{8,9},{9,8},{10,11... | collective-permute-start | bytes 10420232 | tf_op jit(solution)/shard_map/ppermute | solution.py:55
  434.9 1.0 copy-start.12
  435.9 19.5 %collective-permute-start.9 = (bf16[128,13568]{1,0:T(8,128)(2,1)}, bf16[128,13568]{1,0:T(8,128)(2,1)}, u32[]{:S(2)}, u32[]{:S(2)}) collective-permute-start(bf16[128,13568]{1,0:T(8,128)(2,1)} %constant_dynamic-update-slice_fusion.8.refs_7_), channel_id=1, source_target_pairs={{0,1},{1,0},{2,3},{3,2},{4,5},{5,4},{6,7},{7,6},{8,9},{9,8},{10,11... | collective-permute-start | bytes 10420232 | tf_op jit(solution)/shard_map/ppermute | solution.py:55
  436.0 9.9 %copy-start.13 = (bf16[256,2048]{0,1:T(8,128)(2,1)S(1)}, bf16[256,2048]{0,1:T(8,128)(2,1)}, u32[]{:S(2)}) copy-start(bf16[256,2048]{0,1:T(8,128)(2,1)} %copy-done.12) | copy-start | bytes 3145732
  448.4 307.9 %collective-permute-start.17 = (bf16[13568,256]{1,0:T(8,128)(2,1)}, bf16[13568,256]{1,0:T(8,128)(2,1)}, u32[]{:S(2)}, u32[]{:S(2)}) collective-permute-start(bf16[13568,256]{1,0:T(8,128)(2,1)} %get-tuple-element.52.refs_6_), channel_id=1, source_target_pairs={{0,1},{1,0},{2,3},{3,2},{4,5},{5,4},{6,7},{7,6},{8,9},{9,8},{10,11... | collective-permute-start | bytes 20840456 | tf_op jit(solution)/shard_map/ppermute | solution.py:55
  606.4 9.0 copy-start.23
  606.4 9.0 copy-start.27
  613.8 1.8 copy-start.34
  613.8 1.8 copy-start.30
  615.4 2.8 copy-start.7
  617.7 14.9 %collective-permute-start.16 = (bf16[1024,256]{1,0:T(8,128)(2,1)}, bf16[1024,256]{1,0:T(8,128)(2,1)}, u32[]{:S(2)}, u32[]{:S(2)}) collective-permute-start(bf16[1024,256]{1,0:T(8,128)(2,1)} %get-tuple-element.112.refs_15_), channel_id=1, source_target_pairs={{0,1},{1,0},{2,3},{3,2},{4,5},{5,4},{6,7},{7,6},{8,9},{9,8},{10,11... | collective-permute-start | bytes 1572872 | tf_op jit(solution)/shard_map/ppermute | solution.py:55
  617.7 14.9 %collective-permute-start.14 = (bf16[4096,256]{1,0:T(8,128)(2,1)}, bf16[4096,256]{1,0:T(8,128)(2,1)}, u32[]{:S(2)}, u32[]{:S(2)}) collective-permute-start(bf16[4096,256]{1,0:T(8,128)(2,1)} %bitcast.58.refs_11_), channel_id=1, source_target_pairs={{0,1},{1,0},{2,3},{3,2},{4,5},{5,4},{6,7},{7,6},{8,9},{9,8},{10,11... | collective-permute-start | bytes 6291464 | tf_op jit(solution)/shard_map/ppermute | solution.py:55
  618.2 14.4 %collective-permute-start.15 = (bf16[1024,256]{1,0:T(8,128)(2,1)}, bf16[1024,256]{1,0:T(8,128)(2,1)}, u32[]{:S(2)}, u32[]{:S(2)}) collective-permute-start(bf16[1024,256]{1,0:T(8,128)(2,1)} %convert_element_type.112.refs_13_), channel_id=1, source_target_pairs={{0,1},{1,0},{2,3},{3,2},{4,5},{5,4},{6,7},{7,6},{8,9},{9,8},{10,11... | collective-permute-start | bytes 1572872 | tf_op jit(solution)/shard_map/ppermute | solution.py:55
  625.2 1.7 copy-start
  625.2 3.0 copy-start.2
  626.8 5.2 copy-start.31
  913.0 4.4 copy-start.8
  913.0 4.5 copy-start.28

commit v11 on v10

--- a/solution.py
+++ b/solution.py
@@ -399,7 +399,7 @@
     return out[: len(shards)], *out[len(shards) :]
 
 
-def scatter_kernel(n_h, sections, periods, left_starts, lefts, rights, out, scratch, peers, prefetch, beside, after):
+def scatter_kernel(n_h, sections, periods, left_starts, lefts, rights, out, scratch, peers, begin, prefetch, beside, after):
     (right_buf, own, s1, r1, s2, r2, s3, r3, load_sem, send1, recv1, send2, recv2, send3, recv3) = scratch
     h, x, y = (lax.axis_index(name) for name in ("h", "x", "y"))
     to_x, to_y = {"x": 1 - x}, {"y": 1 - y}
@@ -411,6 +411,7 @@
     n = sum(sections)
     cells = right_buf.shape[2] // 2
     greet([{"h": lax.rem(h + d, n_h)} for d in range(1, n_h)] + [to_x, to_y] + peers)
+    begin()
 
     def loads(i, section, k):
         slot = lax.rem(i, 3)
@@ -544,40 +545,90 @@
     return pl.ds(pl.multiple_of(k * CHUNK, CHUNK), CHUNK)
 
 
-def product_kernel(n_h, sections, periods, left_starts, n_weights, with_sum, *refs):
+def eighth_of(part):
+    c, x, y = (lax.axis_index(name) for name in ("c", "x", "y"))
+    return lax.rem(c + part // 4, 2) * 4 + lax.rem(x + part // 2 % 2, 2) * 2 + lax.rem(y + part % 2, 2)
+
+
+def product_kernel(n_h, sections, periods, left_starts, n_weights, *refs):
     lefts, vector = refs[:2]
     n_rights = 2 * len(sections)
     rights, weights = refs[2 : 2 + n_rights], refs[2 + n_rights : 2 + n_rights + n_weights]
     rest = refs[2 + n_rights + n_weights :]
+    split = n_weights == 8
     out, product = rest[:2]
-    total_out = rest[2] if with_sum else None
-    weight_buf, product_buf, weight_sem, product_sem, *scratch = rest[3 if with_sum else 2 :]
+    summed, turned, *fetched = rest[2:6] if split else (None, None)
+    rest = rest[6:] if split else rest[2:]
+    total, swap_send, swap_recv = rest[:3] if split else (None, None, None)
+    weight_buf, product_buf, weight_sem, product_sem, *scratch = rest[3:] if split else rest
     begin, count = sum(sections[:-1]), sections[-1]
-    cells = vector.shape[0]
-
-    def weight_loads(k):
+    cells, features = vector.shape
+    c = lax.axis_index("c")
+    middle = weights[0].shape[1] // CHUNK
+    spans = []
+    if split:
+        spans = [(0, 0, 2), (0, 2, 8), (0, 8, middle)]
+        spans += [(1, 0, (count - middle) // 2), (1, (count - middle) // 2, count - middle)]
+
+    def weight_loads(k, half, at):
         slot = lax.rem(k, 3)
-        size = weights[0].shape[0]
+        columns = chunk_of(at)
+        sources = [weight.at[:, columns] for weight in weights]
+        if split:
+            sources = [weight.at[:, columns] for weight in weights[4 * half : 4 * half + 4]]
+            sources += [fetched[half].at[part, :, columns] for part in range(4)]
+        size = features // len(sources)
         return [
             pltpu.make_async_copy(
-                weight.at[:, chunk_of(k)],
-                weight_buf.at[slot, pl.ds(part * size, size)],
-                weight_sem.at[slot, part],
+                source, weight_buf.at[slot, pl.ds(part * size, size)], weight_sem.at[slot, part]
             )
-            for part, weight in enumerate(weights)
+            for part, source in enumerate(sources)
         ]
+
+    def swap_copy(span, part):
+        half, low, high = spans[span]
+        columns = pl.ds(low * CHUNK, (high - low) * CHUNK)
+        return pltpu.make_async_remote_copy(
+            src_ref=weights[4 * half + part].at[:, columns],
+            dst_ref=fetched[half].at[part, :, columns],
+            send_sem=swap_send.at[span, part],
+            recv_sem=swap_recv.at[span, part],
+            device_id={"c": 1 - c},
+            device_id_type=MESH,
+        )
+
+    def start():
+        for span in range(len(spans)):
+            for part in range(4):
+                swap_copy(span, part).start()
 
     def product_store(k):
         slot = lax.rem(k, 2)
         return pltpu.make_async_copy(product_buf.at[slot], product.at[chunk_of(k)], product_sem.at[slot])
 
     def prefetch(section, k):
-        if section == len(sections) - 1:
-            for copy in weight_loads(k):
+        if section != len(sections) - 1:
+            return
+        if not split:
+            for copy in weight_loads(k, 0, k):
                 copy.start()
+            return
+        for span, (half, low, _) in enumerate(spans):
+
+            @pl.when(k == half * middle + low)
+            def _(span=span):
+                for part in range(4):
+                    swap_copy(span, part).wait_recv()
+
+        for half, here in enumerate((k < middle, k >= middle)):
+
+            @pl.when(here)
+            def _(half=half):
+                for copy in weight_loads(k, half, k - half * middle):
+                    copy.start()
 
     def multiply(k, right):
-        for copy in weight_loads(k):
+        for copy in weight_loads(k, 0, 0):
             copy.wait()
         weight = weight_buf[lax.rem(k, 3)]
 
@@ -588,16 +639,16 @@
         value = jnp.dot(vector[...], weight, preferred_element_type=jnp.float32)
         product_buf[lax.rem(k, 2)] = value.T.astype(product_buf.dtype)
         product_store(k).start()
-        if with_sum:
+        if split:
             term = jnp.dot(weight, right[:, :cells], preferred_element_type=jnp.float32)
 
             @pl.when(k == 0)
             def _():
-                total_out[...] = term
+                total[...] = term
 
             @pl.when(k > 0)
             def _():
-                total_out[...] += term
+                total[...] += term
 
     def beside(i, right, odd):
         if begin == 0:
@@ -609,10 +660,21 @@
                 multiply(i - begin, right)
 
     scatter_kernel(
-        n_h, sections, periods, left_starts, lefts, rights, out, scratch, [], prefetch, beside, lambda p: None
+        n_h, sections, periods, left_starts, lefts, rights, out, scratch, [{"c": 1 - c}] if split else [],
+        start, prefetch, beside, lambda p: None,
     )
     for k in range(max(count - 2, 0), count):
         product_store(k).wait()
+    if split:
+        size = features // 8
+        for part in range(8):
+            block = total[part * size : (part + 1) * size]
+            place = pl.ds(pl.multiple_of(eighth_of(part) * size, size), size)
+            summed[:, place] = block.T
+            turned[place] = block.astype(turned.dtype)
+        for span in range(len(spans)):
+            for part in range(4):
+                swap_copy(span, part).wait_send()
 
 
 def attention_kernel(n_h, sections, periods, left_starts, scale, *refs):
@@ -621,7 +683,7 @@
     rights, weight = refs[11 : 11 + n_rights], refs[11 + n_rights]
     (out, turned_own, turned_other, lefts_next, dh0b, d_qkv, d_pairs, by_core, by_y, d_query, weight_buf, turned,
      da1, vector_rows, send_left, got_left, send, recv, local, *scratch) = refs[12 + n_rights :]
-    x, y, c = (lax.axis_index(name) for name in ("x", "y", "c"))
+    y, c = lax.axis_index("y"), lax.axis_index("c")
     f32, b16 = jnp.float32, jnp.bfloat16
     cells, width = query.shape
     slots = 4 * cells
@@ -743,10 +805,7 @@
     def halves():
         for kind, source in enumerate((vector_rows, dh0b)):
             for part in range(8):
-                eighth = (
-                    lax.rem(c + part // 4, 2) * 4 + lax.rem(x + part // 2 % 2, 2) * 2 + lax.rem(y + part % 2, 2)
-                )
-                lanes = pl.ds(pl.multiple_of(eighth * (width // 8), width // 8), width // 8)
+                lanes = pl.ds(pl.multiple_of(eighth_of(part) * (width // 8), width // 8), width // 8)
                 block = source[:, lanes].astype(f32).T.astype(b16)
                 rows = slice(part % 4 * (width // 8), (part % 4 + 1) * (width // 8))
                 if part < 4:
@@ -767,7 +826,7 @@
     n_chunk_pairs = (sum(sections) + 1) // 2
     scatter_kernel(
         n_h, sections, periods, left_starts, lefts, rights, out, scratch, [{"c": 1 - c}],
-        lambda section, k: None, beside, after,
+        lambda: None, lambda section, k: None, beside, after,
     )
     lefts_next[0] = left_one[...]
     to_other_left().wait_recv()
@@ -825,13 +884,19 @@
     return part, *more
 
 
-def scatter_product(lefts, left_starts, rights, vector, weights, product_type, with_sum, collective_id):
+def scatter_product(lefts, left_starts, rights, vector, weights, product_type, collective_id):
     (cells, features), columns = vector.shape, rights[-1][0].shape[0]
-    dma = pltpu.SemaphoreType.DMA
+    dma, bf16, f32 = pltpu.SemaphoreType.DMA, jnp.bfloat16, jnp.float32
     vmem, hbm = pl.BlockSpec(memory_space=pltpu.VMEM), pl.BlockSpec(memory_space=pl.ANY)
+    shapes, specs, scratch = [jax.ShapeDtypeStruct((columns, cells), product_type)], [hbm], []
+    if len(weights) == 8:
+        shapes += [jax.ShapeDtypeStruct((cells, features), f32), jax.ShapeDtypeStruct((features, cells), bf16)]
+        shapes += [jax.ShapeDtypeStruct((4,) + weights[k].shape, bf16) for k in (0, 4)]
+        specs += [vmem, vmem, hbm, hbm]
+        scratch = [pltpu.VMEM((features, cells), f32), dma((5, 4)), dma((5, 4))]
 
     def kernel(n_h, sections, periods, *refs):
-        product_kernel(n_h, sections, periods, left_starts, len(weights), with_sum, *refs)
+        product_kernel(n_h, sections, periods, left_starts, len(weights), *refs)
 
     return scatter_call(
         kernel,
@@ -839,11 +904,11 @@
         rights,
         [vector],
         weights,
-        [jax.ShapeDtypeStruct((columns, cells), product_type)]
-        + [jax.ShapeDtypeStruct((features, cells), jnp.float32)] * with_sum,
-        [hbm] + [vmem] * with_sum,
-        [
-            pltpu.VMEM((3, features, CHUNK), jnp.bfloat16),
+        shapes,
+        specs,
+        scratch
+        + [
+            pltpu.VMEM((3, features, CHUNK), bf16),
             pltpu.VMEM((2, CHUNK, cells), product_type),
             dma((3, len(weights))),
             dma((2,)),
@@ -956,7 +1021,7 @@
     vectors = jnp.stack([gain_one, shift_one, gain_two, shift_two], axis=1)
     vectors = jnp.pad(vectors, ((0, 0), (0, 124)))
     pad = ((0, 0), (0, padded - genes))
-    quarter = padded // CHUNK // 4 * CHUNK
+    quarter, middle = padded // CHUNK // 4 * CHUNK, padded // CHUNK // 2 * CHUNK
     gene_cuts = [0, quarter, 2 * quarter, 3 * quarter, padded]
     shards = [
         jnp.pad(w_enc.T, pad),
@@ -964,12 +1029,13 @@
         by_owner(w_out, 1),
         by_owner(w_up, 1),
         by_owner(w_down, 1),
-        jnp.pad(w_dec.T, pad),
+        w_dec.T[:, :middle],
+        jnp.pad(w_dec.T[:, middle:], pad),
     ]
     cuts = [gene_cuts, [0, width // 2 * 3, 3 * width + 128], [0, width]]
     cuts += [[0, 2 * width, 4 * width], [0, width // 2, width]]
-    cuts += [[0, padded]]
-    order = [(0, 0), (0, 1), (0, 2), (0, 3), (1, 0), (1, 1), (2, 0), (3, 0), (3, 1), (4, 0), (4, 1), (5, 0)]
+    cuts += [[0, middle], [0, padded - middle]]
+    order = [(0, 0), (0, 1), (0, 2), (0, 3), (1, 0), (1, 1), (2, 0), (3, 0), (3, 1), (4, 0), (4, 1), (5, 0), (6, 0)]
     gathered, xb, h0, a1, query, kv_all = gather_all(
         shards, 5, cuts, order, counts.T, scale[None, :], pe.T, 0
     )
@@ -982,12 +1048,11 @@
     kv_pairs, query_b = kv_all, query
     query = query.reshape(rows, heads, head_width)
     kv_all = kv_all.reshape(slots, -1)
-    dec_own = gathered[5]
-    middle = dec_own.shape[1] // 256 * 128
-    by_x, by_y = swap(dec_own, "x"), swap(dec_own, "y")
-    far = (swap(by_x[:, :middle], "y"), swap(by_y[:, middle:], "x"))
-    dec_parts = [dec_own, by_y, by_x, jnp.concatenate(far, axis=1)]
-    dec_parts += [swap(part, "c") for part in dec_parts]
+    dec_left, dec_right = gathered[5:]
+    left_x, right_y = swap(dec_left, "x"), swap(dec_right, "y")
+    left_y, right_x = swap(dec_left, "y"), swap(dec_right, "x")
+    dec_parts = [dec_left, left_y, left_x, swap(left_x, "y")]
+    dec_parts += [dec_right, right_y, right_x, swap(right_y, "x")]
     keys = kv_all[:, :width].reshape(slots, heads, head_width)
     values = kv_all[:, width:].reshape(slots, heads, head_width)
 
@@ -1015,13 +1080,12 @@
     )
     h2 = h1 + matmul(act, down_all)
     hb = h2.astype(jnp.bfloat16)
-    grad_dec, logits, dh2 = scatter_product(
-        left_of(hb, 1), [0], [cot_pair], relative(hb, 1), dec_parts, jnp.bfloat16, True, 1
+    grad_dec, logits, dh2, dfb_turned, *_ = scatter_product(
+        left_of(hb, 1), [0], [cot_pair], relative(hb, 1), dec_parts, jnp.bfloat16, 1
     )
     own_rows = grad_dec.shape[1]
     grad_dec = columns_of(grad_dec)[:, :genes].T
     logits = logits[:genes].T
-    dh2 = relative(dh2, 0).T
     dfb = dh2.astype(jnp.bfloat16)
     d_act = contract_cols(dfb, down_all)
     d_hidden = (d_act * slope).astype(jnp.bfloat16)
@@ -1034,7 +1098,7 @@
     d_attended = from_owner(d_attended, 1)
     lefts = [left_of(a2, 1), left_of(act, act.shape[1] // width), left_of(attended_b, 1)]
     pieces = (4 * width,) + (width,) * 4
-    rights = [both_cores(d_hidden.T), both_cores(dfb.T, 4), both_cores(dab.T)]
+    rights = [both_cores(d_hidden.T), both_cores(dfb_turned, 4), both_cores(dab.T)]
     operands = [query_b, kv_pairs, d_attended, log_total[:, :, 0], seg_all[:, None], seg_all[None, :rows], h0, dh1]
     operands += [jnp.pad(jnp.stack([g1f, grad_gain_two, grad_shift_two]), ((0, 5), (0, 0))), left_of(a1, 1)[0]]
     grads, d_qkv, d_qkv_other, lefts, dh0b = scatter_attention(
@@ -1062,7 +1126,6 @@
         dh0b,
         [enc_all],
         jnp.float32,
-        False,
         3,
     )
     ends = [0]

time: 946 us -> 953 us (level)
  waiting for transfers between devices: 42.4 us -> 64 us
  local copies, waits for them, and re-layouts: 95.3 us -> 74.4 us
    ppermute x18 -> x16, waiting for transfers between devices: 42.4 us -> 64 us  [swap(): return lax.ppermute(value, axis, [(0, 1), (1, 0)])]
    unnamed x98 -> x94, local copies, waits for them, and re-layouts: 21.4 us -> 9.8 us
  transfers between devices with their start and end apart: 18 -> 16, of which waited for: 5 -> 6; matrix products, arithmetic and copies ran while one was open for 15% -> 13% of each run, Pallas kernels for 27% -> 27%
where the time goes in v11:
time: 953 us; the launch traced here: 947 us
  Pallas kernels  703 us (74%)
  local copies, waits for them, and re-layouts  74.4 us (8%)
  waiting for transfers between devices  64 us (7%)
  matrix products  54.2 us (6%)
  other arithmetic  41.7 us (4%)
    pallas_call x3, Pallas kernels, scatter_call(): pl.pallas_call(functools.partial(kernel, inner_h, sections, periods), out...  418 us
    pallas_call x1, Pallas kernels, gather_all(): pl.pallas_call(functools.partial(front_kernel, n_h, jobs, len(shards), n_...  285 us
    ppermute x16, waiting for transfers between devices, swap(): return lax.ppermute(value, axis, [(0, 1), (1, 0)])  64 us
    dot_general x3, matrix products, matmul(): return jnp.dot(left, right, preferred_element_type=jnp.float32)  26.5 us
  transfers between devices with their start and end apart: 16, of which 6 were waited for; matrix products, arithmetic and copies ran while one was open for 13% of the time, Pallas kernels for 27%

profile of v11, /device:TPU:0, one launch (start us, length us, event | category | flops | bytes accessed | tf_op | source)
XLA Modules:
  0.0 947.5 jit_solution(18441300539692494949)
XLA Ops:
  0.7 1.1 slice.128
  1.9 1.8 slice.127.refs_5_
  4.5 0.9 slice.129
  6.8 1.2 broadcast_divide_fusion
  8.1 2.1 pad.24.refs_0_
  10.4 0.9 copy.214.refs_4_
  11.5 0.9 reshape.373.refs_3_
  12.7 0.9 reshape.371.refs_2_
  14.4 1.9 multiply_sine_fusion.1
  16.3 1.1 pad_maximum_fusion.2
  17.4 284.8 %shard_map.238 = (bf16[2,2,2,128,13568]{4,3,2,1,0:T(8,128)(2,1)}, bf16[2,2,2,128,3200]{4,3,2,1,0:T(8,128)(2,1)}, bf16[2,2,2,128,1024]{4,3,2,1,0:T(8,128)(2,1)}, ...) custom-call(bf16[32,13568]{1,0:T(8,128)(2,1)} %pad.24.refs_0_, ...), custom_call_target="tpu_custom_call" | custom-call | tf_op jit(solution)/shard_map/pallas_call | solution.py:360
  302.3 1.2 copy.235
  305.4 2.1 collective-permute-start.3
  307.4 7.7 pad.28.refs_2_
  317.0 4.0 fusion.23
  321.0 4.0 copy.218
  325.2 2.6 copy.215
  328.0 4.5 fusion
  332.4 4.4 fusion.1
  336.9 6.6 fusion.11
  343.5 0.8 copy.219
  344.4 1.3 copy.220
  345.7 2.3 fusion.26
  348.8 1.0 slice.133
  351.7 17.3 %multiply_add_fusion = (f32[256,4096]{0,1:T(8,128)}, f32[256,4096]{0,1:T(8,128)}, f32[256,4096]{0,1:T(8,128)}) fusion(bf16[256,1024]{0,1:T(8,128)(2,1)S(1)} %add_convert_fusion, bf16[1024,4096]{1,0:T(8,128)(2,1)} %bitcast.189), kind=kOutput, calls=%fused_computation.12 | convolution fusion | flops 2218786816 | bytes 21495808 | tf_op jit(solution)/shard_map/dot_general | solution.py:51
  369.1 4.1 multiply_convert_fusion
  373.2 1.0 constant_dynamic-slice_fusion.23
  374.8 6.8 fusion.10
  387.7 1.4 collective-permute-done.10
  389.1 2.0 collective-permute-start.7
  391.1 1.0 copy-done.14
  392.1 2.1 collective-permute-start.4
  394.2 2.0 copy.227.refs_1_
  396.9 1.3 log_add_fusion.refs_4_
  398.2 1.8 maximum_bitcast_fusion.3.refs_10_
  400.0 1.8 maximum_bitcast_fusion.refs_0_
  401.9 1.0 maximum_bitcast_fusion.1
  402.9 1.1 maximum_bitcast_fusion.2
  404.4 2.0 pad_maximum_fusion.refs_0_
  406.5 26.0 %collective-permute-done.2.refs_5_ = bf16[128,6656]{1,0:T(8,128)(2,1)} collective-permute-done((bf16[128,6656]{1,0:T(8,128)(2,1)}, bf16[128,6656]{1,0:T(8,128)(2,1)}, u32[]{:S(2)}, u32[]{:S(2)}) %collective-permute-start.2) | collective-permute-done | bytes 1703968 | tf_op jit(solution)/shard_map/ppermute | solution.py:55
  432.5 35.1 %collective-permute-done.4.refs_7_ = bf16[128,6656]{1,0:T(8,128)(2,1)} collective-permute-done((bf16[128,6656]{1,0:T(8,128)(2,1)}, bf16[128,6656]{1,0:T(8,128)(2,1)}, u32[]{:S(2)}, u32[]{:S(2)}) %collective-permute-start.4) | collective-permute-done | bytes 1703968 | tf_op jit(solution)/shard_map/ppermute | solution.py:55
  467.8 137.8 %shard_map.239 = (f32[53,32,256]{2,1,0:T(8,128)}, bf16[13568,256]{1,0:T(8,128)(2,1)}, f32[256,1024]{1,0:T(8,128)}, bf16[1024,256]{1,0:T(8,128)(2,1)}, bf16[4,128...) custom-call(bf16[1,512,512]{2,1,0:T(8,128)(2,1)} %maximum_bitcast_fusion.refs_0_, bf16[256,1024]{1,0:T(8,128)(2,1)} %copy.227.refs_1_, ...), custom_call_target="tpu_custom_call" | custom-call | tf_op jit(solution)/shard_map/pallas_call | solution.py:855
  605.6 2.5 copy.231
  608.1 8.6 fusion.3
  616.7 6.4 fusion.27
  624.3 2.4 convert_bitcast_fusion.1
  627.3 6.8 slice_bitcast_fusion
  634.2 1.3 slice_bitcast_fusion.1
  635.5 1.3 copy.244.refs_8_
  636.8 1.6 convolution_convert_fusion
  638.3 1.2 copy.232
  639.6 1.0 copy.243.refs_3_
  641.3 122.4 %shard_map.240 = (f32[36,32,256]{2,1,0:T(8,128)}, bf16[3072,256]{1,0:T(8,128)(2,1)}, bf16[3072,256]{1,0:T(8,128)(2,1)}, bf16[3,512,512]{2,1,0:T(8,128)(2,1)}, bf16[256,1024]{1,0:T(8,128)(2,1)}) custom-call(bf16[6,512,512]{2,1,0:T(8,128)(2,1)} %pad_maximum_fusion.refs_0_, bf16[256,1024]{1,0:T(8,128)(2,1)} %get-tuple-element.39.refs_1_, ...), custom_call_target="tpu_custom_call" | custom-call | tf_op jit(solution)/shard_map/pallas_call | solution.py:855
  763.6 157.6 %shard_map.241 = (f32[66,32,256]{2,1,0:T(8,128)}, f32[13568,256]{1,0:T(8,128)}) custom-call(bf16[3,512,512]{2,1,0:T(8,128)(2,1)} %get-tuple-element.52.refs_0_, bf16[256,1024]{1,0:T(8,128)(2,1)} %get-tuple-element.53.refs_1_, bf16[3072,256]{1,0:T(8,128)(2,1)} %get-tuple-element.54.refs_2_, bf16[3072,256]{1,0:T(8,128)(2,1)} %get-tuple-element.55.refs_3_, ...), custom_call_target="tpu_custom_call" | custom-call | tf_op jit(solution)/shard_map/pallas_call | solution.py:855
  921.3 1.7 slice_bitcast_fusion.3
  923.0 1.0 slice_bitcast_fusion.5
  924.0 1.6 slice_reduce_fusion.1
  925.7 12.2 %bitcast_divide_fusion = f32[256,13500]{0,1:T(8,128)} fusion(bf16[256,13500]{0,1:T(8,128)(2,1)} %param.15, f32[13568,256]{1,0:T(8,128)} %get-tuple-element.58, f32[256]{0:T(256)S(1)} %copy-done.30), kind=kLoop, calls=%fused_computation.4 | loop fusion | flops 17280000 | bytes 34562048 | tf_op jit(solution)/shard_map/div | solution.py:1143
  938.0 1.3 slice_bitcast_fusion.2
  940.2 0.9 reshape_reshape.11
  941.1 1.0 copy.251
  942.1 1.0 copy.253
  944.0 1.2 reshape.396
  945.9 1.3 reshape.395
  (173 shorter events, 22.7 us)
Async XLA Ops:
  0.6 9.5 %copy-start.18 = (bf16[128,1024]{1,0:T(8,128)(2,1)S(1)}, bf16[128,1024]{1,0:T(8,128)(2,1)}, u32[]{:S(2)}) copy-start(bf16[128,1024]{1,0:T(8,128)(2,1)} %param.26) | copy-start | bytes 786436
  0.7 10.6 %copy-start.19 = (bf16[32,4096]{1,0:T(8,128)(2,1)S(1)}, bf16[32,4096]{1,0:T(8,128)(2,1)}, u32[]{:S(2)}) copy-start(bf16[32,4096]{1,0:T(8,128)(2,1)} %param.25) | copy-start | bytes 786436
  0.7 11.7 %copy-start.26 = (bf16[32,1024]{1,0:T(8,128)(2,1)S(1)}, bf16[32,1024]{1,0:T(8,128)(2,1)}, u32[]{:S(2)}) copy-start(bf16[32,1024]{1,0:T(8,128)(2,1)} %param.22) | copy-start | bytes 196612
  1.8 11.8 %copy-start.37 = (bf16[32]{0:T(256)(128)(2,1)S(1)}, bf16[32]{0:T(256)(128)(2,1)}, u32[]{:S(2)}) copy-start(bf16[32]{0:T(256)(128)(2,1)} %param.28) | copy-start | bytes 196
  1.8 11.8 %copy-start.38 = (bf16[32]{0:T(256)(128)(2,1)S(1)}, bf16[32]{0:T(256)(128)(2,1)}, u32[]{:S(2)}) copy-start(bf16[32]{0:T(256)(128)(2,1)} %param.27) | copy-start | bytes 196
  1.9 11.8 %copy-start.39 = (bf16[32]{0:T(256)(128)(2,1)S(1)}, bf16[32]{0:T(256)(128)(2,1)}, u32[]{:S(2)}) copy-start(bf16[32]{0:T(256)(128)(2,1)} %param.24) | copy-start | bytes 196
  1.9 11.8 %copy-start.40 = (bf16[32]{0:T(256)(128)(2,1)S(1)}, bf16[32]{0:T(256)(128)(2,1)}, u32[]{:S(2)}) copy-start(bf16[32]{0:T(256)(128)(2,1)} %param.23) | copy-start | bytes 196
  1.9 11.9 %copy-start.23 = (bf16[32,3072]{1,0:T(8,128)(2,1)S(1)}, bf16[32,3072]{1,0:T(8,128)(2,1)}, u32[]{:S(2)}) copy-start(bf16[32,3072]{1,0:T(8,128)(2,1)} %param.21) | copy-start | bytes 589828
  305.0 79.4 %collective-permute-start.11 = (bf16[256,512]{0,1:T(8,128)(2,1)}, bf16[256,512]{0,1:T(8,128)(2,1)}, u32[]{:S(2)}, u32[]{:S(2)}) collective-permute-start(bf16[256,512]{0,1:T(8,128)(2,1)} %pad_maximum_fusion.7), channel_id=1, source_target_pairs={{0,1},{1,0},{2,3},{3,2},{4,5},{5,4},{6,7},{7,6},{8,9},{9,8},{10,11... | collective-permute-start | bytes 786440 | tf_op jit(solution)/shard_map/ppermute | solution.py:55
  305.4 83.7 %collective-permute-start.5 = (bf16[128,6912]{1,0:T(8,128)(2,1)}, bf16[128,6912]{1,0:T(8,128)(2,1)}, u32[]{:S(2)}, u32[]{:S(2)}) collective-permute-start(bf16[128,6912]{1,0:T(8,128)(2,1)} %get-tuple-element.46.refs_8_), channel_id=1, source_target_pairs={{0,2},{2,0},{1,3},{3,1},{4,6},{6,4},{5,7},{7,5},{8,10},{10,8},{9,1... | collective-permute-start | bytes 5308424 | tf_op jit(solution)/shard_map/ppermute | solution.py:55
  305.4 86.8 %collective-permute-start.3 = (bf16[128,6656]{1,0:T(8,128)(2,1)}, bf16[128,6656]{1,0:T(8,128)(2,1)}, u32[]{:S(2)}, u32[]{:S(2)}) collective-permute-start(bf16[128,6656]{1,0:T(8,128)(2,1)} %get-tuple-element.45.refs_4_), channel_id=1, source_target_pairs={{0,4},{4,0},{1,5},{5,1},{2,6},{6,2},{3,7},{7,3},{8,12},{12,8},{9,1... | collective-permute-start | bytes 5111816 | tf_op jit(solution)/shard_map/ppermute | solution.py:55
  315.2 152.6 %collective-permute-start.1 = (bf16[13568,256]{1,0:T(8,128)(2,1)}, bf16[13568,256]{1,0:T(8,128)(2,1)}, u32[]{:S(2)}, u32[]{:S(2)}) collective-permute-start(bf16[13568,256]{1,0:T(8,128)(2,1)} %pad.28.refs_2_), channel_id=1, source_target_pairs={{0,1},{1,0},{2,3},{3,2},{4,5},{5,4},{6,7},{7,6},{8,9},{9,8},{10,11... | collective-permute-start | bytes 20840456 | tf_op jit(solution)/shard_map/ppermute | solution.py:55
  316.2 0.8 copy-start.4
  316.3 11.4 %copy-start.34 = (s32[256]{0:T(256)}, s32[256]{0:T(256)S(1)}, u32[]{:S(2)}) copy-start(s32[256]{0:T(256)S(1)} %slice_reduce_fusion) | copy-start | bytes 3076
  321.0 4.0 copy-start.5
  336.8 6.7 copy-start.27
  336.8 7.5 copy-start.3
  336.8 8.8 copy-start
  348.0 21.0 %copy-start.28 = (f32[256]{0:T(256)}, f32[256]{0:T(256)S(1)}, u32[]{:S(2)}) copy-start(f32[256]{0:T(256)S(1)} %broadcast_multiply_fusion) | copy-start | bytes 3076
  348.2 0.6 copy-start.35
  348.2 20.9 %copy-start.31 = (f32[256]{0:T(256)}, f32[256]{0:T(256)S(1)}, u32[]{:S(2)}) copy-start(f32[256]{0:T(256)S(1)} %fusion.18) | copy-start | bytes 3076
  350.6 18.5 %copy-start.24 = (f32[1,1024]{1,0:T(1,128)}, f32[1,1024]{1,0:T(1,128)S(1)}, u32[]{:S(2)}) copy-start(f32[1,1024]{1,0:T(1,128)S(1)} %get-tuple-element.158) | copy-start | bytes 12292
  350.9 0.8 copy-start.6
  374.3 16.8 %collective-permute-start.9 = (bf16[256,2048]{0,1:T(8,128)(2,1)S(1)}, bf16[256,2048]{0,1:T(8,128)(2,1)S(1)}, u32[]{:S(2)}, u32[]{:S(2)}) collective-permute-start(bf16[256,2048]{0,1:T(8,128)(2,1)S(1)} %pad_maximum_fusion.3), channel_id=1, source_target_pairs={{0,1},{1,0},{2,3},{3,2},{4,5},{5,4},{6,7},{7,6},{8,9},{9,8},{10,11... | collective-permute-start | bytes 3145736 | tf_op jit(solution)/shard_map/ppermute | solution.py:55
  374.8 9.6 %copy-start.7 = (bf16[256,1024]{0,1:T(8,128)(2,1)S(1)}, bf16[256,1024]{0,1:T(8,128)(2,1)}, u32[]{:S(2)}) copy-start(bf16[256,1024]{0,1:T(8,128)(2,1)} %copy-done.6) | copy-start | bytes 1572868
  374.8 11.3 %copy-start.2 = (bf16[256,4,2,2,2,32]{0,5,1,3,2,4:T(8,128)(2,1)S(1)}, bf16[256,4,2,2,2,32]{0,5,1,3,2,4:T(8,128)(2,1)}, u32[]{:S(2)}) copy-start(bf16[256,4,2,2,2,32]{0,5,1,3,2,4:T(8,128)(2,1)} %copy.219) | copy-start | bytes 1572868
  381.7 7.4 copy-start.8
  381.7 16.5 %copy-start.17 = (bf16[256,128]{0,1:T(8,128)(2,1)S(1)}, bf16[256,128]{0,1:T(8,128)(2,1)}, u32[]{:S(2)}) copy-start(bf16[256,128]{0,1:T(8,128)(2,1)} %get-tuple-element.154) | copy-start | bytes 196612
  384.3 7.8 copy-start.16
  384.4 19.6 %copy-start.11 = (bf16[256,512]{0,1:T(8,128)(2,1)S(1)}, bf16[256,512]{0,1:T(8,128)(2,1)}, u32[]{:S(2)}) copy-start(bf16[256,512]{0,1:T(8,128)(2,1)} %get-tuple-element.143) | copy-start | bytes 786436
  384.4 1.6 collective-permute-start
  386.0 6.1 copy-start.20
  386.0 1.5 collective-permute-start.8
  387.5 6.7 copy-start.21
  387.5 1.5 collective-permute-start.10
  389.1 5.1 copy-start.22
  389.1 43.5 %collective-permute-start.6 = (bf16[128,6912]{1,0:T(8,128)(2,1)S(1)}, bf16[128,6912]{1,0:T(8,128)(2,1)}, u32[]{:S(2)}, u32[]{:S(2)}) collective-permute-start(bf16[128,6912]{1,0:T(8,128)(2,1)S(1)} %copy-done.8), channel_id=1, source_target_pairs={{0,4},{4,0},{1,5},{5,1},{2,6},{6,2},{3,7},{7,3},{8,12},{12,8},{9,1... | collective-permute-start | bytes 5308424 | tf_op jit(solution)/shard_map/ppermute | solution.py:55
  389.1 78.7 %collective-permute-start.7 = (bf16[128,6912]{1,0:T(8,128)(2,1)}, bf16[128,6912]{1,0:T(8,128)(2,1)}, u32[]{:S(2)}, u32[]{:S(2)}) collective-permute-start(bf16[128,6912]{1,0:T(8,128)(2,1)} %collective-permute-done.5.refs_9_), channel_id=1, source_target_pairs={{0,4},{4,0},{1,5},{5,1},{2,6},{6,2},{3,7},{7,3},{8,12},{12,8},{9,1... | collective-permute-start | bytes 5308424 | tf_op jit(solution)/shard_map/ppermute | solution.py:55
  391.1 1.0 copy-start.14
  392.1 40.4 %collective-permute-start.2 = (bf16[128,6656]{1,0:T(8,128)(2,1)}, bf16[128,6656]{1,0:T(8,128)(2,1)}, u32[]{:S(2)}, u32[]{:S(2)}) collective-permute-start(bf16[128,6656]{1,0:T(8,128)(2,1)} %get-tuple-element.45.refs_4_), channel_id=1, source_target_pairs={{0,2},{2,0},{1,3},{3,1},{4,6},{6,4},{5,7},{7,5},{8,10},{10,8},{9,1... | collective-permute-start | bytes 5111816 | tf_op jit(solution)/shard_map/ppermute | solution.py:55
  392.1 75.5 %collective-permute-start.4 = (bf16[128,6656]{1,0:T(8,128)(2,1)}, bf16[128,6656]{1,0:T(8,128)(2,1)}, u32[]{:S(2)}, u32[]{:S(2)}) collective-permute-start(bf16[128,6656]{1,0:T(8,128)(2,1)} %collective-permute-done.3.refs_6_), channel_id=1, source_target_pairs={{0,2},{2,0},{1,3},{3,1},{4,6},{6,4},{5,7},{7,5},{8,10},{10,8},{9,1... | collective-permute-start | bytes 5111816 | tf_op jit(solution)/shard_map/ppermute | solution.py:55
  396.2 7.8 copy-start.12
  396.2 7.8 copy-start.13
  396.2 7.8 copy-start.15
  432.5 331.1 %collective-permute-start.15 = (bf16[13568,256]{1,0:T(8,128)(2,1)}, bf16[13568,256]{1,0:T(8,128)(2,1)}, u32[]{:S(2)}, u32[]{:S(2)}) collective-permute-start(bf16[13568,256]{1,0:T(8,128)(2,1)} %get-tuple-element.56.refs_6_), channel_id=1, source_target_pairs={{0,1},{1,0},{2,3},{3,2},{4,5},{5,4},{6,7},{7,6},{8,9},{9,8},{10,11... | collective-permute-start | bytes 20840456 | tf_op jit(solution)/shard_map/ppermute | solution.py:55
  616.7 6.8 copy-start.25
  616.7 6.8 copy-start.29
  623.1 0.7 copy-start.36
  623.1 0.7 copy-start.32
  623.5 3.8 copy-start.9
  626.7 14.5 %collective-permute-start.14 = (bf16[1024,256]{1,0:T(8,128)(2,1)}, bf16[1024,256]{1,0:T(8,128)(2,1)}, u32[]{:S(2)}, u32[]{:S(2)}) collective-permute-start(bf16[1024,256]{1,0:T(8,128)(2,1)} %get-tuple-element.116.refs_15_), channel_id=1, source_target_pairs={{0,1},{1,0},{2,3},{3,2},{4,5},{5,4},{6,7},{7,6},{8,9},{9,8},{10,11... | collective-permute-start | bytes 1572872 | tf_op jit(solution)/shard_map/ppermute | solution.py:55
  626.7 14.6 %collective-permute-start.12 = (bf16[4096,256]{1,0:T(8,128)(2,1)}, bf16[4096,256]{1,0:T(8,128)(2,1)}, u32[]{:S(2)}, u32[]{:S(2)}) collective-permute-start(bf16[4096,256]{1,0:T(8,128)(2,1)} %bitcast.57.refs_11_), channel_id=1, source_target_pairs={{0,1},{1,0},{2,3},{3,2},{4,5},{5,4},{6,7},{7,6},{8,9},{9,8},{10,11... | collective-permute-start | bytes 6291464 | tf_op jit(solution)/shard_map/ppermute | solution.py:55
  627.2 14.0 %collective-permute-start.13 = (bf16[1024,256]{1,0:T(8,128)(2,1)}, bf16[1024,256]{1,0:T(8,128)(2,1)}, u32[]{:S(2)}, u32[]{:S(2)}) collective-permute-start(bf16[1024,256]{1,0:T(8,128)(2,1)} %get-tuple-element.51.refs_13_), channel_id=1, source_target_pairs={{0,1},{1,0},{2,3},{3,2},{4,5},{5,4},{6,7},{7,6},{8,9},{9,8},{10,11... | collective-permute-start | bytes 1572872 | tf_op jit(solution)/shard_map/ppermute | solution.py:55
  634.2 2.6 copy-start.1
  635.5 5.2 copy-start.33
  921.3 4.3 copy-start.10
  921.3 4.4 copy-start.30

commit v12 on v10

--- a/solution.py
+++ b/solution.py
@@ -35,20 +35,10 @@
     )
 
 
-def contract_rows(left, right):
-    return lax.dot_general(
-        left, right, (((0,), (0,)), ((), ())), preferred_element_type=jnp.float32
-    )
-
-
 def contract_cols(left, right):
     return lax.dot_general(
         left, right, (((1,), (1,)), ((), ())), preferred_element_type=jnp.float32
     )
-
-
-def matmul(left, right):
-    return jnp.dot(left, right, preferred_element_type=jnp.float32)
 
 
 def swap(value, axis):
@@ -73,15 +63,6 @@
     order = list(range(axis)) + [axis + 3, axis + 1, axis + 2, axis, axis + 4]
     order += list(range(axis + 5, split.ndim))
     return split.transpose(order).reshape(at)
-
-
-def relative(value, axis):
-    eighth = value.shape[axis] // 8
-    mine = lax.axis_index("c") * 4 + lax.axis_index("x") * 2 + lax.axis_index("y")
-    parts = [
-        lax.dynamic_slice_in_dim(value, (mine ^ part) * eighth, eighth, axis) for part in range(8)
-    ]
-    return jnp.concatenate(parts, axis=axis)
 
 
 def greet(peers):
@@ -197,15 +178,32 @@
         landed(j)
 
 
-def front_kernel(n_h, jobs, n_arrays, n_full, *refs):
-    shards, (counts, tail, scale, pe) = refs[:n_arrays], refs[n_arrays : n_arrays + 4]
-    rest = refs[n_arrays + 4 :]
-    wholes, (xb, h0, a1, query, pairs) = rest[:n_arrays], rest[n_arrays : n_arrays + 5]
-    (count_buf, enc_buf, xb_buf, total, qkv_buf, mine, count_sem, enc_sem, xb_sem, qkv_sem, kv_sem,
-     kv_send, kv_recv, *sems) = rest[n_arrays + 5 :]
+def gene_tail(counts):
+    tail = counts[counts.shape[0] // CHUNK * CHUNK :]
+    return jnp.pad(tail, ((0, CHUNK - tail.shape[0]), (0, 0)))
+
+
+def eighth_of(part):
+    c, x, y = (lax.axis_index(name) for name in ("c", "x", "y"))
+    return lax.rem(c + part // 4, 2) * 4 + lax.rem(x + part // 2 % 2, 2) * 2 + lax.rem(y + part % 2, 2)
+
+
+def front_kernel(n_h, jobs, n_arrays, n_full, owners, scale_s, *refs):
+    shards = refs[:n_arrays]
+    counts, cot, tail, cot_tail, scale, pe, seg_keys, seg_mine = refs[n_arrays : n_arrays + 8]
+    rest = refs[n_arrays + 8 :]
+    wholes = rest[:n_arrays]
+    (xb, xb_other, cot_own, cot_other, pairs, lefts, left_one, left_last, h0, query, log_total, h1, slope,
+     act, hb) = rest[n_arrays : n_arrays + 15]
+    (a1, a2, plain, attended, turned, gains, perm, count_buf, enc_buf, xb_buf, total, qkv_buf, mine, pairs_buf, out_buf,
+     up_buf, down_buf, own_left, send_left, count_sem, enc_sem, xb_sem, fetch_sem, kv_sem, kv_send, kv_recv, cot_sem,
+     cot_send, cot_recv, left_sem, left_send, left_recv, *sems) = rest[n_arrays + 15 :]
     y, c = lax.axis_index("y"), lax.axis_index("c")
+    to_core = {"c": 1 - c}
     f32, b16 = jnp.float32, jnp.bfloat16
-    width = h0.shape[1]
+    cells, width = h0.shape
+    slots, head = 4 * cells, 64
+    n_pairs = width // 128
     n_chunks = xb.shape[0] // CHUNK
     by_chunk = lambda k: pl.ds(pl.multiple_of(k * CHUNK, CHUNK), CHUNK)
 
@@ -273,16 +271,18 @@
         for k in range(max(low, high - 2), high):
             store(jnp.int32(k)).wait()
 
-    def fetch_qkv():
-        return pltpu.make_async_copy(wholes[1], qkv_buf, qkv_sem.at[0])
+    def fetch(k):
+        buffer = (qkv_buf, out_buf, up_buf, down_buf)[k]
+        return pltpu.make_async_copy(wholes[1 + k], buffer, fetch_sem.at[k])
 
     def project():
-        fetch_qkv().wait()
+        fetch(0).wait()
         vectors = qkv_buf[:, :, :, :, 3 * width :].reshape(width, 128).astype(f32)
         value = total[...]
         centred = value - jnp.mean(value, axis=0, keepdims=True)
         variance = jnp.mean(centred * centred, axis=0, keepdims=True)
         normed = centred * lax.rsqrt(variance + eps) * vectors[:, 0:1] + vectors[:, 1:2]
+        gains[...] = vectors.T[0:8]
         h0[...] = value.T
         a1[...] = normed.T.astype(b16)
 
@@ -317,32 +317,189 @@
             device_id_type=MESH,
         )
 
+    def swap_cot(k):
+        source = (cot.at[pl.ds(0, (n_chunks - 1) * CHUNK)], cot_tail)[k]
+        place = pl.ds((n_chunks - 1) * CHUNK * k, ((n_chunks - 1) * CHUNK, CHUNK)[k])
+        return (
+            pltpu.make_async_copy(source, cot_own.at[place], cot_sem.at[k]),
+            pltpu.make_async_remote_copy(
+                src_ref=source, dst_ref=cot_other.at[place], send_sem=cot_send.at[k], recv_sem=cot_recv.at[k],
+                device_id=to_core, device_id_type=MESH,
+            ),
+        )
+
+    def swap_xb():
+        return pltpu.make_async_remote_copy(
+            src_ref=xb, dst_ref=xb_other, send_sem=cot_send.at[2], recv_sem=cot_recv.at[2],
+            device_id=to_core, device_id_type=MESH,
+        )
+
+    def make_perm():
+        place = lax.broadcasted_iota(jnp.int32, (8, width), 1)
+        size = width // 8 // owners
+        within, at = lax.rem(place, size), lax.div(place, size)
+        at_h, at = lax.rem(at, owners), lax.div(at, owners)
+        wanted = at_h * 8 + lax.rem(lax.div(at, 2), 2) * 4 + lax.rem(at, 2) * 2 + lax.div(at, 4)
+        wanted = (wanted * size + within)[0:1]
+        for k in range(width // CHUNK):
+            row = lax.broadcasted_iota(jnp.int32, (CHUNK, width), 0) + k * CHUNK
+            perm[k * CHUNK : (k + 1) * CHUNK] = jnp.where(row == wanted, 1.0, 0.0).astype(b16)
+
+    def fetch_pairs():
+        return pltpu.make_async_copy(pairs, pairs_buf, kv_sem.at[1])
+
+    def attend(j, carry):
+        lanes = by_lanes(j)
+        keys = pairs_buf[:, :, :, lanes].reshape(slots, 128)
+        values = pairs_buf[:, :, :, by_lanes(n_pairs + j)].reshape(slots, 128).astype(f32).T.astype(b16)
+        for half in (0, 1):
+            side = slice(half * head, (half + 1) * head)
+            scores = lax.dot_general(
+                keys[:, side], query[:, lanes][:, side], (((1,), (1,)), ((), ())), preferred_element_type=f32
+            )
+            scores = jnp.where(seg_keys[...] == seg_mine[...], scores * scale_s, -1000000000.0)
+            top = jnp.max(scores, axis=0, keepdims=True)
+            expo = jnp.exp(scores - top)
+            whole = jnp.sum(expo, axis=0, keepdims=True)
+            log_total[pl.ds(2 * j + half, 1), :] = top + jnp.log(whole)
+            probs = (expo * (1.0 / whole)).astype(b16)
+            turned[side] = jnp.dot(values[side], probs, preferred_element_type=f32)
+        plain[:, lanes] = turned[...].T.astype(b16)
+        return carry
+
+    def by_lanes(j):
+        return pl.ds(pl.multiple_of(j * 128, 128), 128)
+
+    def leave_attention():
+        attended[...] = jnp.dot(plain[...], perm[...], preferred_element_type=f32).astype(b16)
+        fetch(1).wait()
+        for k in range(width // CHUNK):
+            columns = slice(k * CHUNK, (k + 1) * CHUNK)
+            weight = out_buf[:, :, :, :, columns].reshape(width, CHUNK)
+            h1[:, columns] = h0[:, columns] + jnp.dot(attended[...], weight, preferred_element_type=f32)
+        value = h1[...]
+        centred = value - jnp.mean(value, axis=1, keepdims=True)
+        variance = jnp.mean(centred * centred, axis=1, keepdims=True)
+        a2[...] = (centred * lax.rsqrt(variance + eps) * gains[2:3] + gains[3:4]).astype(b16)
+
+    def widen(k, carry):
+        weight = up_buf[:, :, :, :, by_chunk(k)].reshape(width, CHUNK)
+        value = jnp.dot(a2[...], weight, preferred_element_type=f32)
+        share = 0.5 * (1.0 + lax.erf(value * (0.5**0.5)))
+        act[:, by_chunk(k)] = (value * share).astype(b16)
+        slope[:, by_chunk(k)] = share + value * jnp.exp(-0.5 * value * value) * (2.0 * math.pi) ** -0.5
+        return carry
+
+    def narrow(k, carry):
+        weight = down_buf[:, :, :, :, by_chunk(k)].reshape(4 * width, CHUNK)
+        value = h1[:, by_chunk(k)] + jnp.dot(act[...], weight, preferred_element_type=f32)
+        hb[:, by_chunk(k)] = value.astype(b16)
+        return carry
+
+    def left_copies(k):
+        target = (lefts.at[pl.ds(0, 6)], left_one, left_last)[k]
+        source = pl.ds((0, 6, 7)[k], (6, 1, 1)[k])
+        return (
+            pltpu.make_async_copy(own_left.at[source], target.at[:, :, pl.ds(0, cells)], left_sem.at[k]),
+            pltpu.make_async_remote_copy(
+                src_ref=send_left.at[source], dst_ref=target.at[:, :, pl.ds(cells, cells)],
+                send_sem=left_send.at[k], recv_sem=left_recv.at[k], device_id=to_core, device_id_type=MESH,
+            ),
+        )
+
+    def make_left(source, k):
+        size = source.shape[1] // 8
+        pieces = size // (width // 8)
+        step = size // owners // pieces
+        for part in range(8):
+            lanes = pl.ds(pl.multiple_of(eighth_of(part) * size, size), size)
+            block = source[:, lanes].astype(f32).T.astype(b16)
+            target = own_left if part < 4 else send_left
+            base = part % 4 * (width // 8)
+            if pieces == 1:
+                target[k, base : base + size] = block
+                continue
+            for piece in range(pieces):
+                for at in range(owners):
+                    rows = block[(at * pieces + piece) * step : (at * pieces + piece + 1) * step]
+                    target[k + piece, base + at * step : base + (at + 1) * step] = rows
+
     arrays = [array for array, *_ in jobs]
+    last_of = [max(j for j, array in enumerate(arrays) if array == k) for k in range(5)]
     enc_jobs = [j for j, array in enumerate(arrays) if array == 0]
-    qkv_jobs = [j for j, array in enumerate(arrays) if array == 1]
-    at = max(qkv_jobs) + 3
+    at = last_of[1] + 3
 
     def between(step, landed):
+        if step == 0:
+            for k in (0, 1):
+                for copy in swap_cot(k):
+                    copy.start()
+        if step == 1:
+            make_perm()
         if step - 3 in enc_jobs:
             landed(step - 3)
             encode_job(*jobs[step - 3][1:3])
+        if step == enc_jobs[-1] + 3:
+            swap_xb().start()
         if step == at:
-            for j in qkv_jobs:
+            for j in range(last_of[1] + 1):
                 landed(j)
-            fetch_qkv().start()
+            fetch(0).start()
             project()
         if step == at + 2:
             kv_own().wait()
             kv_copy(0).wait_recv()
             kv_copy(1).start()
+            make_left(a1, 6)
+            for copy in left_copies(1):
+                copy.start()
+        if step == at + 3:
+            for j in range(last_of[3] + 1):
+                landed(j)
+            fetch(1).start()
+            fetch(2).start()
+            kv_copy(1).wait_recv()
+            fetch_pairs().start()
+            fetch_pairs().wait()
+            lax.fori_loop(0, n_pairs // 2, attend, 0)
+        if step == at + 4:
+            lax.fori_loop(n_pairs // 2, n_pairs, attend, 0)
+        if step == at + 5:
+            for j in range(last_of[4] + 1):
+                landed(j)
+            fetch(3).start()
+            leave_attention()
+            fetch(2).wait()
+            lax.fori_loop(0, 2 * width // CHUNK, widen, 0)
+        if step == at + 6:
+            lax.fori_loop(2 * width // CHUNK, 4 * width // CHUNK, widen, 0)
+        if step == at + 7:
+            fetch(3).wait()
+            lax.fori_loop(0, width // CHUNK, narrow, 0)
+            make_left(hb, 7)
+            for copy in left_copies(2):
+                copy.start()
+        if step == at + 8:
+            make_left(a2, 0)
+            make_left(act, 1)
+            make_left(attended, 5)
+            for copy in left_copies(0):
+                copy.start()
 
     gather_kernel(n_h, jobs, n_full, shards, wholes, sems, between)
     kv_copy(0).wait_send()
-    kv_copy(1).wait()
-
-
-def gather_all(shards, n_full, cuts, order, counts, scale, pe, collective_id):
-    n_h = lax.axis_size("h")
+    kv_copy(1).wait_send()
+    for k in (0, 1):
+        for copy in swap_cot(k):
+            copy.wait()
+    swap_xb().wait()
+    for k in range(3):
+        for copy in left_copies(k):
+            copy.wait()
+
+
+def gather_all(shards, cuts, order, counts, cot, scale, pe, seg, scale_s, collective_id):
+    owners = n_h = lax.axis_size("h")
     if any(shard.shape[0] % 16 for shard in shards):
         shards = [lax.all_gather(s, "h", axis=0, tiled=True) for s in shards]
         n_h = 1
@@ -353,39 +510,60 @@
     n, others, dma = len(jobs), max(n_h - 1, 1), pltpu.SemaphoreType.DMA
     shapes = [(n_h * s.shape[0], s.shape[1]) for s in shards]
     (genes, cells), width, padded = counts.shape, pe.shape[0], shards[0].shape[1]
-    tail = counts[genes // CHUNK * CHUNK :]
-    tail = jnp.pad(tail, ((0, CHUNK - tail.shape[0]), (0, 0)))
+    slots, half = seg.shape[0], width // 2
     bf16, f32 = jnp.bfloat16, jnp.float32
     vmem, hbm = pl.BlockSpec(memory_space=pltpu.VMEM), pl.BlockSpec(memory_space=pl.ANY)
+    shape = jax.ShapeDtypeStruct
+    hbm_out = [shape((padded, cells), bf16)] * 4 + [shape((2, 2, cells, 2 * width), bf16)]
+    hbm_out += [shape((k, half, 2 * cells), bf16) for k in (6, 1, 1)]
+    vmem_out = [
+        shape((cells, width), f32),
+        shape((cells, width), bf16),
+        shape((width // 64, cells), f32),
+        shape((cells, width), f32),
+        shape((cells, 4 * width), f32),
+        shape((cells, 4 * width), bf16),
+        shape((cells, width), bf16),
+    ]
+    eighth = width // 8
     out = pl.pallas_call(
-        functools.partial(front_kernel, n_h, jobs, len(shards), n_full),
-        out_shape=[
-            jax.ShapeDtypeStruct((2, 2, 2) + shape if k < n_full else shape, bf16)
-            for k, shape in enumerate(shapes)
-        ]
-        + [
-            jax.ShapeDtypeStruct((padded, cells), bf16),
-            jax.ShapeDtypeStruct((cells, width), f32),
-            jax.ShapeDtypeStruct((cells, width), bf16),
-            jax.ShapeDtypeStruct((cells, width), bf16),
-            jax.ShapeDtypeStruct((2, 2, cells, 2 * width), bf16),
-        ],
-        in_specs=[hbm] * (len(shards) + 2) + [vmem] * 2,
-        out_specs=[hbm] * (len(shards) + 1) + [vmem] * 3 + [hbm],
+        functools.partial(front_kernel, n_h, jobs, len(shards), len(shards), owners, scale_s),
+        out_shape=[shape((2, 2, 2) + k, bf16) for k in shapes] + hbm_out + vmem_out,
+        in_specs=[hbm] * (len(shards) + 4) + [vmem] * 4,
+        out_specs=[hbm] * (len(shards) + len(hbm_out)) + [vmem] * len(vmem_out),
         scratch_shapes=[
+            pltpu.VMEM((cells, width), bf16),
+            pltpu.VMEM((cells, width), bf16),
+            pltpu.VMEM((cells, width), bf16),
+            pltpu.VMEM((cells, width), bf16),
+            pltpu.VMEM((128, cells), f32),
+            pltpu.VMEM((8, width), f32),
+            pltpu.VMEM((width, width), bf16),
             pltpu.VMEM((2, CHUNK, cells), bf16),
-            pltpu.VMEM((2, 2, 2, 2, width // 8, CHUNK), bf16),
+            pltpu.VMEM((2, 2, 2, 2, eighth, CHUNK), bf16),
             pltpu.VMEM((2, CHUNK, cells), bf16),
             pltpu.VMEM((width, cells), f32),
-            pltpu.VMEM((2, 2, 2, width // 8, shards[1].shape[1]), bf16),
+            pltpu.VMEM((2, 2, 2, eighth, shards[1].shape[1]), bf16),
             pltpu.VMEM((cells, 2 * width), bf16),
+            pltpu.VMEM((2, 2, cells, 2 * width), bf16),
+            pltpu.VMEM((2, 2, 2, eighth, width), bf16),
+            pltpu.VMEM((2, 2, 2, eighth, 4 * width), bf16),
+            pltpu.VMEM((2, 2, 2, 4 * eighth, width), bf16),
+            pltpu.VMEM((8, half, cells), bf16),
+            pltpu.VMEM((8, half, cells), bf16),
             dma((2,)),
             dma((2,)),
             dma((2,)),
-            dma((1,)),
-            dma((1,)),
+            dma((4,)),
             dma((2,)),
             dma((2,)),
+            dma((2,)),
+            dma((2,)),
+            dma((3,)),
+            dma((3,)),
+            dma((3,)),
+            dma((3,)),
+            dma((3,)),
             dma((n,)),
             dma((n, others)),
             dma((n, others)),
@@ -393,9 +571,11 @@
             dma((n, 8)),
         ],
         compiler_params=pltpu.CompilerParams(
-            collective_id=collective_id, has_side_effects=True, vmem_limit_bytes=60 * 2**20
+            collective_id=collective_id, has_side_effects=True, vmem_limit_bytes=63 * 2**20
         ),
-    )(*shards, counts, tail, scale, pe)
+    )(
+        *shards, counts, cot, gene_tail(counts), gene_tail(cot), scale, pe, seg[:, None], seg[None, :cells]
+    )
     return out[: len(shards)], *out[len(shards) :]
 
 
@@ -621,7 +801,7 @@
     rights, weight = refs[11 : 11 + n_rights], refs[11 + n_rights]
     (out, turned_own, turned_other, lefts_next, dh0b, d_qkv, d_pairs, by_core, by_y, d_query, weight_buf, turned,
      da1, vector_rows, send_left, got_left, send, recv, local, *scratch) = refs[12 + n_rights :]
-    x, y, c = (lax.axis_index(name) for name in ("x", "y", "c"))
+    y, c = lax.axis_index("y"), lax.axis_index("c")
     f32, b16 = jnp.float32, jnp.bfloat16
     cells, width = query.shape
     slots = 4 * cells
@@ -743,10 +923,7 @@
     def halves():
         for kind, source in enumerate((vector_rows, dh0b)):
             for part in range(8):
-                eighth = (
-                    lax.rem(c + part // 4, 2) * 4 + lax.rem(x + part // 2 % 2, 2) * 2 + lax.rem(y + part % 2, 2)
-                )
-                lanes = pl.ds(pl.multiple_of(eighth * (width // 8), width // 8), width // 8)
+                lanes = pl.ds(pl.multiple_of(eighth_of(part) * (width // 8), width // 8), width // 8)
                 block = source[:, lanes].astype(f32).T.astype(b16)
                 rows = slice(part % 4 * (width // 8), (part % 4 + 1) * (width // 8))
                 if part < 4:
@@ -893,18 +1070,6 @@
     )
 
 
-def own_half(left):
-    half = left.shape[1] // 2
-    return jnp.concatenate([left[:, :half], swap(left[:, half:], "c")], axis=0)
-
-
-def left_of(left, pieces):
-    left = own_half(relative(left, 1)).T
-    n_h = lax.axis_size("h")
-    left = left.reshape(4, n_h, pieces, -1, left.shape[1])
-    return left.transpose(2, 0, 1, 3, 4).reshape(pieces, -1, left.shape[-1])
-
-
 def both_cores(right, times=1):
     return right, swap(right, "c"), times
 
@@ -932,17 +1097,13 @@
 ):
     rows = counts.shape[0]
     width = w_qkv.shape[1] // 3
-    heads = HEADS
-    head_width = width // heads
-    att_scale = head_width ** (-0.5)
+    att_scale = (width // HEADS) ** (-0.5)
     group_size = 4
     slots = rows * group_size
     scale = 10000.0 / library
     genes = counts.shape[1]
     padded = -(-genes // CHUNK) * CHUNK
     counts_f = counts.astype(jnp.float32)
-    cot = jnp.pad(cotangent.T, ((0, padded - genes), (0, 0)))
-    cot_pair = both_cores(cot)
     pe = by_owner(positions(coords, width), 1)
     ends = jnp.cumsum(lengths[0])
     group = [
@@ -952,7 +1113,6 @@
     ]
     place = jnp.concatenate([at * rows + jnp.arange(rows, dtype=jnp.int32) for at in group])
     seg_all = jnp.sum((place[:, None] >= ends[None, :]).astype(jnp.int32), axis=1)
-    same = (seg_all[:rows, None] == seg_all[None, :])[None]
     vectors = jnp.stack([gain_one, shift_one, gain_two, shift_two], axis=1)
     vectors = jnp.pad(vectors, ((0, 0), (0, 124)))
     pad = ((0, 0), (0, padded - genes))
@@ -968,61 +1128,27 @@
     ]
     cuts = [gene_cuts, [0, width // 2 * 3, 3 * width + 128], [0, width]]
     cuts += [[0, 2 * width, 4 * width], [0, width // 2, width]]
-    cuts += [[0, padded]]
-    order = [(0, 0), (0, 1), (0, 2), (0, 3), (1, 0), (1, 1), (2, 0), (3, 0), (3, 1), (4, 0), (4, 1), (5, 0)]
-    gathered, xb, h0, a1, query, kv_all = gather_all(
-        shards, 5, cuts, order, counts.T, scale[None, :], pe.T, 0
-    )
-    xb_pair = both_cores(xb)
-    enc_all, qkv_all, out_all, up_all, down_all = (
-        w.reshape(-1, w.shape[-1]) for w in gathered[:5]
+    cuts += [gene_cuts]
+    order = [(0, 0), (0, 1), (0, 2), (0, 3), (1, 0), (1, 1), (2, 0), (3, 0), (3, 1), (4, 0), (4, 1)]
+    order += [(5, 0), (5, 1), (5, 2), (5, 3)]
+    (gathered, xb, xb_other, cot, cot_other, kv_pairs, lefts, left_one, left_last, h0, query, log_total, h1, slope, _,
+     hb) = gather_all(
+        shards, cuts, order, counts.T, cotangent.T, scale[None, :], pe.T, seg_all, att_scale, 0
+    )
+    enc_all, qkv_all, out_all, up_all, down_all, dec_all = (
+        w.reshape(-1, w.shape[-1]) for w in gathered
     )
     vectors = qkv_all[:, 3 * width :].astype(jnp.float32).T
     g1f, b1f, g2f, b2f = vectors[0], vectors[1], vectors[2], vectors[3]
-    kv_pairs, query_b = kv_all, query
-    query = query.reshape(rows, heads, head_width)
-    kv_all = kv_all.reshape(slots, -1)
-    dec_own = gathered[5]
-    middle = dec_own.shape[1] // 256 * 128
-    by_x, by_y = swap(dec_own, "x"), swap(dec_own, "y")
-    far = (swap(by_x[:, :middle], "y"), swap(by_y[:, middle:], "x"))
-    dec_parts = [dec_own, by_y, by_x, jnp.concatenate(far, axis=1)]
-    dec_parts += [swap(part, "c") for part in dec_parts]
-    keys = kv_all[:, :width].reshape(slots, heads, head_width)
-    values = kv_all[:, width:].reshape(slots, heads, head_width)
-
-    def scores_of():
-        raw = (
-            jnp.einsum("qhd,khd->hqk", query, keys, preferred_element_type=jnp.float32) * att_scale
-        )
-        return jnp.where(same, raw, -1000000000.0)
-
-    scores = scores_of()
-    top = jnp.max(scores, axis=-1, keepdims=True)
-    expo = jnp.exp(scores - top)
-    total = jnp.sum(expo, axis=-1, keepdims=True)
-    log_total = top + jnp.log(total)
-    probs_b = (expo / total).astype(jnp.bfloat16)
-    attended = jnp.einsum("hqk,khd->qhd", probs_b, values, preferred_element_type=jnp.float32)
-    attended_b = attended.reshape(rows, width).astype(jnp.bfloat16)
-    attended_b = by_owner(attended_b, 1)
-    h1 = h0 + matmul(attended_b, out_all)
-    a2 = layer_norm(h1, g2f, b2f).astype(jnp.bfloat16)
-    hidden = matmul(a2, up_all)
-    act, pull = jax.vjp(lambda v: jax.nn.gelu(v, approximate=False), hidden)
-    act, slope = lax.optimization_barrier(
-        (act.astype(jnp.bfloat16), pull(jnp.ones_like(hidden))[0])
-    )
-    h2 = h1 + matmul(act, down_all)
-    hb = h2.astype(jnp.bfloat16)
     grad_dec, logits, dh2 = scatter_product(
-        left_of(hb, 1), [0], [cot_pair], relative(hb, 1), dec_parts, jnp.bfloat16, True, 1
+        left_last, [0], [(cot, cot_other, 1)], hb, [dec_all], jnp.bfloat16, True, 1
     )
     own_rows = grad_dec.shape[1]
     grad_dec = columns_of(grad_dec)[:, :genes].T
     logits = logits[:genes].T
-    dh2 = relative(dh2, 0).T
-    dfb = dh2.astype(jnp.bfloat16)
+    dfb_turned = dh2.astype(jnp.bfloat16)
+    dh2 = dh2.T
+    dfb = dfb_turned.T
     d_act = contract_cols(dfb, down_all)
     d_hidden = (d_act * slope).astype(jnp.bfloat16)
     da2 = contract_cols(d_hidden, up_all)
@@ -1032,13 +1158,12 @@
     dab = dh1.astype(jnp.bfloat16)
     d_attended = contract_cols(dab, out_all).astype(jnp.bfloat16)
     d_attended = from_owner(d_attended, 1)
-    lefts = [left_of(a2, 1), left_of(act, act.shape[1] // width), left_of(attended_b, 1)]
     pieces = (4 * width,) + (width,) * 4
-    rights = [both_cores(d_hidden.T), both_cores(dfb.T, 4), both_cores(dab.T)]
-    operands = [query_b, kv_pairs, d_attended, log_total[:, :, 0], seg_all[:, None], seg_all[None, :rows], h0, dh1]
-    operands += [jnp.pad(jnp.stack([g1f, grad_gain_two, grad_shift_two]), ((0, 5), (0, 0))), left_of(a1, 1)[0]]
+    rights = [both_cores(d_hidden.T), both_cores(dfb_turned, 4), both_cores(dab.T)]
+    operands = [query, kv_pairs, d_attended, log_total, seg_all[:, None], seg_all[None, :rows], h0, dh1]
+    operands += [jnp.pad(jnp.stack([g1f, grad_gain_two, grad_shift_two]), ((0, 5), (0, 0))), left_one[0]]
     grads, d_qkv, d_qkv_other, lefts, dh0b = scatter_attention(
-        jnp.concatenate(lefts, axis=0),
+        lefts,
         [sum(pieces[:k]) // CHUNK for k in range(len(pieces) + 1)],
         rights,
         operands,
@@ -1058,7 +1183,7 @@
     grads, d_xb = scatter_product(
         lefts,
         [0, 3 * width // CHUNK, (3 * width + rows) // CHUNK],
-        [(d_qkv, d_qkv_other, 1), (unit, unit, 1), xb_pair],
+        [(d_qkv, d_qkv_other, 1), (unit, unit, 1), (xb, xb_other, 1)],
         dh0b,
         [enc_all],
         jnp.float32,

time: 946 us -> 1080 us (1.14)
  Pallas kernels: 699 us -> 966 us
  waiting for transfers between devices: 42.4 us -> 0.01 us
  matrix products: 53.3 us -> 16.4 us
  local copies, waits for them, and re-layouts: 95.3 us -> 61.9 us
  other arithmetic: 39.1 us -> 23.5 us
    pallas_call x1, Pallas kernels: 285 us -> 543 us  [gather_all(): pl.pallas_call(functools.partial(front_kernel, n_h, jobs, len(shards), le...]
    ppermute x18 -> x3, waiting for transfers between devices: 42.4 us -> 0.01 us  [swap(): return lax.ppermute(value, axis, [(0, 1), (1, 0)])]
    dot_general x5 -> x0, matrix products: 36.1 us -> none  [the longest x3 25 us: matmul(): return jnp.dot(left, right, preferred_element_type=jnp.float32)]
    unnamed x98 -> x39, local copies, waits for them, and re-layouts: 21.4 us -> 5.68 us
    slice x7 -> x3, local copies, waits for them, and re-layouts: 17.1 us -> 2.57 us  [the longest x2 1.82 us: gene_tail(): tail = counts[counts.shape[0] // CHUNK * CHUNK:]]
  transfers between devices with their start and end apart: 18 -> 3, of which waited for: 5 -> 0; matrix products, arithmetic and copies ran while one was open for 15% -> 4% of each run, Pallas kernels for 27% -> 0%
where the time goes in v12:
time: 1080 us; the launch traced here: 1070 us
  Pallas kernels  966 us (89%)
  local copies, waits for them, and re-layouts  61.9 us (6%)
  other arithmetic  23.5 us (2%)
  matrix products  16.4 us (2%)
    pallas_call x1, Pallas kernels, gather_all(): pl.pallas_call(functools.partial(front_kernel, n_h, jobs, len(shards), le...  543 us
    pallas_call x3, Pallas kernels, scatter_call(): pl.pallas_call(functools.partial(kernel, inner_h, sections, periods), out...  424 us
  transfers between devices with their start and end apart: 3, of which 0 were waited for; matrix products, arithmetic and copies ran while one was open for 4% of the time, Pallas kernels for 0%

profile of v12, /device:TPU:0, one launch (start us, length us, event | category | flops | bytes accessed | tf_op | source)
XLA Modules:
  0.0 1070.8 jit_solution(1920170919944093962)
XLA Ops:
  1.5 0.3 copy.138
  1.8 0.8 slice_reduce_fusion
  2.6 0.8 slice_convert_fusion.1
  3.3 0.9 slice.91
  4.3 0.9 slice.92
  5.2 0.7 pad.25.refs_8_
  5.9 0.7 pad.26.refs_9_
  6.5 1.3 broadcast_divide_fusion
  7.8 2.1 pad.22.refs_0_
  9.9 2.1 pad.24.refs_5_
  12.1 0.2 copy.136
  12.3 0.9 copy.139.refs_4_
  13.1 0.2 reshape.280
  13.4 0.9 reshape.281.refs_3_
  14.3 0.2 reshape.278
  14.6 0.9 reshape.279.refs_2_
  15.6 0.7 fusion.4.refs_1_
  16.3 1.9 multiply_sine_fusion.1
  18.2 1.1 pad_maximum_fusion
  19.3 542.6 %shard_map.238 = (bf16[2,2,2,128,13568]{4,3,2,1,0:T(8,128)(2,1)}, bf16[2,2,2,128,3200]{4,3,2,1,0:T(8,128)(2,1)}, bf16[2,2,2,128,1024]{4,3,2,1,0:T(8,128)(2,1)}, ...) custom-call(bf16[32,13568]{1,0:T(8,128)(2,1)} %pad.22.refs_0_, ...), custom_call_target="tpu_custom_call" | custom-call | tf_op jit(solution)/shard_map/pallas_call | solution.py:529
  561.9 144.4 %shard_map.239 = (f32[53,32,256]{2,1,0:T(8,128)}, bf16[13568,256]{1,0:T(8,128)(2,1)}, f32[1024,256]{1,0:T(8,128)}) custom-call(bf16[1,512,512]{2,1,0:T(8,128)(2,1)} %get-tuple-element.42.refs_0_, bf16[256,1024]{1,0:T(8,128)(2,1)} %get-tuple-element.43.refs_1_, bf16[13568,256]{1,0:T(8,128)(2,1)} %get-tuple-element.44.refs_2_, ...), custom_call_target="tpu_custom_call" | custom-call | tf_op jit(solution)/shard_map/pallas_call | solution.py:973
  706.3 2.1 convert_element_type.67.refs_13_
  708.4 5.8 copy.141
  714.2 8.4 fusion
  722.6 6.4 fusion.9
  729.1 0.3 copy.143
  729.4 1.0 slice.94
  730.4 0.1 copy.161
  730.6 0.3 copy.144
  731.0 0.1 reduce_sum.51
  731.1 0.2 multiply_reduce_fusion.2
  731.4 0.5 multiply_reduce_fusion
  731.9 0.4 copy-done.4
  732.3 1.2 convert_bitcast_fusion.1
  733.5 0.5 collective-permute-start.2
  734.0 7.0 slice_bitcast_fusion
  741.0 1.3 copy.149.refs_8_
  742.3 1.6 convolution_convert_fusion
  743.9 1.4 copy.145
  745.3 1.0 copy.148.refs_3_
  746.3 1.3 copy.164
  747.7 0.6 select_maximum_fusion.refs_9_
  748.3 0.7 fusion.3.refs_4_.refs_5_
  749.0 122.6 %shard_map.240 = (f32[36,32,256]{2,1,0:T(8,128)}, bf16[3072,256]{1,0:T(8,128)(2,1)}, bf16[3072,256]{1,0:T(8,128)(2,1)}, bf16[3,512,512]{2,1,0:T(8,128)(2,1)}, bf16[256,1024]{1,0:T(8,128)(2,1)}) custom-call(bf16[6,512,512]{2,1,0:T(8,128)(2,1)} %get-tuple-element.48.refs_0_, bf16[256,1024]{1,0:T(8,128)(2,1)} %get-tuple-element.49.refs_1_, ...), custom_call_target="tpu_custom_call" | custom-call | tf_op jit(solution)/shard_map/pallas_call | solution.py:973
  871.5 156.9 %shard_map.241 = (f32[66,32,256]{2,1,0:T(8,128)}, f32[13568,256]{1,0:T(8,128)}) custom-call(bf16[3,512,512]{2,1,0:T(8,128)(2,1)} %get-tuple-element.61.refs_0_, bf16[256,1024]{1,0:T(8,128)(2,1)} %get-tuple-element.62.refs_1_, bf16[3072,256]{1,0:T(8,128)(2,1)} %get-tuple-element.63.refs_2_, bf16[3072,256]{1,0:T(8,128)(2,1)} %get-tuple-element.64.refs_3_, ...), custom_call_target="tpu_custom_call" | custom-call | tf_op jit(solution)/shard_map/pallas_call | solution.py:973
  1028.5 1.7 slice_bitcast_fusion.3
  1030.2 1.0 slice_bitcast_fusion.5
  1031.2 1.6 slice_reduce_fusion.1
  1032.8 0.9 fusion.7
  1033.7 0.7 slice_bitcast_fusion.6
  1034.4 1.3 copy.162
  1035.7 12.2 %bitcast_divide_fusion = f32[256,13500]{0,1:T(8,128)} fusion(bf16[256,13500]{0,1:T(8,128)(2,1)} %param.15, f32[13568,256]{1,0:T(8,128)} %get-tuple-element.68, f32[256]{0:T(256)S(1)} %copy-done.12), kind=kLoop, calls=%fused_computation | loop fusion | flops 17280000 | bytes 34562048 | tf_op jit(solution)/shard_map/div | solution.py:1205
  1047.8 0.8 copy.163
  1048.7 0.9 reshape_reshape.11
  1049.6 1.7 copy.156
  1051.3 2.2 copy.158
  1053.5 2.1 copy.153
  1055.6 2.1 reshape_reshape.10
  1057.7 2.1 copy.154
  1059.8 2.3 reshape.298
  1062.1 1.9 reshape_reshape.9
  1064.0 2.2 copy.152
  1066.2 2.4 reshape.297
  1068.6 2.0 slice_bitcast_fusion.1
  (57 shorter events, 0.7 us)
Async XLA Ops:
  0.6 11.4 %copy-start.8 = (bf16[128,1024]{1,0:T(8,128)(2,1)S(1)}, bf16[128,1024]{1,0:T(8,128)(2,1)}, u32[]{:S(2)}) copy-start(bf16[128,1024]{1,0:T(8,128)(2,1)} %param.26) | copy-start | bytes 786436
  0.7 12.5 %copy-start.9 = (bf16[32,4096]{1,0:T(8,128)(2,1)S(1)}, bf16[32,4096]{1,0:T(8,128)(2,1)}, u32[]{:S(2)}) copy-start(bf16[32,4096]{1,0:T(8,128)(2,1)} %param.25) | copy-start | bytes 786436
  1.5 12.8 %copy-start.11 = (bf16[32,1024]{1,0:T(8,128)(2,1)S(1)}, bf16[32,1024]{1,0:T(8,128)(2,1)}, u32[]{:S(2)}) copy-start(bf16[32,1024]{1,0:T(8,128)(2,1)} %param.22) | copy-start | bytes 196612
  1.8 12.8 %copy-start.2 = (s32[1024,1]{1,0:T(8,128)}, s32[1024,1]{1,0:T(8,128)S(1)}, u32[]{:S(2)}) copy-start(s32[1024,1]{1,0:T(8,128)S(1)} %convert_element_type.66.refs_12_.refs_5_) | copy-start | bytes 12292
  4.2 11.3 %copy-start.13 = (bf16[32]{0:T(256)(128)(2,1)S(1)}, bf16[32]{0:T(256)(128)(2,1)}, u32[]{:S(2)}) copy-start(bf16[32]{0:T(256)(128)(2,1)} %param.28) | copy-start | bytes 196
  4.3 11.3 %copy-start.14 = (bf16[32]{0:T(256)(128)(2,1)S(1)}, bf16[32]{0:T(256)(128)(2,1)}, u32[]{:S(2)}) copy-start(bf16[32]{0:T(256)(128)(2,1)} %param.27) | copy-start | bytes 196
  4.3 11.3 %copy-start.15 = (bf16[32]{0:T(256)(128)(2,1)S(1)}, bf16[32]{0:T(256)(128)(2,1)}, u32[]{:S(2)}) copy-start(bf16[32]{0:T(256)(128)(2,1)} %param.24) | copy-start | bytes 196
  4.3 11.2 %copy-start.16 = (bf16[32]{0:T(256)(128)(2,1)S(1)}, bf16[32]{0:T(256)(128)(2,1)}, u32[]{:S(2)}) copy-start(bf16[32]{0:T(256)(128)(2,1)} %param.23) | copy-start | bytes 196
  5.2 10.4 copy-start.10
  708.4 40.6 %collective-permute-start.1 = (bf16[1024,256]{1,0:T(8,128)(2,1)}, bf16[1024,256]{1,0:T(8,128)(2,1)}, u32[]{:S(2)}, u32[]{:S(2)}) collective-permute-start(bf16[1024,256]{1,0:T(8,128)(2,1)} %convert_element_type.67.refs_13_), channel_id=1, source_target_pairs={{0,1},{1,0},{2,3},{3,2},{4,5},{5,4},{6,7},{7,6},{8,9},{9,8},{10,11... | collective-permute-start | bytes 1572872 | tf_op jit(solution)/shard_map/ppermute | solution.py:45
  729.1 1.5 copy-start.3
  731.1 1.2 copy-start.4
  733.5 15.5 %collective-permute-start.2 = (bf16[1024,256]{1,0:T(8,128)(2,1)}, bf16[1024,256]{1,0:T(8,128)(2,1)}, u32[]{:S(2)}, u32[]{:S(2)}) collective-permute-start(bf16[1024,256]{1,0:T(8,128)(2,1)} %get-tuple-element.128.refs_15_), channel_id=1, source_target_pairs={{0,1},{1,0},{2,3},{3,2},{4,5},{5,4},{6,7},{7,6},{8,9},{9,8},{10,11... | collective-permute-start | bytes 1572872 | tf_op jit(solution)/shard_map/ppermute | solution.py:45
  734.0 15.0 %collective-permute-start = (bf16[4096,256]{1,0:T(8,128)(2,1)}, bf16[4096,256]{1,0:T(8,128)(2,1)}, u32[]{:S(2)}, u32[]{:S(2)}) collective-permute-start(bf16[4096,256]{1,0:T(8,128)(2,1)} %bitcast.39.refs_11_), channel_id=1, source_target_pairs={{0,1},{1,0},{2,3},{3,2},{4,5},{5,4},{6,7},{7,6},{8,9},{9,8},{10,11... | collective-permute-start | bytes 6291464 | tf_op jit(solution)/shard_map/ppermute | solution.py:45
  734.0 8.3 copy-start.5
  743.9 2.4 copy-start.6
  1028.5 4.3 copy-start.7
  1030.2 5.5 copy-start.12
  1051.3 17.3 %copy-start = (f32[53,4,8,256]{3,2,0,1:T(8,128)S(1)}, f32[53,4,8,256]{3,2,0,1:T(8,128)}, u32[]{:S(2)}) copy-start(f32[53,4,8,256]{3,2,0,1:T(8,128)} %copy.164) | copy-start | bytes 5210116
  1051.3 17.3 %copy-start.1 = (f32[53,4,8,256]{3,2,0,1:T(8,128)S(1)}, f32[53,4,8,256]{3,2,0,1:T(8,128)}, u32[]{:S(2)}) copy-start(f32[53,4,8,256]{3,2,0,1:T(8,128)} %copy.162) | copy-start | bytes 5210116

commit v13 on v12

--- a/solution.py
+++ b/solution.py
@@ -193,11 +193,11 @@
     counts, cot, tail, cot_tail, scale, pe, seg_keys, seg_mine = refs[n_arrays : n_arrays + 8]
     rest = refs[n_arrays + 8 :]
     wholes = rest[:n_arrays]
-    (xb, xb_other, cot_own, cot_other, pairs, lefts, left_one, left_last, h0, query, log_total, h1, slope,
-     act, hb) = rest[n_arrays : n_arrays + 15]
+    (xb, xb_other, cot_other, pairs, lefts, left_one, left_last, h0, query, log_total, h1, slope,
+     act, hb) = rest[n_arrays : n_arrays + 14]
     (a1, a2, plain, attended, turned, gains, perm, count_buf, enc_buf, xb_buf, total, qkv_buf, mine, pairs_buf, out_buf,
-     up_buf, down_buf, own_left, send_left, count_sem, enc_sem, xb_sem, fetch_sem, kv_sem, kv_send, kv_recv, cot_sem,
-     cot_send, cot_recv, left_sem, left_send, left_recv, *sems) = rest[n_arrays + 15 :]
+     up_buf, down_buf, own_left, send_left, count_sem, enc_sem, xb_sem, fetch_sem, kv_sem, kv_send, kv_recv,
+     cot_send, cot_recv, left_sem, left_send, left_recv, *sems) = rest[n_arrays + 14 :]
     y, c = lax.axis_index("y"), lax.axis_index("c")
     to_core = {"c": 1 - c}
     f32, b16 = jnp.float32, jnp.bfloat16
@@ -320,12 +320,9 @@
     def swap_cot(k):
         source = (cot.at[pl.ds(0, (n_chunks - 1) * CHUNK)], cot_tail)[k]
         place = pl.ds((n_chunks - 1) * CHUNK * k, ((n_chunks - 1) * CHUNK, CHUNK)[k])
-        return (
-            pltpu.make_async_copy(source, cot_own.at[place], cot_sem.at[k]),
-            pltpu.make_async_remote_copy(
-                src_ref=source, dst_ref=cot_other.at[place], send_sem=cot_send.at[k], recv_sem=cot_recv.at[k],
-                device_id=to_core, device_id_type=MESH,
-            ),
+        return pltpu.make_async_remote_copy(
+            src_ref=source, dst_ref=cot_other.at[place], send_sem=cot_send.at[k], recv_sem=cot_recv.at[k],
+            device_id=to_core, device_id_type=MESH,
         )
 
     def swap_xb():
@@ -432,8 +429,7 @@
     def between(step, landed):
         if step == 0:
             for k in (0, 1):
-                for copy in swap_cot(k):
-                    copy.start()
+                swap_cot(k).start()
         if step == 1:
             make_perm()
         if step - 3 in enc_jobs:
@@ -490,8 +486,7 @@
     kv_copy(0).wait_send()
     kv_copy(1).wait_send()
     for k in (0, 1):
-        for copy in swap_cot(k):
-            copy.wait()
+        swap_cot(k).wait()
     swap_xb().wait()
     for k in range(3):
         for copy in left_copies(k):
@@ -514,7 +509,7 @@
     bf16, f32 = jnp.bfloat16, jnp.float32
     vmem, hbm = pl.BlockSpec(memory_space=pltpu.VMEM), pl.BlockSpec(memory_space=pl.ANY)
     shape = jax.ShapeDtypeStruct
-    hbm_out = [shape((padded, cells), bf16)] * 4 + [shape((2, 2, cells, 2 * width), bf16)]
+    hbm_out = [shape((padded, cells), bf16)] * 3 + [shape((2, 2, cells, 2 * width), bf16)]
     hbm_out += [shape((k, half, 2 * cells), bf16) for k in (6, 1, 1)]
     vmem_out = [
         shape((cells, width), f32),
@@ -558,7 +553,6 @@
             dma((2,)),
             dma((2,)),
             dma((2,)),
-            dma((2,)),
             dma((3,)),
             dma((3,)),
             dma((3,)),
@@ -579,7 +573,7 @@
     return out[: len(shards)], *out[len(shards) :]
 
 
-def scatter_kernel(n_h, sections, periods, left_starts, lefts, rights, out, scratch, peers, prefetch, beside, after):
+def scatter_kernel(n_h, sections, periods, left_starts, lefts, rights, tail, out, scratch, peers, prefetch, beside, after):
     (right_buf, own, s1, r1, s2, r2, s3, r3, load_sem, send1, recv1, send2, recv2, send3, recv3) = scratch
     h, x, y = (lax.axis_index(name) for name in ("h", "x", "y"))
     to_x, to_y = {"x": 1 - x}, {"y": 1 - y}
@@ -592,11 +586,11 @@
     cells = right_buf.shape[2] // 2
     greet([{"h": lax.rem(h + d, n_h)} for d in range(1, n_h)] + [to_x, to_y] + peers)
 
-    def loads(i, section, k):
+    def loads(i, section, k, last=False):
         slot = lax.rem(i, 3)
         return [
             pltpu.make_async_copy(
-                rights[2 * section + half].at[chunk_of(k)],
+                tail if last and not half else rights[2 * section + half].at[chunk_of(k)],
                 right_buf.at[slot, :, pl.ds(half * cells, cells)],
                 load_sem.at[slot, half],
             )
@@ -608,8 +602,17 @@
 
             @pl.when((i >= start) & (i < start + count))
             def _(section=section, start=start):
-                for copy in loads(i, section, lax.rem(i - start, periods[section])):
-                    copy.start()
+                k = lax.rem(i - start, periods[section])
+                ends = [(False, k >= 0)]
+                if tail is not None:
+                    ends = [(False, k < periods[section] - 1), (True, k == periods[section] - 1)]
+                for last, here in ends:
+
+                    @pl.when(here)
+                    def _(last=last):
+                        for copy in loads(i, section, k, last):
+                            copy.start()
+
                 prefetch(section, i - start)
 
     def hop(i, source, target, send_sem, recv_sem, to):
@@ -729,6 +732,7 @@
     n_rights = 2 * len(sections)
     rights, weights = refs[2 : 2 + n_rights], refs[2 + n_rights : 2 + n_rights + n_weights]
     rest = refs[2 + n_rights + n_weights :]
+    tail, rest = (rest[0], rest[1:]) if with_sum else (None, rest)
     out, product = rest[:2]
     total_out = rest[2] if with_sum else None
     weight_buf, product_buf, weight_sem, product_sem, *scratch = rest[3 if with_sum else 2 :]
@@ -789,7 +793,7 @@
                 multiply(i - begin, right)
 
     scatter_kernel(
-        n_h, sections, periods, left_starts, lefts, rights, out, scratch, [], prefetch, beside, lambda p: None
+        n_h, sections, periods, left_starts, lefts, rights, tail, out, scratch, [], prefetch, beside, lambda p: None
     )
     for k in range(max(count - 2, 0), count):
         product_store(k).wait()
@@ -943,7 +947,7 @@
 
     n_chunk_pairs = (sum(sections) + 1) // 2
     scatter_kernel(
-        n_h, sections, periods, left_starts, lefts, rights, out, scratch, [{"c": 1 - c}],
+        n_h, sections, periods, left_starts, lefts, rights, None, out, scratch, [{"c": 1 - c}],
         lambda section, k: None, beside, after,
     )
     lefts_next[0] = left_one[...]
@@ -957,7 +961,7 @@
 
 
 def scatter_call(kernel, lefts, rights, operands, more_operands, out_shapes, out_specs, scratch, collective_id):
-    periods = [own.shape[0] // CHUNK for own, *_ in rights]
+    periods = [other.shape[0] // CHUNK for _, other, _ in rights]
     sections = [period * times for period, (*_, times) in zip(periods, rights)]
     n, cells = sum(sections), rights[0][0].shape[1]
     w = lefts.shape[1] // 4
@@ -1003,12 +1007,12 @@
 
 
 def scatter_product(lefts, left_starts, rights, vector, weights, product_type, with_sum, collective_id):
-    (cells, features), columns = vector.shape, rights[-1][0].shape[0]
+    (cells, features), columns = vector.shape, rights[-1][1].shape[0]
     dma = pltpu.SemaphoreType.DMA
     vmem, hbm = pl.BlockSpec(memory_space=pltpu.VMEM), pl.BlockSpec(memory_space=pl.ANY)
 
     def kernel(n_h, sections, periods, *refs):
-        product_kernel(n_h, sections, periods, left_starts, len(weights), with_sum, *refs)
+        product_kernel(n_h, sections, periods, left_starts, len(weights) - with_sum, with_sum, *refs)
 
     return scatter_call(
         kernel,
@@ -1131,7 +1135,7 @@
     cuts += [gene_cuts]
     order = [(0, 0), (0, 1), (0, 2), (0, 3), (1, 0), (1, 1), (2, 0), (3, 0), (3, 1), (4, 0), (4, 1)]
     order += [(5, 0), (5, 1), (5, 2), (5, 3)]
-    (gathered, xb, xb_other, cot, cot_other, kv_pairs, lefts, left_one, left_last, h0, query, log_total, h1, slope, _,
+    (gathered, xb, xb_other, cot_other, kv_pairs, lefts, left_one, left_last, h0, query, log_total, h1, slope, _,
      hb) = gather_all(
         shards, cuts, order, counts.T, cotangent.T, scale[None, :], pe.T, seg_all, att_scale, 0
     )
@@ -1141,7 +1145,7 @@
     vectors = qkv_all[:, 3 * width :].astype(jnp.float32).T
     g1f, b1f, g2f, b2f = vectors[0], vectors[1], vectors[2], vectors[3]
     grad_dec, logits, dh2 = scatter_product(
-        left_last, [0], [(cot, cot_other, 1)], hb, [dec_all], jnp.bfloat16, True, 1
+        left_last, [0], [(cotangent.T, cot_other, 1)], hb, [dec_all, gene_tail(cotangent.T)], jnp.bfloat16, True, 1
     )
     own_rows = grad_dec.shape[1]
     grad_dec = columns_of(grad_dec)[:, :genes].T

time: 1080 us -> 926 us (0.86)
  Pallas kernels: 966 us -> 815 us
    pallas_call x1, Pallas kernels: 543 us -> 402 us  [gather_all(): pl.pallas_call(functools.partial(front_kernel, n_h, jobs, len(shards), le...]
where the time goes in v13:
time: 926 us; the launch traced here: 920 us
  Pallas kernels  815 us (88%)
  local copies, waits for them, and re-layouts  61.9 us (7%)
  other arithmetic  23.4 us (3%)
  matrix products  16.4 us (2%)
    pallas_call x3, Pallas kernels, scatter_call(): pl.pallas_call(functools.partial(kernel, inner_h, sections, periods), out...  413 us
    pallas_call x1, Pallas kernels, gather_all(): pl.pallas_call(functools.partial(front_kernel, n_h, jobs, len(shards), le...  402 us
  transfers between devices with their start and end apart: 3, of which 0 were waited for; matrix products, arithmetic and copies ran while one was open for 4% of the time, Pallas kernels for 0%

profile of v13, /device:TPU:0, one launch (start us, length us, event | category | flops | bytes accessed | tf_op | source)
XLA Modules:
  0.0 919.7 jit_solution(15562957433985531200)
XLA Ops:
  1.5 0.3 copy.138
  1.8 0.7 slice_reduce_fusion
  2.6 0.8 slice_convert_fusion.1
  3.3 0.9 slice.93
  4.3 0.9 slice.92
  5.2 0.7 pad.27.refs_9_.refs_5_
  5.9 0.7 pad.26.refs_8_
  6.5 1.2 broadcast_divide_fusion
  7.8 2.1 pad.23.refs_0_
  9.9 2.1 pad.25.refs_5_
  12.0 0.2 copy.136
  12.2 0.9 copy.139.refs_4_
  13.1 0.2 reshape.280
  13.4 0.9 reshape.281.refs_3_
  14.2 0.2 reshape.278
  14.5 0.9 reshape.279.refs_2_
  15.6 0.7 fusion.4.refs_1_
  16.3 1.9 multiply_sine_fusion.1
  18.2 1.1 pad_maximum_fusion
  19.3 402.1 %shard_map.238 = (bf16[2,2,2,128,13568]{4,3,2,1,0:T(8,128)(2,1)}, bf16[2,2,2,128,3200]{4,3,2,1,0:T(8,128)(2,1)}, bf16[2,2,2,128,1024]{4,3,2,1,0:T(8,128)(2,1)}, ...) custom-call(bf16[32,13568]{1,0:T(8,128)(2,1)} %pad.23.refs_0_, ...), custom_call_target="tpu_custom_call" | custom-call | tf_op jit(solution)/shard_map/pallas_call | solution.py:524
  421.3 133.6 %shard_map.239 = (f32[53,32,256]{2,1,0:T(8,128)}, bf16[13568,256]{1,0:T(8,128)(2,1)}, f32[1024,256]{1,0:T(8,128)}) custom-call(bf16[1,512,512]{2,1,0:T(8,128)(2,1)} %get-tuple-element.41.refs_0_, bf16[256,1024]{1,0:T(8,128)(2,1)} %get-tuple-element.42.refs_1_, bf16[13500,256]{1,0:T(8,128)(2,1)} %bitcast.101, bf16[13568,256]{1,0:T(8,128)(2,1)} %get-tuple-element.43.refs_3_, ...), custom_call_target="tpu_custom_call" | custom-call | tf_op jit(solution)/shard_map/pallas_call | solution.py:977
  554.9 2.1 convert_element_type.68.refs_13_
  557.0 5.8 copy.141
  562.8 8.4 fusion
  571.3 6.4 fusion.9
  577.7 0.3 copy.143
  578.0 1.0 slice.95
  579.0 0.1 copy.161
  579.2 0.3 copy.144
  579.6 0.1 reduce_sum.51
  579.7 0.2 multiply_reduce_fusion.2
  580.0 0.5 multiply_reduce_fusion
  580.5 0.4 copy-done.4
  580.9 1.2 convert_bitcast_fusion.1
  582.1 0.5 collective-permute-start.2
  582.6 7.0 slice_bitcast_fusion
  589.6 1.3 copy.149.refs_8_
  590.9 1.6 convolution_convert_fusion
  592.5 1.4 copy.145
  593.9 1.0 copy.148.refs_3_
  595.0 1.3 copy.164
  596.3 0.6 select_maximum_fusion.refs_9_
  596.9 0.7 fusion.3.refs_4_.refs_5_
  597.6 122.9 %shard_map.240 = (f32[36,32,256]{2,1,0:T(8,128)}, bf16[3072,256]{1,0:T(8,128)(2,1)}, bf16[3072,256]{1,0:T(8,128)(2,1)}, bf16[3,512,512]{2,1,0:T(8,128)(2,1)}, bf16[256,1024]{1,0:T(8,128)(2,1)}) custom-call(bf16[6,512,512]{2,1,0:T(8,128)(2,1)} %get-tuple-element.46.refs_0_, bf16[256,1024]{1,0:T(8,128)(2,1)} %get-tuple-element.47.refs_1_, ...), custom_call_target="tpu_custom_call" | custom-call | tf_op jit(solution)/shard_map/pallas_call | solution.py:977
  720.5 156.9 %shard_map.241 = (f32[66,32,256]{2,1,0:T(8,128)}, f32[13568,256]{1,0:T(8,128)}) custom-call(bf16[3,512,512]{2,1,0:T(8,128)(2,1)} %get-tuple-element.59.refs_0_, bf16[256,1024]{1,0:T(8,128)(2,1)} %get-tuple-element.60.refs_1_, bf16[3072,256]{1,0:T(8,128)(2,1)} %get-tuple-element.61.refs_2_, bf16[3072,256]{1,0:T(8,128)(2,1)} %get-tuple-element.62.refs_3_, ...), custom_call_target="tpu_custom_call" | custom-call | tf_op jit(solution)/shard_map/pallas_call | solution.py:977
  877.5 1.7 slice_bitcast_fusion.3
  879.1 1.0 slice_bitcast_fusion.5
  880.2 1.6 slice_reduce_fusion.1
  881.8 0.9 fusion.7
  882.6 0.7 slice_bitcast_fusion.6
  883.3 1.3 copy.162
  884.6 12.2 %bitcast_divide_fusion = f32[256,13500]{0,1:T(8,128)} fusion(bf16[256,13500]{0,1:T(8,128)(2,1)} %param.15, f32[13568,256]{1,0:T(8,128)} %get-tuple-element.66, f32[256]{0:T(256)S(1)} %copy-done.12), kind=kLoop, calls=%fused_computation | loop fusion | flops 17280000 | bytes 34562048 | tf_op jit(solution)/shard_map/div | solution.py:1209
  896.8 0.8 copy.163
  897.6 0.9 reshape_reshape.11
  898.6 1.7 copy.156
  900.3 2.2 copy.158
  902.4 2.1 copy.153
  904.6 2.1 reshape_reshape.10
  906.7 2.1 copy.154
  908.8 2.3 reshape.298
  911.0 1.9 reshape_reshape.9
  913.0 2.2 copy.152
  915.2 2.4 reshape.297
  917.6 2.0 slice_bitcast_fusion.1
  (57 shorter events, 0.7 us)
Async XLA Ops:
  0.6 11.4 %copy-start.8 = (bf16[128,1024]{1,0:T(8,128)(2,1)S(1)}, bf16[128,1024]{1,0:T(8,128)(2,1)}, u32[]{:S(2)}) copy-start(bf16[128,1024]{1,0:T(8,128)(2,1)} %param.26) | copy-start | bytes 786436
  0.7 12.4 %copy-start.9 = (bf16[32,4096]{1,0:T(8,128)(2,1)S(1)}, bf16[32,4096]{1,0:T(8,128)(2,1)}, u32[]{:S(2)}) copy-start(bf16[32,4096]{1,0:T(8,128)(2,1)} %param.25) | copy-start | bytes 786436
  1.5 12.8 %copy-start.11 = (bf16[32,1024]{1,0:T(8,128)(2,1)S(1)}, bf16[32,1024]{1,0:T(8,128)(2,1)}, u32[]{:S(2)}) copy-start(bf16[32,1024]{1,0:T(8,128)(2,1)} %param.22) | copy-start | bytes 196612
  1.8 12.7 %copy-start.2 = (s32[1024,1]{1,0:T(8,128)}, s32[1024,1]{1,0:T(8,128)S(1)}, u32[]{:S(2)}) copy-start(s32[1024,1]{1,0:T(8,128)S(1)} %convert_element_type.67.refs_12_.refs_5_) | copy-start | bytes 12292
  4.2 11.2 %copy-start.13 = (bf16[32]{0:T(256)(128)(2,1)S(1)}, bf16[32]{0:T(256)(128)(2,1)}, u32[]{:S(2)}) copy-start(bf16[32]{0:T(256)(128)(2,1)} %param.28) | copy-start | bytes 196
  4.2 11.2 %copy-start.14 = (bf16[32]{0:T(256)(128)(2,1)S(1)}, bf16[32]{0:T(256)(128)(2,1)}, u32[]{:S(2)}) copy-start(bf16[32]{0:T(256)(128)(2,1)} %param.27) | copy-start | bytes 196
  4.2 11.2 %copy-start.15 = (bf16[32]{0:T(256)(128)(2,1)S(1)}, bf16[32]{0:T(256)(128)(2,1)}, u32[]{:S(2)}) copy-start(bf16[32]{0:T(256)(128)(2,1)} %param.24) | copy-start | bytes 196
  4.3 11.2 %copy-start.16 = (bf16[32]{0:T(256)(128)(2,1)S(1)}, bf16[32]{0:T(256)(128)(2,1)}, u32[]{:S(2)}) copy-start(bf16[32]{0:T(256)(128)(2,1)} %param.23) | copy-start | bytes 196
  5.2 10.4 %copy-start.10 = (bf16[32,3072]{1,0:T(8,128)(2,1)S(1)}, bf16[32,3072]{1,0:T(8,128)(2,1)}, u32[]{:S(2)}) copy-start(bf16[32,3072]{1,0:T(8,128)(2,1)} %param.21) | copy-start | bytes 589828
  557.0 40.6 %collective-permute-start.1 = (bf16[1024,256]{1,0:T(8,128)(2,1)}, bf16[1024,256]{1,0:T(8,128)(2,1)}, u32[]{:S(2)}, u32[]{:S(2)}) collective-permute-start(bf16[1024,256]{1,0:T(8,128)(2,1)} %convert_element_type.68.refs_13_), channel_id=1, source_target_pairs={{0,1},{1,0},{2,3},{3,2},{4,5},{5,4},{6,7},{7,6},{8,9},{9,8},{10,11... | collective-permute-start | bytes 1572872 | tf_op jit(solution)/shard_map/ppermute | solution.py:45
  577.7 1.5 copy-start.3
  579.7 1.2 copy-start.4
  582.1 15.5 %collective-permute-start.2 = (bf16[1024,256]{1,0:T(8,128)(2,1)}, bf16[1024,256]{1,0:T(8,128)(2,1)}, u32[]{:S(2)}, u32[]{:S(2)}) collective-permute-start(bf16[1024,256]{1,0:T(8,128)(2,1)} %get-tuple-element.126.refs_15_), channel_id=1, source_target_pairs={{0,1},{1,0},{2,3},{3,2},{4,5},{5,4},{6,7},{7,6},{8,9},{9,8},{10,11... | collective-permute-start | bytes 1572872 | tf_op jit(solution)/shard_map/ppermute | solution.py:45
  582.6 15.0 %collective-permute-start = (bf16[4096,256]{1,0:T(8,128)(2,1)}, bf16[4096,256]{1,0:T(8,128)(2,1)}, u32[]{:S(2)}, u32[]{:S(2)}) collective-permute-start(bf16[4096,256]{1,0:T(8,128)(2,1)} %bitcast.39.refs_11_), channel_id=1, source_target_pairs={{0,1},{1,0},{2,3},{3,2},{4,5},{5,4},{6,7},{7,6},{8,9},{9,8},{10,11... | collective-permute-start | bytes 6291464 | tf_op jit(solution)/shard_map/ppermute | solution.py:45
  582.6 8.3 copy-start.5
  592.5 2.5 copy-start.6
  877.4 4.3 copy-start.7
  879.1 5.5 copy-start.12
  900.2 17.3 %copy-start = (f32[53,4,8,256]{3,2,0,1:T(8,128)S(1)}, f32[53,4,8,256]{3,2,0,1:T(8,128)}, u32[]{:S(2)}) copy-start(f32[53,4,8,256]{3,2,0,1:T(8,128)} %copy.164) | copy-start | bytes 5210116
  900.2 17.3 %copy-start.1 = (f32[53,4,8,256]{3,2,0,1:T(8,128)S(1)}, f32[53,4,8,256]{3,2,0,1:T(8,128)}, u32[]{:S(2)}) copy-start(f32[53,4,8,256]{3,2,0,1:T(8,128)} %copy.162) | copy-start | bytes 5210116

commit v14 on v13

--- a/solution.py
+++ b/solution.py
@@ -384,7 +384,8 @@
         value = jnp.dot(a2[...], weight, preferred_element_type=f32)
         share = 0.5 * (1.0 + lax.erf(value * (0.5**0.5)))
         act[:, by_chunk(k)] = (value * share).astype(b16)
-        slope[:, by_chunk(k)] = share + value * jnp.exp(-0.5 * value * value) * (2.0 * math.pi) ** -0.5
+        steep = share + value * jnp.exp(-0.5 * value * value) * (2.0 * math.pi) ** -0.5
+        slope[by_chunk(k)] = steep.T
         return carry
 
     def narrow(k, carry):
@@ -501,7 +502,7 @@
     jobs = []
     for array, piece in order:
         low, high = cuts[array][piece], cuts[array][piece + 1]
-        jobs.append((array, low, high, low + (high - low) // 256 * 128))
+        jobs.append((array, low, high, low + (high - low) // (512 if array in (3, 4) else 256) * 128))
     n, others, dma = len(jobs), max(n_h - 1, 1), pltpu.SemaphoreType.DMA
     shapes = [(n_h * s.shape[0], s.shape[1]) for s in shards]
     (genes, cells), width, padded = counts.shape, pe.shape[0], shards[0].shape[1]
@@ -516,7 +517,7 @@
         shape((cells, width), bf16),
         shape((width // 64, cells), f32),
         shape((cells, width), f32),
-        shape((cells, 4 * width), f32),
+        shape((4 * width, cells), f32),
         shape((cells, 4 * width), bf16),
         shape((cells, width), bf16),
     ]
@@ -524,7 +525,7 @@
     out = pl.pallas_call(
         functools.partial(front_kernel, n_h, jobs, len(shards), len(shards), owners, scale_s),
         out_shape=[shape((2, 2, 2) + k, bf16) for k in shapes] + hbm_out + vmem_out,
-        in_specs=[hbm] * (len(shards) + 4) + [vmem] * 4,
+        in_specs=[vmem] * len(shards) + [hbm] * 4 + [vmem] * 4,
         out_specs=[hbm] * (len(shards) + len(hbm_out)) + [vmem] * len(vmem_out),
         scratch_shapes=[
             pltpu.VMEM((cells, width), bf16),
@@ -1154,7 +1155,7 @@
     dh2 = dh2.T
     dfb = dfb_turned.T
     d_act = contract_cols(dfb, down_all)
-    d_hidden = (d_act * slope).astype(jnp.bfloat16)
+    d_hidden = (d_act * slope.T).astype(jnp.bfloat16)
     da2 = contract_cols(d_hidden, up_all)
     norm_pull = jax.vjp(layer_norm, h1, g2f, b2f)[1]
     dh1_norm, grad_gain_two, grad_shift_two = norm_pull(da2)
@@ -1179,10 +1180,13 @@
     for columns in (4 * width, 4 * width, width):
         ends.append(ends[-1] + columns // CHUNK)
     grad_up, grad_down, grad_out = (grads[low:high] for low, high in zip(ends, ends[1:]))
-    grad_up, grad_out = columns_of(grad_up), columns_of(grad_out)
-    grad_down = grad_down.reshape(4, -1, own_rows, CHUNK).transpose(0, 2, 1, 3)
-    grad_down = grad_down.reshape(4 * own_rows, -1)
-    grad_out, grad_up, grad_down = (from_owner(g, 1) for g in (grad_out, grad_up, grad_down))
+    n_h = lax.axis_size("h")
+    by_half = (2, 2, 2, 2, own_rows, n_h // 2, -1)
+    grad_up = grad_up.reshape(by_half).transpose(4, 3, 5, 1, 2, 0, 6).reshape(own_rows, -1)
+    by_pair = (-1, 2, 2, own_rows, 2, n_h, width // (8 * n_h))
+    grad_out, grad_down = (
+        g.reshape(by_pair).transpose(0, 3, 5, 2, 4, 1, 6).reshape(-1, width) for g in (grad_out, grad_down)
+    )
     unit = jnp.eye(rows, dtype=jnp.bfloat16)
     grads, d_xb = scatter_product(
         lefts,

time: 926 us -> 908 us (0.981)
  Pallas kernels: 815 us -> 804 us
    reshape x1 -> x6, local copies, waits for them, and re-layouts: 0.04 us -> 14.2 us  [the longest x4 9.83 us: on_device(): g.reshape(by_pair).transpose(0, 3, 5, 2, 4, 1, 6).reshape(-1, width)]
    pallas_call x1, Pallas kernels: 402 us -> 391 us  [gather_all(): pl.pallas_call(functools.partial(front_kernel, n_h, jobs, len(shards), le...]
  transfers between devices with their start and end apart: 3 -> 3, of which waited for: 0 -> 0; matrix products, arithmetic and copies ran while one was open for 4% -> 3% of each run, Pallas kernels for 0% -> 0%
where the time goes in v14:
time: 908 us; the launch traced here: 902 us
  Pallas kernels  804 us (89%)
  local copies, waits for them, and re-layouts  58 us (6%)
  other arithmetic  23.8 us (3%)
  matrix products  12.7 us (1%)
    pallas_call x3, Pallas kernels, scatter_call(): pl.pallas_call(functools.partial(kernel, inner_h, sections, periods), out...  413 us
    pallas_call x1, Pallas kernels, gather_all(): pl.pallas_call(functools.partial(front_kernel, n_h, jobs, len(shards), le...  391 us
  transfers between devices with their start and end apart: 3, of which 0 were waited for; matrix products, arithmetic and copies ran while one was open for 3% of the time, Pallas kernels for 0%

profile of v14, /device:TPU:0, one launch (start us, length us, event | category | flops | bytes accessed | tf_op | source)
XLA Modules:
  0.0 901.5 jit_solution(1052155221828415815)
XLA Ops:
  1.5 0.3 copy.103
  1.8 0.8 slice_reduce_fusion
  2.6 0.8 slice_convert_fusion.1
  3.3 0.9 slice.93
  4.3 0.9 slice.92
  5.2 0.7 pad.27.refs_9_.refs_5_
  5.9 0.7 pad.26.refs_8_
  6.5 1.3 broadcast_divide_fusion
  7.8 2.1 pad.23.refs_0_
  9.9 2.1 pad.25.refs_5_
  12.1 0.2 copy.101
  12.3 0.9 copy.104.refs_4_
  13.1 0.2 reshape.286
  13.3 0.1 copy.129
  13.4 0.9 reshape.287.refs_3_
  14.3 0.2 reshape.284
  14.5 0.1 copy.130
  14.6 0.9 reshape.285.refs_2_
  15.6 0.7 fusion.7.refs_1_
  16.3 1.9 multiply_sine_fusion.1
  18.2 1.1 pad_maximum_fusion
  19.3 391.3 %shard_map.238 = (bf16[2,2,2,128,13568]{4,3,2,1,0:T(8,128)(2,1)}, bf16[2,2,2,128,3200]{4,3,2,1,0:T(8,128)(2,1)}, bf16[2,2,2,128,1024]{4,3,2,1,0:T(8,128)(2,1)}, ...) custom-call(bf16[32,13568]{1,0:T(8,128)(2,1)} %pad.23.refs_0_, ...), custom_call_target="tpu_custom_call" | custom-call | tf_op jit(solution)/shard_map/pallas_call | solution.py:525
  410.6 133.6 %shard_map.239 = (f32[53,32,256]{2,1,0:T(8,128)}, bf16[13568,256]{1,0:T(8,128)(2,1)}, f32[1024,256]{1,0:T(8,128)}) custom-call(bf16[1,512,512]{2,1,0:T(8,128)(2,1)} %get-tuple-element.41.refs_0_, bf16[256,1024]{1,0:T(8,128)(2,1)} %get-tuple-element.42.refs_1_, bf16[13500,256]{1,0:T(8,128)(2,1)} %bitcast.95, bf16[13568,256]{1,0:T(8,128)(2,1)} %get-tuple-element.43.refs_3_, ...), custom_call_target="tpu_custom_call" | custom-call | tf_op jit(solution)/shard_map/pallas_call | solution.py:978
  544.3 2.2 convert_element_type.71.refs_13_
  546.5 8.7 fusion
  555.2 2.4 fusion.12
  557.7 0.3 copy.107
  558.0 1.0 slice.95
  559.0 0.1 copy.123
  559.2 0.3 copy.108
  559.6 0.1 reduce_sum.51
  559.7 0.2 multiply_reduce_fusion.2
  560.0 0.5 multiply_reduce_fusion
  560.5 0.4 copy-done.5
  560.9 1.2 convert_bitcast_fusion.1
  562.1 0.5 collective-permute-start.2
  562.6 7.1 slice_bitcast_fusion
  569.7 1.3 copy.114.refs_8_
  571.0 1.6 convolution_convert_fusion
  572.6 1.4 copy.109
  574.0 1.0 copy.113.refs_3_
  575.0 1.3 copy.126
  576.4 0.6 select_maximum_fusion.refs_9_
  577.0 0.7 fusion.6.refs_4_.refs_5_
  577.7 122.7 %shard_map.240 = (f32[36,32,256]{2,1,0:T(8,128)}, bf16[3072,256]{1,0:T(8,128)(2,1)}, bf16[3072,256]{1,0:T(8,128)(2,1)}, bf16[3,512,512]{2,1,0:T(8,128)(2,1)}, bf16[256,1024]{1,0:T(8,128)(2,1)}) custom-call(bf16[6,512,512]{2,1,0:T(8,128)(2,1)} %get-tuple-element.46.refs_0_, bf16[256,1024]{1,0:T(8,128)(2,1)} %get-tuple-element.47.refs_1_, ...), custom_call_target="tpu_custom_call" | custom-call | tf_op jit(solution)/shard_map/pallas_call | solution.py:978
  700.4 156.8 %shard_map.241 = (f32[66,32,256]{2,1,0:T(8,128)}, f32[13568,256]{1,0:T(8,128)}) custom-call(bf16[3,512,512]{2,1,0:T(8,128)(2,1)} %get-tuple-element.59.refs_0_, bf16[256,1024]{1,0:T(8,128)(2,1)} %get-tuple-element.60.refs_1_, bf16[3072,256]{1,0:T(8,128)(2,1)} %get-tuple-element.61.refs_2_, bf16[3072,256]{1,0:T(8,128)(2,1)} %get-tuple-element.62.refs_3_, ...), custom_call_target="tpu_custom_call" | custom-call | tf_op jit(solution)/shard_map/pallas_call | solution.py:978
  857.3 1.7 slice_bitcast_fusion.3
  858.9 1.0 slice_bitcast_fusion.4
  860.0 1.7 slice_reduce_fusion.1
  861.6 0.9 fusion.10
  862.5 0.7 slice.84
  863.2 1.3 copy.124
  864.5 12.4 %bitcast_divide_fusion = f32[256,13500]{0,1:T(8,128)} fusion(bf16[256,13500]{0,1:T(8,128)(2,1)} %param.15, f32[13568,256]{1,0:T(8,128)} %get-tuple-element.66, f32[256]{0:T(256)S(1)} %copy-done.13), kind=kLoop, calls=%fused_computation | loop fusion | flops 17280000 | bytes 34562048 | tf_op jit(solution)/shard_map/div | solution.py:1213
  876.8 0.8 copy.125
  877.6 0.9 reshape.307
  878.6 3.0 copy.119
  881.5 4.6 reshape.308
  886.1 2.1 reshape.305
  888.2 2.2 copy.118
  890.5 2.3 reshape.306
  892.7 2.0 reshape.303
  894.7 2.2 copy.117
  896.9 2.4 reshape.304
  899.3 2.0 slice_bitcast_fusion.1
  (61 shorter events, 0.4 us)
Async XLA Ops:
  0.6 11.4 %copy-start.9 = (bf16[128,1024]{1,0:T(8,128)(2,1)S(1)}, bf16[128,1024]{1,0:T(8,128)(2,1)}, u32[]{:S(2)}) copy-start(bf16[128,1024]{1,0:T(8,128)(2,1)} %param.26) | copy-start | bytes 786436
  0.7 12.5 %copy-start.10 = (bf16[32,4096]{1,0:T(8,128)(2,1)S(1)}, bf16[32,4096]{1,0:T(8,128)(2,1)}, u32[]{:S(2)}) copy-start(bf16[32,4096]{1,0:T(8,128)(2,1)} %param.25) | copy-start | bytes 786436
  1.5 12.8 %copy-start.12 = (bf16[32,1024]{1,0:T(8,128)(2,1)S(1)}, bf16[32,1024]{1,0:T(8,128)(2,1)}, u32[]{:S(2)}) copy-start(bf16[32,1024]{1,0:T(8,128)(2,1)} %param.22) | copy-start | bytes 196612
  1.8 12.8 %copy-start.3 = (s32[1024,1]{1,0:T(8,128)}, s32[1024,1]{1,0:T(8,128)S(1)}, u32[]{:S(2)}) copy-start(s32[1024,1]{1,0:T(8,128)S(1)} %convert_element_type.70.refs_12_.refs_5_) | copy-start | bytes 12292
  4.2 11.3 %copy-start.14 = (bf16[32]{0:T(256)(128)(2,1)S(1)}, bf16[32]{0:T(256)(128)(2,1)}, u32[]{:S(2)}) copy-start(bf16[32]{0:T(256)(128)(2,1)} %param.28) | copy-start | bytes 196
  4.2 11.3 %copy-start.15 = (bf16[32]{0:T(256)(128)(2,1)S(1)}, bf16[32]{0:T(256)(128)(2,1)}, u32[]{:S(2)}) copy-start(bf16[32]{0:T(256)(128)(2,1)} %param.27) | copy-start | bytes 196
  4.3 11.3 %copy-start.16 = (bf16[32]{0:T(256)(128)(2,1)S(1)}, bf16[32]{0:T(256)(128)(2,1)}, u32[]{:S(2)}) copy-start(bf16[32]{0:T(256)(128)(2,1)} %param.24) | copy-start | bytes 196
  4.3 11.2 %copy-start.17 = (bf16[32]{0:T(256)(128)(2,1)S(1)}, bf16[32]{0:T(256)(128)(2,1)}, u32[]{:S(2)}) copy-start(bf16[32]{0:T(256)(128)(2,1)} %param.23) | copy-start | bytes 196
  5.2 10.4 %copy-start.11 = (bf16[32,3072]{1,0:T(8,128)(2,1)S(1)}, bf16[32,3072]{1,0:T(8,128)(2,1)}, u32[]{:S(2)}) copy-start(bf16[32,3072]{1,0:T(8,128)(2,1)} %param.21) | copy-start | bytes 589828
  544.3 11.0 %slice-start = ((s8[8388608]{0:T(1024)(128)(4,1)}), s8[4194304]{0:T(1024)(128)(4,1)S(1)}, s32[]{:S(2)}) async-start(s8[8388608]{0:T(1024)(128)(4,1)} %bitcast.99), calls=%async_computation | async-start | bytes 8388608
  546.5 31.2 %collective-permute-start.1 = (bf16[1024,256]{1,0:T(8,128)(2,1)}, bf16[1024,256]{1,0:T(8,128)(2,1)}, u32[]{:S(2)}, u32[]{:S(2)}) collective-permute-start(bf16[1024,256]{1,0:T(8,128)(2,1)} %convert_element_type.71.refs_13_), channel_id=1, source_target_pairs={{0,1},{1,0},{2,3},{3,2},{4,5},{5,4},{6,7},{7,6},{8,9},{9,8},{10,11... | collective-permute-start | bytes 1572872 | tf_op jit(solution)/shard_map/ppermute | solution.py:45
  546.5 8.7 copy-start
  546.5 8.7 slice-start.1
  557.7 1.5 copy-start.4
  559.7 1.2 copy-start.5
  562.1 15.5 %collective-permute-start.2 = (bf16[1024,256]{1,0:T(8,128)(2,1)}, bf16[1024,256]{1,0:T(8,128)(2,1)}, u32[]{:S(2)}, u32[]{:S(2)}) collective-permute-start(bf16[1024,256]{1,0:T(8,128)(2,1)} %get-tuple-element.78.refs_15_), channel_id=1, source_target_pairs={{0,1},{1,0},{2,3},{3,2},{4,5},{5,4},{6,7},{7,6},{8,9},{9,8},{10,11... | collective-permute-start | bytes 1572872 | tf_op jit(solution)/shard_map/ppermute | solution.py:45
  562.6 15.0 %collective-permute-start = (bf16[4096,256]{1,0:T(8,128)(2,1)}, bf16[4096,256]{1,0:T(8,128)(2,1)}, u32[]{:S(2)}, u32[]{:S(2)}) collective-permute-start(bf16[4096,256]{1,0:T(8,128)(2,1)} %get-tuple-element.96.refs_11_), channel_id=1, source_target_pairs={{0,1},{1,0},{2,3},{3,2},{4,5},{5,4},{6,7},{7,6},{8,9},{9,8},{10,11... | collective-permute-start | bytes 6291464 | tf_op jit(solution)/shard_map/ppermute | solution.py:45
  562.6 8.4 copy-start.6
  572.6 2.5 copy-start.7
  857.2 4.4 copy-start.8
  858.9 5.5 copy-start.13
  881.5 17.7 %copy-start.1 = (f32[53,4,8,256]{3,2,0,1:T(8,128)S(1)}, f32[53,4,8,256]{3,2,0,1:T(8,128)}, u32[]{:S(2)}) copy-start(f32[53,4,8,256]{3,2,0,1:T(8,128)} %copy.126) | copy-start | bytes 5210116
  881.5 17.7 %copy-start.2 = (f32[53,4,8,256]{3,2,0,1:T(8,128)S(1)}, f32[53,4,8,256]{3,2,0,1:T(8,128)}, u32[]{:S(2)}) copy-start(f32[53,4,8,256]{3,2,0,1:T(8,128)} %copy.124) | copy-start | bytes 5210116

commit v15 on v14

--- a/solution.py
+++ b/solution.py
@@ -800,11 +800,24 @@
         product_store(k).wait()
 
 
+def order_columns(target, chunks, first, n_h):
+    columns, rows = target.shape[1], chunks.shape[1]
+    block = columns // (8 * n_h)
+    for run in range(target.shape[0] // rows):
+        for k in range(8 * n_h):
+            at, h = k // n_h, k % n_h
+            place = (h * 8 + at // 2 % 2 * 4 + at % 2 * 2 + at // 4) * block
+            chunk, start = k * block // CHUNK, k * block % CHUNK
+            target[run * rows : (run + 1) * rows, place : place + block] = chunks[
+                first + run * columns // CHUNK + chunk, :, start : start + block
+            ]
+
+
 def attention_kernel(n_h, sections, periods, left_starts, scale, *refs):
     lefts, query, pairs, d_out, log_total, seg_keys, seg_mine, h0, dh1, vectors, left_one = refs[:11]
     n_rights = 2 * len(sections)
     rights, weight = refs[11 : 11 + n_rights], refs[11 + n_rights]
-    (out, turned_own, turned_other, lefts_next, dh0b, d_qkv, d_pairs, by_core, by_y, d_query, weight_buf, turned,
+    (out, turned_own, turned_other, lefts_next, dh0b, grad_up, grad_down, grad_out, d_qkv, d_pairs, by_core, by_y, d_query, weight_buf, turned,
      da1, vector_rows, send_left, got_left, send, recv, local, *scratch) = refs[12 + n_rights :]
     y, c = lax.axis_index("y"), lax.axis_index("c")
     f32, b16 = jnp.float32, jnp.bfloat16
@@ -955,6 +968,10 @@
     to_other_left().wait_recv()
     for kind in (0, 1):
         lefts_next[1 + kind, :, cells:] = got_left[kind]
+    if n_h > 1:
+        order_columns(grad_up, out, 0, n_h)
+        order_columns(grad_down, out, 4 * width // CHUNK, n_h)
+        order_columns(grad_out, out, 8 * width // CHUNK, n_h)
     keep_turned().wait()
     send_turned().wait()
     for copy in (to_core(), to_y(), to_other_left()):
@@ -1036,6 +1053,7 @@
 
 def scatter_attention(lefts, left_starts, rights, operands, weight, scale, collective_id):
     cells, width = operands[0].shape
+    own_rows = width // (8 * lax.axis_size("h"))
     bf16, f32, dma = jnp.bfloat16, jnp.float32, pltpu.SemaphoreType.DMA
     vmem, hbm = pl.BlockSpec(memory_space=pltpu.VMEM), pl.BlockSpec(memory_space=pl.ANY)
 
@@ -1053,8 +1071,11 @@
             jax.ShapeDtypeStruct((3 * width, cells), bf16),
             jax.ShapeDtypeStruct((3,) + lefts.shape[1:], bf16),
             jax.ShapeDtypeStruct((cells, width), bf16),
+            jax.ShapeDtypeStruct((own_rows, 4 * width), f32),
+            jax.ShapeDtypeStruct((4 * own_rows, width), f32),
+            jax.ShapeDtypeStruct((own_rows, width), f32),
         ],
-        [hbm, hbm, vmem, vmem],
+        [hbm, hbm, vmem, vmem, vmem, vmem, vmem],
         [
             pltpu.VMEM((cells, 3 * width), bf16),
             pltpu.VMEM((2, width // 128, 4 * cells, 128), bf16),
@@ -1167,7 +1188,7 @@
     rights = [both_cores(d_hidden.T), both_cores(dfb_turned, 4), both_cores(dab.T)]
     operands = [query, kv_pairs, d_attended, log_total, seg_all[:, None], seg_all[None, :rows], h0, dh1]
     operands += [jnp.pad(jnp.stack([g1f, grad_gain_two, grad_shift_two]), ((0, 5), (0, 0))), left_one[0]]
-    grads, d_qkv, d_qkv_other, lefts, dh0b = scatter_attention(
+    grads, d_qkv, d_qkv_other, lefts, dh0b, *ordered = scatter_attention(
         lefts,
         [sum(pieces[:k]) // CHUNK for k in range(len(pieces) + 1)],
         rights,
@@ -1176,17 +1197,20 @@
         att_scale,
         2,
     )
-    ends = [0]
-    for columns in (4 * width, 4 * width, width):
-        ends.append(ends[-1] + columns // CHUNK)
-    grad_up, grad_down, grad_out = (grads[low:high] for low, high in zip(ends, ends[1:]))
-    n_h = lax.axis_size("h")
-    by_half = (2, 2, 2, 2, own_rows, n_h // 2, -1)
-    grad_up = grad_up.reshape(by_half).transpose(4, 3, 5, 1, 2, 0, 6).reshape(own_rows, -1)
-    by_pair = (-1, 2, 2, own_rows, 2, n_h, width // (8 * n_h))
-    grad_out, grad_down = (
-        g.reshape(by_pair).transpose(0, 3, 5, 2, 4, 1, 6).reshape(-1, width) for g in (grad_out, grad_down)
-    )
+    if own_rows % 16 == 0:
+        grad_up, grad_down, grad_out = ordered
+    else:
+        ends = [0]
+        for columns in (4 * width, 4 * width, width):
+            ends.append(ends[-1] + columns // CHUNK)
+        grad_up, grad_down, grad_out = (grads[low:high] for low, high in zip(ends, ends[1:]))
+        n_h = lax.axis_size("h")
+        by_half = (2, 2, 2, 2, own_rows, n_h // 2, -1)
+        grad_up = grad_up.reshape(by_half).transpose(4, 3, 5, 1, 2, 0, 6).reshape(own_rows, -1)
+        by_pair = (-1, 2, 2, own_rows, 2, n_h, width // (8 * n_h))
+        grad_out, grad_down = (
+            g.reshape(by_pair).transpose(0, 3, 5, 2, 4, 1, 6).reshape(-1, width) for g in (grad_out, grad_down)
+        )
     unit = jnp.eye(rows, dtype=jnp.bfloat16)
     grads, d_xb = scatter_product(
         lefts,

time: 908 us -> 890 us (0.980)
  local copies, waits for them, and re-layouts: 58 us -> 35.6 us
    reshape x6 -> x0, local copies, waits for them, and re-layouts: 14.2 us -> none  [the longest x4 9.83 us: on_device(): g.reshape(by_pair).transpose(0, 3, 5, 2, 4, 1, 6).reshape(-1, width)]
  transfers between devices with their start and end apart: 3 -> 3, of which waited for: 0 -> 0; matrix products, arithmetic and copies ran while one was open for 3% -> 4% of each run, Pallas kernels for 0% -> 0%
where the time goes in v15:
time: 890 us; the launch traced here: 884 us
  Pallas kernels  806 us (91%)
  local copies, waits for them, and re-layouts  35.6 us (4%)
  other arithmetic  26 us (3%)
  matrix products  13.5 us (2%)
    pallas_call x3, Pallas kernels, scatter_call(): pl.pallas_call(functools.partial(kernel, inner_h, sections, periods), out...  415 us
    pallas_call x1, Pallas kernels, gather_all(): pl.pallas_call(functools.partial(front_kernel, n_h, jobs, len(shards), le...  391 us
  transfers between devices with their start and end apart: 3, of which 0 were waited for; matrix products, arithmetic and copies ran while one was open for 4% of the time, Pallas kernels for 0%

profile of v15, /device:TPU:0, one launch (start us, length us, event | category | flops | bytes accessed | tf_op | source)
XLA Modules:
  0.0 883.8 jit_solution(3631086389649208016)
XLA Ops:
  1.5 0.0 copy-start.10
  1.5 0.3 copy.94
  1.8 0.0 copy-start.1
  1.8 0.7 slice_reduce_fusion
  2.6 0.8 slice_convert_fusion.1
  3.3 0.9 slice.81
  4.2 0.0 copy-start.13
  4.2 0.0 copy-start.14
  4.2 0.0 copy-start.15
  4.3 0.9 slice.80
  5.2 0.7 pad.27.refs_9_.refs_5_
  5.9 0.7 pad.26.refs_8_
  6.5 1.2 broadcast_divide_fusion
  7.8 2.1 pad.23.refs_0_
  9.9 2.1 pad.25.refs_5_
  12.0 0.2 copy.92
  12.2 0.9 copy.95.refs_4_
  13.1 0.2 reshape.268
  13.3 0.1 copy.117
  13.4 0.9 reshape.269.refs_3_
  14.3 0.2 reshape.266
  14.4 0.1 copy.118
  14.6 0.9 reshape.267.refs_2_
  15.5 0.1 copy.89
  15.6 0.7 fusion.7.refs_1_
  16.3 1.9 multiply_sine_fusion.1
  18.2 1.1 pad_maximum_fusion
  19.3 391.4 %shard_map.238 = (bf16[2,2,2,128,13568]{4,3,2,1,0:T(8,128)(2,1)}, bf16[2,2,2,128,3200]{4,3,2,1,0:T(8,128)(2,1)}, bf16[2,2,2,128,1024]{4,3,2,1,0:T(8,128)(2,1)}, ...) custom-call(bf16[32,13568]{1,0:T(8,128)(2,1)} %pad.23.refs_0_, ...), custom_call_target="tpu_custom_call" | custom-call | tf_op jit(solution)/shard_map/pallas_call | solution.py:525
  410.6 133.6 %shard_map.239 = (f32[53,32,256]{2,1,0:T(8,128)}, bf16[13568,256]{1,0:T(8,128)(2,1)}, f32[1024,256]{1,0:T(8,128)}) custom-call(bf16[1,512,512]{2,1,0:T(8,128)(2,1)} %get-tuple-element.43.refs_0_, bf16[256,1024]{1,0:T(8,128)(2,1)} %get-tuple-element.44.refs_1_, bf16[13500,256]{1,0:T(8,128)(2,1)} %bitcast.92, bf16[13568,256]{1,0:T(8,128)(2,1)} %get-tuple-element.45.refs_3_, ...), custom_call_target="tpu_custom_call" | custom-call | tf_op jit(solution)/shard_map/pallas_call | solution.py:995
  544.3 0.0 slice-start
  544.3 2.2 convert_element_type.71.refs_13_
  546.5 8.7 fusion
  555.3 2.4 fusion.11
  557.7 0.3 copy.98
  558.1 1.0 slice.83
  559.0 0.1 copy.111
  559.3 1.6 copy.99
  560.8 1.4 reduce_sum.51
  562.2 0.2 multiply_reduce_fusion.2
  562.5 0.5 multiply_reduce_fusion
  563.0 2.4 convert_bitcast_fusion.1
  565.4 0.5 collective-permute-start.2
  565.9 7.2 slice_bitcast_fusion
  573.1 0.1 copy.114
  573.2 1.3 slice_bitcast_fusion.1
  574.5 1.3 copy.105.refs_8_
  575.8 2.3 convolution_convert_fusion
  578.2 0.2 copy.100
  578.4 1.0 copy.104.refs_3_
  579.4 0.6 select_maximum_fusion.refs_9_
  580.1 0.7 fusion.6.refs_4_.refs_5_
  580.8 0.8 copy-done.3
  581.5 123.2 %shard_map.240 = (f32[36,32,256]{2,1,0:T(8,128)}, bf16[3072,256]{1,0:T(8,128)(2,1)}, bf16[3072,256]{1,0:T(8,128)(2,1)}, bf16[3,512,512]{2,1,0:T(8,128)(2,1)}, bf...) custom-call(bf16[6,512,512]{2,1,0:T(8,128)(2,1)} %get-tuple-element.48.refs_0_, ...), custom_call_target="tpu_custom_call" | custom-call | tf_op jit(solution)/shard_map/pallas_call | solution.py:995
  704.7 157.7 %shard_map.241 = (f32[66,32,256]{2,1,0:T(8,128)}, f32[13568,256]{1,0:T(8,128)}) custom-call(bf16[3,512,512]{2,1,0:T(8,128)(2,1)} %get-tuple-element.61.refs_0_, bf16[256,1024]{1,0:T(8,128)(2,1)} %get-tuple-element.62.refs_1_, bf16[3072,256]{1,0:T(8,128)(2,1)} %get-tuple-element.63.refs_2_, bf16[3072,256]{1,0:T(8,128)(2,1)} %get-tuple-element.64.refs_3_, ...), custom_call_target="tpu_custom_call" | custom-call | tf_op jit(solution)/shard_map/pallas_call | solution.py:995
  862.4 1.6 slice_bitcast_fusion.3
  864.0 1.0 slice_bitcast_fusion.4
  865.1 1.6 slice_reduce_fusion.1
  866.7 12.2 %bitcast_divide_fusion = f32[256,13500]{0,1:T(8,128)} fusion(bf16[256,13500]{0,1:T(8,128)(2,1)} %param.15, f32[13568,256]{1,0:T(8,128)} %get-tuple-element.68, f32[256]{0:T(256)S(1)} %copy-done.11), kind=kLoop, calls=%fused_computation | loop fusion | flops 17280000 | bytes 34562048 | tf_op jit(solution)/shard_map/div | solution.py:1237
  878.9 0.1 copy.112
  879.0 1.3 slice_bitcast_fusion.2
  880.3 0.8 copy.113
  881.1 0.7 copy.123
  881.8 0.8 copy.124
  882.6 0.8 copy.125
  (50 shorter events, 0.3 us)
Async XLA Ops:
  0.6 11.4 %copy-start.6 = (bf16[128,1024]{1,0:T(8,128)(2,1)S(1)}, bf16[128,1024]{1,0:T(8,128)(2,1)}, u32[]{:S(2)}) copy-start(bf16[128,1024]{1,0:T(8,128)(2,1)} %param.26) | copy-start | bytes 786436
  0.7 12.4 %copy-start.7 = (bf16[32,4096]{1,0:T(8,128)(2,1)S(1)}, bf16[32,4096]{1,0:T(8,128)(2,1)}, u32[]{:S(2)}) copy-start(bf16[32,4096]{1,0:T(8,128)(2,1)} %param.25) | copy-start | bytes 786436
  1.5 12.8 %copy-start.10 = (bf16[32,1024]{1,0:T(8,128)(2,1)S(1)}, bf16[32,1024]{1,0:T(8,128)(2,1)}, u32[]{:S(2)}) copy-start(bf16[32,1024]{1,0:T(8,128)(2,1)} %param.22) | copy-start | bytes 196612
  1.8 12.7 %copy-start.1 = (s32[1024,1]{1,0:T(8,128)}, s32[1024,1]{1,0:T(8,128)S(1)}, u32[]{:S(2)}) copy-start(s32[1024,1]{1,0:T(8,128)S(1)} %convert_element_type.70.refs_12_.refs_5_) | copy-start | bytes 12292
  4.2 11.2 %copy-start.12 = (bf16[32]{0:T(256)(128)(2,1)S(1)}, bf16[32]{0:T(256)(128)(2,1)}, u32[]{:S(2)}) copy-start(bf16[32]{0:T(256)(128)(2,1)} %param.28) | copy-start | bytes 196
  4.2 11.2 %copy-start.13 = (bf16[32]{0:T(256)(128)(2,1)S(1)}, bf16[32]{0:T(256)(128)(2,1)}, u32[]{:S(2)}) copy-start(bf16[32]{0:T(256)(128)(2,1)} %param.27) | copy-start | bytes 196
  4.2 11.2 %copy-start.14 = (bf16[32]{0:T(256)(128)(2,1)S(1)}, bf16[32]{0:T(256)(128)(2,1)}, u32[]{:S(2)}) copy-start(bf16[32]{0:T(256)(128)(2,1)} %param.24) | copy-start | bytes 196
  4.2 11.2 %copy-start.15 = (bf16[32]{0:T(256)(128)(2,1)S(1)}, bf16[32]{0:T(256)(128)(2,1)}, u32[]{:S(2)}) copy-start(bf16[32]{0:T(256)(128)(2,1)} %param.23) | copy-start | bytes 196
  5.2 10.4 %copy-start.8 = (bf16[32,3072]{1,0:T(8,128)(2,1)S(1)}, bf16[32,3072]{1,0:T(8,128)(2,1)}, u32[]{:S(2)}) copy-start(bf16[32,3072]{1,0:T(8,128)(2,1)} %param.21) | copy-start | bytes 589828
  544.3 11.0 %slice-start = ((s8[8388608]{0:T(1024)(128)(4,1)}), s8[4194304]{0:T(1024)(128)(4,1)S(1)}, s32[]{:S(2)}) async-start(s8[8388608]{0:T(1024)(128)(4,1)} %bitcast.96), calls=%async_computation | async-start | bytes 8388608
  546.5 34.2 %collective-permute-start.1 = (bf16[1024,256]{1,0:T(8,128)(2,1)}, bf16[1024,256]{1,0:T(8,128)(2,1)}, u32[]{:S(2)}, u32[]{:S(2)}) collective-permute-start(bf16[1024,256]{1,0:T(8,128)(2,1)} %convert_element_type.71.refs_13_), channel_id=1, source_target_pairs={{0,1},{1,0},{2,3},{3,2},{4,5},{5,4},{6,7},{7,6},{8,9},{9,8},{10,11... | collective-permute-start | bytes 1572872 | tf_op jit(solution)/shard_map/ppermute | solution.py:45
  546.5 8.7 copy-start
  546.5 8.7 slice-start.1
  565.4 15.4 %collective-permute-start.2 = (bf16[1024,256]{1,0:T(8,128)(2,1)}, bf16[1024,256]{1,0:T(8,128)(2,1)S(1)}, u32[]{:S(2)}, u32[]{:S(2)}) collective-permute-start(bf16[1024,256]{1,0:T(8,128)(2,1)} %get-tuple-element.82.refs_15_), channel_id=1, source_target_pairs={{0,1},{1,0},{2,3},{3,2},{4,5},{5,4},{6,7},{7,6},{8,9},{9,8},{10,11... | collective-permute-start | bytes 1572872 | tf_op jit(solution)/shard_map/ppermute | solution.py:45
  565.9 14.9 %collective-permute-start = (bf16[4096,256]{1,0:T(8,128)(2,1)}, bf16[4096,256]{1,0:T(8,128)(2,1)}, u32[]{:S(2)}, u32[]{:S(2)}) collective-permute-start(bf16[4096,256]{1,0:T(8,128)(2,1)} %get-tuple-element.98.refs_11_), channel_id=1, source_target_pairs={{0,1},{1,0},{2,3},{3,2},{4,5},{5,4},{6,7},{7,6},{8,9},{9,8},{10,11... | collective-permute-start | bytes 6291464 | tf_op jit(solution)/shard_map/ppermute | solution.py:45
  565.9 7.2 copy-start.2
  580.7 0.8 copy-start.3
  862.4 4.3 copy-start.11
  878.9 2.2 copy-start.9
  878.9 2.9 copy-start.5
  878.9 3.7 copy-start.4

commit v16 on v15

--- a/solution.py
+++ b/solution.py
@@ -735,8 +735,8 @@
     rest = refs[2 + n_rights + n_weights :]
     tail, rest = (rest[0], rest[1:]) if with_sum else (None, rest)
     out, product = rest[:2]
-    total_out = rest[2] if with_sum else None
-    weight_buf, product_buf, weight_sem, product_sem, *scratch = rest[3 if with_sum else 2 :]
+    total_out, rounded = rest[2:4] if with_sum else (None, None)
+    weight_buf, product_buf, weight_sem, product_sem, *scratch = rest[4 if with_sum else 2 :]
     begin, count = sum(sections[:-1]), sections[-1]
     cells = vector.shape[0]
 
@@ -796,6 +796,8 @@
     scatter_kernel(
         n_h, sections, periods, left_starts, lefts, rights, tail, out, scratch, [], prefetch, beside, lambda p: None
     )
+    if with_sum:
+        rounded[...] = total_out[...].astype(rounded.dtype)
     for k in range(max(count - 2, 0), count):
         product_store(k).wait()
 
@@ -1039,8 +1041,8 @@
         [vector],
         weights,
         [jax.ShapeDtypeStruct((columns, cells), product_type)]
-        + [jax.ShapeDtypeStruct((features, cells), jnp.float32)] * with_sum,
-        [hbm] + [vmem] * with_sum,
+        + [jax.ShapeDtypeStruct((features, cells), kind) for kind in (jnp.float32, jnp.bfloat16)] * with_sum,
+        [hbm] + [vmem] * (2 * with_sum),
         [
             pltpu.VMEM((3, features, CHUNK), jnp.bfloat16),
             pltpu.VMEM((2, CHUNK, cells), product_type),
@@ -1166,13 +1168,12 @@
     )
     vectors = qkv_all[:, 3 * width :].astype(jnp.float32).T
     g1f, b1f, g2f, b2f = vectors[0], vectors[1], vectors[2], vectors[3]
-    grad_dec, logits, dh2 = scatter_product(
+    grad_dec, logits, dh2, dfb_turned = scatter_product(
         left_last, [0], [(cotangent.T, cot_other, 1)], hb, [dec_all, gene_tail(cotangent.T)], jnp.bfloat16, True, 1
     )
     own_rows = grad_dec.shape[1]
     grad_dec = columns_of(grad_dec)[:, :genes].T
     logits = logits[:genes].T
-    dfb_turned = dh2.astype(jnp.bfloat16)
     dh2 = dh2.T
     dfb = dfb_turned.T
     d_act = contract_cols(dfb, down_all)

time: 890 us -> 884 us (level)
  transfers between devices with their start and end apart: 3 -> 3, of which waited for: 0 -> 0; matrix products, arithmetic and copies ran while one was open for 4% -> 3% of each run, Pallas kernels for 0% -> 0%
where the time goes in v16:
time: 884 us; the launch traced here: 878 us
  Pallas kernels  806 us (91%)
  local copies, waits for them, and re-layouts  35 us (4%)
  other arithmetic  21.3 us (2%)
  matrix products  12.8 us (1%)
    pallas_call x3, Pallas kernels, scatter_call(): pl.pallas_call(functools.partial(kernel, inner_h, sections, periods), out...  415 us
    pallas_call x1, Pallas kernels, gather_all(): pl.pallas_call(functools.partial(front_kernel, n_h, jobs, len(shards), le...  391 us
  transfers between devices with their start and end apart: 3, of which 0 were waited for; matrix products, arithmetic and copies ran while one was open for 3% of the time, Pallas kernels for 0%

profile of v16, /device:TPU:0, one launch (start us, length us, event | category | flops | bytes accessed | tf_op | source)
XLA Modules:
  0.0 878.2 jit_solution(14313058472588482487)
XLA Ops:
  1.5 0.0 copy-start.13
  1.5 0.3 copy.94
  1.8 0.0 copy-start.2
  1.8 0.7 slice_reduce_fusion
  2.6 0.8 slice_convert_fusion.1
  3.3 0.9 slice.81
  4.2 0.0 copy-start.16
  4.2 0.0 copy-start.17
  4.2 0.0 copy-start.18
  4.3 0.9 slice.80
  5.2 0.7 pad.27.refs_9_.refs_5_
  5.8 0.7 pad.26.refs_8_
  6.5 1.2 broadcast_divide_fusion
  7.7 2.1 pad.23.refs_0_
  9.8 2.1 pad.25.refs_5_
  12.0 0.2 copy.92
  12.2 0.9 copy.95.refs_4_
  13.0 0.2 reshape.268
  13.2 0.1 copy.117
  13.3 0.9 reshape.269.refs_3_
  14.2 0.2 reshape.266
  14.4 0.1 copy.118
  14.5 0.9 reshape.267.refs_2_
  15.4 0.1 copy.89
  15.6 0.7 fusion.7.refs_1_
  16.2 1.9 multiply_sine_fusion.1
  18.1 1.1 pad_maximum_fusion
  19.2 391.4 %shard_map.238 = (bf16[2,2,2,128,13568]{4,3,2,1,0:T(8,128)(2,1)}, bf16[2,2,2,128,3200]{4,3,2,1,0:T(8,128)(2,1)}, bf16[2,2,2,128,1024]{4,3,2,1,0:T(8,128)(2,1)}, ...) custom-call(bf16[32,13568]{1,0:T(8,128)(2,1)} %pad.23.refs_0_, ...), custom_call_target="tpu_custom_call" | custom-call | tf_op jit(solution)/shard_map/pallas_call | solution.py:525
  410.6 133.9 %shard_map.239 = (f32[53,32,256]{2,1,0:T(8,128)}, bf16[13568,256]{1,0:T(8,128)(2,1)}, f32[1024,256]{1,0:T(8,128)}, bf16[1024,256]{1,0:T(8,128)(2,1)}) custom-call(bf16[1,512,512]{2,1,0:T(8,128)(2,1)} %get-tuple-element.44.refs_0_, bf16[256,1024]{1,0:T(8,128)(2,1)} %get-tuple-element.45.refs_1_, bf16[13500,256]{1,0:T(8,128)(2,1)} %bitcast.92, ...), custom_call_target="tpu_custom_call" | custom-call | tf_op jit(solution)/shard_map/pallas_call | solution.py:997
  544.5 0.1 collective-permute-start.1
  544.6 8.7 fusion
  553.4 2.4 fusion.11
  555.8 0.3 copy.98
  556.2 1.0 slice.83
  557.1 0.1 copy.111
  557.4 0.3 copy.99
  557.7 0.1 reduce_sum.51
  557.9 0.2 multiply_reduce_fusion.2
  558.1 0.5 multiply_reduce_fusion
  558.7 0.4 copy-done.6
  559.1 1.2 convert_bitcast_fusion.1
  560.2 0.5 collective-permute-start.2
  560.7 0.0 collective-permute-start
  560.8 7.2 slice_bitcast_fusion
  567.9 0.1 copy.114
  568.1 1.3 slice_bitcast_fusion.1
  569.4 1.3 copy.105.refs_8_
  570.7 1.6 convolution_convert_fusion
  572.2 1.2 copy.100
  573.5 1.0 copy.104.refs_3_
  574.5 0.6 select_maximum_fusion.refs_9_
  575.2 0.7 fusion.6.refs_4_.refs_5_
  575.9 123.2 %shard_map.240 = (f32[36,32,256]{2,1,0:T(8,128)}, bf16[3072,256]{1,0:T(8,128)(2,1)}, bf16[3072,256]{1,0:T(8,128)(2,1)}, bf16[3,512,512]{2,1,0:T(8,128)(2,1)}, bf...) custom-call(bf16[6,512,512]{2,1,0:T(8,128)(2,1)} %get-tuple-element.49.refs_0_, ...), custom_call_target="tpu_custom_call" | custom-call | tf_op jit(solution)/shard_map/pallas_call | solution.py:997
  699.1 157.8 %shard_map.241 = (f32[66,32,256]{2,1,0:T(8,128)}, f32[13568,256]{1,0:T(8,128)}) custom-call(bf16[3,512,512]{2,1,0:T(8,128)(2,1)} %get-tuple-element.63.refs_0_, bf16[256,1024]{1,0:T(8,128)(2,1)} %get-tuple-element.64.refs_1_, bf16[3072,256]{1,0:T(8,128)(2,1)} %get-tuple-element.65.refs_2_, bf16[3072,256]{1,0:T(8,128)(2,1)} %get-tuple-element.66.refs_3_, ...), custom_call_target="tpu_custom_call" | custom-call | tf_op jit(solution)/shard_map/pallas_call | solution.py:997
  856.9 1.6 slice_bitcast_fusion.3
  858.5 1.0 slice_bitcast_fusion.4
  859.5 1.6 slice_reduce_fusion.1
  861.1 12.2 %bitcast_divide_fusion = f32[256,13500]{0,1:T(8,128)} fusion(bf16[256,13500]{0,1:T(8,128)(2,1)} %param.15, f32[13568,256]{1,0:T(8,128)} %get-tuple-element.70, f32[256]{0:T(256)S(1)} %copy-done.14), kind=kLoop, calls=%fused_computation | loop fusion | flops 17280000 | bytes 34562048 | tf_op jit(solution)/shard_map/div | solution.py:1238
  873.3 0.1 copy.112
  873.5 1.3 slice_bitcast_fusion.2
  874.8 0.8 copy.113
  875.5 0.7 copy.123
  876.2 0.8 copy.124
  877.0 0.8 copy.125
  (50 shorter events, 0.3 us)
Async XLA Ops:
  0.6 11.3 %copy-start.9 = (bf16[128,1024]{1,0:T(8,128)(2,1)S(1)}, bf16[128,1024]{1,0:T(8,128)(2,1)}, u32[]{:S(2)}) copy-start(bf16[128,1024]{1,0:T(8,128)(2,1)} %param.26) | copy-start | bytes 786436
  0.7 12.4 %copy-start.10 = (bf16[32,4096]{1,0:T(8,128)(2,1)S(1)}, bf16[32,4096]{1,0:T(8,128)(2,1)}, u32[]{:S(2)}) copy-start(bf16[32,4096]{1,0:T(8,128)(2,1)} %param.25) | copy-start | bytes 786436
  1.5 12.7 %copy-start.13 = (bf16[32,1024]{1,0:T(8,128)(2,1)S(1)}, bf16[32,1024]{1,0:T(8,128)(2,1)}, u32[]{:S(2)}) copy-start(bf16[32,1024]{1,0:T(8,128)(2,1)} %param.22) | copy-start | bytes 196612
  1.8 12.7 %copy-start.2 = (s32[1024,1]{1,0:T(8,128)}, s32[1024,1]{1,0:T(8,128)S(1)}, u32[]{:S(2)}) copy-start(s32[1024,1]{1,0:T(8,128)S(1)} %convert_element_type.67.refs_12_.refs_5_) | copy-start | bytes 12292
  4.2 11.2 %copy-start.15 = (bf16[32]{0:T(256)(128)(2,1)S(1)}, bf16[32]{0:T(256)(128)(2,1)}, u32[]{:S(2)}) copy-start(bf16[32]{0:T(256)(128)(2,1)} %param.28) | copy-start | bytes 196
  4.2 11.2 %copy-start.16 = (bf16[32]{0:T(256)(128)(2,1)S(1)}, bf16[32]{0:T(256)(128)(2,1)}, u32[]{:S(2)}) copy-start(bf16[32]{0:T(256)(128)(2,1)} %param.27) | copy-start | bytes 196
  4.2 11.2 %copy-start.17 = (bf16[32]{0:T(256)(128)(2,1)S(1)}, bf16[32]{0:T(256)(128)(2,1)}, u32[]{:S(2)}) copy-start(bf16[32]{0:T(256)(128)(2,1)} %param.24) | copy-start | bytes 196
  4.2 11.2 %copy-start.18 = (bf16[32]{0:T(256)(128)(2,1)S(1)}, bf16[32]{0:T(256)(128)(2,1)}, u32[]{:S(2)}) copy-start(bf16[32]{0:T(256)(128)(2,1)} %param.23) | copy-start | bytes 196
  5.2 10.4 %copy-start.11 = (bf16[32,3072]{1,0:T(8,128)(2,1)S(1)}, bf16[32,3072]{1,0:T(8,128)(2,1)}, u32[]{:S(2)}) copy-start(bf16[32,3072]{1,0:T(8,128)(2,1)} %param.21) | copy-start | bytes 589828
  544.5 31.3 %collective-permute-start.1 = (bf16[1024,256]{1,0:T(8,128)(2,1)}, bf16[1024,256]{1,0:T(8,128)(2,1)}, u32[]{:S(2)}, u32[]{:S(2)}) collective-permute-start(bf16[1024,256]{1,0:T(8,128)(2,1)} %get-tuple-element.53.refs_13_), channel_id=1, source_target_pairs={{0,1},{1,0},{2,3},{3,2},{4,5},{5,4},{6,7},{7,6},{8,9},{9,8},{10,11... | collective-permute-start | bytes 1572872 | tf_op jit(solution)/shard_map/ppermute | solution.py:45
  544.6 8.8 copy-start
  544.6 8.8 copy-start.1
  555.8 1.5 copy-start.3
  557.8 1.2 copy-start.6
  560.2 15.6 %collective-permute-start.2 = (bf16[1024,256]{1,0:T(8,128)(2,1)}, bf16[1024,256]{1,0:T(8,128)(2,1)}, u32[]{:S(2)}, u32[]{:S(2)}) collective-permute-start(bf16[1024,256]{1,0:T(8,128)(2,1)} %get-tuple-element.84.refs_15_), channel_id=1, source_target_pairs={{0,1},{1,0},{2,3},{3,2},{4,5},{5,4},{6,7},{7,6},{8,9},{9,8},{10,11... | collective-permute-start | bytes 1572872 | tf_op jit(solution)/shard_map/ppermute | solution.py:45
  560.7 15.1 %collective-permute-start = (bf16[4096,256]{1,0:T(8,128)(2,1)}, bf16[4096,256]{1,0:T(8,128)(2,1)}, u32[]{:S(2)}, u32[]{:S(2)}) collective-permute-start(bf16[4096,256]{1,0:T(8,128)(2,1)} %get-tuple-element.100.refs_11_), channel_id=1, source_target_pairs={{0,1},{1,0},{2,3},{3,2},{4,5},{5,4},{6,7},{7,6},{8,9},{9,8},{10,11... | collective-permute-start | bytes 6291464 | tf_op jit(solution)/shard_map/ppermute | solution.py:45
  560.8 7.2 copy-start.5
  567.9 2.8 copy-start.4
  856.9 4.2 copy-start.14
  873.3 2.2 copy-start.12
  873.3 2.9 copy-start.8
  873.3 3.7 copy-start.7
